TPU v7x, 32 devices: a whole 2x2x4 slice. The times are simulated.
32 devices in a mesh: groups: 2 (over y), region: 4 (over z), feat: 2 (over x), sub: 2 (over core).
Axes of the slice: x: 2, y: 2, z: 4, core: 2. Of those that a mesh axis runs over, the one named last changes fastest.
Arguments:
- node_latent: bfloat16 [6144, 512], P(('groups', 'region', 'feat')), parts along dimension 0, may hold values from -6 to 6
- edge_latent: bfloat16 [49152, 512], P(('groups', 'region', 'feat', 'sub')), parts along dimension 0, may hold values from -6 to 6
- edge_source: int32 [49152], P(('groups', 'region', 'feat', 'sub')), parts along dimension 0, may hold values from 0 to 527, as said below
- receivers: int32 [49152], P(('groups', 'region', 'feat', 'sub')), parts along dimension 0, may hold values from 0 to 383
- near_rows: int32 [16, 4, 32], P(('groups', 'region', 'feat')), parts along dimension 0, may hold values from 0 to 383
- far_rows: int32 [16, 8, 2], P(('groups', 'region', 'feat')), parts along dimension 0, may hold values from 0 to 383
- edge_in_weight: bfloat16 [3, 512, 512], P(None, ('feat', 'sub')), may hold values from -0.15625 to 0.15625
- edge_out_weight: bfloat16 [512, 512], P(('feat', 'sub')), may hold values from -0.25 to 0.25
- node_in_weight: bfloat16 [2, 512, 512], P(None, ('feat', 'sub')), may hold values from -0.1875 to 0.1875
- node_out_weight: bfloat16 [512, 512], P(('feat', 'sub')), may hold values from -0.25 to 0.25
- edge_in_bias: float32 [512], replicated, may hold values from -4 to 4
- edge_out_bias: float32 [512], replicated, may hold values from -4 to 4
- edge_gain: float32 [512], replicated, may hold values from 0.5 to 1.5
- edge_offset: float32 [512], replicated, may hold values from -3 to 3
- node_in_bias: float32 [512], replicated, may hold values from -4 to 4
- node_out_bias: float32 [512], replicated, may hold values from -4 to 4
- node_gain: float32 [512], replicated, may hold values from 0.5 to 1.5
- node_offset: float32 [512], replicated, may hold values from -3 to 3
Outputs:
- edge_new: bfloat16 [49152, 512], P(('groups', 'region', 'feat', 'sub')), parts along dimension 0
- node_new: bfloat16 [6144, 512], P(('groups', 'region', 'feat')), parts along dimension 0
There are 2 independent parts, one for each index of `groups`. A program takes and returns all parts, laid end to end along the dimension named above; an argument that names none is the same for every part. Nothing has to cross between parts.
Inputs may be any that keep to these rules, and one draw needn't show every extreme that they name: `edge_source`: each partition's block of 3072 edges holds every halo slot value 384 to 527 at least once; the other values of the block are local nodes.
All inputs are finite; a program needn't handle non-finite values.
Results may differ from a plain program's by a relative error of at most 0.0051.
Values may be sent and summed in bfloat16 or wider, within the bound.
No kernel may reach another device: no remote copies, remote signals or barrier semaphores. Data moves between devices by JAX's collectives and lax.ppermute only.
A program may use at most 64 MiB of HBM per device.

v0:
```python
import jax
import jax.numpy as jnp
from jax import lax
from jax.sharding import PartitionSpec as P

near_offsets = (1, 2, -1, -2)


def layer_norm(values, gain, offset):
    average = jnp.mean(values, axis=-1, keepdims=True)
    centred = values - average
    spread = jnp.mean(centred * centred, axis=-1, keepdims=True)
    return centred * lax.rsqrt(spread + 1e-05) * gain + offset


def node_update(latent, summed, node_in, node_out, in_bias, out_bias, gain, offset):
    preact = jnp.dot(latent, node_in[0], preferred_element_type=jnp.float32)
    preact = (
        preact
        + jnp.dot(summed.astype(jnp.bfloat16), node_in[1], preferred_element_type=jnp.float32)
        + in_bias
    )
    hidden = jax.nn.silu(preact).astype(jnp.bfloat16)
    output = jnp.dot(hidden, node_out, preferred_element_type=jnp.float32) + out_bias
    return (latent.astype(jnp.float32) + layer_norm(output, gain, offset)).astype(jnp.bfloat16)


def shards(
    node_latent,
    edge_latent,
    edge_source,
    receivers,
    near_rows,
    far_rows,
    edge_in_weight,
    edge_out_weight,
    node_in_weight,
    node_out_weight,
    edge_in_bias,
    edge_out_bias,
    edge_gain,
    edge_offset,
    node_in_bias,
    node_out_bias,
    node_gain,
    node_offset,
):
    edge_in, edge_out, node_in, node_out = (
        lax.all_gather(edge_in_weight, ("feat", "sub"), axis=1, tiled=True),
        lax.all_gather(edge_out_weight, ("feat", "sub"), axis=0, tiled=True),
        lax.all_gather(node_in_weight, ("feat", "sub"), axis=1, tiled=True),
        lax.all_gather(node_out_weight, ("feat", "sub"), axis=0, tiled=True),
    )
    node_count = node_latent.shape[0]
    width = edge_in.shape[2]
    near_cap = near_rows.shape[2]
    far_cap = far_rows.shape[2]
    part_count = far_rows.shape[1]
    sender_proj = jnp.dot(node_latent, edge_in[1], preferred_element_type=jnp.float32).astype(
        jnp.bfloat16
    )
    recv_proj = jnp.dot(node_latent, edge_in[2], preferred_element_type=jnp.float32)
    near_send = jnp.take(sender_proj, near_rows[0], axis=0)
    far_send = jnp.take(sender_proj, far_rows[0], axis=0)
    edge_part = jnp.dot(edge_latent, edge_in[0], preferred_element_type=jnp.float32)
    my_place = lax.axis_index(("region", "feat"))
    send_slab = jnp.zeros((part_count, near_cap, width), jnp.bfloat16)
    for which, offset in enumerate(near_offsets):
        target = (my_place + offset) % part_count
        send_slab = lax.dynamic_update_slice_in_dim(send_slab, near_send[which][None], target, 0)
    combined = jnp.concatenate([send_slab, far_send], axis=1)
    arrived = lax.all_to_all(combined, ("region", "feat"), split_axis=0, concat_axis=0, tiled=True)
    near_parts = []
    for which, offset in enumerate(near_offsets):
        source_part = (my_place - offset) % part_count
        near_parts.append(
            lax.dynamic_index_in_dim(arrived, source_part, 0, keepdims=False)[:near_cap]
        )
    near_got = jnp.concatenate(near_parts, axis=0)
    far_got = arrived[:, near_cap:].reshape(part_count * far_cap, width)
    source_table = jnp.concatenate([sender_proj, near_got, far_got], axis=0)
    preact = edge_part + jnp.take(source_table, edge_source, axis=0).astype(jnp.float32)
    preact = preact + jnp.take(recv_proj, receivers, axis=0) + edge_in_bias
    hidden = jax.nn.silu(preact).astype(jnp.bfloat16)
    output = jnp.dot(hidden, edge_out, preferred_element_type=jnp.float32) + edge_out_bias
    edge_new = (
        edge_latent.astype(jnp.float32) + layer_norm(output, edge_gain, edge_offset)
    ).astype(jnp.bfloat16)
    one_hot = (receivers[None, :] == jnp.arange(node_count, dtype=jnp.int32)[:, None]).astype(
        jnp.bfloat16
    )
    partial_sums = jnp.dot(one_hot, edge_new, preferred_element_type=jnp.float32)
    summed = lax.psum(partial_sums, "sub")
    node_new = node_update(
        node_latent, summed, node_in, node_out, node_in_bias, node_out_bias, node_gain, node_offset
    )
    return (edge_new, node_new)


def solution(mesh):
    return jax.shard_map(
        shards,
        mesh=mesh,
        in_specs=(
            P(("groups", "region", "feat"), None),
            P(("groups", "region", "feat", "sub"), None),
            P(("groups", "region", "feat", "sub")),
            P(("groups", "region", "feat", "sub")),
            P(("groups", "region", "feat"), None, None),
            P(("groups", "region", "feat"), None, None),
            P(None, ("feat", "sub"), None),
            P(("feat", "sub"), None),
            P(None, ("feat", "sub"), None),
            P(("feat", "sub"), None),
            P(),
            P(),
            P(),
            P(),
            P(),
            P(),
            P(),
            P(),
        ),
        out_specs=(
            P(("groups", "region", "feat", "sub"), None),
            P(("groups", "region", "feat"), None),
        ),
        check_vma=False,
    )
```

profile of v0, /device:TPU:0, one launch (start us, length us, event | category | flops | bytes accessed | tf_op | source)
XLA Modules:
  0.0 96.3 jit_solution(8991313224457450266)
XLA Ops:
  11.4 0.7 compare_select_fusion
  12.1 0.7 compare_select_fusion.1
  12.8 0.7 compare_and_fusion
  13.9 11.5 %all_gather.13 = bf16[512,512]{1,0:T(8,128)(2,1)} all-gather(bf16[128,512]{1,0:T(8,128)(2,1)} %param.25), channel_id=1, replica_groups=mesh['groups'=2,'region'=4,'feat'=2,'sub'=2] {'feat','sub'}, dimensions={0}, use_global_device_ids=true | all-gather | bytes 655360 | tf_op jit(solution)/shard_map/all_gather | solution.py:50
  25.4 2.6 %copy.24 = bf16[1536,512]{0,1:T(8,128)(2,1)} copy(bf16[1536,512]{1,0:T(8,128)(2,1)} %param.19) | data formatting | bytes 3145728 | tf_op args[1]
  28.0 7.7 %all_gather.15 = bf16[512,512]{1,0:T(8,128)(2,1)} all-gather(bf16[128,512]{1,0:T(8,128)(2,1)S(1)} %copy-done.5), channel_id=1, replica_groups=mesh['groups'=2,'region'=4,'feat'=2,'sub'=2] {'feat','sub'}, dimensions={0}, use_global_device_ids=true | all-gather | bytes 655360 | tf_op jit(solution)/shard_map/all_gather | solution.py:52
  35.8 1.4 %constant_dynamic-update-slice_fusion.1 = (bf16[528,512]{1,0:T(8,128)(2,1)S(1)}, bf16[384,512]{1,0:T(8,128)(2,1)S(1)}) fusion(bf16[384,512]{1,0:T(8,128)(2,1)S(1)} %copy-done.2, bf16[3,512,512]{2,1,0:T(8,128)(2,1)} %all-gather.3.cloned.1.call-done), kind=kOutput, calls=%fused_computation.50 | convolution fusion | flops 201523200 | bytes 1703936 | tf_op jit(solution)/shard_map/dot_general | solution.py:59
  37.2 0.8 gather_fusion
  39.0 0.8 pad_maximum_fusion
  39.7 5.4 %all-to-all-start = ((bf16[8,34,512]{2,1,0:T(8,128)(2,1)}), bf16[8,34,512]{2,1,0:T(8,128)(2,1)S(1)}, u32[]{:S(2)}, u32[]{:S(2)}) async-start(bf16[8,34,512]{2,1,0:T(8,128)(2,1)} %pad_maximum_fusion), calls=%async_computation | async-start | bytes 655360 | tf_op jit(solution)/shard_map/all_to_all | solution.py:72
  45.1 8.7 %all-gather.5.cloned.1.call-done = bf16[2,512,512]{2,1,0:T(8,128)(2,1)} async-done(((bf16[2,128,512]{2,1,0:T(8,128)(2,1)}), bf16[2,512,512]{2,1,0:T(8,128)(2,1)}) %all-gather.5.cloned.1.call-update) | async-done | bytes 1048592 | tf_op jit(solution)/shard_map/all_gather | solution.py:51
  53.8 2.3 %fusion.6 = f32[384,512]{1,0:T(8,128)} fusion(bf16[384,512]{1,0:T(8,128)(2,1)S(1)} %copy-done.2, bf16[2,512,512]{2,1,0:T(8,128)(2,1)} %all-gather.5.cloned.1.call-done), kind=kOutput, calls=%fused_computation.24 | convolution fusion | flops 201326592 | bytes 1703936 | tf_op jit(solution)/shard_map/dot_general | solution.py:17
  56.1 1.4 %fusion.7 = f32[384,512]{1,0:T(8,128)S(1)} fusion(bf16[384,512]{1,0:T(8,128)(2,1)S(1)} %copy-done.2, bf16[3,512,512]{2,1,0:T(8,128)(2,1)} %all-gather.3.cloned.1.call-done), kind=kOutput, calls=%fused_computation.26 | convolution fusion | flops 201326592 | bytes 1703936 | tf_op jit(solution)/shard_map/dot_general | solution.py:62
  57.5 5.0 %gather_fusion.3 = f32[1536,512]{1,0:T(8,128)} fusion(f32[384,512]{1,0:T(8,128)S(1)} %fusion.7, s32[2048]{0:T(1024)S(1)} %get-tuple-element.12), kind=kCustom, calls=%fused_computation.3 | custom fusion | bytes 6297600 | tf_op jit(solution)/shard_map/jit(_take)/gather | solution.py:83
  62.6 5.4 %gather_fusion.2 = bf16[1536,512]{1,0:T(8,128)(2,1)} fusion(bf16[528,512]{1,0:T(8,128)(2,1)S(1)} %constant_dynamic-update-slice_fusion, s32[2048]{0:T(1024)S(1)} %get-tuple-element.13), kind=kCustom, calls=%fused_computation.2 | custom fusion | bytes 3151872 | tf_op jit(solution)/shard_map/jit(_take)/gather | solution.py:82
  68.0 5.8 %fusion.20 = (f32[1536]{0:T(1024)S(1)}, f32[1536,512]{0,1:T(8,128)S(1)}) fusion(f32[512]{0:T(512)} %param.29, bf16[512,512]{1,0:T(8,128)(2,1)} %all_gather.13, f32[1536,512]{1,0:T(8,128)} %gather_fusion.3, bf16[1536,512]{1,0:T(8,128)(2,1)} %param.19, f32[512]{0:T(512)} %param.28, bf16[1536,512]{1,0:T(8,128)(2,1)} %gather_fusion.2, ...), kind=kOutput, calls=%fused_computation.71 | convolution fusion | flops 1620834816 | bytes 10499072 | tf_op jit(solution)/shard_map/dot_general | solution.py:85
  74.2 0.9 copy-done
  75.2 0.7 add_convert_fusion
  75.9 1.2 %copy-done.1 = bf16[1536,512]{0,1:T(8,128)(2,1)} copy-done((bf16[1536,512]{0,1:T(8,128)(2,1)}, bf16[1536,512]{0,1:T(8,128)(2,1)S(1)}, u32[]{:S(2)}) %copy-start.1) | copy-done | bytes 1572888
  77.1 0.8 fusion.2
  78.0 2.7 %copy.27 = bf16[1536,512]{1,0:T(8,128)(2,1)} copy(bf16[1536,512]{0,1:T(8,128)(2,1)} %copy-done.1) | data formatting | bytes 3145728
  80.7 5.6 %all-reduce.1 = bf16[384,512]{1,0:T(8,128)(2,1)S(1)} all-reduce(f32[384,512]{1,0:T(8,128)S(1)} %fusion.2), channel_id=1, replica_groups=mesh['groups'=2,'region'=4,'feat'=2,'sub'=2] {'sub'}, use_global_device_ids=true, to_apply=%region_2.3 | all-reduce | flops 196608 | bytes 1179648 | tf_op jit(solution)/shard_map/psum | solution.py:93
  86.3 1.9 %fusion.21 = (f32[384]{0:T(512)S(1)}, f32[384,512]{1,0:T(8,128)S(1)}) fusion(f32[512]{0:T(512)S(1)} %copy-done.11, bf16[512,512]{1,0:T(8,128)(2,1)S(1)} %copy-done.4, f32[384,512]{1,0:T(8,128)S(1)} %copy-done.3, bf16[2,512,512]{2,1,0:T(8,128)(2,1)} %all-gather.5.cloned.1.call-done, f32[512]{0:T(512)S(1)} %copy-done.12, bf16[384,512]{1,0:T(8,128)(2,1)S(1)} %all-reduce.1), kind=kOutput, calls=%fused_computation.72 | convolution fusion | flops 404422272 | bytes 3020288 | tf_op jit(solution)/shard_map/dot_general | solution.py:24
  88.5 1.0 %add_convert_fusion.1 = bf16[384,512]{1,0:T(8,128)(2,1)} fusion(bf16[384,512]{1,0:T(8,128)(2,1)S(1)} %copy-done.2, f32[384,512]{1,0:T(8,128)S(1)} %get-tuple-element.11, f32[512]{0:T(512)S(1)} %copy-done.9, f32[512]{0:T(512)S(1)} %copy-done.10, f32[384]{0:T(512)S(1)} %add_rsqrt_fusion.1, f32[384]{0:T(512)S(1)} %broadcast_multiply_fusion.1), kind=kLoop, calls=%fused_computation.18 | loop fusion | flops 1376256 | bytes 1580032 | tf_op jit(solution)/shard_map/convert_element_type | solution.py:25
  (62 shorter events, 6.2 us)
Async XLA Ops:
  7.2 20.9 %copy-start.5 = (bf16[128,512]{1,0:T(8,128)(2,1)S(1)}, bf16[128,512]{1,0:T(8,128)(2,1)}, u32[]{:S(2)}) copy-start(bf16[128,512]{1,0:T(8,128)(2,1)} %param.27) | copy-start | bytes 393220
  7.2 28.6 %copy-start.2 = (bf16[384,512]{1,0:T(8,128)(2,1)S(1)}, bf16[384,512]{1,0:T(8,128)(2,1)}, u32[]{:S(2)}) copy-start(bf16[384,512]{1,0:T(8,128)(2,1)} %param.18) | copy-start | bytes 1179652
  7.2 28.6 %all-gather.3.cloned.1.call-start = ((), (), s32[]{:S(2)}) async-start(), calls=%async_computation.1 | async-start | bytes 1966080 | tf_op jit(solution)/shard_map/all_gather | solution.py:49
  7.9 45.8 %all-gather.5.cloned.1.call-start = ((), (), s32[]{:S(2)}) async-start(), calls=%async_computation.2 | async-start | bytes 1310720 | tf_op jit(solution)/shard_map/all_gather | solution.py:51
  39.7 22.7 %all-to-all-start = ((bf16[8,34,512]{2,1,0:T(8,128)(2,1)}), bf16[8,34,512]{2,1,0:T(8,128)(2,1)S(1)}, u32[]{:S(2)}, u32[]{:S(2)}) async-start(bf16[8,34,512]{2,1,0:T(8,128)(2,1)} %pad_maximum_fusion), calls=%async_computation | async-start | bytes 655360 | tf_op jit(solution)/shard_map/all_to_all | solution.py:72
  73.8 1.4 %copy-start = (bf16[1536,512]{0,1:T(8,128)(2,1)S(1)}, bf16[1536,512]{0,1:T(8,128)(2,1)}, u32[]{:S(2)}) copy-start(bf16[1536,512]{0,1:T(8,128)(2,1)} %copy.24) | copy-start | bytes 4718596
  73.8 1.4 %copy-start.7 = (f32[512]{0:T(512)S(1)}, f32[512]{0:T(512)}, u32[]{:S(2)}) copy-start(f32[512]{0:T(512)} %param.31) | copy-start | bytes 6148
  73.8 1.4 %copy-start.8 = (f32[512]{0:T(512)S(1)}, f32[512]{0:T(512)}, u32[]{:S(2)}) copy-start(f32[512]{0:T(512)} %param.30) | copy-start | bytes 6148
  75.2 1.9 %copy-start.6 = (s32[1536]{0:T(1024)S(1)}, s32[1536]{0:T(1024)}, u32[]{:S(2)}) copy-start(s32[1536]{0:T(1024)} %param.21) | copy-start | bytes 18436
  75.9 1.2 %copy-start.1 = (bf16[1536,512]{0,1:T(8,128)(2,1)}, bf16[1536,512]{0,1:T(8,128)(2,1)S(1)}, u32[]{:S(2)}) copy-start(bf16[1536,512]{0,1:T(8,128)(2,1)S(1)} %add_convert_fusion) | copy-start | bytes 4718596
  77.9 8.3 %copy-start.3 = (f32[384,512]{1,0:T(8,128)S(1)}, f32[384,512]{1,0:T(8,128)}, u32[]{:S(2)}) copy-start(f32[384,512]{1,0:T(8,128)} %fusion.6) | copy-start | bytes 2359300
  77.9 8.3 %copy-start.4 = (bf16[512,512]{1,0:T(8,128)(2,1)S(1)}, bf16[512,512]{1,0:T(8,128)(2,1)}, u32[]{:S(2)}) copy-start(bf16[512,512]{1,0:T(8,128)(2,1)} %all_gather.15) | copy-start | bytes 1572868
  77.9 8.3 %copy-start.11 = (f32[512]{0:T(512)S(1)}, f32[512]{0:T(512)}, u32[]{:S(2)}) copy-start(f32[512]{0:T(512)} %param.33) | copy-start | bytes 6148
  78.0 8.3 %copy-start.12 = (f32[512]{0:T(512)S(1)}, f32[512]{0:T(512)}, u32[]{:S(2)}) copy-start(f32[512]{0:T(512)} %param.32) | copy-start | bytes 6148
  86.3 2.2 %copy-start.9 = (f32[512]{0:T(512)S(1)}, f32[512]{0:T(512)}, u32[]{:S(2)}) copy-start(f32[512]{0:T(512)} %param.35) | copy-start | bytes 6148
  86.3 2.2 %copy-start.10 = (f32[512]{0:T(512)S(1)}, f32[512]{0:T(512)}, u32[]{:S(2)}) copy-start(f32[512]{0:T(512)} %param.34) | copy-start | bytes 6148
Sparse Core Ops, SparseCore 0:
  9.6 23.0 all-gather.2
  34.2 19.4 all-gather.4
where the time goes:
time: 97 us; the launch traced here: 96.3 us
  blocking collectives  24.9 us (26%)
  local copies, waits for them, and re-layouts  19.8 us (20%)
  between operations  14.4 us (15%)
  matrix products  13.6 us (14%)
  waiting for transfers between devices  10.1 us (10%)
  other arithmetic  8.23 us (8%)
  starting transfers between devices  5.43 us (6%)
    all_gather x1, blocking collectives, shards(): lax.all_gather(edge_out_weight, ('feat', 'sub'), axis=0, tiled=True)  11.5 us
    all_gather x1, waiting for transfers between devices, shards(): lax.all_gather(node_in_weight, ('feat', 'sub'), axis=1, tiled=True)  8.68 us
    all_gather x1, blocking collectives, shards(): lax.all_gather(node_out_weight, ('feat', 'sub'), axis=0, tiled=True)  7.73 us
    unnamed x32, local copies, waits for them, and re-layouts  7.48 us
    dot_general x1, matrix products, shards(): jnp.dot(hidden, edge_out, preferred_element_type=jnp.float32)  5.77 us
    psum x1, blocking collectives, shards(): summed = lax.psum(partial_sums, 'sub')  5.59 us
    gather x1, local copies, waits for them, and re-layouts, shards(): jnp.take(source_table, edge_source, axis=0).astype(jnp.float32)  5.43 us
    all_to_all x1, starting transfers between devices, shards(): lax.all_to_all(combined, ('region', 'feat'), split_axis=0, concat_axis=0,...  5.36 us
  transfers between devices with their start and end apart: 3, of which 1 were waited for; matrix products, arithmetic and copies ran while one was open for 21% of the time, Pallas kernels for 0%

commit v1 on v0

v1 whole, which is shorter than its diff:
```python
import functools

import jax
import jax.numpy as jnp
from jax import lax
from jax.experimental import pallas as pl
from jax.experimental.pallas import tpu as pltpu
from jax.sharding import PartitionSpec as P

near_offsets = (1, 2, -1, -2)
tile_rows = 16
lanes = 128
direct_parts = 8
bf16 = jnp.bfloat16
f32 = jnp.float32
vmem = pl.BlockSpec(memory_space=pltpu.VMEM)
smem = pl.BlockSpec(memory_space=pltpu.SMEM)


def wrap(value, count):
    return jnp.where(value < 0, value + count, value)


def as_columns(row):
    return jnp.transpose(jnp.broadcast_to(row, (lanes, row.shape[1])))


def one_hot(columns, width):
    place = lax.broadcasted_iota(jnp.int32, columns.shape, 1)
    return jnp.concatenate(
        [
            jnp.where(columns == place + start, 1.0, 0.0).astype(bf16)
            for start in range(0, width, lanes)
        ],
        axis=1,
    )


def silu(values):
    half = 0.5 * values
    return half + half * jnp.tanh(half)


def layer_norm(values, gain, offset):
    average = jnp.mean(values, axis=-1, keepdims=True)
    centred = values - average
    spread = jnp.mean(centred * centred, axis=-1, keepdims=True)
    return centred * lax.rsqrt(spread + 1e-05) * gain + offset


def pick_kernel(part_count, near_cap, far_cap, far_ref, near_ref, latent_ref, *out_refs):
    me = lax.axis_index("region") * lax.axis_size("feat") + lax.axis_index("feat")
    near = near_ref[...]
    row = jnp.concatenate([near[which : which + 1] for which in range(len(near_offsets))], axis=1)
    near_columns = as_columns(row)
    far_columns = jnp.full((part_count * tile_rows, lanes), -1, jnp.int32)
    row_place = lax.broadcasted_iota(jnp.int32, far_columns.shape, 0)
    for shift in range(part_count):
        target = lax.rem(me + shift, part_count)
        for slot in range(far_cap):
            far_columns = jnp.where(
                row_place == shift * tile_rows + slot,
                far_ref[target * far_cap + slot],
                far_columns,
            )
    hot = one_hot(jnp.concatenate([near_columns, far_columns], axis=0), latent_ref.shape[0])
    picked = jnp.dot(hot, latent_ref[...], preferred_element_type=f32).astype(bf16)
    far_start = len(near_offsets) * near_cap
    for shift in range(part_count):
        far = picked[far_start + shift * tile_rows : far_start + (shift + 1) * tile_rows]
        which = near_shift(shift, part_count)
        if which is None:
            out_refs[shift][...] = far
        else:
            out_refs[shift][:near_cap] = picked[which * near_cap : (which + 1) * near_cap]
            out_refs[shift][near_cap:] = far


def near_shift(shift, part_count):
    for which, offset in enumerate(near_offsets):
        if offset % part_count == shift:
            return which
    return None


def exchange_direct(node_latent, near_rows, far_rows, part_count):
    near_cap, far_cap = near_rows.shape[2], far_rows.shape[2]
    width = node_latent.shape[1]
    shapes = []
    for shift in range(part_count):
        rows = tile_rows if near_shift(shift, part_count) is None else near_cap + tile_rows
        shapes.append(jax.ShapeDtypeStruct((rows, width), bf16))
    blocks = pl.pallas_call(
        functools.partial(pick_kernel, part_count, near_cap, far_cap),
        out_shape=shapes,
        in_specs=[smem, vmem, vmem],
        out_specs=[vmem] * part_count,
        name="pick_halo",
    )(far_rows.reshape(-1), near_rows[0], node_latent)
    got = [blocks[0]]
    for shift in range(1, part_count):
        pairs = [(part, (part + shift) % part_count) for part in range(part_count)]
        got.append(lax.ppermute(blocks[shift], ("region", "feat"), pairs))
    return got


def exchange_all(node_latent, near_rows, far_rows, part_count):
    near_send = jnp.take(node_latent, near_rows[0], axis=0, mode="clip")
    far_send = jnp.take(node_latent, far_rows[0], axis=0, mode="clip")
    got = []
    for which, offset in enumerate(near_offsets):
        pairs = [(part, (part + offset) % part_count) for part in range(part_count)]
        got.append(lax.ppermute(near_send[which], ("region", "feat"), pairs))
    far = lax.all_to_all(far_send, ("region", "feat"), split_axis=0, concat_axis=0, tiled=True)
    got.append(far.reshape(-1, far.shape[2]))
    return got


def gather_kernel(
    part_count, near_cap, far_cap, by_shift, source_ref, receiver_ref, latent_ref, *refs
):
    got_refs, out_ref, table = refs[:-2], refs[-2], refs[-1]
    node_count, width = latent_ref.shape
    far_start = node_count + len(near_offsets) * near_cap

    @pl.when(pl.program_id(0) == 0)
    def _():
        table[:node_count] = latent_ref[...]
        if by_shift:
            for shift in range(part_count):
                which = near_shift(shift, part_count)
                start = 0
                if which is not None:
                    start = near_cap
                    place = node_count + which * near_cap
                    table[place : place + near_cap] = got_refs[shift][:near_cap]
                place = far_start + shift * tile_rows
                table[place : place + tile_rows] = got_refs[shift][start : start + tile_rows]
            used = far_start + part_count * tile_rows
        else:
            for which in range(len(near_offsets)):
                place = node_count + which * near_cap
                table[place : place + near_cap] = got_refs[which][...]
            used = far_start + got_refs[-1].shape[0]
            table[far_start:used] = got_refs[-1][...]
        if used < table.shape[0]:
            table[used:] = jnp.zeros((table.shape[0] - used, width), bf16)

    source = source_ref[0]
    if by_shift:
        me = lax.axis_index("region") * lax.axis_size("feat") + lax.axis_index("feat")
        far = source - far_start
        part = lax.div(far, far_cap)
        slot = far - part * far_cap
        shifted = far_start + wrap(me - part, part_count) * tile_rows + slot
        source = jnp.where(far >= 0, shifted, source)
    sent = one_hot(as_columns(source), table.shape[0])
    out_ref[:, :width] = jnp.dot(sent, table[...], preferred_element_type=f32).astype(bf16)
    received = one_hot(as_columns(receiver_ref[0]), node_count)
    out_ref[:, width:] = jnp.dot(
        received, latent_ref[...], preferred_element_type=f32
    ).astype(bf16)


def place_rows(whole, pieces, order):
    for piece, owner in zip(pieces, order):
        rows = piece.shape[-2]
        spot = pl.ds(pl.multiple_of(owner * rows, rows), rows)
        if len(whole.shape) == 3:
            whole[:, spot, :] = piece[...]
        else:
            whole[spot, :] = piece[...]


def owners():
    feat, feats = lax.axis_index("feat"), lax.axis_size("feat")
    sub, subs = lax.axis_index("sub"), lax.axis_size("sub")
    order = []
    for turn in range(subs):
        for shift in range(feats):
            order.append(
                wrap(feat - shift, feats) * subs + wrap(sub - turn, subs)
            )
    return order


def gather_rows(weight):
    feats, subs = lax.axis_size("feat"), lax.axis_size("sub")
    own = [weight]
    for shift in range(1, feats):
        own.append(lax.ppermute(weight, "feat", [(at, (at + shift) % feats) for at in range(feats)]))
    pieces = list(own)
    for turn in range(1, subs):
        pairs = [(at, (at + turn) % subs) for at in range(subs)]
        pieces += [lax.ppermute(piece, "sub", pairs) for piece in own]
    return pieces


def edge_kernel(pieces_count, *refs):
    edge_ref, gathered_ref, receiver_ref = refs[:3]
    in_pieces = refs[3 : 3 + pieces_count]
    out_pieces = refs[3 + pieces_count : 3 + 2 * pieces_count]
    in_bias, out_bias, gain, offset, new_ref, sum_ref, in_weight, out_weight, total = refs[
        3 + 2 * pieces_count :
    ]
    width = edge_ref.shape[1]
    step = pl.program_id(0)

    @pl.when(step == 0)
    def _():
        order = owners()
        place_rows(in_weight, in_pieces, order)
        place_rows(out_weight, out_pieces, order)

    edges = edge_ref[...]
    preact = jnp.dot(edges, in_weight[0], preferred_element_type=f32)
    preact += jnp.dot(gathered_ref[:, :width], in_weight[1], preferred_element_type=f32)
    preact += jnp.dot(gathered_ref[:, width:], in_weight[2], preferred_element_type=f32)
    hidden = silu(preact + in_bias[...]).astype(bf16)
    output = jnp.dot(hidden, out_weight[...], preferred_element_type=f32) + out_bias[...]
    edge_new = (edges.astype(f32) + layer_norm(output, gain[...], offset[...])).astype(bf16)
    new_ref[...] = edge_new
    receiver = receiver_ref[0]
    node_place = lax.broadcasted_iota(jnp.int32, (total.shape[0], receiver.shape[1]), 0)
    hot = jnp.where(node_place == receiver, 1.0, 0.0).astype(bf16)
    part = jnp.dot(hot, edge_new, preferred_element_type=f32)

    @pl.when(step == 0)
    def _():
        total[...] = part

    @pl.when(step > 0)
    def _():
        total[...] += part

    @pl.when(step == pl.num_programs(0) - 1)
    def _():
        sum_ref[...] = total[...].astype(bf16)


def node_kernel(pieces_count, *refs):
    latent_ref, own_ref, other_ref = refs[:3]
    in_pieces = refs[3 : 3 + pieces_count]
    out_pieces = refs[3 + pieces_count : 3 + 2 * pieces_count]
    in_bias, out_bias, gain, offset, new_ref, in_weight, out_weight = refs[3 + 2 * pieces_count :]
    order = owners()
    place_rows(in_weight, in_pieces, order)
    place_rows(out_weight, out_pieces, order)
    latent = latent_ref[...]
    summed = (own_ref[...].astype(f32) + other_ref[...].astype(f32)).astype(bf16)
    preact = jnp.dot(latent, in_weight[0], preferred_element_type=f32)
    preact += jnp.dot(summed, in_weight[1], preferred_element_type=f32)
    hidden = silu(preact + in_bias[...]).astype(bf16)
    output = jnp.dot(hidden, out_weight[...], preferred_element_type=f32) + out_bias[...]
    new_ref[...] = (
        latent.astype(f32) + layer_norm(output, gain[...], offset[...])
    ).astype(bf16)


def shards(
    node_latent,
    edge_latent,
    edge_source,
    receivers,
    near_rows,
    far_rows,
    edge_in_weight,
    edge_out_weight,
    node_in_weight,
    node_out_weight,
    edge_in_bias,
    edge_out_bias,
    edge_gain,
    edge_offset,
    node_in_bias,
    node_out_bias,
    node_gain,
    node_offset,
):
    node_count, width = node_latent.shape
    edge_count = edge_latent.shape[0]
    near_cap, far_cap = near_rows.shape[2], far_rows.shape[2]
    part_count = far_rows.shape[1]
    block = 512
    steps = edge_count // block

    edge_in = gather_rows(edge_in_weight)
    edge_out = gather_rows(edge_out_weight)
    node_in = gather_rows(node_in_weight)
    node_out = gather_rows(node_out_weight)
    pieces_count = len(edge_in)

    by_shift = part_count <= direct_parts
    exchange = exchange_direct if by_shift else exchange_all
    got = exchange(node_latent, near_rows, far_rows, part_count)
    far_space = part_count * tile_rows if by_shift else got[-1].shape[0]
    table_rows = node_count + len(near_offsets) * near_cap + far_space
    table_rows = -(-table_rows // lanes) * lanes

    source_blocks = edge_source.reshape(steps, 1, block)
    receiver_blocks = receivers.reshape(steps, 1, block)
    index_spec = pl.BlockSpec((1, 1, block), lambda step: (step, 0, 0))

    def whole(array):
        return pl.BlockSpec(array.shape, lambda step: (0,) * array.ndim)

    gathered = pl.pallas_call(
        functools.partial(gather_kernel, part_count, near_cap, far_cap, by_shift),
        grid=(steps,),
        out_shape=jax.ShapeDtypeStruct((edge_count, 2 * width), bf16),
        in_specs=[index_spec, index_spec, whole(node_latent)] + [whole(rows) for rows in got],
        out_specs=pl.BlockSpec((block, 2 * width), lambda step: (step, 0)),
        scratch_shapes=[pltpu.VMEM((table_rows, width), bf16)],
        cost_estimate=pl.CostEstimate(
            flops=2 * edge_count * width * (table_rows + node_count),
            bytes_accessed=4 * edge_count * width,
            transcendentals=0,
        ),
        name="gather_latents",
    )(source_blocks, receiver_blocks, node_latent, *got)

    rows = [value.reshape(1, -1) for value in (edge_in_bias, edge_out_bias, edge_gain, edge_offset)]
    edge_new, partial_sums = pl.pallas_call(
        functools.partial(edge_kernel, pieces_count),
        grid=(steps,),
        out_shape=[
            jax.ShapeDtypeStruct((edge_count, width), bf16),
            jax.ShapeDtypeStruct((node_count, width), bf16),
        ],
        in_specs=[
            pl.BlockSpec((block, width), lambda step: (step, 0)),
            pl.BlockSpec((block, 2 * width), lambda step: (step, 0)),
            index_spec,
        ]
        + [whole(piece) for piece in edge_in + edge_out]
        + [whole(row) for row in rows],
        out_specs=[
            pl.BlockSpec((block, width), lambda step: (step, 0)),
            pl.BlockSpec((node_count, width), lambda step: (0, 0)),
        ],
        scratch_shapes=[
            pltpu.VMEM((3, pieces_count * edge_in_weight.shape[1], width), bf16),
            pltpu.VMEM((pieces_count * edge_out_weight.shape[0], width), bf16),
            pltpu.VMEM((node_count, width), f32),
        ],
        compiler_params=pltpu.CompilerParams(vmem_limit_bytes=40 << 20),
        cost_estimate=pl.CostEstimate(
            flops=2 * edge_count * width * (4 * width + node_count),
            bytes_accessed=8 * edge_count * width,
            transcendentals=edge_count * width,
        ),
        name="edge_update",
    )(edge_latent, gathered, receiver_blocks, *edge_in, *edge_out, *rows)

    subs = lax.axis_size("sub")
    other_sums = lax.ppermute(partial_sums, "sub", [(at, (at + 1) % subs) for at in range(subs)])

    rows = [value.reshape(1, -1) for value in (node_in_bias, node_out_bias, node_gain, node_offset)]
    node_new = pl.pallas_call(
        functools.partial(node_kernel, pieces_count),
        out_shape=jax.ShapeDtypeStruct((node_count, width), bf16),
        in_specs=[vmem] * (3 + 2 * pieces_count + 4),
        out_specs=vmem,
        scratch_shapes=[
            pltpu.VMEM((2, pieces_count * node_in_weight.shape[1], width), bf16),
            pltpu.VMEM((pieces_count * node_out_weight.shape[0], width), bf16),
        ],
        compiler_params=pltpu.CompilerParams(vmem_limit_bytes=40 << 20),
        cost_estimate=pl.CostEstimate(
            flops=2 * node_count * width * 3 * width,
            bytes_accessed=10 * node_count * width,
            transcendentals=node_count * width,
        ),
        name="node_update",
    )(node_latent, partial_sums, other_sums, *node_in, *node_out, *rows)
    return (edge_new, node_new)


def solution(mesh):
    return jax.shard_map(
        shards,
        mesh=mesh,
        in_specs=(
            P(("groups", "region", "feat"), None),
            P(("groups", "region", "feat", "sub"), None),
            P(("groups", "region", "feat", "sub")),
            P(("groups", "region", "feat", "sub")),
            P(("groups", "region", "feat"), None, None),
            P(("groups", "region", "feat"), None, None),
            P(None, ("feat", "sub"), None),
            P(("feat", "sub"), None),
            P(None, ("feat", "sub"), None),
            P(("feat", "sub"), None),
            P(),
            P(),
            P(),
            P(),
            P(),
            P(),
            P(),
            P(),
        ),
        out_specs=(
            P(("groups", "region", "feat", "sub"), None),
            P(("groups", "region", "feat"), None),
        ),
        check_vma=False,
    )
```

time: 97 us -> 68.9 us (0.71)
  blocking collectives: 24.9 us -> 0 us
  Pallas kernels: 0 us -> 17.6 us
  starting transfers between devices: 5.43 us -> 19.3 us
  matrix products: 13.6 us -> 0 us
  between operations: 14.4 us -> 0.87 us
  waiting for transfers between devices: 10.1 us -> 22.8 us
  local copies, waits for them, and re-layouts: 19.8 us -> 7.91 us
  other arithmetic: 8.23 us -> 0 us
    ppermute x0 -> x20, waiting for transfers between devices: none -> 22.8 us  [the longest x4 14.1 us: gather_rows(): lax.ppermute(weight, 'feat', [(at, (at + shift) % feats) for at in range(...]
    ppermute x0 -> x20, starting transfers between devices: none -> 19.3 us  [the longest x7 11 us: exchange_direct(): got.append(lax.ppermute(blocks[shift], ('region', 'feat'), pairs))]
    all_gather x2 -> x0, blocking collectives: 19.3 us -> none  [the longest x1 11.5 us: shards(): lax.all_gather(edge_out_weight, ('feat', 'sub'), axis=0, tiled=True)]
    pallas_call x0 -> x4, Pallas kernels: none -> 17.6 us  [the longest x1 8.35 us: shards(): pl.pallas_call(functools.partial(edge_kernel, pieces_count), grid=(steps,...]
    dot_general x6 -> x0, matrix products: 13.6 us -> none  [the longest x1 5.77 us: shards(): jnp.dot(hidden, edge_out, preferred_element_type=jnp.float32)]
    gather x5 -> x0, local copies, waits for them, and re-layouts: 11.8 us -> none  [the longest x1 5.43 us: shards(): jnp.take(source_table, edge_source, axis=0).astype(jnp.float32)]
    all_gather x2 -> x0, waiting for transfers between devices: 8.7 us -> none  [the longest x1 8.68 us: shards(): lax.all_gather(node_in_weight, ('feat', 'sub'), axis=1, tiled=True)]
    psum x1 -> x0, blocking collectives: 5.59 us -> none  [shards(): summed = lax.psum(partial_sums, 'sub')]
  transfers between devices with their start and end apart: 3 -> 20, of which waited for: 1 -> 7; matrix products, arithmetic and copies ran while one was open for 21% -> 6% of each run, Pallas kernels for 0% -> 23%
where the time goes in v1:
time: 68.9 us; the launch traced here: 68.5 us
  waiting for transfers between devices  22.8 us (33%)
  starting transfers between devices  19.3 us (28%)
  Pallas kernels  17.6 us (26%)
  local copies, waits for them, and re-layouts  7.91 us (11%)
  between operations  0.87 us (1%)
    ppermute x4, waiting for transfers between devices, gather_rows(): lax.ppermute(weight, 'feat', [(at, (at + shift) % feats) for at in range(...  14.1 us
    ppermute x7, starting transfers between devices, exchange_direct(): got.append(lax.ppermute(blocks[shift], ('region', 'feat'), pairs))  11 us
    pallas_call x1, Pallas kernels, shards(): pl.pallas_call(functools.partial(edge_kernel, pieces_count), grid=(steps,...  8.35 us
    ppermute x7, waiting for transfers between devices, exchange_direct(): got.append(lax.ppermute(blocks[shift], ('region', 'feat'), pairs))  7.38 us
    ppermute x4, starting transfers between devices, gather_rows(): lax.ppermute(weight, 'feat', [(at, (at + shift) % feats) for at in range(...  7.11 us
    pallas_call x1, Pallas kernels, shards(): pl.pallas_call(functools.partial(gather_kernel, part_count, near_cap, far...  5.13 us
    unnamed x41, local copies, waits for them, and re-layouts  4.69 us
    pallas_call x1, Pallas kernels, exchange_direct(): pl.pallas_call(functools.partial(pick_kernel, part_count, near_cap, far_c...  2.09 us
  transfers between devices with their start and end apart: 20, of which 7 were waited for; matrix products, arithmetic and copies ran while one was open for 6% of the time, Pallas kernels for 23%

profile of v1, /device:TPU:0, one launch (start us, length us, event | category | flops | bytes accessed | tf_op | source)
XLA Modules:
  0.0 68.5 jit_solution(10294873702868209584)
XLA Ops:
  0.6 3.0 %collective-permute-start.7 = (bf16[3,128,512]{2,1,0:T(8,128)(2,1)}, bf16[3,128,512]{2,1,0:T(8,128)(2,1)S(1)}, u32[]{:S(2)}, u32[]{:S(2)}) collective-permute-start(bf16[3,128,512]{2,1,0:T(8,128)(2,1)} %refs_3_.2), channel_id=1, source_target_pairs={{0,2},{2,0},{1,3},{3,1},{4,6},{6,4},{5,7},{7,5},{8,10},{10,8},{9,1... | collective-permute-start | bytes 1179656 | tf_op jit(solution)/shard_map/ppermute | solution.py:191
  3.6 9.3 %collective-permute-done.7.refs_4_ = bf16[3,128,512]{2,1,0:T(8,128)(2,1)S(1)} collective-permute-done((bf16[3,128,512]{2,1,0:T(8,128)(2,1)}, bf16[3,128,512]{2,1,0:T(8,128)(2,1)S(1)}, u32[]{:S(2)}, u32[]{:S(2)}) %collective-permute-start.7) | collective-permute-done | bytes 393248 | tf_op jit(solution)/shard_map/ppermute | solution.py:191
  13.0 0.8 %copy.21 = s32[1,8,2]{2,1,0:T(8,128)S(1)} copy(s32[1,8,2]{1,2,0:T(2,128)} %param.23) | data formatting | bytes 128 | tf_op args[5]
  14.3 2.1 %pick_halo.1 = (bf16[16,512]{1,0:T(8,128)(2,1)}, bf16[48,512]{1,0:T(8,128)(2,1)}, bf16[48,512]{1,0:T(8,128)(2,1)}, bf16[16,512]{1,0:T(8,128)(2,1)}, bf16[16,512]...) custom-call(s32[16]{0:T(128)} %reshape.39.far_ref, ...), custom_call_target="tpu_custom_call" | custom-call | tf_op jit(solution)/shard_map/pick_halo/pallas_call | solution.py:93
  16.4 2.8 %collective-permute-start.2 = (bf16[16,512]{1,0:T(8,128)(2,1)}, bf16[16,512]{1,0:T(8,128)(2,1)S(1)}, u32[]{:S(2)}, u32[]{:S(2)}) collective-permute-start(bf16[16,512]{1,0:T(8,128)(2,1)} %get-tuple-element.15), channel_id=1, source_target_pairs={{0,6},{2,8},{4,10},{6,12},{8,14},{10,0},{12,2},{14,4},{1,7},{3,9},... | collective-permute-start | bytes 49160 | tf_op jit(solution)/shard_map/ppermute | solution.py:103
  19.2 1.5 %collective-permute-start.10 = (bf16[128,512]{1,0:T(8,128)(2,1)}, bf16[128,512]{1,0:T(8,128)(2,1)}, u32[]{:S(2)}, u32[]{:S(2)}) collective-permute-start(bf16[128,512]{1,0:T(8,128)(2,1)} %refs_7_.2), channel_id=1, source_target_pairs={{0,2},{2,0},{1,3},{3,1},{4,6},{6,4},{5,7},{7,5},{8,10},{10,8},{9,1... | collective-permute-start | bytes 393224 | tf_op jit(solution)/shard_map/ppermute | solution.py:191
  20.7 1.0 %collective-permute-start.3 = (bf16[16,512]{1,0:T(8,128)(2,1)}, bf16[16,512]{1,0:T(8,128)(2,1)S(1)}, u32[]{:S(2)}, u32[]{:S(2)}) collective-permute-start(bf16[16,512]{1,0:T(8,128)(2,1)} %get-tuple-element.16), channel_id=1, source_target_pairs={{0,8},{2,10},{4,12},{6,14},{8,0},{10,2},{12,4},{14,6},{1,9},{3,11}... | collective-permute-start | bytes 49160 | tf_op jit(solution)/shard_map/ppermute | solution.py:103
  22.2 2.9 %collective-permute-start.4 = (bf16[16,512]{1,0:T(8,128)(2,1)}, bf16[16,512]{1,0:T(8,128)(2,1)S(1)}, u32[]{:S(2)}, u32[]{:S(2)}) collective-permute-start(bf16[16,512]{1,0:T(8,128)(2,1)} %get-tuple-element.17), channel_id=1, source_target_pairs={{0,10},{2,12},{4,14},{6,0},{8,2},{10,4},{12,6},{14,8},{1,11},{3,13... | collective-permute-start | bytes 49160 | tf_op jit(solution)/shard_map/ppermute | solution.py:103
  25.1 0.7 collective-permute-done.3.refs_4_
  25.7 1.8 %collective-permute-start = (bf16[48,512]{1,0:T(8,128)(2,1)}, bf16[48,512]{1,0:T(8,128)(2,1)}, u32[]{:S(2)}, u32[]{:S(2)}) collective-permute-start(bf16[48,512]{1,0:T(8,128)(2,1)} %get-tuple-element.13), channel_id=1, source_target_pairs={{0,2},{2,4},{4,6},{6,8},{8,10},{10,12},{12,14},{14,0},{1,3},{3,5},... | collective-permute-start | bytes 147464 | tf_op jit(solution)/shard_map/ppermute | solution.py:103
  27.6 1.4 %collective-permute-start.1 = (bf16[48,512]{1,0:T(8,128)(2,1)}, bf16[48,512]{1,0:T(8,128)(2,1)}, u32[]{:S(2)}, u32[]{:S(2)}) collective-permute-start(bf16[48,512]{1,0:T(8,128)(2,1)} %get-tuple-element.14), channel_id=1, source_target_pairs={{0,4},{2,6},{4,8},{6,10},{8,12},{10,14},{12,0},{14,2},{1,5},{3,7},... | collective-permute-start | bytes 147464 | tf_op jit(solution)/shard_map/ppermute | solution.py:103
  29.0 3.9 %collective-permute-done.refs_1_ = bf16[48,512]{1,0:T(8,128)(2,1)} collective-permute-done((bf16[48,512]{1,0:T(8,128)(2,1)}, bf16[48,512]{1,0:T(8,128)(2,1)}, u32[]{:S(2)}, u32[]{:S(2)}) %collective-permute-start) | collective-permute-done | bytes 49184 | tf_op jit(solution)/shard_map/ppermute | solution.py:103
  32.9 2.3 %collective-permute-done.1.refs_2_ = bf16[48,512]{1,0:T(8,128)(2,1)} collective-permute-done((bf16[48,512]{1,0:T(8,128)(2,1)}, bf16[48,512]{1,0:T(8,128)(2,1)}, u32[]{:S(2)}, u32[]{:S(2)}) %collective-permute-start.1) | collective-permute-done | bytes 49184 | tf_op jit(solution)/shard_map/ppermute | solution.py:103
  35.2 1.2 %collective-permute-start.6 = (bf16[48,512]{1,0:T(8,128)(2,1)}, bf16[48,512]{1,0:T(8,128)(2,1)}, u32[]{:S(2)}, u32[]{:S(2)}) collective-permute-start(bf16[48,512]{1,0:T(8,128)(2,1)} %get-tuple-element.19), channel_id=1, source_target_pairs={{0,14},{2,0},{4,2},{6,4},{8,6},{10,8},{12,10},{14,12},{1,15},{3,1}... | collective-permute-start | bytes 147464 | tf_op jit(solution)/shard_map/ppermute | solution.py:103
  36.4 1.3 %reshape.38.receiver_ref.refs_2_ = s32[3,1,512]{2,1,0:T(1,128)} reshape(s32[1536]{0:T(1024)} %param.21) | data formatting | bytes 12288 | tf_op jit(solution)/shard_map/reshape | solution.py:301
  37.7 1.3 %reshape.37.source_ref = s32[3,1,512]{2,1,0:T(1,128)} reshape(s32[1536]{0:T(1024)} %param.20) | data formatting | bytes 12288 | tf_op jit(solution)/shard_map/reshape | solution.py:300
  39.7 2.6 %collective-permute-start.14 = (bf16[2,128,512]{2,1,0:T(8,128)(2,1)}, bf16[2,128,512]{2,1,0:T(8,128)(2,1)S(1)}, u32[]{:S(2)}, u32[]{:S(2)}) collective-permute-start(bf16[2,128,512]{2,1,0:T(8,128)(2,1)} %refs_3_.3), channel_id=1, source_target_pairs={{0,2},{2,0},{1,3},{3,1},{4,6},{6,4},{5,7},{7,5},{8,10},{10,8},{9,1... | collective-permute-start | bytes 786440 | tf_op jit(solution)/shard_map/ppermute | solution.py:191
  42.3 5.1 %gather_latents.1.refs_1_ = bf16[1536,1024]{1,0:T(8,128)(2,1)} custom-call(s32[3,1,512]{2,1,0:T(1,128)} %reshape.37.source_ref, s32[3,1,512]{2,1,0:T(1,128)} %reshape.38.receiver_ref.refs_2_, bf16[384,512]{1,0:T(8,128)(2,1)} %refs_0_.3, bf16[16,512]{1,0:T(8,128)(2,1)} %get-tuple-element.12.refs_0_, bf16[48,512]{1,0:T(8,128)(2,1)} %collective-permute-done.refs_1_, ...), custom_call_target="tpu_custom_call" | custom-call | flops 1610612736 | bytes 3145728 | tf_op jit(solution)/shard_map/gather_latents/pallas_call | solution.py:307
  48.2 0.7 copy-done.14
  48.9 1.9 %copy-done.15 = bf16[1536,1024]{1,0:T(8,128)(2,1)S(1)} copy-done((bf16[1536,1024]{1,0:T(8,128)(2,1)S(1)}, bf16[1536,1024]{1,0:T(8,128)(2,1)}, u32[]{:S(2)}) %copy-start.15) | copy-done | bytes 3145752
  50.8 8.3 %edge_update.1 = (bf16[1536,512]{1,0:T(8,128)(2,1)}, bf16[384,512]{1,0:T(8,128)(2,1)S(1)}) custom-call(bf16[1536,512]{1,0:T(8,128)(2,1)S(1)} %copy-done.8, bf16[1536,1024]{1,0:T(8,128)(2,1)S(1)} %copy-done.15, s32[3,1,512]{2,1,0:T(1,128)S(1)} %copy-done.3, bf16[3,128,512]{2,1,0:T(8,128)(2,1)S(1)} %copy-done.9, ...), custom_call_target="tpu_custom_call" | custom-call | flops 3825205248 | bytes 6291456 | tf_op jit(solution)/shard_map/edge_update/pallas_call | solution.py:323
  60.3 4.8 %collective-permute-done.17.refs_8_ = bf16[128,512]{1,0:T(8,128)(2,1)S(1)} collective-permute-done((bf16[128,512]{1,0:T(8,128)(2,1)S(1)}, bf16[128,512]{1,0:T(8,128)(2,1)S(1)}, u32[]{:S(2)}, u32[]{:S(2)}) %collective-permute-start.17) | collective-permute-done | bytes 131104 | tf_op jit(solution)/shard_map/ppermute | solution.py:191
  65.1 1.3 %collective-permute-done.19.refs_10_ = bf16[128,512]{1,0:T(8,128)(2,1)S(1)} collective-permute-done((bf16[128,512]{1,0:T(8,128)(2,1)S(1)}, bf16[128,512]{1,0:T(8,128)(2,1)S(1)}, u32[]{:S(2)}, u32[]{:S(2)}) %collective-permute-start.19) | collective-permute-done | bytes 131104 | tf_op jit(solution)/shard_map/ppermute | solution.py:195
  66.5 2.0 %node_update.1 = bf16[384,512]{1,0:T(8,128)(2,1)} custom-call(bf16[384,512]{1,0:T(8,128)(2,1)S(1)} %copy-done, bf16[384,512]{1,0:T(8,128)(2,1)S(1)} %get-tuple-element.21.refs_1_, bf16[384,512]{1,0:T(8,128)(2,1)S(1)} %collective-permute-done.13.refs_2_, bf16[2,128,512]{2,1,0:T(8,128)(2,1)S(1)} %copy-done.1, ...), custom_call_target="tpu_custom_call" | custom-call | flops 603979776 | bytes 1966080 | tf_op jit(solution)/shard_map/node_update/pallas_call | solution.py:359
  (64 shorter events, 3.6 us)
Async XLA Ops:
  0.6 12.3 %collective-permute-start.7 = (bf16[3,128,512]{2,1,0:T(8,128)(2,1)}, bf16[3,128,512]{2,1,0:T(8,128)(2,1)S(1)}, u32[]{:S(2)}, u32[]{:S(2)}) collective-permute-start(bf16[3,128,512]{2,1,0:T(8,128)(2,1)} %refs_3_.2), channel_id=1, source_target_pairs={{0,2},{2,0},{1,3},{3,1},{4,6},{6,4},{5,7},{7,5},{8,10},{10,8},{9,1... | collective-permute-start | bytes 1179656 | tf_op jit(solution)/shard_map/ppermute | solution.py:191
  3.6 43.8 %collective-permute-start.8 = (bf16[3,128,512]{2,1,0:T(8,128)(2,1)}, bf16[3,128,512]{2,1,0:T(8,128)(2,1)S(1)}, u32[]{:S(2)}, u32[]{:S(2)}) collective-permute-start(bf16[3,128,512]{2,1,0:T(8,128)(2,1)} %refs_3_.2), channel_id=1, source_target_pairs={{0,1},{1,0},{2,3},{3,2},{4,5},{5,4},{6,7},{7,6},{8,9},{9,8},{10,11... | collective-permute-start | bytes 1179656 | tf_op jit(solution)/shard_map/ppermute | solution.py:195
  13.0 34.5 %collective-permute-start.9 = (bf16[3,128,512]{2,1,0:T(8,128)(2,1)S(1)}, bf16[3,128,512]{2,1,0:T(8,128)(2,1)S(1)}, u32[]{:S(2)}, u32[]{:S(2)}) collective-permute-start(bf16[3,128,512]{2,1,0:T(8,128)(2,1)S(1)} %collective-permute-done.7.refs_4_), channel_id=1, source_target_pairs={{0,1},{1,0},{2,3},{3,2},{4,5},{5,4},{6,7},{7,6},{8,9},{9,8},{10,11... | collective-permute-start | bytes 1179656 | tf_op jit(solution)/shard_map/ppermute | solution.py:195
  16.4 5.7 %collective-permute-start.2 = (bf16[16,512]{1,0:T(8,128)(2,1)}, bf16[16,512]{1,0:T(8,128)(2,1)S(1)}, u32[]{:S(2)}, u32[]{:S(2)}) collective-permute-start(bf16[16,512]{1,0:T(8,128)(2,1)} %get-tuple-element.15), channel_id=1, source_target_pairs={{0,6},{2,8},{4,10},{6,12},{8,14},{10,0},{12,2},{14,4},{1,7},{3,9},... | collective-permute-start | bytes 49160 | tf_op jit(solution)/shard_map/ppermute | solution.py:103
  19.2 23.0 %collective-permute-start.10 = (bf16[128,512]{1,0:T(8,128)(2,1)}, bf16[128,512]{1,0:T(8,128)(2,1)}, u32[]{:S(2)}, u32[]{:S(2)}) collective-permute-start(bf16[128,512]{1,0:T(8,128)(2,1)} %refs_7_.2), channel_id=1, source_target_pairs={{0,2},{2,0},{1,3},{3,1},{4,6},{6,4},{5,7},{7,5},{8,10},{10,8},{9,1... | collective-permute-start | bytes 393224 | tf_op jit(solution)/shard_map/ppermute | solution.py:191
  20.7 5.0 %collective-permute-start.3 = (bf16[16,512]{1,0:T(8,128)(2,1)}, bf16[16,512]{1,0:T(8,128)(2,1)S(1)}, u32[]{:S(2)}, u32[]{:S(2)}) collective-permute-start(bf16[16,512]{1,0:T(8,128)(2,1)} %get-tuple-element.16), channel_id=1, source_target_pairs={{0,8},{2,10},{4,12},{6,14},{8,0},{10,2},{12,4},{14,6},{1,9},{3,11}... | collective-permute-start | bytes 49160 | tf_op jit(solution)/shard_map/ppermute | solution.py:103
  22.2 5.4 %collective-permute-start.4 = (bf16[16,512]{1,0:T(8,128)(2,1)}, bf16[16,512]{1,0:T(8,128)(2,1)S(1)}, u32[]{:S(2)}, u32[]{:S(2)}) collective-permute-start(bf16[16,512]{1,0:T(8,128)(2,1)} %get-tuple-element.17), channel_id=1, source_target_pairs={{0,10},{2,12},{4,14},{6,0},{8,2},{10,4},{12,6},{14,8},{1,11},{3,13... | collective-permute-start | bytes 49160 | tf_op jit(solution)/shard_map/ppermute | solution.py:103
  25.7 7.1 %collective-permute-start = (bf16[48,512]{1,0:T(8,128)(2,1)}, bf16[48,512]{1,0:T(8,128)(2,1)}, u32[]{:S(2)}, u32[]{:S(2)}) collective-permute-start(bf16[48,512]{1,0:T(8,128)(2,1)} %get-tuple-element.13), channel_id=1, source_target_pairs={{0,2},{2,4},{4,6},{6,8},{8,10},{10,12},{12,14},{14,0},{1,3},{3,5},... | collective-permute-start | bytes 147464 | tf_op jit(solution)/shard_map/ppermute | solution.py:103
  27.6 7.7 %collective-permute-start.1 = (bf16[48,512]{1,0:T(8,128)(2,1)}, bf16[48,512]{1,0:T(8,128)(2,1)}, u32[]{:S(2)}, u32[]{:S(2)}) collective-permute-start(bf16[48,512]{1,0:T(8,128)(2,1)} %get-tuple-element.14), channel_id=1, source_target_pairs={{0,4},{2,6},{4,8},{6,10},{8,12},{10,14},{12,0},{14,2},{1,5},{3,7},... | collective-permute-start | bytes 147464 | tf_op jit(solution)/shard_map/ppermute | solution.py:103
  32.9 6.1 %collective-permute-start.5 = (bf16[48,512]{1,0:T(8,128)(2,1)}, bf16[48,512]{1,0:T(8,128)(2,1)S(1)}, u32[]{:S(2)}, u32[]{:S(2)}) collective-permute-start(bf16[48,512]{1,0:T(8,128)(2,1)} %get-tuple-element.18), channel_id=1, source_target_pairs={{0,12},{2,14},{4,0},{6,2},{8,4},{10,6},{12,8},{14,10},{1,13},{3,15... | collective-permute-start | bytes 147464 | tf_op jit(solution)/shard_map/ppermute | solution.py:103
  35.2 4.4 %collective-permute-start.6 = (bf16[48,512]{1,0:T(8,128)(2,1)}, bf16[48,512]{1,0:T(8,128)(2,1)}, u32[]{:S(2)}, u32[]{:S(2)}) collective-permute-start(bf16[48,512]{1,0:T(8,128)(2,1)} %get-tuple-element.19), channel_id=1, source_target_pairs={{0,14},{2,0},{4,2},{6,4},{8,6},{10,8},{12,10},{14,12},{1,15},{3,1}... | collective-permute-start | bytes 147464 | tf_op jit(solution)/shard_map/ppermute | solution.py:103
  39.0 8.4 %collective-permute-start.11 = (bf16[128,512]{1,0:T(8,128)(2,1)}, bf16[128,512]{1,0:T(8,128)(2,1)}, u32[]{:S(2)}, u32[]{:S(2)}) collective-permute-start(bf16[128,512]{1,0:T(8,128)(2,1)} %refs_7_.2), channel_id=1, source_target_pairs={{0,1},{1,0},{2,3},{3,2},{4,5},{5,4},{6,7},{7,6},{8,9},{9,8},{10,11... | collective-permute-start | bytes 393224 | tf_op jit(solution)/shard_map/ppermute | solution.py:195
  39.7 20.1 %collective-permute-start.14 = (bf16[2,128,512]{2,1,0:T(8,128)(2,1)}, bf16[2,128,512]{2,1,0:T(8,128)(2,1)S(1)}, u32[]{:S(2)}, u32[]{:S(2)}) collective-permute-start(bf16[2,128,512]{2,1,0:T(8,128)(2,1)} %refs_3_.3), channel_id=1, source_target_pairs={{0,2},{2,0},{1,3},{3,1},{4,6},{6,4},{5,7},{7,5},{8,10},{10,8},{9,1... | collective-permute-start | bytes 786440 | tf_op jit(solution)/shard_map/ppermute | solution.py:191
  42.2 5.2 %collective-permute-start.12 = (bf16[128,512]{1,0:T(8,128)(2,1)}, bf16[128,512]{1,0:T(8,128)(2,1)}, u32[]{:S(2)}, u32[]{:S(2)}) collective-permute-start(bf16[128,512]{1,0:T(8,128)(2,1)} %collective-permute-done.10.refs_8_), channel_id=1, source_target_pairs={{0,1},{1,0},{2,3},{3,2},{4,5},{5,4},{6,7},{7,6},{8,9},{9,8},{10,11... | collective-permute-start | bytes 393224 | tf_op jit(solution)/shard_map/ppermute | solution.py:195
  50.8 15.7 %copy-start.4 = (f32[512]{0:T(512)S(1)}, f32[512]{0:T(512)}, u32[]{:S(2)}) copy-start(f32[512]{0:T(512)} %param.32) | copy-start | bytes 6148
  50.8 15.7 %copy-start.5 = (f32[512]{0:T(512)S(1)}, f32[512]{0:T(512)}, u32[]{:S(2)}) copy-start(f32[512]{0:T(512)} %param.33) | copy-start | bytes 6148
  50.8 15.7 %copy-start.6 = (f32[512]{0:T(512)S(1)}, f32[512]{0:T(512)}, u32[]{:S(2)}) copy-start(f32[512]{0:T(512)} %param.34) | copy-start | bytes 6148
  50.8 15.7 %copy-start.7 = (f32[512]{0:T(512)S(1)}, f32[512]{0:T(512)}, u32[]{:S(2)}) copy-start(f32[512]{0:T(512)} %param.35) | copy-start | bytes 6148
  59.2 7.3 %collective-permute-start.13 = (bf16[384,512]{1,0:T(8,128)(2,1)S(1)}, bf16[384,512]{1,0:T(8,128)(2,1)S(1)}, u32[]{:S(2)}, u32[]{:S(2)}) collective-permute-start(bf16[384,512]{1,0:T(8,128)(2,1)S(1)} %get-tuple-element.21.refs_1_), channel_id=1, source_target_pairs={{0,1},{1,0},{2,3},{3,2},{4,5},{5,4},{6,7},{7,6},{8,9},{9,8},{10,11... | collective-permute-start | bytes 1179656 | tf_op jit(solution)/shard_map/ppermute | solution.py:356
  59.6 5.4 %collective-permute-start.17 = (bf16[128,512]{1,0:T(8,128)(2,1)S(1)}, bf16[128,512]{1,0:T(8,128)(2,1)S(1)}, u32[]{:S(2)}, u32[]{:S(2)}) collective-permute-start(bf16[128,512]{1,0:T(8,128)(2,1)S(1)} %copy-done.2), channel_id=1, source_target_pairs={{0,2},{2,0},{1,3},{3,1},{4,6},{6,4},{5,7},{7,5},{8,10},{10,8},{9,1... | collective-permute-start | bytes 393224 | tf_op jit(solution)/shard_map/ppermute | solution.py:191
  59.7 6.8 %collective-permute-start.15 = (bf16[2,128,512]{2,1,0:T(8,128)(2,1)S(1)}, bf16[2,128,512]{2,1,0:T(8,128)(2,1)S(1)}, u32[]{:S(2)}, u32[]{:S(2)}) collective-permute-start(bf16[2,128,512]{2,1,0:T(8,128)(2,1)S(1)} %copy-done.1), channel_id=1, source_target_pairs={{0,1},{1,0},{2,3},{3,2},{4,5},{5,4},{6,7},{7,6},{8,9},{9,8},{10,11... | collective-permute-start | bytes 786440 | tf_op jit(solution)/shard_map/ppermute | solution.py:195
  59.8 6.7 %collective-permute-start.16 = (bf16[2,128,512]{2,1,0:T(8,128)(2,1)S(1)}, bf16[2,128,512]{2,1,0:T(8,128)(2,1)S(1)}, u32[]{:S(2)}, u32[]{:S(2)}) collective-permute-start(bf16[2,128,512]{2,1,0:T(8,128)(2,1)S(1)} %collective-permute-done.14.refs_4_), channel_id=1, source_target_pairs={{0,1},{1,0},{2,3},{3,2},{4,5},{5,4},{6,7},{7,6},{8,9},{9,8},{10,11... | collective-permute-start | bytes 786440 | tf_op jit(solution)/shard_map/ppermute | solution.py:195
  60.2 4.8 %collective-permute-start.18 = (bf16[128,512]{1,0:T(8,128)(2,1)S(1)}, bf16[128,512]{1,0:T(8,128)(2,1)S(1)}, u32[]{:S(2)}, u32[]{:S(2)}) collective-permute-start(bf16[128,512]{1,0:T(8,128)(2,1)S(1)} %copy-done.2), channel_id=1, source_target_pairs={{0,1},{1,0},{2,3},{3,2},{4,5},{5,4},{6,7},{7,6},{8,9},{9,8},{10,11... | collective-permute-start | bytes 393224 | tf_op jit(solution)/shard_map/ppermute | solution.py:195
  65.1 1.3 %collective-permute-start.19 = (bf16[128,512]{1,0:T(8,128)(2,1)S(1)}, bf16[128,512]{1,0:T(8,128)(2,1)S(1)}, u32[]{:S(2)}, u32[]{:S(2)}) collective-permute-start(bf16[128,512]{1,0:T(8,128)(2,1)S(1)} %collective-permute-done.17.refs_8_), channel_id=1, source_target_pairs={{0,1},{1,0},{2,3},{3,2},{4,5},{5,4},{6,7},{7,6},{8,9},{9,8},{10,11... | collective-permute-start | bytes 393224 | tf_op jit(solution)/shard_map/ppermute | solution.py:195
  (16 other events, 91.9 us)

commit v2 on v1

--- a/solution.py
+++ b/solution.py
@@ -10,7 +10,7 @@
 near_offsets = (1, 2, -1, -2)
 tile_rows = 16
 lanes = 128
-direct_parts = 8
+padded_parts = 8
 bf16 = jnp.bfloat16
 f32 = jnp.float32
 vmem = pl.BlockSpec(memory_space=pltpu.VMEM)
@@ -48,60 +48,47 @@
     return centred * lax.rsqrt(spread + 1e-05) * gain + offset
 
 
-def pick_kernel(part_count, near_cap, far_cap, far_ref, near_ref, latent_ref, *out_refs):
-    me = lax.axis_index("region") * lax.axis_size("feat") + lax.axis_index("feat")
-    near = near_ref[...]
+def my_part():
+    return lax.axis_index("region") * lax.axis_size("feat") + lax.axis_index("feat")
+
+
+def pick_kernel(part_count, near_cap, far_cap, far_ref, near_ref, latent_ref, out_ref):
+    me = my_part()
+    near = near_ref[0]
     row = jnp.concatenate([near[which : which + 1] for which in range(len(near_offsets))], axis=1)
-    near_columns = as_columns(row)
-    far_columns = jnp.full((part_count * tile_rows, lanes), -1, jnp.int32)
-    row_place = lax.broadcasted_iota(jnp.int32, far_columns.shape, 0)
-    for shift in range(part_count):
-        target = lax.rem(me + shift, part_count)
+    columns = [as_columns(row)]
+    tile_place = lax.broadcasted_iota(jnp.int32, (tile_rows, lanes), 0)
+    far = [as_columns(far_ref[0, slot : slot + 1]) for slot in range(far_cap)]
+    for part in range(part_count):
+        tile = jnp.full((tile_rows, lanes), -1, jnp.int32)
         for slot in range(far_cap):
-            far_columns = jnp.where(
-                row_place == shift * tile_rows + slot,
-                far_ref[target * far_cap + slot],
-                far_columns,
-            )
-    hot = one_hot(jnp.concatenate([near_columns, far_columns], axis=0), latent_ref.shape[0])
+            tile = jnp.where(tile_place == slot, far[slot][part : part + 1], tile)
+        columns.append(tile)
+    hot = one_hot(jnp.concatenate(columns, axis=0), latent_ref.shape[0])
     picked = jnp.dot(hot, latent_ref[...], preferred_element_type=f32).astype(bf16)
+    for which, offset in enumerate(near_offsets):
+        target = lax.rem(me + (offset + part_count), part_count)
+        out_ref[target, :near_cap] = picked[which * near_cap : (which + 1) * near_cap]
     far_start = len(near_offsets) * near_cap
-    for shift in range(part_count):
-        far = picked[far_start + shift * tile_rows : far_start + (shift + 1) * tile_rows]
-        which = near_shift(shift, part_count)
-        if which is None:
-            out_refs[shift][...] = far
-        else:
-            out_refs[shift][:near_cap] = picked[which * near_cap : (which + 1) * near_cap]
-            out_refs[shift][near_cap:] = far
-
-
-def near_shift(shift, part_count):
-    for which, offset in enumerate(near_offsets):
-        if offset % part_count == shift:
-            return which
-    return None
-
-
-def exchange_direct(node_latent, near_rows, far_rows, part_count):
+    for part in range(part_count):
+        out_ref[part, near_cap:] = picked[
+            far_start + part * tile_rows : far_start + (part + 1) * tile_rows
+        ]
+
+
+def exchange_padded(node_latent, near_rows, far_rows, part_count):
     near_cap, far_cap = near_rows.shape[2], far_rows.shape[2]
-    width = node_latent.shape[1]
-    shapes = []
-    for shift in range(part_count):
-        rows = tile_rows if near_shift(shift, part_count) is None else near_cap + tile_rows
-        shapes.append(jax.ShapeDtypeStruct((rows, width), bf16))
+    block = (part_count, near_cap + tile_rows, node_latent.shape[1])
     blocks = pl.pallas_call(
         functools.partial(pick_kernel, part_count, near_cap, far_cap),
-        out_shape=shapes,
-        in_specs=[smem, vmem, vmem],
-        out_specs=[vmem] * part_count,
+        out_shape=jax.ShapeDtypeStruct(block, bf16),
+        in_specs=[vmem, vmem, vmem],
+        out_specs=vmem,
         name="pick_halo",
-    )(far_rows.reshape(-1), near_rows[0], node_latent)
-    got = [blocks[0]]
-    for shift in range(1, part_count):
-        pairs = [(part, (part + shift) % part_count) for part in range(part_count)]
-        got.append(lax.ppermute(blocks[shift], ("region", "feat"), pairs))
-    return got
+    )(jnp.transpose(far_rows, (0, 2, 1)), near_rows, node_latent)
+    return [
+        lax.all_to_all(blocks, ("region", "feat"), split_axis=0, concat_axis=0, tiled=True)
+    ]
 
 
 def exchange_all(node_latent, near_rows, far_rows, part_count):
@@ -117,7 +104,7 @@
 
 
 def gather_kernel(
-    part_count, near_cap, far_cap, by_shift, source_ref, receiver_ref, latent_ref, *refs
+    part_count, near_cap, far_cap, padded, source_ref, receiver_ref, latent_ref, *refs
 ):
     got_refs, out_ref, table = refs[:-2], refs[-2], refs[-1]
     node_count, width = latent_ref.shape
@@ -126,34 +113,30 @@
     @pl.when(pl.program_id(0) == 0)
     def _():
         table[:node_count] = latent_ref[...]
-        if by_shift:
-            for shift in range(part_count):
-                which = near_shift(shift, part_count)
-                start = 0
-                if which is not None:
-                    start = near_cap
-                    place = node_count + which * near_cap
-                    table[place : place + near_cap] = got_refs[shift][:near_cap]
-                place = far_start + shift * tile_rows
-                table[place : place + tile_rows] = got_refs[shift][start : start + tile_rows]
+        for which, offset in enumerate(near_offsets):
+            place = node_count + which * near_cap
+            if padded:
+                origin = lax.rem(my_part() + (part_count - offset), part_count)
+                table[place : place + near_cap] = got_refs[0][origin, :near_cap]
+            else:
+                table[place : place + near_cap] = got_refs[which][...]
+        if padded:
+            for part in range(part_count):
+                place = far_start + part * tile_rows
+                table[place : place + tile_rows] = got_refs[0][part, near_cap:]
             used = far_start + part_count * tile_rows
         else:
-            for which in range(len(near_offsets)):
-                place = node_count + which * near_cap
-                table[place : place + near_cap] = got_refs[which][...]
             used = far_start + got_refs[-1].shape[0]
             table[far_start:used] = got_refs[-1][...]
         if used < table.shape[0]:
             table[used:] = jnp.zeros((table.shape[0] - used, width), bf16)
 
     source = source_ref[0]
-    if by_shift:
-        me = lax.axis_index("region") * lax.axis_size("feat") + lax.axis_index("feat")
+    if padded:
         far = source - far_start
         part = lax.div(far, far_cap)
-        slot = far - part * far_cap
-        shifted = far_start + wrap(me - part, part_count) * tile_rows + slot
-        source = jnp.where(far >= 0, shifted, source)
+        spread = far_start + part * (tile_rows - far_cap) + far
+        source = jnp.where(far >= 0, spread, source)
     sent = one_hot(as_columns(source), table.shape[0])
     out_ref[:, :width] = jnp.dot(sent, table[...], preferred_element_type=f32).astype(bf16)
     received = one_hot(as_columns(receiver_ref[0]), node_count)
@@ -175,25 +158,28 @@
 def owners():
     feat, feats = lax.axis_index("feat"), lax.axis_size("feat")
     sub, subs = lax.axis_index("sub"), lax.axis_size("sub")
-    order = []
-    for turn in range(subs):
-        for shift in range(feats):
-            order.append(
-                wrap(feat - shift, feats) * subs + wrap(sub - turn, subs)
-            )
-    return order
-
-
-def gather_rows(weight):
-    feats, subs = lax.axis_size("feat"), lax.axis_size("sub")
-    own = [weight]
-    for shift in range(1, feats):
-        own.append(lax.ppermute(weight, "feat", [(at, (at + shift) % feats) for at in range(feats)]))
-    pieces = list(own)
-    for turn in range(1, subs):
-        pairs = [(at, (at + turn) % subs) for at in range(subs)]
-        pieces += [lax.ppermute(piece, "sub", pairs) for piece in own]
-    return pieces
+    own = [(0, turn) for turn in range(subs)]
+    rest = [(shift, turn) for turn in range(subs) for shift in range(1, feats)]
+    return [
+        wrap(feat - shift, feats) * subs + wrap(sub - turn, subs) for shift, turn in own + rest
+    ]
+
+
+def from_feats(weight):
+    feats = lax.axis_size("feat")
+    return [
+        lax.ppermute(weight, "feat", [(at, (at + shift) % feats) for at in range(feats)])
+        for shift in range(1, feats)
+    ]
+
+
+def from_subs(pieces):
+    subs = lax.axis_size("sub")
+    return [
+        lax.ppermute(piece, "sub", [(at, (at + turn) % subs) for at in range(subs)])
+        for turn in range(1, subs)
+        for piece in pieces
+    ]
 
 
 def edge_kernel(pieces_count, *refs):
@@ -284,16 +270,13 @@
     block = 512
     steps = edge_count // block
 
-    edge_in = gather_rows(edge_in_weight)
-    edge_out = gather_rows(edge_out_weight)
-    node_in = gather_rows(node_in_weight)
-    node_out = gather_rows(node_out_weight)
-    pieces_count = len(edge_in)
-
-    by_shift = part_count <= direct_parts
-    exchange = exchange_direct if by_shift else exchange_all
+    far_edge = [from_feats(edge_in_weight), from_feats(edge_out_weight)]
+    near_edge = [from_subs([edge_in_weight]), from_subs([edge_out_weight])]
+
+    padded = part_count <= padded_parts
+    exchange = exchange_padded if padded else exchange_all
     got = exchange(node_latent, near_rows, far_rows, part_count)
-    far_space = part_count * tile_rows if by_shift else got[-1].shape[0]
+    far_space = part_count * tile_rows if padded else got[-1].shape[0]
     table_rows = node_count + len(near_offsets) * near_cap + far_space
     table_rows = -(-table_rows // lanes) * lanes
 
@@ -305,7 +288,7 @@
         return pl.BlockSpec(array.shape, lambda step: (0,) * array.ndim)
 
     gathered = pl.pallas_call(
-        functools.partial(gather_kernel, part_count, near_cap, far_cap, by_shift),
+        functools.partial(gather_kernel, part_count, near_cap, far_cap, padded),
         grid=(steps,),
         out_shape=jax.ShapeDtypeStruct((edge_count, 2 * width), bf16),
         in_specs=[index_spec, index_spec, whole(node_latent)] + [whole(rows) for rows in got],
@@ -318,6 +301,20 @@
         ),
         name="gather_latents",
     )(source_blocks, receiver_blocks, node_latent, *got)
+
+    far_edge, gathered, node_in_weight, node_out_weight = lax.optimization_barrier(
+        (far_edge, gathered, node_in_weight, node_out_weight)
+    )
+    edge_in, edge_out = [
+        [weight] + near + far + from_subs(far)
+        for weight, near, far in zip((edge_in_weight, edge_out_weight), near_edge, far_edge)
+    ]
+    far_node = [from_feats(node_in_weight), from_feats(node_out_weight)]
+    node_in, node_out = [
+        [weight] + from_subs([weight]) + far + from_subs(far)
+        for weight, far in zip((node_in_weight, node_out_weight), far_node)
+    ]
+    pieces_count = len(edge_in)
 
     rows = [value.reshape(1, -1) for value in (edge_in_bias, edge_out_bias, edge_gain, edge_offset)]
     edge_new, partial_sums = pl.pallas_call(

time: 68.9 us -> 48.9 us (0.71)
  waiting for transfers between devices: 22.8 us -> 15.7 us
  starting transfers between devices: 19.3 us -> 12.5 us
  local copies, waits for them, and re-layouts: 7.91 us -> 3.17 us
  Pallas kernels: 17.6 us -> 16.4 us
    ppermute x19 -> x12, waiting for transfers between devices: 22.8 us -> 7.34 us  [the longest x4 5.31 us: from_feats(): lax.ppermute(weight, 'feat', [(at, (at + shift) % feats) for at in range(...]
    ppermute x19 -> x12, starting transfers between devices: 18.8 us -> 5.1 us  [the longest x4 4 us: from_feats(): lax.ppermute(weight, 'feat', [(at, (at + shift) % feats) for at in range(...]
    all_to_all x0 -> x1, waiting for transfers between devices: none -> 8.35 us  [exchange_padded(): lax.all_to_all(blocks, ('region', 'feat'), split_axis=0, concat_axis=0, t...]
    all_to_all x0 -> x1, starting transfers between devices: none -> 7.26 us  [exchange_padded(): lax.all_to_all(blocks, ('region', 'feat'), split_axis=0, concat_axis=0, t...]
    unnamed x41 -> x36, local copies, waits for them, and re-layouts: 4.69 us -> 1.96 us
    pallas_call x1, Pallas kernels: 8.35 us -> 7.22 us  [shards(): pl.pallas_call(functools.partial(edge_kernel, pieces_count), grid=(steps,...]
    reshape x1, local copies, waits for them, and re-layouts: 1.3 us -> 0.6 us  [shards(): source_blocks = edge_source.reshape(steps, 1, block)]
    reshape x1, local copies, waits for them, and re-layouts: 1.3 us -> 0.61 us  [shards(): receiver_blocks = receivers.reshape(steps, 1, block)]
  transfers between devices with their start and end apart: 20 -> 14, of which waited for: 7 -> 6; matrix products, arithmetic and copies ran while one was open for 6% -> 2% of each run, Pallas kernels for 23% -> 25%
where the time goes in v2:
time: 48.9 us; the launch traced here: 48.6 us
  Pallas kernels  16.4 us (34%)
  waiting for transfers between devices  15.7 us (32%)
  starting transfers between devices  12.5 us (26%)
  local copies, waits for them, and re-layouts  3.17 us (6%)
  between operations  0.82 us (2%)
    all_to_all x1, waiting for transfers between devices, exchange_padded(): lax.all_to_all(blocks, ('region', 'feat'), split_axis=0, concat_axis=0, t...  8.35 us
    all_to_all x1, starting transfers between devices, exchange_padded(): lax.all_to_all(blocks, ('region', 'feat'), split_axis=0, concat_axis=0, t...  7.26 us
    pallas_call x1, Pallas kernels, shards(): pl.pallas_call(functools.partial(edge_kernel, pieces_count), grid=(steps,...  7.22 us
    ppermute x4, waiting for transfers between devices, from_feats(): lax.ppermute(weight, 'feat', [(at, (at + shift) % feats) for at in range(...  5.31 us
    pallas_call x1, Pallas kernels, shards(): pl.pallas_call(functools.partial(gather_kernel, part_count, near_cap, far...  4.96 us
    ppermute x4, starting transfers between devices, from_feats(): lax.ppermute(weight, 'feat', [(at, (at + shift) % feats) for at in range(...  4 us
    pallas_call x1, Pallas kernels, exchange_padded(): pl.pallas_call(functools.partial(pick_kernel, part_count, near_cap, far_c...  2.23 us
    ppermute x8, waiting for transfers between devices, from_subs(): lax.ppermute(piece, 'sub', [(at, (at + turn) % subs) for at in range(subs)])  2.03 us
  transfers between devices with their start and end apart: 14, of which 6 were waited for; matrix products, arithmetic and copies ran while one was open for 2% of the time, Pallas kernels for 25%

profile of v2, /device:TPU:0, one launch (start us, length us, event | category | flops | bytes accessed | tf_op | source)
XLA Modules:
  0.0 48.6 jit_solution(12211859167338641526)
XLA Ops:
  0.7 2.2 %pick_halo.1 = bf16[8,48,512]{2,1,0:T(8,128)(2,1)} custom-call(s32[1,2,8]{2,1,0:T(2,128)} %bitcast.17, s32[1,4,32]{2,1,0:T(4,128)} %near_ref.1, bf16[384,512]{1,0:T(8,128)(2,1)} %refs_0_.3), custom_call_target="tpu_custom_call" | custom-call | tf_op jit(solution)/shard_map/pick_halo/pallas_call | solution.py:82
  2.9 7.3 %all-to-all-start = ((bf16[8,48,512]{2,1,0:T(8,128)(2,1)}), bf16[8,48,512]{2,1,0:T(8,128)(2,1)}, u32[]{:S(2)}, u32[]{:S(2)}) async-start(bf16[8,48,512]{2,1,0:T(8,128)(2,1)} %pick_halo.1), calls=%async_computation | async-start | bytes 786432 | tf_op jit(solution)/shard_map/all_to_all | solution.py:90
  10.2 2.0 %collective-permute-start = (bf16[3,128,512]{2,1,0:T(8,128)(2,1)S(1)}, bf16[3,128,512]{2,1,0:T(8,128)(2,1)S(1)}, u32[]{:S(2)}, u32[]{:S(2)}) collective-permute-start(bf16[3,128,512]{2,1,0:T(8,128)(2,1)S(1)} %copy-done.9), channel_id=1, source_target_pairs={{0,2},{2,0},{1,3},{3,1},{4,6},{6,4},{5,7},{7,5},{8,10},{10,8},{9,1... | collective-permute-start | bytes 1179656 | tf_op jit(solution)/shard_map/ppermute | solution.py:171
  12.2 0.2 collective-permute-start.1
  12.4 0.6 %reshape.35.receiver_ref.refs_2_ = s32[3,1,512]{2,1,0:T(1,128)} reshape(s32[1536]{0:T(1024)S(1)} %copy-done.16) | data formatting | bytes 12288 | tf_op jit(solution)/shard_map/reshape | solution.py:284
  13.0 0.6 %reshape.34.source_ref = s32[3,1,512]{2,1,0:T(1,128)} reshape(s32[1536]{0:T(1024)S(1)} %copy-done.17) | data formatting | bytes 12288 | tf_op jit(solution)/shard_map/reshape | solution.py:283
  13.6 0.0 copy-start.12
  13.6 8.3 %all-to-all-done.refs_0_ = bf16[8,48,512]{2,1,0:T(8,128)(2,1)} async-done(((bf16[8,48,512]{2,1,0:T(8,128)(2,1)}), bf16[8,48,512]{2,1,0:T(8,128)(2,1)}, u32[]{:S(2)}, u32[]{:S(2)}) %all-to-all-start) | async-done | bytes 393248 | tf_op jit(solution)/shard_map/all_to_all | solution.py:90
  22.0 5.0 %gather_latents.1.refs_1_ = bf16[1536,1024]{1,0:T(8,128)(2,1)} custom-call(s32[3,1,512]{2,1,0:T(1,128)} %reshape.34.source_ref, s32[3,1,512]{2,1,0:T(1,128)} %reshape.35.receiver_ref.refs_2_, bf16[384,512]{1,0:T(8,128)(2,1)} %refs_0_.3, bf16[8,48,512]{2,1,0:T(8,128)(2,1)} %all-to-all-done.refs_0_), custom_call_target="tpu_custom_call" | custom-call | flops 1610612736 | bytes 3145728 | tf_op jit(solution)/shard_map/gather_latents/pallas_call | solution.py:290
  26.9 1.0 %collective-permute-done.1.refs_9_ = bf16[128,512]{1,0:T(8,128)(2,1)S(1)} collective-permute-done((bf16[128,512]{1,0:T(8,128)(2,1)S(1)}, bf16[128,512]{1,0:T(8,128)(2,1)S(1)}, u32[]{:S(2)}, u32[]{:S(2)}) %collective-permute-start.1) | collective-permute-done | bytes 131104 | tf_op jit(solution)/shard_map/ppermute | solution.py:171
  28.0 0.5 %collective-permute-start.4 = (bf16[128,512]{1,0:T(8,128)(2,1)S(1)}, bf16[128,512]{1,0:T(8,128)(2,1)S(1)}, u32[]{:S(2)}, u32[]{:S(2)}) collective-permute-start(bf16[128,512]{1,0:T(8,128)(2,1)S(1)} %copy-done.10), channel_id=1, source_target_pairs={{0,1},{1,0},{2,3},{3,2},{4,5},{5,4},{6,7},{7,6},{8,9},{9,8},{10,11... | collective-permute-start | bytes 393224 | tf_op jit(solution)/shard_map/ppermute | solution.py:179
  28.5 0.9 %collective-permute-start.8 = (bf16[2,128,512]{2,1,0:T(8,128)(2,1)S(1)}, bf16[2,128,512]{2,1,0:T(8,128)(2,1)S(1)}, u32[]{:S(2)}, u32[]{:S(2)}) collective-permute-start(bf16[2,128,512]{2,1,0:T(8,128)(2,1)S(1)} %copy-done.1), channel_id=1, source_target_pairs={{0,2},{2,0},{1,3},{3,1},{4,6},{6,4},{5,7},{7,5},{8,10},{10,8},{9,1... | collective-permute-start | bytes 786440 | tf_op jit(solution)/shard_map/ppermute | solution.py:171
  29.4 0.5 %collective-permute-done.4.refs_8_ = bf16[128,512]{1,0:T(8,128)(2,1)S(1)} collective-permute-done((bf16[128,512]{1,0:T(8,128)(2,1)S(1)}, bf16[128,512]{1,0:T(8,128)(2,1)S(1)}, u32[]{:S(2)}, u32[]{:S(2)}) %collective-permute-start.4) | collective-permute-done | bytes 131104 | tf_op jit(solution)/shard_map/ppermute | solution.py:179
  29.9 0.2 collective-permute-done.5.refs_10_
  30.1 1.9 %copy-done.15 = bf16[1536,1024]{1,0:T(8,128)(2,1)S(1)} copy-done((bf16[1536,1024]{1,0:T(8,128)(2,1)S(1)}, bf16[1536,1024]{1,0:T(8,128)(2,1)}, u32[]{:S(2)}) %copy-start.15) | copy-done | bytes 3145752
  32.0 7.2 %edge_update.1 = (bf16[1536,512]{1,0:T(8,128)(2,1)}, bf16[384,512]{1,0:T(8,128)(2,1)S(1)}) custom-call(bf16[1536,512]{1,0:T(8,128)(2,1)S(1)} %copy-done.8, bf16[1536,1024]{1,0:T(8,128)(2,1)S(1)} %copy-done.15, s32[3,1,512]{2,1,0:T(1,128)S(1)} %copy-done.3, bf16[3,128,512]{2,1,0:T(8,128)(2,1)S(1)} %copy-done.9, ...), custom_call_target="tpu_custom_call" | custom-call | flops 3825205248 | bytes 6291456 | tf_op jit(solution)/shard_map/edge_update/pallas_call | solution.py:320
  39.3 0.1 collective-permute-start.6
  39.4 0.9 %collective-permute-start.11 = (bf16[128,512]{1,0:T(8,128)(2,1)S(1)}, bf16[128,512]{1,0:T(8,128)(2,1)S(1)}, u32[]{:S(2)}, u32[]{:S(2)}) collective-permute-start(bf16[128,512]{1,0:T(8,128)(2,1)S(1)} %copy-done.2), channel_id=1, source_target_pairs={{0,2},{2,0},{1,3},{3,1},{4,6},{6,4},{5,7},{7,5},{8,10},{10,8},{9,1... | collective-permute-start | bytes 393224 | tf_op jit(solution)/shard_map/ppermute | solution.py:171
  40.3 0.1 collective-permute-start.7
  40.4 0.4 collective-permute-start.9
  40.8 0.1 collective-permute-start.10
  40.9 4.3 %collective-permute-done.11.refs_9_ = bf16[128,512]{1,0:T(8,128)(2,1)S(1)} collective-permute-done((bf16[128,512]{1,0:T(8,128)(2,1)S(1)}, bf16[128,512]{1,0:T(8,128)(2,1)S(1)}, u32[]{:S(2)}, u32[]{:S(2)}) %collective-permute-start.11) | collective-permute-done | bytes 131104 | tf_op jit(solution)/shard_map/ppermute | solution.py:171
  45.2 1.3 %collective-permute-done.12.refs_10_ = bf16[128,512]{1,0:T(8,128)(2,1)S(1)} collective-permute-done((bf16[128,512]{1,0:T(8,128)(2,1)S(1)}, bf16[128,512]{1,0:T(8,128)(2,1)S(1)}, u32[]{:S(2)}, u32[]{:S(2)}) %collective-permute-start.12) | collective-permute-done | bytes 131104 | tf_op jit(solution)/shard_map/ppermute | solution.py:179
  46.6 2.0 %node_update.1 = bf16[384,512]{1,0:T(8,128)(2,1)} custom-call(bf16[384,512]{1,0:T(8,128)(2,1)S(1)} %copy-done, bf16[384,512]{1,0:T(8,128)(2,1)S(1)} %get-tuple-element.13.refs_1_, bf16[384,512]{1,0:T(8,128)(2,1)S(1)} %collective-permute-done.6.refs_2_, bf16[2,128,512]{2,1,0:T(8,128)(2,1)S(1)} %copy-done.1, ...), custom_call_target="tpu_custom_call" | custom-call | flops 603979776 | bytes 1966080 | tf_op jit(solution)/shard_map/node_update/pallas_call | solution.py:356
  (46 shorter events, 0.1 us)
Async XLA Ops:
  2.9 19.0 %all-to-all-start = ((bf16[8,48,512]{2,1,0:T(8,128)(2,1)}), bf16[8,48,512]{2,1,0:T(8,128)(2,1)}, u32[]{:S(2)}, u32[]{:S(2)}) async-start(bf16[8,48,512]{2,1,0:T(8,128)(2,1)} %pick_halo.1), calls=%async_computation | async-start | bytes 786432 | tf_op jit(solution)/shard_map/all_to_all | solution.py:90
  10.2 17.8 %collective-permute-start = (bf16[3,128,512]{2,1,0:T(8,128)(2,1)S(1)}, bf16[3,128,512]{2,1,0:T(8,128)(2,1)S(1)}, u32[]{:S(2)}, u32[]{:S(2)}) collective-permute-start(bf16[3,128,512]{2,1,0:T(8,128)(2,1)S(1)} %copy-done.9), channel_id=1, source_target_pairs={{0,2},{2,0},{1,3},{3,1},{4,6},{6,4},{5,7},{7,5},{8,10},{10,8},{9,1... | collective-permute-start | bytes 1179656 | tf_op jit(solution)/shard_map/ppermute | solution.py:171
  12.2 17.7 %collective-permute-start.2 = (bf16[3,128,512]{2,1,0:T(8,128)(2,1)S(1)}, bf16[3,128,512]{2,1,0:T(8,128)(2,1)S(1)}, u32[]{:S(2)}, u32[]{:S(2)}) collective-permute-start(bf16[3,128,512]{2,1,0:T(8,128)(2,1)S(1)} %copy-done.9), channel_id=1, source_target_pairs={{0,1},{1,0},{2,3},{3,2},{4,5},{5,4},{6,7},{7,6},{8,9},{9,8},{10,11... | collective-permute-start | bytes 1179656 | tf_op jit(solution)/shard_map/ppermute | solution.py:179
  12.2 15.8 %collective-permute-start.1 = (bf16[128,512]{1,0:T(8,128)(2,1)S(1)}, bf16[128,512]{1,0:T(8,128)(2,1)S(1)}, u32[]{:S(2)}, u32[]{:S(2)}) collective-permute-start(bf16[128,512]{1,0:T(8,128)(2,1)S(1)} %copy-done.10), channel_id=1, source_target_pairs={{0,2},{2,0},{1,3},{3,1},{4,6},{6,4},{5,7},{7,5},{8,10},{10,8},{9,1... | collective-permute-start | bytes 393224 | tf_op jit(solution)/shard_map/ppermute | solution.py:171
  13.6 14.9 %copy-start.1 = (bf16[2,128,512]{2,1,0:T(8,128)(2,1)S(1)}, bf16[2,128,512]{2,1,0:T(8,128)(2,1)}, u32[]{:S(2)}) copy-start(bf16[2,128,512]{2,1,0:T(8,128)(2,1)} %refs_3_.2) | copy-start | bytes 786436
  13.6 16.5 %copy-start.3 = (s32[3,1,512]{2,1,0:T(1,128)S(1)}, s32[3,1,512]{2,1,0:T(1,128)}, u32[]{:S(2)}) copy-start(s32[3,1,512]{2,1,0:T(1,128)} %reshape.35.receiver_ref.refs_2_) | copy-start | bytes 18436
  13.6 16.5 %copy-start.8 = (bf16[1536,512]{1,0:T(8,128)(2,1)S(1)}, bf16[1536,512]{1,0:T(8,128)(2,1)}, u32[]{:S(2)}) copy-start(bf16[1536,512]{1,0:T(8,128)(2,1)} %refs_0_.2) | copy-start | bytes 4718596
  13.6 16.5 %copy-start.11 = (f32[512]{0:T(512)S(1)}, f32[512]{0:T(512)}, u32[]{:S(2)}) copy-start(f32[512]{0:T(512)} %param.28) | copy-start | bytes 6148
  13.6 16.5 %copy-start.12 = (f32[512]{0:T(512)S(1)}, f32[512]{0:T(512)}, u32[]{:S(2)}) copy-start(f32[512]{0:T(512)} %param.29) | copy-start | bytes 6148
  13.6 16.5 %copy-start.13 = (f32[512]{0:T(512)S(1)}, f32[512]{0:T(512)}, u32[]{:S(2)}) copy-start(f32[512]{0:T(512)} %param.30) | copy-start | bytes 6148
  13.6 16.5 %copy-start.14 = (f32[512]{0:T(512)S(1)}, f32[512]{0:T(512)}, u32[]{:S(2)}) copy-start(f32[512]{0:T(512)} %param.31) | copy-start | bytes 6148
  28.0 2.1 %collective-permute-start.3 = (bf16[3,128,512]{2,1,0:T(8,128)(2,1)S(1)}, bf16[3,128,512]{2,1,0:T(8,128)(2,1)S(1)}, u32[]{:S(2)}, u32[]{:S(2)}) collective-permute-start(bf16[3,128,512]{2,1,0:T(8,128)(2,1)S(1)} %collective-permute-done.refs_5_), channel_id=1, source_target_pairs={{0,1},{1,0},{2,3},{3,2},{4,5},{5,4},{6,7},{7,6},{8,9},{9,8},{10,11... | collective-permute-start | bytes 1179656 | tf_op jit(solution)/shard_map/ppermute | solution.py:179
  28.0 1.9 %collective-permute-start.4 = (bf16[128,512]{1,0:T(8,128)(2,1)S(1)}, bf16[128,512]{1,0:T(8,128)(2,1)S(1)}, u32[]{:S(2)}, u32[]{:S(2)}) collective-permute-start(bf16[128,512]{1,0:T(8,128)(2,1)S(1)} %copy-done.10), channel_id=1, source_target_pairs={{0,1},{1,0},{2,3},{3,2},{4,5},{5,4},{6,7},{7,6},{8,9},{9,8},{10,11... | collective-permute-start | bytes 393224 | tf_op jit(solution)/shard_map/ppermute | solution.py:179
  28.5 1.6 %collective-permute-start.5 = (bf16[128,512]{1,0:T(8,128)(2,1)S(1)}, bf16[128,512]{1,0:T(8,128)(2,1)S(1)}, u32[]{:S(2)}, u32[]{:S(2)}) collective-permute-start(bf16[128,512]{1,0:T(8,128)(2,1)S(1)} %collective-permute-done.1.refs_9_), channel_id=1, source_target_pairs={{0,1},{1,0},{2,3},{3,2},{4,5},{5,4},{6,7},{7,6},{8,9},{9,8},{10,11... | collective-permute-start | bytes 393224 | tf_op jit(solution)/shard_map/ppermute | solution.py:179
  28.5 11.9 %collective-permute-start.8 = (bf16[2,128,512]{2,1,0:T(8,128)(2,1)S(1)}, bf16[2,128,512]{2,1,0:T(8,128)(2,1)S(1)}, u32[]{:S(2)}, u32[]{:S(2)}) collective-permute-start(bf16[2,128,512]{2,1,0:T(8,128)(2,1)S(1)} %copy-done.1), channel_id=1, source_target_pairs={{0,2},{2,0},{1,3},{3,1},{4,6},{6,4},{5,7},{7,5},{8,10},{10,8},{9,1... | collective-permute-start | bytes 786440 | tf_op jit(solution)/shard_map/ppermute | solution.py:171
  32.0 14.6 %copy-start.5 = (f32[512]{0:T(512)S(1)}, f32[512]{0:T(512)}, u32[]{:S(2)}) copy-start(f32[512]{0:T(512)} %param.33) | copy-start | bytes 6148
  32.0 14.6 %copy-start.6 = (f32[512]{0:T(512)S(1)}, f32[512]{0:T(512)}, u32[]{:S(2)}) copy-start(f32[512]{0:T(512)} %param.34) | copy-start | bytes 6148
  32.0 14.6 %copy-start.7 = (f32[512]{0:T(512)S(1)}, f32[512]{0:T(512)}, u32[]{:S(2)}) copy-start(f32[512]{0:T(512)} %param.35) | copy-start | bytes 6148
  39.3 7.3 %collective-permute-start.6 = (bf16[384,512]{1,0:T(8,128)(2,1)S(1)}, bf16[384,512]{1,0:T(8,128)(2,1)S(1)}, u32[]{:S(2)}, u32[]{:S(2)}) collective-permute-start(bf16[384,512]{1,0:T(8,128)(2,1)S(1)} %get-tuple-element.13.refs_1_), channel_id=1, source_target_pairs={{0,1},{1,0},{2,3},{3,2},{4,5},{5,4},{6,7},{7,6},{8,9},{9,8},{10,11... | collective-permute-start | bytes 1179656 | tf_op jit(solution)/shard_map/ppermute | solution.py:353
  39.4 5.8 %collective-permute-start.11 = (bf16[128,512]{1,0:T(8,128)(2,1)S(1)}, bf16[128,512]{1,0:T(8,128)(2,1)S(1)}, u32[]{:S(2)}, u32[]{:S(2)}) collective-permute-start(bf16[128,512]{1,0:T(8,128)(2,1)S(1)} %copy-done.2), channel_id=1, source_target_pairs={{0,2},{2,0},{1,3},{3,1},{4,6},{6,4},{5,7},{7,5},{8,10},{10,8},{9,1... | collective-permute-start | bytes 393224 | tf_op jit(solution)/shard_map/ppermute | solution.py:171
  40.3 6.2 %collective-permute-start.7 = (bf16[2,128,512]{2,1,0:T(8,128)(2,1)S(1)}, bf16[2,128,512]{2,1,0:T(8,128)(2,1)S(1)}, u32[]{:S(2)}, u32[]{:S(2)}) collective-permute-start(bf16[2,128,512]{2,1,0:T(8,128)(2,1)S(1)} %copy-done.1), channel_id=1, source_target_pairs={{0,1},{1,0},{2,3},{3,2},{4,5},{5,4},{6,7},{7,6},{8,9},{9,8},{10,11... | collective-permute-start | bytes 786440 | tf_op jit(solution)/shard_map/ppermute | solution.py:179
  40.4 6.1 %collective-permute-start.9 = (bf16[2,128,512]{2,1,0:T(8,128)(2,1)S(1)}, bf16[2,128,512]{2,1,0:T(8,128)(2,1)S(1)}, u32[]{:S(2)}, u32[]{:S(2)}) collective-permute-start(bf16[2,128,512]{2,1,0:T(8,128)(2,1)S(1)} %collective-permute-done.8.refs_5_), channel_id=1, source_target_pairs={{0,1},{1,0},{2,3},{3,2},{4,5},{5,4},{6,7},{7,6},{8,9},{9,8},{10,11... | collective-permute-start | bytes 786440 | tf_op jit(solution)/shard_map/ppermute | solution.py:179
  40.8 4.3 %collective-permute-start.10 = (bf16[128,512]{1,0:T(8,128)(2,1)S(1)}, bf16[128,512]{1,0:T(8,128)(2,1)S(1)}, u32[]{:S(2)}, u32[]{:S(2)}) collective-permute-start(bf16[128,512]{1,0:T(8,128)(2,1)S(1)} %copy-done.2), channel_id=1, source_target_pairs={{0,1},{1,0},{2,3},{3,2},{4,5},{5,4},{6,7},{7,6},{8,9},{9,8},{10,11... | collective-permute-start | bytes 393224 | tf_op jit(solution)/shard_map/ppermute | solution.py:179
  45.2 1.3 %collective-permute-start.12 = (bf16[128,512]{1,0:T(8,128)(2,1)S(1)}, bf16[128,512]{1,0:T(8,128)(2,1)S(1)}, u32[]{:S(2)}, u32[]{:S(2)}) collective-permute-start(bf16[128,512]{1,0:T(8,128)(2,1)S(1)} %collective-permute-done.11.refs_9_), channel_id=1, source_target_pairs={{0,1},{1,0},{2,3},{3,2},{4,5},{5,4},{6,7},{7,6},{8,9},{9,8},{10,11... | collective-permute-start | bytes 393224 | tf_op jit(solution)/shard_map/ppermute | solution.py:179
  (8 other events, 83.4 us)

commit v3 on v2

--- a/solution.py
+++ b/solution.py
@@ -11,10 +11,10 @@
 tile_rows = 16
 lanes = 128
 padded_parts = 8
+grant = 56 << 20
 bf16 = jnp.bfloat16
 f32 = jnp.float32
 vmem = pl.BlockSpec(memory_space=pltpu.VMEM)
-smem = pl.BlockSpec(memory_space=pltpu.SMEM)
 
 
 def wrap(value, count):
@@ -84,6 +84,7 @@
         out_shape=jax.ShapeDtypeStruct(block, bf16),
         in_specs=[vmem, vmem, vmem],
         out_specs=vmem,
+        cost_estimate=pl.CostEstimate(flops=0, bytes_accessed=0, transcendentals=0),
         name="pick_halo",
     )(jnp.transpose(far_rows, (0, 2, 1)), near_rows, node_latent)
     return [
@@ -104,55 +105,77 @@
 
 
 def gather_kernel(
-    part_count, near_cap, far_cap, padded, source_ref, receiver_ref, latent_ref, *refs
+    node_count,
+    near_cap,
+    far_cap,
+    far_stride,
+    halo_space,
+    source_ref,
+    receiver_ref,
+    latent_ref,
+    node_in_ref,
+    node_out_ref,
+    out_ref,
+    pack_ref,
+    sems,
 ):
-    got_refs, out_ref, table = refs[:-2], refs[-2], refs[-1]
-    node_count, width = latent_ref.shape
-    far_start = node_count + len(near_offsets) * near_cap
+    width = latent_ref.shape[1]
+    halo_start = 2 * width
+    count = node_in_ref.shape[0]
+    copies = [
+        pltpu.make_async_copy(node_in_ref, pack_ref.at[pl.ds(0, count)], sems.at[0]),
+        pltpu.make_async_copy(node_out_ref, pack_ref.at[count], sems.at[1]),
+    ]
 
     @pl.when(pl.program_id(0) == 0)
     def _():
-        table[:node_count] = latent_ref[...]
-        for which, offset in enumerate(near_offsets):
-            place = node_count + which * near_cap
-            if padded:
-                origin = lax.rem(my_part() + (part_count - offset), part_count)
-                table[place : place + near_cap] = got_refs[0][origin, :near_cap]
-            else:
-                table[place : place + near_cap] = got_refs[which][...]
+        for copy in copies:
+            copy.start()
+
+    columns = as_columns(source_ref[0])
+    latent = latent_ref[...]
+    sent = one_hot(columns, node_count)
+    out_ref[:, :width] = jnp.dot(sent, latent, preferred_element_type=f32).astype(bf16)
+    received = one_hot(as_columns(receiver_ref[0]), node_count)
+    out_ref[:, width:halo_start] = jnp.dot(
+        received, latent, preferred_element_type=f32
+    ).astype(bf16)
+    slot = columns - node_count
+    far = slot - len(near_offsets) * near_cap
+    part = lax.div(far, far_cap)
+    slot = jnp.where(far >= 0, slot + part * (far_stride - far_cap), slot)
+    out_ref[:, halo_start:] = one_hot(slot, halo_space)
+
+    @pl.when(pl.program_id(0) == pl.num_programs(0) - 1)
+    def _():
+        for copy in copies:
+            copy.wait()
+
+
+def place_halo(table, part_count, near_cap, padded, got_refs):
+    far_start = len(near_offsets) * near_cap
+    for which, offset in enumerate(near_offsets):
+        place = which * near_cap
         if padded:
-            for part in range(part_count):
-                place = far_start + part * tile_rows
-                table[place : place + tile_rows] = got_refs[0][part, near_cap:]
-            used = far_start + part_count * tile_rows
+            origin = lax.rem(my_part() + (part_count - offset), part_count)
+            table[place : place + near_cap] = got_refs[0][origin, :near_cap]
         else:
-            used = far_start + got_refs[-1].shape[0]
-            table[far_start:used] = got_refs[-1][...]
-        if used < table.shape[0]:
-            table[used:] = jnp.zeros((table.shape[0] - used, width), bf16)
-
-    source = source_ref[0]
+            table[place : place + near_cap] = got_refs[which][...]
     if padded:
-        far = source - far_start
-        part = lax.div(far, far_cap)
-        spread = far_start + part * (tile_rows - far_cap) + far
-        source = jnp.where(far >= 0, spread, source)
-    sent = one_hot(as_columns(source), table.shape[0])
-    out_ref[:, :width] = jnp.dot(sent, table[...], preferred_element_type=f32).astype(bf16)
-    received = one_hot(as_columns(receiver_ref[0]), node_count)
-    out_ref[:, width:] = jnp.dot(
-        received, latent_ref[...], preferred_element_type=f32
-    ).astype(bf16)
-
-
-def place_rows(whole, pieces, order):
-    for piece, owner in zip(pieces, order):
-        rows = piece.shape[-2]
-        spot = pl.ds(pl.multiple_of(owner * rows, rows), rows)
-        if len(whole.shape) == 3:
-            whole[:, spot, :] = piece[...]
-        else:
-            whole[spot, :] = piece[...]
+        for part in range(part_count):
+            place = far_start + part * tile_rows
+            table[place : place + tile_rows] = got_refs[0][part, near_cap:]
+        used = far_start + part_count * tile_rows
+    else:
+        used = far_start + got_refs[-1].shape[0]
+        table[far_start:used] = got_refs[-1][...]
+    if used < table.shape[0]:
+        table[used:] = jnp.zeros((table.shape[0] - used, table.shape[1]), bf16)
+
+
+def place_rows(whole, start, piece, owner):
+    rows = piece.shape[0]
+    whole[pl.ds(pl.multiple_of(start + owner * rows, rows), rows), :] = piece
 
 
 def owners():
@@ -182,26 +205,34 @@
     ]
 
 
-def edge_kernel(pieces_count, *refs):
+def edge_kernel(pieces_count, got_count, part_count, near_cap, padded, *refs):
     edge_ref, gathered_ref, receiver_ref = refs[:3]
-    in_pieces = refs[3 : 3 + pieces_count]
-    out_pieces = refs[3 + pieces_count : 3 + 2 * pieces_count]
-    in_bias, out_bias, gain, offset, new_ref, sum_ref, in_weight, out_weight, total = refs[
-        3 + 2 * pieces_count :
+    got_refs = refs[3 : 3 + got_count]
+    in_pieces = refs[3 + got_count : 3 + got_count + pieces_count]
+    out_pieces = refs[3 + got_count + pieces_count : 3 + got_count + 2 * pieces_count]
+    in_bias, out_bias, gain, offset, new_ref, sum_ref, in_weight, out_weight, halo, total = refs[
+        3 + got_count + 2 * pieces_count :
     ]
     width = edge_ref.shape[1]
     step = pl.program_id(0)
 
     @pl.when(step == 0)
     def _():
-        order = owners()
-        place_rows(in_weight, in_pieces, order)
-        place_rows(out_weight, out_pieces, order)
+        for in_piece, out_piece, owner in zip(in_pieces, out_pieces, owners()):
+            for which in range(in_piece.shape[0]):
+                place_rows(in_weight, which * width, in_piece[which], owner)
+            place_rows(out_weight, 0, out_piece[...], owner)
+        place_halo(halo, part_count, near_cap, padded, got_refs)
+        in_weight[3 * width :] = jnp.dot(
+            halo[...], in_weight[width : 2 * width], preferred_element_type=f32
+        ).astype(bf16)
 
     edges = edge_ref[...]
-    preact = jnp.dot(edges, in_weight[0], preferred_element_type=f32)
-    preact += jnp.dot(gathered_ref[:, :width], in_weight[1], preferred_element_type=f32)
-    preact += jnp.dot(gathered_ref[:, width:], in_weight[2], preferred_element_type=f32)
+    preact = jnp.dot(
+        jnp.concatenate([edges, gathered_ref[...]], axis=1),
+        in_weight[...],
+        preferred_element_type=f32,
+    )
     hidden = silu(preact + in_bias[...]).astype(bf16)
     output = jnp.dot(hidden, out_weight[...], preferred_element_type=f32) + out_bias[...]
     edge_new = (edges.astype(f32) + layer_norm(output, gain[...], offset[...])).astype(bf16)
@@ -226,18 +257,21 @@
 
 def node_kernel(pieces_count, *refs):
     latent_ref, own_ref, other_ref = refs[:3]
-    in_pieces = refs[3 : 3 + pieces_count]
-    out_pieces = refs[3 + pieces_count : 3 + 2 * pieces_count]
-    in_bias, out_bias, gain, offset, new_ref, in_weight, out_weight = refs[3 + 2 * pieces_count :]
-    order = owners()
-    place_rows(in_weight, in_pieces, order)
-    place_rows(out_weight, out_pieces, order)
+    pieces = refs[3 : 3 + pieces_count]
+    in_bias, out_bias, gain, offset, new_ref, weights = refs[3 + pieces_count :]
+    width = latent_ref.shape[1]
+    for piece, owner in zip(pieces, owners()):
+        for which in range(piece.shape[0]):
+            place_rows(weights, which * width, piece[which], owner)
     latent = latent_ref[...]
     summed = (own_ref[...].astype(f32) + other_ref[...].astype(f32)).astype(bf16)
-    preact = jnp.dot(latent, in_weight[0], preferred_element_type=f32)
-    preact += jnp.dot(summed, in_weight[1], preferred_element_type=f32)
+    preact = jnp.dot(
+        jnp.concatenate([latent, summed], axis=1),
+        weights[: 2 * width],
+        preferred_element_type=f32,
+    )
     hidden = silu(preact + in_bias[...]).astype(bf16)
-    output = jnp.dot(hidden, out_weight[...], preferred_element_type=f32) + out_bias[...]
+    output = jnp.dot(hidden, weights[2 * width :], preferred_element_type=f32) + out_bias[...]
     new_ref[...] = (
         latent.astype(f32) + layer_norm(output, gain[...], offset[...])
     ).astype(bf16)
@@ -276,9 +310,9 @@
     padded = part_count <= padded_parts
     exchange = exchange_padded if padded else exchange_all
     got = exchange(node_latent, near_rows, far_rows, part_count)
-    far_space = part_count * tile_rows if padded else got[-1].shape[0]
-    table_rows = node_count + len(near_offsets) * near_cap + far_space
-    table_rows = -(-table_rows // lanes) * lanes
+    far_stride = tile_rows if padded else far_cap
+    halo_space = len(near_offsets) * near_cap + part_count * far_stride
+    halo_space = -(-halo_space // lanes) * lanes
 
     source_blocks = edge_source.reshape(steps, 1, block)
     receiver_blocks = receivers.reshape(steps, 1, block)
@@ -287,38 +321,39 @@
     def whole(array):
         return pl.BlockSpec(array.shape, lambda step: (0,) * array.ndim)
 
-    gathered = pl.pallas_call(
-        functools.partial(gather_kernel, part_count, near_cap, far_cap, padded),
+    hbm = pl.BlockSpec(memory_space=pl.ANY)
+    gathered_width = 2 * width + halo_space
+    gathered, node_weight = pl.pallas_call(
+        functools.partial(
+            gather_kernel, node_count, near_cap, far_cap, far_stride, halo_space
+        ),
         grid=(steps,),
-        out_shape=jax.ShapeDtypeStruct((edge_count, 2 * width), bf16),
-        in_specs=[index_spec, index_spec, whole(node_latent)] + [whole(rows) for rows in got],
-        out_specs=pl.BlockSpec((block, 2 * width), lambda step: (step, 0)),
-        scratch_shapes=[pltpu.VMEM((table_rows, width), bf16)],
-        cost_estimate=pl.CostEstimate(
-            flops=2 * edge_count * width * (table_rows + node_count),
-            bytes_accessed=4 * edge_count * width,
-            transcendentals=0,
-        ),
+        out_shape=[
+            jax.ShapeDtypeStruct((edge_count, gathered_width), bf16),
+            jax.ShapeDtypeStruct((node_in_weight.shape[0] + 1,) + node_out_weight.shape, bf16),
+        ],
+        in_specs=[index_spec, index_spec, whole(node_latent), hbm, hbm],
+        out_specs=[pl.BlockSpec((block, gathered_width), lambda step: (step, 0)), hbm],
+        scratch_shapes=[pltpu.SemaphoreType.DMA((2,))],
+        compiler_params=pltpu.CompilerParams(vmem_limit_bytes=grant),
+        cost_estimate=pl.CostEstimate(flops=0, bytes_accessed=0, transcendentals=0),
         name="gather_latents",
-    )(source_blocks, receiver_blocks, node_latent, *got)
-
-    far_edge, gathered, node_in_weight, node_out_weight = lax.optimization_barrier(
-        (far_edge, gathered, node_in_weight, node_out_weight)
+    )(source_blocks, receiver_blocks, node_latent, node_in_weight, node_out_weight)
+
+    far_edge, gathered, node_weight = lax.optimization_barrier(
+        (far_edge, gathered, node_weight)
     )
     edge_in, edge_out = [
         [weight] + near + far + from_subs(far)
         for weight, near, far in zip((edge_in_weight, edge_out_weight), near_edge, far_edge)
     ]
-    far_node = [from_feats(node_in_weight), from_feats(node_out_weight)]
-    node_in, node_out = [
-        [weight] + from_subs([weight]) + far + from_subs(far)
-        for weight, far in zip((node_in_weight, node_out_weight), far_node)
-    ]
+    far_node = from_feats(node_weight)
+    node_pieces = [node_weight] + from_subs([node_weight]) + far_node + from_subs(far_node)
     pieces_count = len(edge_in)
 
     rows = [value.reshape(1, -1) for value in (edge_in_bias, edge_out_bias, edge_gain, edge_offset)]
     edge_new, partial_sums = pl.pallas_call(
-        functools.partial(edge_kernel, pieces_count),
+        functools.partial(edge_kernel, pieces_count, len(got), part_count, near_cap, padded),
         grid=(steps,),
         out_shape=[
             jax.ShapeDtypeStruct((edge_count, width), bf16),
@@ -326,9 +361,10 @@
         ],
         in_specs=[
             pl.BlockSpec((block, width), lambda step: (step, 0)),
-            pl.BlockSpec((block, 2 * width), lambda step: (step, 0)),
+            pl.BlockSpec((block, gathered_width), lambda step: (step, 0)),
             index_spec,
         ]
+        + [whole(rows) for rows in got]
         + [whole(piece) for piece in edge_in + edge_out]
         + [whole(row) for row in rows],
         out_specs=[
@@ -336,18 +372,19 @@
             pl.BlockSpec((node_count, width), lambda step: (0, 0)),
         ],
         scratch_shapes=[
-            pltpu.VMEM((3, pieces_count * edge_in_weight.shape[1], width), bf16),
-            pltpu.VMEM((pieces_count * edge_out_weight.shape[0], width), bf16),
+            pltpu.VMEM((3 * width + halo_space, width), bf16),
+            pltpu.VMEM((width, width), bf16),
+            pltpu.VMEM((halo_space, width), bf16),
             pltpu.VMEM((node_count, width), f32),
         ],
-        compiler_params=pltpu.CompilerParams(vmem_limit_bytes=40 << 20),
+        compiler_params=pltpu.CompilerParams(vmem_limit_bytes=grant),
         cost_estimate=pl.CostEstimate(
             flops=2 * edge_count * width * (4 * width + node_count),
             bytes_accessed=8 * edge_count * width,
             transcendentals=edge_count * width,
         ),
         name="edge_update",
-    )(edge_latent, gathered, receiver_blocks, *edge_in, *edge_out, *rows)
+    )(edge_latent, gathered, receiver_blocks, *got, *edge_in, *edge_out, *rows)
 
     subs = lax.axis_size("sub")
     other_sums = lax.ppermute(partial_sums, "sub", [(at, (at + 1) % subs) for at in range(subs)])
@@ -356,20 +393,19 @@
     node_new = pl.pallas_call(
         functools.partial(node_kernel, pieces_count),
         out_shape=jax.ShapeDtypeStruct((node_count, width), bf16),
-        in_specs=[vmem] * (3 + 2 * pieces_count + 4),
+        in_specs=[vmem] * (3 + pieces_count + 4),
         out_specs=vmem,
         scratch_shapes=[
-            pltpu.VMEM((2, pieces_count * node_in_weight.shape[1], width), bf16),
-            pltpu.VMEM((pieces_count * node_out_weight.shape[0], width), bf16),
-        ],
-        compiler_params=pltpu.CompilerParams(vmem_limit_bytes=40 << 20),
+            pltpu.VMEM((3 * width, width), bf16),
+        ],
+        compiler_params=pltpu.CompilerParams(vmem_limit_bytes=grant),
         cost_estimate=pl.CostEstimate(
             flops=2 * node_count * width * 3 * width,
             bytes_accessed=10 * node_count * width,
             transcendentals=node_count * width,
         ),
         name="node_update",
-    )(node_latent, partial_sums, other_sums, *node_in, *node_out, *rows)
+    )(node_latent, partial_sums, other_sums, *node_pieces, *rows)
     return (edge_new, node_new)
 
 

time: 48.9 us -> 50.5 us (1.033)
  Pallas kernels: 16.4 us -> 31.7 us
  waiting for transfers between devices: 15.7 us -> 2.73 us
    pallas_call x2, Pallas kernels: 12.2 us -> 25.8 us  [the longest x1 15.1 us: shards(): pl.pallas_call(functools.partial(gather_kernel, node_count, near_cap, far...]
    all_to_all x1, waiting for transfers between devices: 8.35 us -> 0.01 us  [exchange_padded(): lax.all_to_all(blocks, ('region', 'feat'), split_axis=0, concat_axis=0, t...]
    ppermute x4 -> x3, waiting for transfers between devices: 5.31 us -> 0.01 us  [from_feats(): lax.ppermute(weight, 'feat', [(at, (at + shift) % feats) for at in range(...]
    all_to_all x1, starting transfers between devices: 7.26 us -> 4.87 us  [exchange_padded(): lax.all_to_all(blocks, ('region', 'feat'), split_axis=0, concat_axis=0, t...]
    pallas_call x1, Pallas kernels: 1.99 us -> 3.75 us  [shards(): pl.pallas_call(functools.partial(node_kernel, pieces_count), out_shape=ja...]
    ppermute x1, waiting for transfers between devices: 0.01 us -> 1.41 us  [shards(): lax.ppermute(partial_sums, 'sub', [(at, (at + 1) % subs) for at in range(...]
    ppermute x4 -> x3, starting transfers between devices: 4 us -> 5.1 us  [from_feats(): lax.ppermute(weight, 'feat', [(at, (at + shift) % feats) for at in range(...]
    ppermute x8 -> x6, starting transfers between devices: 1.11 us -> 1.83 us  [from_subs(): lax.ppermute(piece, 'sub', [(at, (at + turn) % subs) for at in range(subs)])]
  transfers between devices with their start and end apart: 14 -> 11, of which waited for: 6 -> 3; matrix products, arithmetic and copies ran while one was open for 2% -> 2% of each run, Pallas kernels for 25% -> 56%
where the time goes in v3:
time: 50.5 us; the launch traced here: 50.2 us
  Pallas kernels  31.7 us (63%)
  starting transfers between devices  12 us (24%)
  local copies, waits for them, and re-layouts  2.96 us (6%)
  waiting for transfers between devices  2.73 us (5%)
  between operations  0.79 us (2%)
    pallas_call x1, Pallas kernels, shards(): pl.pallas_call(functools.partial(gather_kernel, node_count, near_cap, far...  15.1 us
    pallas_call x1, Pallas kernels, shards(): pl.pallas_call(functools.partial(edge_kernel, pieces_count, len(got), par...  10.7 us
    ppermute x3, starting transfers between devices, from_feats(): lax.ppermute(weight, 'feat', [(at, (at + shift) % feats) for at in range(...  5.1 us
    all_to_all x1, starting transfers between devices, exchange_padded(): lax.all_to_all(blocks, ('region', 'feat'), split_axis=0, concat_axis=0, t...  4.87 us
    pallas_call x1, Pallas kernels, shards(): pl.pallas_call(functools.partial(node_kernel, pieces_count), out_shape=ja...  3.75 us
    pallas_call x1, Pallas kernels, exchange_padded(): pl.pallas_call(functools.partial(pick_kernel, part_count, near_cap, far_c...  2.18 us
    ppermute x6, starting transfers between devices, from_subs(): lax.ppermute(piece, 'sub', [(at, (at + turn) % subs) for at in range(subs)])  1.83 us
    unnamed x30, local copies, waits for them, and re-layouts  1.75 us
  transfers between devices with their start and end apart: 11, of which 3 were waited for; matrix products, arithmetic and copies ran while one was open for 2% of the time, Pallas kernels for 56%

profile of v3, /device:TPU:0, one launch (start us, length us, event | category | flops | bytes accessed | tf_op | source)
XLA Modules:
  0.0 50.2 jit_solution(865923877627234463)
XLA Ops:
  0.7 3.0 %collective-permute-start = (bf16[3,128,512]{2,1,0:T(8,128)(2,1)}, bf16[3,128,512]{2,1,0:T(8,128)(2,1)S(1)}, u32[]{:S(2)}, u32[]{:S(2)}) collective-permute-start(bf16[3,128,512]{2,1,0:T(8,128)(2,1)} %refs_4_.1), channel_id=1, source_target_pairs={{0,2},{2,0},{1,3},{3,1},{4,6},{6,4},{5,7},{7,5},{8,10},{10,8},{9,1... | collective-permute-start | bytes 1179656 | tf_op jit(solution)/shard_map/ppermute | solution.py:194
  3.7 2.2 %pick_halo.1 = bf16[8,48,512]{2,1,0:T(8,128)(2,1)} custom-call(s32[1,2,8]{2,1,0:T(2,128)} %bitcast.13, s32[1,4,32]{2,1,0:T(4,128)} %near_ref.1, bf16[384,512]{1,0:T(8,128)(2,1)} %refs_0_.3), custom_call_target="tpu_custom_call" | custom-call | tf_op jit(solution)/shard_map/pick_halo/pallas_call | solution.py:82
  5.9 4.9 %all-to-all-start = ((bf16[8,48,512]{2,1,0:T(8,128)(2,1)}), bf16[8,48,512]{2,1,0:T(8,128)(2,1)S(1)}, u32[]{:S(2)}, u32[]{:S(2)}) async-start(bf16[8,48,512]{2,1,0:T(8,128)(2,1)} %pick_halo.1), calls=%async_computation | async-start | bytes 786432 | tf_op jit(solution)/shard_map/all_to_all | solution.py:91
  10.7 2.0 %collective-permute-start.1 = (bf16[128,512]{1,0:T(8,128)(2,1)S(1)}, bf16[128,512]{1,0:T(8,128)(2,1)S(1)}, u32[]{:S(2)}, u32[]{:S(2)}) collective-permute-start(bf16[128,512]{1,0:T(8,128)(2,1)S(1)} %copy-done.11), channel_id=1, source_target_pairs={{0,2},{2,0},{1,3},{3,1},{4,6},{6,4},{5,7},{7,5},{8,10},{10,8},{9,1... | collective-permute-start | bytes 393224 | tf_op jit(solution)/shard_map/ppermute | solution.py:194
  12.8 0.6 %reshape.35.receiver_ref.refs_2_ = s32[3,1,512]{2,1,0:T(1,128)} reshape(s32[1536]{0:T(1024)S(1)} %copy-done.5) | data formatting | bytes 12288 | tf_op jit(solution)/shard_map/reshape | solution.py:318
  13.4 0.6 %reshape.34.source_ref = s32[3,1,512]{2,1,0:T(1,128)} reshape(s32[1536]{0:T(1024)S(1)} %copy-done.6) | data formatting | bytes 12288 | tf_op jit(solution)/shard_map/reshape | solution.py:317
  14.0 15.1 %gather_latents.1 = (bf16[1536,1280]{1,0:T(8,128)(2,1)}, bf16[3,128,512]{2,1,0:T(8,128)(2,1)}) custom-call(s32[3,1,512]{2,1,0:T(1,128)} %reshape.34.source_ref, s32[3,1,512]{2,1,0:T(1,128)} %reshape.35.receiver_ref.refs_2_, bf16[384,512]{1,0:T(8,128)(2,1)} %refs_0_.3, bf16[2,128,512]{2,1,0:T(8,128)(2,1)} %node_in_ref.1, bf16[128,512]{1,0:T(8,128)(2,1)} %node_out_ref.1), custom_call_target="tpu_custom_call" | custom-call | tf_op jit(solution)/shard_map/gather_latents/pallas_call | solution.py:326
  29.2 0.6 %collective-permute-start.3 = (bf16[3,128,512]{2,1,0:T(8,128)(2,1)S(1)}, bf16[3,128,512]{2,1,0:T(8,128)(2,1)S(1)}, u32[]{:S(2)}, u32[]{:S(2)}) collective-permute-start(bf16[3,128,512]{2,1,0:T(8,128)(2,1)S(1)} %collective-permute-done.refs_6_), channel_id=1, source_target_pairs={{0,1},{1,0},{2,3},{3,2},{4,5},{5,4},{6,7},{7,6},{8,9},{9,8},{10,11... | collective-permute-start | bytes 1179656 | tf_op jit(solution)/shard_map/ppermute | solution.py:202
  29.7 0.1 collective-permute-start.4
  29.8 0.4 collective-permute-start.5
  30.3 0.9 %collective-permute-done.4.refs_9_ = bf16[128,512]{1,0:T(8,128)(2,1)S(1)} collective-permute-done((bf16[128,512]{1,0:T(8,128)(2,1)S(1)}, bf16[128,512]{1,0:T(8,128)(2,1)S(1)}, u32[]{:S(2)}, u32[]{:S(2)}) %collective-permute-start.4) | collective-permute-done | bytes 131104 | tf_op jit(solution)/shard_map/ppermute | solution.py:202
  31.3 0.4 collective-permute-start.7
  31.7 0.2 copy-done.13
  31.9 0.5 copy-done.9
  32.5 0.1 copy-done.4
  32.6 0.1 copy-done.10
  32.7 10.7 %edge_update.1 = (bf16[1536,512]{1,0:T(8,128)(2,1)}, bf16[384,512]{1,0:T(8,128)(2,1)}) custom-call(bf16[1536,512]{1,0:T(8,128)(2,1)} %refs_0_.2, bf16[1536,1280]{1,0:T(8,128)(2,1)} %get-tuple-element.12.refs_1_, s32[3,1,512]{2,1,0:T(1,128)} %reshape.35.receiver_ref.refs_2_, bf16[8,48,512]{2,1,0:T(8,128)(2,1)} %copy-done.4, bf16[3,128,512]{2,1,0:T(8,128)(2,1)} %refs_4_.1, ...), custom_call_target="tpu_custom_call" | custom-call | flops 3825205248 | bytes 6291456 | tf_op jit(solution)/shard_map/edge_update/pallas_call | solution.py:355
  43.4 0.2 collective-permute-start.6
  43.6 0.4 collective-permute-start.9
  44.0 1.4 %collective-permute-done.6.refs_2_ = bf16[384,512]{1,0:T(8,128)(2,1)S(1)} collective-permute-done((bf16[384,512]{1,0:T(8,128)(2,1)}, bf16[384,512]{1,0:T(8,128)(2,1)S(1)}, u32[]{:S(2)}, u32[]{:S(2)}) %collective-permute-start.6) | collective-permute-done | bytes 393248 | tf_op jit(solution)/shard_map/ppermute | solution.py:390
  45.4 0.3 collective-permute-done.9.refs_6_
  45.7 0.4 copy-done.2
  46.1 0.3 copy-done.3
  46.5 3.7 %node_update.1 = bf16[384,512]{1,0:T(8,128)(2,1)} custom-call(bf16[384,512]{1,0:T(8,128)(2,1)} %refs_0_.3, bf16[384,512]{1,0:T(8,128)(2,1)} %get-tuple-element.16.refs_1_, bf16[384,512]{1,0:T(8,128)(2,1)} %copy-done.2, bf16[3,128,512]{2,1,0:T(8,128)(2,1)} %get-tuple-element.17.refs_3_, bf16[3,128,512]{2,1,0:T(8,128)(2,1)} %copy-done.1, ...), custom_call_target="tpu_custom_call" | custom-call | flops 603979776 | bytes 1966080 | tf_op jit(solution)/shard_map/node_update/pallas_call | solution.py:393
  (34 shorter events, 0.2 us)
Async XLA Ops:
  0.6 12.1 %copy-start.7 = (bf16[3,128,512]{2,1,0:T(8,128)(2,1)S(1)}, bf16[3,128,512]{2,1,0:T(8,128)(2,1)}, u32[]{:S(2)}) copy-start(bf16[3,128,512]{2,1,0:T(8,128)(2,1)} %refs_4_.1) | copy-start | bytes 1179652
  0.6 10.1 %copy-start.11 = (bf16[128,512]{1,0:T(8,128)(2,1)S(1)}, bf16[128,512]{1,0:T(8,128)(2,1)}, u32[]{:S(2)}) copy-start(bf16[128,512]{1,0:T(8,128)(2,1)} %refs_8_.1) | copy-start | bytes 393220
  0.7 12.1 %copy-start.5 = (s32[1536]{0:T(1024)S(1)}, s32[1536]{0:T(1024)}, u32[]{:S(2)}) copy-start(s32[1536]{0:T(1024)} %param.21) | copy-start | bytes 18436
  0.7 12.7 %copy-start.6 = (s32[1536]{0:T(1024)S(1)}, s32[1536]{0:T(1024)}, u32[]{:S(2)}) copy-start(s32[1536]{0:T(1024)} %param.20) | copy-start | bytes 18436
  0.7 28.5 %collective-permute-start = (bf16[3,128,512]{2,1,0:T(8,128)(2,1)}, bf16[3,128,512]{2,1,0:T(8,128)(2,1)S(1)}, u32[]{:S(2)}, u32[]{:S(2)}) collective-permute-start(bf16[3,128,512]{2,1,0:T(8,128)(2,1)} %refs_4_.1), channel_id=1, source_target_pairs={{0,2},{2,0},{1,3},{3,1},{4,6},{6,4},{5,7},{7,5},{8,10},{10,8},{9,1... | collective-permute-start | bytes 1179656 | tf_op jit(solution)/shard_map/ppermute | solution.py:194
  5.9 25.8 %all-to-all-start = ((bf16[8,48,512]{2,1,0:T(8,128)(2,1)}), bf16[8,48,512]{2,1,0:T(8,128)(2,1)S(1)}, u32[]{:S(2)}, u32[]{:S(2)}) async-start(bf16[8,48,512]{2,1,0:T(8,128)(2,1)} %pick_halo.1), calls=%async_computation | async-start | bytes 786432 | tf_op jit(solution)/shard_map/all_to_all | solution.py:91
  10.7 18.4 %collective-permute-start.1 = (bf16[128,512]{1,0:T(8,128)(2,1)S(1)}, bf16[128,512]{1,0:T(8,128)(2,1)S(1)}, u32[]{:S(2)}, u32[]{:S(2)}) collective-permute-start(bf16[128,512]{1,0:T(8,128)(2,1)S(1)} %copy-done.11), channel_id=1, source_target_pairs={{0,2},{2,0},{1,3},{3,1},{4,6},{6,4},{5,7},{7,5},{8,10},{10,8},{9,1... | collective-permute-start | bytes 393224 | tf_op jit(solution)/shard_map/ppermute | solution.py:194
  12.8 18.9 %collective-permute-start.2 = (bf16[3,128,512]{2,1,0:T(8,128)(2,1)S(1)}, bf16[3,128,512]{2,1,0:T(8,128)(2,1)S(1)}, u32[]{:S(2)}, u32[]{:S(2)}) collective-permute-start(bf16[3,128,512]{2,1,0:T(8,128)(2,1)S(1)} %copy-done.7), channel_id=1, source_target_pairs={{0,1},{1,0},{2,3},{3,2},{4,5},{5,4},{6,7},{7,6},{8,9},{9,8},{10,11... | collective-permute-start | bytes 1179656 | tf_op jit(solution)/shard_map/ppermute | solution.py:202
  29.1 2.6 %copy-start.12 = (bf16[128,512]{1,0:T(8,128)(2,1)}, bf16[128,512]{1,0:T(8,128)(2,1)S(1)}, u32[]{:S(2)}) copy-start(bf16[128,512]{1,0:T(8,128)(2,1)S(1)} %collective-permute-done.1.refs_10_) | copy-start | bytes 393220
  29.2 2.6 %copy-start.8 = (bf16[3,128,512]{2,1,0:T(8,128)(2,1)}, bf16[3,128,512]{2,1,0:T(8,128)(2,1)S(1)}, u32[]{:S(2)}) copy-start(bf16[3,128,512]{2,1,0:T(8,128)(2,1)S(1)} %collective-permute-done.refs_6_) | copy-start | bytes 1179652
  29.2 2.5 %collective-permute-start.3 = (bf16[3,128,512]{2,1,0:T(8,128)(2,1)S(1)}, bf16[3,128,512]{2,1,0:T(8,128)(2,1)S(1)}, u32[]{:S(2)}, u32[]{:S(2)}) collective-permute-start(bf16[3,128,512]{2,1,0:T(8,128)(2,1)S(1)} %collective-permute-done.refs_6_), channel_id=1, source_target_pairs={{0,1},{1,0},{2,3},{3,2},{4,5},{5,4},{6,7},{7,6},{8,9},{9,8},{10,11... | collective-permute-start | bytes 1179656 | tf_op jit(solution)/shard_map/ppermute | solution.py:202
  29.7 1.5 %collective-permute-start.4 = (bf16[128,512]{1,0:T(8,128)(2,1)S(1)}, bf16[128,512]{1,0:T(8,128)(2,1)S(1)}, u32[]{:S(2)}, u32[]{:S(2)}) collective-permute-start(bf16[128,512]{1,0:T(8,128)(2,1)S(1)} %copy-done.11), channel_id=1, source_target_pairs={{0,1},{1,0},{2,3},{3,2},{4,5},{5,4},{6,7},{7,6},{8,9},{9,8},{10,11... | collective-permute-start | bytes 393224 | tf_op jit(solution)/shard_map/ppermute | solution.py:202
  29.8 1.8 %collective-permute-start.5 = (bf16[128,512]{1,0:T(8,128)(2,1)S(1)}, bf16[128,512]{1,0:T(8,128)(2,1)S(1)}, u32[]{:S(2)}, u32[]{:S(2)}) collective-permute-start(bf16[128,512]{1,0:T(8,128)(2,1)S(1)} %collective-permute-done.1.refs_10_), channel_id=1, source_target_pairs={{0,1},{1,0},{2,3},{3,2},{4,5},{5,4},{6,7},{7,6},{8,9},{9,8},{10,11... | collective-permute-start | bytes 393224 | tf_op jit(solution)/shard_map/ppermute | solution.py:202
  30.2 13.3 %collective-permute-start.8 = (bf16[3,128,512]{2,1,0:T(8,128)(2,1)}, bf16[3,128,512]{2,1,0:T(8,128)(2,1)S(1)}, u32[]{:S(2)}, u32[]{:S(2)}) collective-permute-start(bf16[3,128,512]{2,1,0:T(8,128)(2,1)} %get-tuple-element.17.refs_3_), channel_id=1, source_target_pairs={{0,2},{2,0},{1,3},{3,1},{4,6},{6,4},{5,7},{7,5},{8,10},{10,8},{9,1... | collective-permute-start | bytes 1179656 | tf_op jit(solution)/shard_map/ppermute | solution.py:194
  31.3 12.7 %collective-permute-start.7 = (bf16[3,128,512]{2,1,0:T(8,128)(2,1)}, bf16[3,128,512]{2,1,0:T(8,128)(2,1)S(1)}, u32[]{:S(2)}, u32[]{:S(2)}) collective-permute-start(bf16[3,128,512]{2,1,0:T(8,128)(2,1)} %get-tuple-element.17.refs_3_), channel_id=1, source_target_pairs={{0,1},{1,0},{2,3},{3,2},{4,5},{5,4},{6,7},{7,6},{8,9},{9,8},{10,11... | collective-permute-start | bytes 1179656 | tf_op jit(solution)/shard_map/ppermute | solution.py:202
  31.7 0.8 %copy-start.9 = (bf16[3,128,512]{2,1,0:T(8,128)(2,1)}, bf16[3,128,512]{2,1,0:T(8,128)(2,1)S(1)}, u32[]{:S(2)}) copy-start(bf16[3,128,512]{2,1,0:T(8,128)(2,1)S(1)} %collective-permute-done.2.refs_5_) | copy-start | bytes 1179652
  31.7 0.8 %copy-start.14 = (bf16[128,512]{1,0:T(8,128)(2,1)}, bf16[128,512]{1,0:T(8,128)(2,1)S(1)}, u32[]{:S(2)}) copy-start(bf16[128,512]{1,0:T(8,128)(2,1)S(1)} %collective-permute-done.5.refs_11_) | copy-start | bytes 393220
  31.7 0.9 %copy-start.4 = (bf16[8,48,512]{2,1,0:T(8,128)(2,1)}, bf16[8,48,512]{2,1,0:T(8,128)(2,1)S(1)}, u32[]{:S(2)}) copy-start(bf16[8,48,512]{2,1,0:T(8,128)(2,1)S(1)} %all-to-all-done.refs_3_) | copy-start | bytes 1179652
  31.7 1.0 %copy-start.10 = (bf16[3,128,512]{2,1,0:T(8,128)(2,1)}, bf16[3,128,512]{2,1,0:T(8,128)(2,1)S(1)}, u32[]{:S(2)}) copy-start(bf16[3,128,512]{2,1,0:T(8,128)(2,1)S(1)} %collective-permute-done.3.refs_7_) | copy-start | bytes 1179652
  43.4 2.0 %collective-permute-start.6 = (bf16[384,512]{1,0:T(8,128)(2,1)}, bf16[384,512]{1,0:T(8,128)(2,1)S(1)}, u32[]{:S(2)}, u32[]{:S(2)}) collective-permute-start(bf16[384,512]{1,0:T(8,128)(2,1)} %get-tuple-element.16.refs_1_), channel_id=1, source_target_pairs={{0,1},{1,0},{2,3},{3,2},{4,5},{5,4},{6,7},{7,6},{8,9},{9,8},{10,11... | collective-permute-start | bytes 1179656 | tf_op jit(solution)/shard_map/ppermute | solution.py:390
  43.6 2.1 %copy-start = (bf16[3,128,512]{2,1,0:T(8,128)(2,1)}, bf16[3,128,512]{2,1,0:T(8,128)(2,1)S(1)}, u32[]{:S(2)}) copy-start(bf16[3,128,512]{2,1,0:T(8,128)(2,1)S(1)} %collective-permute-done.8.refs_5_) | copy-start | bytes 1179652
  43.6 2.1 %collective-permute-start.9 = (bf16[3,128,512]{2,1,0:T(8,128)(2,1)S(1)}, bf16[3,128,512]{2,1,0:T(8,128)(2,1)S(1)}, u32[]{:S(2)}, u32[]{:S(2)}) collective-permute-start(bf16[3,128,512]{2,1,0:T(8,128)(2,1)S(1)} %collective-permute-done.8.refs_5_), channel_id=1, source_target_pairs={{0,1},{1,0},{2,3},{3,2},{4,5},{5,4},{6,7},{7,6},{8,9},{9,8},{10,11... | collective-permute-start | bytes 1179656 | tf_op jit(solution)/shard_map/ppermute | solution.py:202
  44.0 1.8 %copy-start.1 = (bf16[3,128,512]{2,1,0:T(8,128)(2,1)}, bf16[3,128,512]{2,1,0:T(8,128)(2,1)S(1)}, u32[]{:S(2)}) copy-start(bf16[3,128,512]{2,1,0:T(8,128)(2,1)S(1)} %collective-permute-done.7.refs_4_) | copy-start | bytes 1179652
  45.4 0.8 %copy-start.2 = (bf16[384,512]{1,0:T(8,128)(2,1)}, bf16[384,512]{1,0:T(8,128)(2,1)S(1)}, u32[]{:S(2)}) copy-start(bf16[384,512]{1,0:T(8,128)(2,1)S(1)} %collective-permute-done.6.refs_2_) | copy-start | bytes 1179652
  (2 other events, 1.4 us)

commit v4 on v3

--- a/solution.py
+++ b/solution.py
@@ -11,7 +11,7 @@
 tile_rows = 16
 lanes = 128
 padded_parts = 8
-grant = 56 << 20
+grant = 24 << 20
 bf16 = jnp.bfloat16
 f32 = jnp.float32
 vmem = pl.BlockSpec(memory_space=pltpu.VMEM)
@@ -84,6 +84,7 @@
         out_shape=jax.ShapeDtypeStruct(block, bf16),
         in_specs=[vmem, vmem, vmem],
         out_specs=vmem,
+        compiler_params=pltpu.CompilerParams(vmem_limit_bytes=grant),
         cost_estimate=pl.CostEstimate(flops=0, bytes_accessed=0, transcendentals=0),
         name="pick_halo",
     )(jnp.transpose(far_rows, (0, 2, 1)), near_rows, node_latent)
@@ -117,22 +118,20 @@
     node_out_ref,
     out_ref,
     pack_ref,
-    sems,
 ):
     width = latent_ref.shape[1]
     halo_start = 2 * width
     count = node_in_ref.shape[0]
-    copies = [
-        pltpu.make_async_copy(node_in_ref, pack_ref.at[pl.ds(0, count)], sems.at[0]),
-        pltpu.make_async_copy(node_out_ref, pack_ref.at[count], sems.at[1]),
-    ]
 
     @pl.when(pl.program_id(0) == 0)
     def _():
-        for copy in copies:
-            copy.start()
-
-    columns = as_columns(source_ref[0])
+        pack_ref[:count] = node_in_ref[...]
+        pack_ref[count] = node_out_ref[...]
+
+    source = source_ref[0]
+    far = source - (node_count + len(near_offsets) * near_cap)
+    spread = source + lax.div(far, far_cap) * (far_stride - far_cap)
+    columns = as_columns(jnp.where(far >= 0, spread, source))
     latent = latent_ref[...]
     sent = one_hot(columns, node_count)
     out_ref[:, :width] = jnp.dot(sent, latent, preferred_element_type=f32).astype(bf16)
@@ -140,16 +139,7 @@
     out_ref[:, width:halo_start] = jnp.dot(
         received, latent, preferred_element_type=f32
     ).astype(bf16)
-    slot = columns - node_count
-    far = slot - len(near_offsets) * near_cap
-    part = lax.div(far, far_cap)
-    slot = jnp.where(far >= 0, slot + part * (far_stride - far_cap), slot)
-    out_ref[:, halo_start:] = one_hot(slot, halo_space)
-
-    @pl.when(pl.program_id(0) == pl.num_programs(0) - 1)
-    def _():
-        for copy in copies:
-            copy.wait()
+    out_ref[:, halo_start:] = one_hot(columns - node_count, halo_space)
 
 
 def place_halo(table, part_count, near_cap, padded, got_refs):
@@ -321,7 +311,7 @@
     def whole(array):
         return pl.BlockSpec(array.shape, lambda step: (0,) * array.ndim)
 
-    hbm = pl.BlockSpec(memory_space=pl.ANY)
+    pack_shape = (node_in_weight.shape[0] + 1,) + node_out_weight.shape
     gathered_width = 2 * width + halo_space
     gathered, node_weight = pl.pallas_call(
         functools.partial(
@@ -330,11 +320,14 @@
         grid=(steps,),
         out_shape=[
             jax.ShapeDtypeStruct((edge_count, gathered_width), bf16),
-            jax.ShapeDtypeStruct((node_in_weight.shape[0] + 1,) + node_out_weight.shape, bf16),
-        ],
-        in_specs=[index_spec, index_spec, whole(node_latent), hbm, hbm],
-        out_specs=[pl.BlockSpec((block, gathered_width), lambda step: (step, 0)), hbm],
-        scratch_shapes=[pltpu.SemaphoreType.DMA((2,))],
+            jax.ShapeDtypeStruct(pack_shape, bf16),
+        ],
+        in_specs=[index_spec, index_spec]
+        + [whole(array) for array in (node_latent, node_in_weight, node_out_weight)],
+        out_specs=[
+            pl.BlockSpec((block, gathered_width), lambda step: (step, 0)),
+            pl.BlockSpec(pack_shape, lambda step: (0, 0, 0)),
+        ],
         compiler_params=pltpu.CompilerParams(vmem_limit_bytes=grant),
         cost_estimate=pl.CostEstimate(flops=0, bytes_accessed=0, transcendentals=0),
         name="gather_latents",

time: 50.5 us -> 45.5 us (0.901)
  Pallas kernels: 31.7 us -> 14.8 us
  local copies, waits for them, and re-layouts: 2.96 us -> 14.2 us
    pallas_call x1, Pallas kernels: 15.1 us -> 2.39 us  [shards(): pl.pallas_call(functools.partial(gather_kernel, node_count, near_cap, far...]
    unnamed x30 -> x46, local copies, waits for them, and re-layouts: 1.75 us -> 12.8 us
    pallas_call x1, Pallas kernels: 3.75 us -> 2.01 us  [shards(): pl.pallas_call(functools.partial(node_kernel, pieces_count), out_shape=ja...]
    pallas_call x1, Pallas kernels: 10.7 us -> 9.22 us  [shards(): pl.pallas_call(functools.partial(edge_kernel, pieces_count, len(got), par...]
    pallas_call x1, Pallas kernels: 2.18 us -> 1.16 us  [exchange_padded(): pl.pallas_call(functools.partial(pick_kernel, part_count, near_cap, far_c...]
    ppermute x3, waiting for transfers between devices: 0.01 us -> 0.95 us  [from_feats(): lax.ppermute(weight, 'feat', [(at, (at + shift) % feats) for at in range(...]
    ppermute x3, starting transfers between devices: 5.1 us -> 5.96 us  [from_feats(): lax.ppermute(weight, 'feat', [(at, (at + shift) % feats) for at in range(...]
    ppermute x6, starting transfers between devices: 1.83 us -> 1.2 us  [from_subs(): lax.ppermute(piece, 'sub', [(at, (at + turn) % subs) for at in range(subs)])]
  transfers between devices with their start and end apart: 11 -> 11, of which waited for: 3 -> 4; matrix products, arithmetic and copies ran while one was open for 2% -> 3% of each run, Pallas kernels for 56% -> 28%
where the time goes in v4:
time: 45.5 us; the launch traced here: 45 us
  Pallas kernels  14.8 us (33%)
  local copies, waits for them, and re-layouts  14.2 us (31%)
  starting transfers between devices  12.2 us (27%)
  waiting for transfers between devices  3.07 us (7%)
  between operations  0.76 us (2%)
    unnamed x46, local copies, waits for them, and re-layouts  12.8 us
    pallas_call x1, Pallas kernels, shards(): pl.pallas_call(functools.partial(edge_kernel, pieces_count, len(got), par...  9.22 us
    ppermute x3, starting transfers between devices, from_feats(): lax.ppermute(weight, 'feat', [(at, (at + shift) % feats) for at in range(...  5.96 us
    all_to_all x1, starting transfers between devices, exchange_padded(): lax.all_to_all(blocks, ('region', 'feat'), split_axis=0, concat_axis=0, t...  4.87 us
    pallas_call x1, Pallas kernels, shards(): pl.pallas_call(functools.partial(gather_kernel, node_count, near_cap, far...  2.39 us
    pallas_call x1, Pallas kernels, shards(): pl.pallas_call(functools.partial(node_kernel, pieces_count), out_shape=ja...  2.01 us
    ppermute x1, waiting for transfers between devices, shards(): lax.ppermute(partial_sums, 'sub', [(at, (at + 1) % subs) for at in range(...  1.21 us
    ppermute x6, starting transfers between devices, from_subs(): lax.ppermute(piece, 'sub', [(at, (at + turn) % subs) for at in range(subs)])  1.2 us
  transfers between devices with their start and end apart: 11, of which 4 were waited for; matrix products, arithmetic and copies ran while one was open for 3% of the time, Pallas kernels for 28%

profile of v4, /device:TPU:0, one launch (start us, length us, event | category | flops | bytes accessed | tf_op | source)
XLA Modules:
  0.0 45.0 jit_solution(11720770631366596158)
XLA Ops:
  0.6 3.0 %collective-permute-start = (bf16[3,128,512]{2,1,0:T(8,128)(2,1)}, bf16[3,128,512]{2,1,0:T(8,128)(2,1)}, u32[]{:S(2)}, u32[]{:S(2)}) collective-permute-start(bf16[3,128,512]{2,1,0:T(8,128)(2,1)} %refs_4_.1), channel_id=1, source_target_pairs={{0,2},{2,0},{1,3},{3,1},{4,6},{6,4},{5,7},{7,5},{8,10},{10,8},{9,1... | collective-permute-start | bytes 1179656 | tf_op jit(solution)/shard_map/ppermute | solution.py:184
  3.6 1.0 %copy-done = bf16[384,512]{1,0:T(8,128)(2,1)S(1)} copy-done((bf16[384,512]{1,0:T(8,128)(2,1)S(1)}, bf16[384,512]{1,0:T(8,128)(2,1)}, u32[]{:S(2)}) %copy-start) | copy-done | bytes 393240
  4.6 0.7 %copy-done.4 = s32[1,4,32]{2,1,0:T(4,128)S(1)} copy-done((s32[1,4,32]{2,1,0:T(4,128)S(1)}, s32[1,4,32]{2,1,0:T(4,128)}, u32[]{:S(2)}) %copy-start.4) | copy-done | bytes 536
  5.3 0.7 %copy-done.9 = s32[1,8,2]{1,2,0:T(2,128)S(1)} copy-done((s32[1,8,2]{1,2,0:T(2,128)S(1)}, s32[1,8,2]{1,2,0:T(2,128)}, u32[]{:S(2)}) %copy-start.9) | copy-done | bytes 88
  6.0 1.2 %pick_halo.1 = bf16[8,48,512]{2,1,0:T(8,128)(2,1)} custom-call(s32[1,2,8]{2,1,0:T(2,128)S(1)} %bitcast.13, s32[1,4,32]{2,1,0:T(4,128)S(1)} %copy-done.4, bf16[384,512]{1,0:T(8,128)(2,1)S(1)} %copy-done), custom_call_target="tpu_custom_call" | custom-call | tf_op jit(solution)/shard_map/pick_halo/pallas_call | solution.py:82
  7.2 4.9 %all-to-all-start = ((bf16[8,48,512]{2,1,0:T(8,128)(2,1)}), bf16[8,48,512]{2,1,0:T(8,128)(2,1)S(1)}, u32[]{:S(2)}, u32[]{:S(2)}) async-start(bf16[8,48,512]{2,1,0:T(8,128)(2,1)} %pick_halo.1), calls=%async_computation | async-start | bytes 786432 | tf_op jit(solution)/shard_map/all_to_all | solution.py:92
  12.1 2.0 %collective-permute-start.1 = (bf16[128,512]{1,0:T(8,128)(2,1)}, bf16[128,512]{1,0:T(8,128)(2,1)}, u32[]{:S(2)}, u32[]{:S(2)}) collective-permute-start(bf16[128,512]{1,0:T(8,128)(2,1)} %refs_8_.1), channel_id=1, source_target_pairs={{0,2},{2,0},{1,3},{3,1},{4,6},{6,4},{5,7},{7,5},{8,10},{10,8},{9,1... | collective-permute-start | bytes 393224 | tf_op jit(solution)/shard_map/ppermute | solution.py:184
  14.1 0.7 %reshape.35.receiver_ref.refs_2_ = s32[3,1,512]{2,1,0:T(1,128)S(1)} reshape(s32[1536]{0:T(1024)} %param.21) | data formatting | bytes 12288 | tf_op jit(solution)/shard_map/reshape | solution.py:308
  14.8 0.7 %reshape.34.source_ref = s32[3,1,512]{2,1,0:T(1,128)S(1)} reshape(s32[1536]{0:T(1024)} %param.20) | data formatting | bytes 12288 | tf_op jit(solution)/shard_map/reshape | solution.py:307
  15.5 2.4 %gather_latents.1 = (bf16[1536,1280]{1,0:T(8,128)(2,1)S(1)}, bf16[3,128,512]{2,1,0:T(8,128)(2,1)S(1)}) custom-call(s32[3,1,512]{2,1,0:T(1,128)S(1)} %reshape.34.source_ref, s32[3,1,512]{2,1,0:T(1,128)S(1)} %reshape.35.receiver_ref.refs_2_, bf16[384,512]{1,0:T(8,128)(2,1)S(1)} %copy-done.1, bf16[2,128,512]{2,1,0:T(8,128)(2,1)S(1)} %copy-done.2, ...), custom_call_target="tpu_custom_call" | custom-call | tf_op jit(solution)/shard_map/gather_latents/pallas_call | solution.py:316
  17.9 1.9 %copy-done.10 = bf16[1536,1280]{1,0:T(8,128)(2,1)} copy-done((bf16[1536,1280]{1,0:T(8,128)(2,1)}, bf16[1536,1280]{1,0:T(8,128)(2,1)S(1)}, u32[]{:S(2)}) %copy-start.10) | copy-done | bytes 3932184
  19.8 0.9 %collective-permute-done.1.refs_10_ = bf16[128,512]{1,0:T(8,128)(2,1)} collective-permute-done((bf16[128,512]{1,0:T(8,128)(2,1)}, bf16[128,512]{1,0:T(8,128)(2,1)}, u32[]{:S(2)}, u32[]{:S(2)}) %collective-permute-start.1) | collective-permute-done | bytes 131104 | tf_op jit(solution)/shard_map/ppermute | solution.py:184
  21.3 0.9 %collective-permute-start.8 = (bf16[3,128,512]{2,1,0:T(8,128)(2,1)S(1)}, bf16[3,128,512]{2,1,0:T(8,128)(2,1)S(1)}, u32[]{:S(2)}, u32[]{:S(2)}) collective-permute-start(bf16[3,128,512]{2,1,0:T(8,128)(2,1)S(1)} %get-tuple-element.17.refs_3_), channel_id=1, source_target_pairs={{0,2},{2,0},{1,3},{3,1},{4,6},{6,4},{5,7},{7,5},{8,10},{10,8},{9,1... | collective-permute-start | bytes 1179656 | tf_op jit(solution)/shard_map/ppermute | solution.py:184
  23.5 0.7 %copy-done.17 = bf16[128,512]{1,0:T(8,128)(2,1)} copy-done((bf16[128,512]{1,0:T(8,128)(2,1)}, bf16[128,512]{1,0:T(8,128)(2,1)S(1)}, u32[]{:S(2)}) %copy-start.17) | copy-done | bytes 131096
  24.2 2.1 %copy-done.11 = bf16[1536,1280]{1,0:T(8,128)(2,1)S(1)} copy-done((bf16[1536,1280]{1,0:T(8,128)(2,1)S(1)}, bf16[1536,1280]{1,0:T(8,128)(2,1)}, u32[]{:S(2)}) %copy-start.11) | copy-done | bytes 3932184
  26.3 1.0 %copy-done.13 = bf16[3,128,512]{2,1,0:T(8,128)(2,1)S(1)} copy-done((bf16[3,128,512]{2,1,0:T(8,128)(2,1)S(1)}, bf16[3,128,512]{2,1,0:T(8,128)(2,1)}, u32[]{:S(2)}) %copy-start.13) | copy-done | bytes 393240
  27.3 0.9 %copy-done.14 = bf16[128,512]{1,0:T(8,128)(2,1)S(1)} copy-done((bf16[128,512]{1,0:T(8,128)(2,1)S(1)}, bf16[128,512]{1,0:T(8,128)(2,1)}, u32[]{:S(2)}) %copy-start.14) | copy-done | bytes 131096
  28.2 0.9 %copy-done.16 = bf16[128,512]{1,0:T(8,128)(2,1)S(1)} copy-done((bf16[128,512]{1,0:T(8,128)(2,1)S(1)}, bf16[128,512]{1,0:T(8,128)(2,1)}, u32[]{:S(2)}) %copy-start.16) | copy-done | bytes 131096
  29.1 0.9 %copy-done.18 = bf16[128,512]{1,0:T(8,128)(2,1)S(1)} copy-done((bf16[128,512]{1,0:T(8,128)(2,1)S(1)}, bf16[128,512]{1,0:T(8,128)(2,1)}, u32[]{:S(2)}) %copy-start.18) | copy-done | bytes 131096
  30.1 0.7 %copy-done.21 = f32[512]{0:T(512)S(1)} copy-done((f32[512]{0:T(512)S(1)}, f32[512]{0:T(512)}, u32[]{:S(2)}) %copy-start.21) | copy-done | bytes 2072
  30.7 0.7 %copy-done.22 = f32[512]{0:T(512)S(1)} copy-done((f32[512]{0:T(512)S(1)}, f32[512]{0:T(512)}, u32[]{:S(2)}) %copy-start.22) | copy-done | bytes 2072
  31.4 9.2 %edge_update.1 = (bf16[1536,512]{1,0:T(8,128)(2,1)}, bf16[384,512]{1,0:T(8,128)(2,1)S(1)}) custom-call(bf16[1536,512]{1,0:T(8,128)(2,1)S(1)} %copy-done.12, bf16[1536,1280]{1,0:T(8,128)(2,1)S(1)} %copy-done.11, s32[3,1,512]{2,1,0:T(1,128)S(1)} %reshape.35.receiver_ref.refs_2_, bf16[8,48,512]{2,1,0:T(8,128)(2,1)S(1)} %all-to-all-done.refs_3_, ...), custom_call_target="tpu_custom_call" | custom-call | flops 3825205248 | bytes 6291456 | tf_op jit(solution)/shard_map/edge_update/pallas_call | solution.py:348
  41.2 1.2 %collective-permute-done.6.refs_2_ = bf16[384,512]{1,0:T(8,128)(2,1)S(1)} collective-permute-done((bf16[384,512]{1,0:T(8,128)(2,1)S(1)}, bf16[384,512]{1,0:T(8,128)(2,1)S(1)}, u32[]{:S(2)}, u32[]{:S(2)}) %collective-permute-start.6) | collective-permute-done | bytes 393248 | tf_op jit(solution)/shard_map/ppermute | solution.py:383
  43.0 2.0 %node_update.1 = bf16[384,512]{1,0:T(8,128)(2,1)} custom-call(bf16[384,512]{1,0:T(8,128)(2,1)S(1)} %copy-done.1, bf16[384,512]{1,0:T(8,128)(2,1)S(1)} %get-tuple-element.16.refs_1_, bf16[384,512]{1,0:T(8,128)(2,1)S(1)} %collective-permute-done.6.refs_2_, bf16[3,128,512]{2,1,0:T(8,128)(2,1)S(1)} %get-tuple-element.17.refs_3_, ...), custom_call_target="tpu_custom_call" | custom-call | flops 603979776 | bytes 1966080 | tf_op jit(solution)/shard_map/node_update/pallas_call | solution.py:386
  (50 shorter events, 3.0 us)
Async XLA Ops:
  0.6 20.1 %collective-permute-start = (bf16[3,128,512]{2,1,0:T(8,128)(2,1)}, bf16[3,128,512]{2,1,0:T(8,128)(2,1)}, u32[]{:S(2)}, u32[]{:S(2)}) collective-permute-start(bf16[3,128,512]{2,1,0:T(8,128)(2,1)} %refs_4_.1), channel_id=1, source_target_pairs={{0,2},{2,0},{1,3},{3,1},{4,6},{6,4},{5,7},{7,5},{8,10},{10,8},{9,1... | collective-permute-start | bytes 1179656 | tf_op jit(solution)/shard_map/ppermute | solution.py:184
  6.0 9.5 %copy-start.1 = (bf16[384,512]{1,0:T(8,128)(2,1)S(1)}, bf16[384,512]{1,0:T(8,128)(2,1)}, u32[]{:S(2)}) copy-start(bf16[384,512]{1,0:T(8,128)(2,1)} %refs_0_.3) | copy-start | bytes 1179652
  6.0 9.5 %copy-start.2 = (bf16[2,128,512]{2,1,0:T(8,128)(2,1)S(1)}, bf16[2,128,512]{2,1,0:T(8,128)(2,1)}, u32[]{:S(2)}) copy-start(bf16[2,128,512]{2,1,0:T(8,128)(2,1)} %node_in_ref.1) | copy-start | bytes 786436
  6.0 9.5 %copy-start.3 = (bf16[128,512]{1,0:T(8,128)(2,1)S(1)}, bf16[128,512]{1,0:T(8,128)(2,1)}, u32[]{:S(2)}) copy-start(bf16[128,512]{1,0:T(8,128)(2,1)} %node_out_ref.1) | copy-start | bytes 393220
  6.0 18.2 %copy-start.12 = (bf16[1536,512]{1,0:T(8,128)(2,1)S(1)}, bf16[1536,512]{1,0:T(8,128)(2,1)}, u32[]{:S(2)}) copy-start(bf16[1536,512]{1,0:T(8,128)(2,1)} %refs_0_.2) | copy-start | bytes 4718596
  6.0 18.2 %copy-start.19 = (f32[512]{0:T(512)S(1)}, f32[512]{0:T(512)}, u32[]{:S(2)}) copy-start(f32[512]{0:T(512)} %param.28) | copy-start | bytes 6148
  6.0 18.2 %copy-start.20 = (f32[512]{0:T(512)S(1)}, f32[512]{0:T(512)}, u32[]{:S(2)}) copy-start(f32[512]{0:T(512)} %param.29) | copy-start | bytes 6148
  7.2 17.0 %all-to-all-start = ((bf16[8,48,512]{2,1,0:T(8,128)(2,1)}), bf16[8,48,512]{2,1,0:T(8,128)(2,1)S(1)}, u32[]{:S(2)}, u32[]{:S(2)}) async-start(bf16[8,48,512]{2,1,0:T(8,128)(2,1)} %pick_halo.1), calls=%async_computation | async-start | bytes 786432 | tf_op jit(solution)/shard_map/all_to_all | solution.py:92
  12.1 8.7 %collective-permute-start.1 = (bf16[128,512]{1,0:T(8,128)(2,1)}, bf16[128,512]{1,0:T(8,128)(2,1)}, u32[]{:S(2)}, u32[]{:S(2)}) collective-permute-start(bf16[128,512]{1,0:T(8,128)(2,1)} %refs_8_.1), channel_id=1, source_target_pairs={{0,2},{2,0},{1,3},{3,1},{4,6},{6,4},{5,7},{7,5},{8,10},{10,8},{9,1... | collective-permute-start | bytes 393224 | tf_op jit(solution)/shard_map/ppermute | solution.py:184
  14.1 9.4 %collective-permute-start.2 = (bf16[3,128,512]{2,1,0:T(8,128)(2,1)}, bf16[3,128,512]{2,1,0:T(8,128)(2,1)}, u32[]{:S(2)}, u32[]{:S(2)}) collective-permute-start(bf16[3,128,512]{2,1,0:T(8,128)(2,1)} %refs_4_.1), channel_id=1, source_target_pairs={{0,1},{1,0},{2,3},{3,2},{4,5},{5,4},{6,7},{7,6},{8,9},{9,8},{10,11... | collective-permute-start | bytes 1179656 | tf_op jit(solution)/shard_map/ppermute | solution.py:192
  17.9 1.9 %copy-start.10 = (bf16[1536,1280]{1,0:T(8,128)(2,1)}, bf16[1536,1280]{1,0:T(8,128)(2,1)S(1)}, u32[]{:S(2)}) copy-start(bf16[1536,1280]{1,0:T(8,128)(2,1)S(1)} %get-tuple-element.12.refs_1_) | copy-start | bytes 11796484
  20.7 3.5 %collective-permute-start.3 = (bf16[3,128,512]{2,1,0:T(8,128)(2,1)}, bf16[3,128,512]{2,1,0:T(8,128)(2,1)}, u32[]{:S(2)}, u32[]{:S(2)}) collective-permute-start(bf16[3,128,512]{2,1,0:T(8,128)(2,1)} %collective-permute-done.refs_6_), channel_id=1, source_target_pairs={{0,1},{1,0},{2,3},{3,2},{4,5},{5,4},{6,7},{7,6},{8,9},{9,8},{10,11... | collective-permute-start | bytes 1179656 | tf_op jit(solution)/shard_map/ppermute | solution.py:192
  20.7 1.8 %collective-permute-start.4 = (bf16[128,512]{1,0:T(8,128)(2,1)}, bf16[128,512]{1,0:T(8,128)(2,1)S(1)}, u32[]{:S(2)}, u32[]{:S(2)}) collective-permute-start(bf16[128,512]{1,0:T(8,128)(2,1)} %refs_8_.1), channel_id=1, source_target_pairs={{0,1},{1,0},{2,3},{3,2},{4,5},{5,4},{6,7},{7,6},{8,9},{9,8},{10,11... | collective-permute-start | bytes 393224 | tf_op jit(solution)/shard_map/ppermute | solution.py:192
  21.2 2.3 %collective-permute-start.5 = (bf16[128,512]{1,0:T(8,128)(2,1)}, bf16[128,512]{1,0:T(8,128)(2,1)S(1)}, u32[]{:S(2)}, u32[]{:S(2)}) collective-permute-start(bf16[128,512]{1,0:T(8,128)(2,1)} %collective-permute-done.1.refs_10_), channel_id=1, source_target_pairs={{0,1},{1,0},{2,3},{3,2},{4,5},{5,4},{6,7},{7,6},{8,9},{9,8},{10,11... | collective-permute-start | bytes 393224 | tf_op jit(solution)/shard_map/ppermute | solution.py:192
  21.3 19.6 %collective-permute-start.8 = (bf16[3,128,512]{2,1,0:T(8,128)(2,1)S(1)}, bf16[3,128,512]{2,1,0:T(8,128)(2,1)S(1)}, u32[]{:S(2)}, u32[]{:S(2)}) collective-permute-start(bf16[3,128,512]{2,1,0:T(8,128)(2,1)S(1)} %get-tuple-element.17.refs_3_), channel_id=1, source_target_pairs={{0,2},{2,0},{1,3},{3,1},{4,6},{6,4},{5,7},{7,5},{8,10},{10,8},{9,1... | collective-permute-start | bytes 1179656 | tf_op jit(solution)/shard_map/ppermute | solution.py:184
  23.2 18.0 %collective-permute-start.7 = (bf16[3,128,512]{2,1,0:T(8,128)(2,1)S(1)}, bf16[3,128,512]{2,1,0:T(8,128)(2,1)S(1)}, u32[]{:S(2)}, u32[]{:S(2)}) collective-permute-start(bf16[3,128,512]{2,1,0:T(8,128)(2,1)S(1)} %get-tuple-element.17.refs_3_), channel_id=1, source_target_pairs={{0,1},{1,0},{2,3},{3,2},{4,5},{5,4},{6,7},{7,6},{8,9},{9,8},{10,11... | collective-permute-start | bytes 1179656 | tf_op jit(solution)/shard_map/ppermute | solution.py:192
  24.2 2.1 %copy-start.11 = (bf16[1536,1280]{1,0:T(8,128)(2,1)S(1)}, bf16[1536,1280]{1,0:T(8,128)(2,1)}, u32[]{:S(2)}) copy-start(bf16[1536,1280]{1,0:T(8,128)(2,1)} %copy-done.10) | copy-start | bytes 11796484
  26.3 1.0 %copy-start.13 = (bf16[3,128,512]{2,1,0:T(8,128)(2,1)S(1)}, bf16[3,128,512]{2,1,0:T(8,128)(2,1)}, u32[]{:S(2)}) copy-start(bf16[3,128,512]{2,1,0:T(8,128)(2,1)} %refs_4_.1) | copy-start | bytes 1179652
  31.4 11.5 %copy-start.5 = (f32[512]{0:T(512)S(1)}, f32[512]{0:T(512)}, u32[]{:S(2)}) copy-start(f32[512]{0:T(512)} %param.32) | copy-start | bytes 6148
  31.4 11.5 %copy-start.6 = (f32[512]{0:T(512)S(1)}, f32[512]{0:T(512)}, u32[]{:S(2)}) copy-start(f32[512]{0:T(512)} %param.33) | copy-start | bytes 6148
  31.4 11.5 %copy-start.7 = (f32[512]{0:T(512)S(1)}, f32[512]{0:T(512)}, u32[]{:S(2)}) copy-start(f32[512]{0:T(512)} %param.34) | copy-start | bytes 6148
  31.4 11.5 %copy-start.8 = (f32[512]{0:T(512)S(1)}, f32[512]{0:T(512)}, u32[]{:S(2)}) copy-start(f32[512]{0:T(512)} %param.35) | copy-start | bytes 6148
  40.6 1.7 %collective-permute-start.6 = (bf16[384,512]{1,0:T(8,128)(2,1)S(1)}, bf16[384,512]{1,0:T(8,128)(2,1)S(1)}, u32[]{:S(2)}, u32[]{:S(2)}) collective-permute-start(bf16[384,512]{1,0:T(8,128)(2,1)S(1)} %get-tuple-element.16.refs_1_), channel_id=1, source_target_pairs={{0,1},{1,0},{2,3},{3,2},{4,5},{5,4},{6,7},{7,6},{8,9},{9,8},{10,11... | collective-permute-start | bytes 1179656 | tf_op jit(solution)/shard_map/ppermute | solution.py:383
  40.8 2.1 %collective-permute-start.9 = (bf16[3,128,512]{2,1,0:T(8,128)(2,1)S(1)}, bf16[3,128,512]{2,1,0:T(8,128)(2,1)S(1)}, u32[]{:S(2)}, u32[]{:S(2)}) collective-permute-start(bf16[3,128,512]{2,1,0:T(8,128)(2,1)S(1)} %collective-permute-done.8.refs_5_), channel_id=1, source_target_pairs={{0,1},{1,0},{2,3},{3,2},{4,5},{5,4},{6,7},{7,6},{8,9},{9,8},{10,11... | collective-permute-start | bytes 1179656 | tf_op jit(solution)/shard_map/ppermute | solution.py:192
  (10 other events, 7.8 us)

commit v5 on v4

--- a/solution.py
+++ b/solution.py
@@ -11,18 +11,28 @@
 tile_rows = 16
 lanes = 128
 padded_parts = 8
-grant = 24 << 20
+grant = 32 << 20
 bf16 = jnp.bfloat16
 f32 = jnp.float32
 vmem = pl.BlockSpec(memory_space=pltpu.VMEM)
 
 
+def in_hbm(array):
+    return pltpu.with_memory_space_constraint(array, pltpu.HBM)
+
+
 def wrap(value, count):
     return jnp.where(value < 0, value + count, value)
 
 
-def as_columns(row):
-    return jnp.transpose(jnp.broadcast_to(row, (lanes, row.shape[1])))
+def as_columns(rows):
+    return jnp.concatenate(
+        [
+            jnp.transpose(jnp.broadcast_to(rows[at : at + 1], (lanes, rows.shape[1])))
+            for at in range(rows.shape[0])
+        ],
+        axis=0,
+    )
 
 
 def one_hot(columns, width):
@@ -54,9 +64,7 @@
 
 def pick_kernel(part_count, near_cap, far_cap, far_ref, near_ref, latent_ref, out_ref):
     me = my_part()
-    near = near_ref[0]
-    row = jnp.concatenate([near[which : which + 1] for which in range(len(near_offsets))], axis=1)
-    columns = [as_columns(row)]
+    columns = [as_columns(near_ref[0])]
     tile_place = lax.broadcasted_iota(jnp.int32, (tile_rows, lanes), 0)
     far = [as_columns(far_ref[0, slot : slot + 1]) for slot in range(far_cap)]
     for part in range(part_count):
@@ -81,13 +89,13 @@
     block = (part_count, near_cap + tile_rows, node_latent.shape[1])
     blocks = pl.pallas_call(
         functools.partial(pick_kernel, part_count, near_cap, far_cap),
-        out_shape=jax.ShapeDtypeStruct(block, bf16),
+        out_shape=pltpu.HBM(block, bf16),
         in_specs=[vmem, vmem, vmem],
         out_specs=vmem,
         compiler_params=pltpu.CompilerParams(vmem_limit_bytes=grant),
         cost_estimate=pl.CostEstimate(flops=0, bytes_accessed=0, transcendentals=0),
         name="pick_halo",
-    )(jnp.transpose(far_rows, (0, 2, 1)), near_rows, node_latent)
+    )(in_hbm(jnp.transpose(far_rows, (0, 2, 1))), in_hbm(near_rows), in_hbm(node_latent))
     return [
         lax.all_to_all(blocks, ("region", "feat"), split_axis=0, concat_axis=0, tiled=True)
     ]
@@ -128,39 +136,39 @@
         pack_ref[:count] = node_in_ref[...]
         pack_ref[count] = node_out_ref[...]
 
-    source = source_ref[0]
+    index_rows = out_ref.shape[0] // lanes
+    here = pl.ds(pl.program_id(0) * index_rows, index_rows)
+    source = source_ref[here]
     far = source - (node_count + len(near_offsets) * near_cap)
     spread = source + lax.div(far, far_cap) * (far_stride - far_cap)
     columns = as_columns(jnp.where(far >= 0, spread, source))
     latent = latent_ref[...]
     sent = one_hot(columns, node_count)
     out_ref[:, :width] = jnp.dot(sent, latent, preferred_element_type=f32).astype(bf16)
-    received = one_hot(as_columns(receiver_ref[0]), node_count)
+    received = one_hot(as_columns(receiver_ref[here]), node_count)
     out_ref[:, width:halo_start] = jnp.dot(
         received, latent, preferred_element_type=f32
     ).astype(bf16)
     out_ref[:, halo_start:] = one_hot(columns - node_count, halo_space)
 
 
-def place_halo(table, part_count, near_cap, padded, got_refs):
+def halo_parts(part_count, near_cap, padded, got_refs):
     far_start = len(near_offsets) * near_cap
+    parts = []
     for which, offset in enumerate(near_offsets):
-        place = which * near_cap
         if padded:
             origin = lax.rem(my_part() + (part_count - offset), part_count)
-            table[place : place + near_cap] = got_refs[0][origin, :near_cap]
+            near = got_refs[0].at[origin, pl.ds(0, near_cap)]
         else:
-            table[place : place + near_cap] = got_refs[which][...]
+            near = got_refs[which]
+        parts.append((near, pl.ds(which * near_cap, near_cap)))
     if padded:
         for part in range(part_count):
-            place = far_start + part * tile_rows
-            table[place : place + tile_rows] = got_refs[0][part, near_cap:]
-        used = far_start + part_count * tile_rows
+            rows = pl.ds(far_start + part * tile_rows, tile_rows)
+            parts.append((got_refs[0].at[part, pl.ds(near_cap, tile_rows)], rows))
     else:
-        used = far_start + got_refs[-1].shape[0]
-        table[far_start:used] = got_refs[-1][...]
-    if used < table.shape[0]:
-        table[used:] = jnp.zeros((table.shape[0] - used, table.shape[1]), bf16)
+        parts.append((got_refs[-1], pl.ds(far_start, got_refs[-1].shape[0])))
+    return parts
 
 
 def place_rows(whole, start, piece, owner):
@@ -195,54 +203,108 @@
     ]
 
 
-def edge_kernel(pieces_count, got_count, part_count, near_cap, padded, *refs):
-    edge_ref, gathered_ref, receiver_ref = refs[:3]
+def edge_kernel(pieces_count, got_count, part_count, near_cap, padded, block, *refs):
+    edge_hbm, gathered_hbm, receiver_hbm = refs[:3]
     got_refs = refs[3 : 3 + got_count]
-    in_pieces = refs[3 + got_count : 3 + got_count + pieces_count]
-    out_pieces = refs[3 + got_count + pieces_count : 3 + got_count + 2 * pieces_count]
-    in_bias, out_bias, gain, offset, new_ref, sum_ref, in_weight, out_weight, halo, total = refs[
-        3 + got_count + 2 * pieces_count :
+    refs = refs[3 + got_count :]
+    in_pieces, out_pieces = refs[:pieces_count], refs[pieces_count : 2 * pieces_count]
+    row_refs = refs[2 * pieces_count : 2 * pieces_count + 4]
+    new_hbm, sum_ref = refs[2 * pieces_count + 4 : 2 * pieces_count + 6]
+    known, in_weight, out_weight, halo, receiver_ref, rows, new_ref, total, sems = refs[
+        2 * pieces_count + 6 :
     ]
-    width = edge_ref.shape[1]
-    step = pl.program_id(0)
-
-    @pl.when(step == 0)
-    def _():
-        for in_piece, out_piece, owner in zip(in_pieces, out_pieces, owners()):
-            for which in range(in_piece.shape[0]):
-                place_rows(in_weight, which * width, in_piece[which], owner)
-            place_rows(out_weight, 0, out_piece[...], owner)
-        place_halo(halo, part_count, near_cap, padded, got_refs)
-        in_weight[3 * width :] = jnp.dot(
-            halo[...], in_weight[width : 2 * width], preferred_element_type=f32
-        ).astype(bf16)
-
-    edges = edge_ref[...]
-    preact = jnp.dot(
-        jnp.concatenate([edges, gathered_ref[...]], axis=1),
-        in_weight[...],
-        preferred_element_type=f32,
-    )
-    hidden = silu(preact + in_bias[...]).astype(bf16)
-    output = jnp.dot(hidden, out_weight[...], preferred_element_type=f32) + out_bias[...]
-    edge_new = (edges.astype(f32) + layer_norm(output, gain[...], offset[...])).astype(bf16)
-    new_ref[...] = edge_new
-    receiver = receiver_ref[0]
-    node_place = lax.broadcasted_iota(jnp.int32, (total.shape[0], receiver.shape[1]), 0)
-    hot = jnp.where(node_place == receiver, 1.0, 0.0).astype(bf16)
-    part = jnp.dot(hot, edge_new, preferred_element_type=f32)
-
-    @pl.when(step == 0)
-    def _():
-        total[...] = part
-
-    @pl.when(step > 0)
-    def _():
-        total[...] += part
-
-    @pl.when(step == pl.num_programs(0) - 1)
-    def _():
-        sum_ref[...] = total[...].astype(bf16)
+    edge_count, width = edge_hbm.shape
+    blocks = edge_count // block
+    taken = []
+
+    def start(source, target):
+        copy = pltpu.make_async_copy(source, target, sems.at[len(taken)])
+        copy.start()
+        taken.append(copy)
+        return copy
+
+    order = owners()
+    first, later, last = [], [], []
+    for which in (1, 0, 2):
+        for piece, owner in zip(in_pieces, order):
+            count = piece.shape[1]
+            spot = pl.ds(pl.multiple_of(which * width + owner * count, count), count)
+            target = first if which == 1 else later
+            target.append(start(piece.at[which], in_weight.at[spot]))
+        if which == 1:
+            for source, spot in halo_parts(part_count, near_cap, padded, got_refs):
+                first.append(start(source, halo.at[spot]))
+    known_copies = []
+    for at in range(blocks):
+        spot = pl.ds(at * block, block)
+        known_copies.append(
+            [
+                start(edge_hbm.at[spot], known.at[spot, pl.ds(0, width)]),
+                start(
+                    gathered_hbm.at[spot],
+                    known.at[spot, pl.ds(width, known.shape[1] - width)],
+                ),
+            ]
+        )
+        if at == 0:
+            for row_ref, row in zip(row_refs, rows):
+                last.append(start(row_ref, row))
+            for piece, owner in zip(out_pieces, order):
+                count = piece.shape[0]
+                spot = pl.ds(pl.multiple_of(owner * count, count), count)
+                last.append(start(piece, out_weight.at[spot]))
+            last.append(start(receiver_hbm, receiver_ref))
+    in_bias, out_bias, gain, offset = rows
+
+    used = len(near_offsets) * near_cap + (
+        part_count * tile_rows if padded else got_refs[-1].shape[0]
+    )
+    if used < halo.shape[0]:
+        halo[used:] = jnp.zeros((halo.shape[0] - used, width), bf16)
+    for copy in first:
+        copy.wait()
+    in_weight[3 * width :] = jnp.dot(
+        halo[...], in_weight[width : 2 * width], preferred_element_type=f32
+    ).astype(bf16)
+    for copy in later:
+        copy.wait()
+
+    def first_dot(at):
+        for copy in known_copies[at]:
+            copy.wait()
+        return jnp.dot(
+            known[at * block : (at + 1) * block], in_weight[...], preferred_element_type=f32
+        )
+
+    preact = first_dot(0)
+    for copy in last:
+        copy.wait()
+    out_copies = []
+    for at in range(blocks):
+        spot = pl.ds(at * block, block)
+        following = first_dot(at + 1) if at + 1 < blocks else None
+        hidden = silu(preact + in_bias[...]).astype(bf16)
+        output = jnp.dot(hidden, out_weight[...], preferred_element_type=f32) + out_bias[...]
+        edges = known[spot, :width].astype(f32)
+        edge_new = (edges + layer_norm(output, gain[...], offset[...])).astype(bf16)
+        new_ref[spot] = edge_new
+        out_copies.append(start(new_ref.at[spot], new_hbm.at[spot]))
+        index_rows = block // lanes
+        receiver = jnp.concatenate(
+            [receiver_ref[at * index_rows + row][None] for row in range(index_rows)], axis=1
+        )
+        node_place = lax.broadcasted_iota(jnp.int32, (total.shape[0], block), 0)
+        hot = jnp.where(node_place == receiver, 1.0, 0.0).astype(bf16)
+        part = jnp.dot(hot, edge_new, preferred_element_type=f32)
+        if at > 0:
+            part += total[...]
+        if at + 1 < blocks:
+            total[...] = part
+        else:
+            sum_ref[...] = part.astype(bf16)
+        preact = following
+    for copy in out_copies:
+        copy.wait()
 
 
 def node_kernel(pieces_count, *refs):
@@ -304,9 +366,8 @@
     halo_space = len(near_offsets) * near_cap + part_count * far_stride
     halo_space = -(-halo_space // lanes) * lanes
 
-    source_blocks = edge_source.reshape(steps, 1, block)
-    receiver_blocks = receivers.reshape(steps, 1, block)
-    index_spec = pl.BlockSpec((1, 1, block), lambda step: (step, 0, 0))
+    source_rows = in_hbm(edge_source.reshape(-1, lanes))
+    receiver_rows = in_hbm(receivers.reshape(-1, lanes))
 
     def whole(array):
         return pl.BlockSpec(array.shape, lambda step: (0,) * array.ndim)
@@ -319,11 +380,13 @@
         ),
         grid=(steps,),
         out_shape=[
-            jax.ShapeDtypeStruct((edge_count, gathered_width), bf16),
-            jax.ShapeDtypeStruct(pack_shape, bf16),
-        ],
-        in_specs=[index_spec, index_spec]
-        + [whole(array) for array in (node_latent, node_in_weight, node_out_weight)],
+            pltpu.HBM((edge_count, gathered_width), bf16),
+            pltpu.HBM(pack_shape, bf16),
+        ],
+        in_specs=[
+            whole(array)
+            for array in (source_rows, receiver_rows, node_latent, node_in_weight, node_out_weight)
+        ],
         out_specs=[
             pl.BlockSpec((block, gathered_width), lambda step: (step, 0)),
             pl.BlockSpec(pack_shape, lambda step: (0, 0, 0)),
@@ -331,7 +394,13 @@
         compiler_params=pltpu.CompilerParams(vmem_limit_bytes=grant),
         cost_estimate=pl.CostEstimate(flops=0, bytes_accessed=0, transcendentals=0),
         name="gather_latents",
-    )(source_blocks, receiver_blocks, node_latent, node_in_weight, node_out_weight)
+    )(
+        source_rows,
+        receiver_rows,
+        in_hbm(node_latent),
+        in_hbm(node_in_weight),
+        in_hbm(node_out_weight),
+    )
 
     far_edge, gathered, node_weight = lax.optimization_barrier(
         (far_edge, gathered, node_weight)
@@ -345,30 +414,31 @@
     pieces_count = len(edge_in)
 
     rows = [value.reshape(1, -1) for value in (edge_in_bias, edge_out_bias, edge_gain, edge_offset)]
+    hbm = pl.BlockSpec(memory_space=pltpu.HBM)
+    edge_operands = [edge_latent, gathered, receivers.reshape(-1, lanes)]
+    edge_operands += got + edge_in + edge_out + rows
+    known_width = 3 * width + halo_space
+    copy_count = 3 * pieces_count + 4 + part_count + 3 * steps + 4 + pieces_count + 1
     edge_new, partial_sums = pl.pallas_call(
-        functools.partial(edge_kernel, pieces_count, len(got), part_count, near_cap, padded),
-        grid=(steps,),
+        functools.partial(
+            edge_kernel, pieces_count, len(got), part_count, near_cap, padded, block
+        ),
         out_shape=[
-            jax.ShapeDtypeStruct((edge_count, width), bf16),
+            pltpu.HBM((edge_count, width), bf16),
             jax.ShapeDtypeStruct((node_count, width), bf16),
         ],
-        in_specs=[
-            pl.BlockSpec((block, width), lambda step: (step, 0)),
-            pl.BlockSpec((block, gathered_width), lambda step: (step, 0)),
-            index_spec,
-        ]
-        + [whole(rows) for rows in got]
-        + [whole(piece) for piece in edge_in + edge_out]
-        + [whole(row) for row in rows],
-        out_specs=[
-            pl.BlockSpec((block, width), lambda step: (step, 0)),
-            pl.BlockSpec((node_count, width), lambda step: (0, 0)),
-        ],
+        in_specs=[hbm] * len(edge_operands),
+        out_specs=[hbm, vmem],
         scratch_shapes=[
-            pltpu.VMEM((3 * width + halo_space, width), bf16),
+            pltpu.VMEM((edge_count, known_width), bf16),
+            pltpu.VMEM((known_width, width), bf16),
             pltpu.VMEM((width, width), bf16),
             pltpu.VMEM((halo_space, width), bf16),
+            pltpu.VMEM((edge_count // lanes, lanes), jnp.int32),
+            [pltpu.VMEM((1, width), f32)] * 4,
+            pltpu.VMEM((edge_count, width), bf16),
             pltpu.VMEM((node_count, width), f32),
+            pltpu.SemaphoreType.DMA((copy_count,)),
         ],
         compiler_params=pltpu.CompilerParams(vmem_limit_bytes=grant),
         cost_estimate=pl.CostEstimate(
@@ -377,7 +447,7 @@
             transcendentals=edge_count * width,
         ),
         name="edge_update",
-    )(edge_latent, gathered, receiver_blocks, *got, *edge_in, *edge_out, *rows)
+    )(*[in_hbm(operand) for operand in edge_operands])
 
     subs = lax.axis_size("sub")
     other_sums = lax.ppermute(partial_sums, "sub", [(at, (at + 1) % subs) for at in range(subs)])

time: 45.5 us -> 37.9 us (0.83)
  local copies, waits for them, and re-layouts: 14.2 us -> 1.05 us
  Pallas kernels: 14.8 us -> 19.1 us
  starting transfers between devices: 12.2 us -> 13 us
  waiting for transfers between devices: 3.07 us -> 3.71 us
    unnamed x46 -> x30, local copies, waits for them, and re-layouts: 12.8 us -> 1.05 us
    pallas_call x1, Pallas kernels: 2.39 us -> 4.9 us  [shards(): pl.pallas_call(functools.partial(gather_kernel, node_count, near_cap, far...]
    reshape x2 -> x0, local copies, waits for them, and re-layouts: 1.41 us -> none  [the longest x1 0.71 us: shards(): receiver_blocks = receivers.reshape(steps, 1, block)]
    pallas_call x1, Pallas kernels: 1.16 us -> 2.15 us  [exchange_padded(): pl.pallas_call(functools.partial(pick_kernel, part_count, near_cap, far_c...]
    ppermute x3, waiting for transfers between devices: 0.95 us -> 1.87 us  [from_feats(): lax.ppermute(weight, 'feat', [(at, (at + shift) % feats) for at in range(...]
    pallas_call x1, Pallas kernels: 9.22 us -> 10 us  [shards(): pl.pallas_call(functools.partial(edge_kernel, pieces_count, len(got), par...]
    ppermute x3, starting transfers between devices: 5.96 us -> 6.76 us  [from_feats(): lax.ppermute(weight, 'feat', [(at, (at + shift) % feats) for at in range(...]
  transfers between devices with their start and end apart: 11 -> 11, of which waited for: 4 -> 4; matrix products, arithmetic and copies ran while one was open for 3% -> 0% of each run, Pallas kernels for 28% -> 45%
where the time goes in v5:
time: 37.9 us; the launch traced here: 37.6 us
  Pallas kernels  19.1 us (50%)
  starting transfers between devices  13 us (34%)
  waiting for transfers between devices  3.71 us (10%)
  local copies, waits for them, and re-layouts  1.05 us (3%)
  between operations  0.75 us (2%)
    pallas_call x1, Pallas kernels, shards(): pl.pallas_call(functools.partial(edge_kernel, pieces_count, len(got), par...  10 us
    ppermute x3, starting transfers between devices, from_feats(): lax.ppermute(weight, 'feat', [(at, (at + shift) % feats) for at in range(...  6.76 us
    pallas_call x1, Pallas kernels, shards(): pl.pallas_call(functools.partial(gather_kernel, node_count, near_cap, far...  4.9 us
    all_to_all x1, starting transfers between devices, exchange_padded(): lax.all_to_all(blocks, ('region', 'feat'), split_axis=0, concat_axis=0, t...  4.88 us
    pallas_call x1, Pallas kernels, exchange_padded(): pl.pallas_call(functools.partial(pick_kernel, part_count, near_cap, far_c...  2.15 us
    pallas_call x1, Pallas kernels, shards(): pl.pallas_call(functools.partial(node_kernel, pieces_count), out_shape=ja...  2.01 us
    ppermute x3, waiting for transfers between devices, from_feats(): lax.ppermute(weight, 'feat', [(at, (at + shift) % feats) for at in range(...  1.87 us
    ppermute x1, waiting for transfers between devices, shards(): lax.ppermute(partial_sums, 'sub', [(at, (at + 1) % subs) for at in range(...  1.21 us
  transfers between devices with their start and end apart: 11, of which 4 were waited for; matrix products, arithmetic and copies ran while one was open for 0% of the time, Pallas kernels for 45%

profile of v5, /device:TPU:0, one launch (start us, length us, event | category | flops | bytes accessed | tf_op | source)
XLA Modules:
  0.0 37.6 jit_solution(5656298606884907336)
XLA Ops:
  0.6 0.0 copy-start.7
  0.7 3.0 %collective-permute-start = (bf16[3,128,512]{2,1,0:T(8,128)(2,1)}, bf16[3,128,512]{2,1,0:T(8,128)(2,1)S(1)}, u32[]{:S(2)}, u32[]{:S(2)}) collective-permute-start(bf16[3,128,512]{2,1,0:T(8,128)(2,1)} %refs_4_.1), channel_id=1, source_target_pairs={{0,2},{2,0},{1,3},{3,1},{4,6},{6,4},{5,7},{7,5},{8,10},{10,8},{9,1... | collective-permute-start | bytes 1179656 | tf_op jit(solution)/shard_map/ppermute | solution.py:192
  3.7 2.1 %pick_halo.1 = bf16[8,48,512]{2,1,0:T(8,128)(2,1)} custom-call(s32[1,2,8]{2,1,0:T(2,128)} %bitcast.18, s32[1,4,32]{2,1,0:T(4,128)} %near_ref.1, bf16[384,512]{1,0:T(8,128)(2,1)} %refs_0_.3), custom_call_target="tpu_custom_call" | custom-call | tf_op jit(solution)/shard_map/pick_halo/pallas_call | solution.py:90
  5.8 4.9 %all-to-all-start = ((bf16[8,48,512]{2,1,0:T(8,128)(2,1)}), bf16[8,48,512]{2,1,0:T(8,128)(2,1)S(1)}, u32[]{:S(2)}, u32[]{:S(2)}) async-start(bf16[8,48,512]{2,1,0:T(8,128)(2,1)} %pick_halo.1), calls=%async_computation | async-start | bytes 786432 | tf_op jit(solution)/shard_map/all_to_all | solution.py:100
  10.7 2.0 %collective-permute-start.1 = (bf16[128,512]{1,0:T(8,128)(2,1)S(1)}, bf16[128,512]{1,0:T(8,128)(2,1)S(1)}, u32[]{:S(2)}, u32[]{:S(2)}) collective-permute-start(bf16[128,512]{1,0:T(8,128)(2,1)S(1)} %copy-done.11), channel_id=1, source_target_pairs={{0,2},{2,0},{1,3},{3,1},{4,6},{6,4},{5,7},{7,5},{8,10},{10,8},{9,1... | collective-permute-start | bytes 393224 | tf_op jit(solution)/shard_map/ppermute | solution.py:192
  12.7 4.9 %gather_latents.1 = (bf16[1536,1280]{1,0:T(8,128)(2,1)}, bf16[3,128,512]{2,1,0:T(8,128)(2,1)}) custom-call(s32[12,128]{1,0:T(8,128)} %bitcast.15, s32[12,128]{1,0:T(8,128)} %bitcast.16, bf16[384,512]{1,0:T(8,128)(2,1)} %refs_0_.3, bf16[2,128,512]{2,1,0:T(8,128)(2,1)} %node_in_ref.1, bf16[128,512]{1,0:T(8,128)(2,1)} %node_out_ref.1), custom_call_target="tpu_custom_call" | custom-call | tf_op jit(solution)/shard_map/gather_latents/pallas_call | solution.py:377
  17.6 1.9 %collective-permute-done.1.refs_10_ = bf16[128,512]{1,0:T(8,128)(2,1)S(1)} collective-permute-done((bf16[128,512]{1,0:T(8,128)(2,1)S(1)}, bf16[128,512]{1,0:T(8,128)(2,1)S(1)}, u32[]{:S(2)}, u32[]{:S(2)}) %collective-permute-start.1) | collective-permute-done | bytes 131104 | tf_op jit(solution)/shard_map/ppermute | solution.py:192
  19.5 0.1 collective-permute-start.3
  19.6 0.5 %collective-permute-start.4 = (bf16[128,512]{1,0:T(8,128)(2,1)S(1)}, bf16[128,512]{1,0:T(8,128)(2,1)S(1)}, u32[]{:S(2)}, u32[]{:S(2)}) collective-permute-start(bf16[128,512]{1,0:T(8,128)(2,1)S(1)} %copy-done.11), channel_id=1, source_target_pairs={{0,1},{1,0},{2,3},{3,2},{4,5},{5,4},{6,7},{7,6},{8,9},{9,8},{10,11... | collective-permute-start | bytes 393224 | tf_op jit(solution)/shard_map/ppermute | solution.py:200
  20.1 0.1 collective-permute-start.5
  20.1 1.7 %collective-permute-start.8 = (bf16[3,128,512]{2,1,0:T(8,128)(2,1)}, bf16[3,128,512]{2,1,0:T(8,128)(2,1)S(1)}, u32[]{:S(2)}, u32[]{:S(2)}) collective-permute-start(bf16[3,128,512]{2,1,0:T(8,128)(2,1)} %get-tuple-element.17.refs_3_), channel_id=1, source_target_pairs={{0,2},{2,0},{1,3},{3,1},{4,6},{6,4},{5,7},{7,5},{8,10},{10,8},{9,1... | collective-permute-start | bytes 1179656 | tf_op jit(solution)/shard_map/ppermute | solution.py:192
  21.9 0.2 collective-permute-start.7
  22.1 0.1 all-to-all-done.refs_3_
  22.1 0.4 %copy-done.13 = bf16[128,512]{1,0:T(8,128)(2,1)} copy-done((bf16[128,512]{1,0:T(8,128)(2,1)}, bf16[128,512]{1,0:T(8,128)(2,1)S(1)}, u32[]{:S(2)}) %copy-start.13) | copy-done | bytes 131096
  22.5 0.3 copy-done.9
  22.8 0.0 copy-done.14
  22.9 0.1 copy-done.6
  23.0 0.1 copy-done.10
  23.2 10.0 %edge_update.1 = (bf16[1536,512]{1,0:T(8,128)(2,1)}, bf16[384,512]{1,0:T(8,128)(2,1)S(1)}) custom-call(bf16[1536,512]{1,0:T(8,128)(2,1)} %refs_0_.2, bf16[1536,1280]{1,0:T(8,128)(2,1)} %get-tuple-element.12.refs_1_, s32[12,128]{1,0:T(8,128)} %bitcast.17, bf16[8,48,512]{2,1,0:T(8,128)(2,1)} %copy-done.6, bf16[3,128,512]{2,1,0:T(8,128)(2,1)} %refs_4_.1, ...), custom_call_target="tpu_custom_call" | custom-call | flops 3825205248 | bytes 6291456 | tf_op jit(solution)/shard_map/edge_update/pallas_call | solution.py:422
  33.2 0.4 %collective-permute-start.6 = (bf16[384,512]{1,0:T(8,128)(2,1)S(1)}, bf16[384,512]{1,0:T(8,128)(2,1)S(1)}, u32[]{:S(2)}, u32[]{:S(2)}) collective-permute-start(bf16[384,512]{1,0:T(8,128)(2,1)S(1)} %get-tuple-element.16.refs_1_), channel_id=1, source_target_pairs={{0,1},{1,0},{2,3},{3,2},{4,5},{5,4},{6,7},{7,6},{8,9},{9,8},{10,11... | collective-permute-start | bytes 1179656 | tf_op jit(solution)/shard_map/ppermute | solution.py:453
  33.6 0.2 collective-permute-start.9
  33.8 1.2 %collective-permute-done.6.refs_2_ = bf16[384,512]{1,0:T(8,128)(2,1)S(1)} collective-permute-done((bf16[384,512]{1,0:T(8,128)(2,1)S(1)}, bf16[384,512]{1,0:T(8,128)(2,1)S(1)}, u32[]{:S(2)}, u32[]{:S(2)}) %collective-permute-start.6) | collective-permute-done | bytes 393248 | tf_op jit(solution)/shard_map/ppermute | solution.py:453
  35.0 0.6 %collective-permute-done.9.refs_6_ = bf16[3,128,512]{2,1,0:T(8,128)(2,1)S(1)} collective-permute-done((bf16[3,128,512]{2,1,0:T(8,128)(2,1)S(1)}, bf16[3,128,512]{2,1,0:T(8,128)(2,1)S(1)}, u32[]{:S(2)}, u32[]{:S(2)}) %collective-permute-start.9) | collective-permute-done | bytes 393248 | tf_op jit(solution)/shard_map/ppermute | solution.py:200
  35.6 2.0 %node_update.1 = bf16[384,512]{1,0:T(8,128)(2,1)} custom-call(bf16[384,512]{1,0:T(8,128)(2,1)S(1)} %copy-done, bf16[384,512]{1,0:T(8,128)(2,1)S(1)} %get-tuple-element.16.refs_1_, bf16[384,512]{1,0:T(8,128)(2,1)S(1)} %collective-permute-done.6.refs_2_, bf16[3,128,512]{2,1,0:T(8,128)(2,1)S(1)} %copy-done.1, ...), custom_call_target="tpu_custom_call" | custom-call | flops 603979776 | bytes 1966080 | tf_op jit(solution)/shard_map/node_update/pallas_call | solution.py:456
  (32 shorter events, 0.1 us)
Async XLA Ops:
  0.6 12.1 %copy-start.7 = (bf16[3,128,512]{2,1,0:T(8,128)(2,1)S(1)}, bf16[3,128,512]{2,1,0:T(8,128)(2,1)}, u32[]{:S(2)}) copy-start(bf16[3,128,512]{2,1,0:T(8,128)(2,1)} %refs_4_.1) | copy-start | bytes 1179652
  0.6 10.0 %copy-start.11 = (bf16[128,512]{1,0:T(8,128)(2,1)S(1)}, bf16[128,512]{1,0:T(8,128)(2,1)}, u32[]{:S(2)}) copy-start(bf16[128,512]{1,0:T(8,128)(2,1)} %refs_8_.1) | copy-start | bytes 393220
  0.7 18.8 %collective-permute-start = (bf16[3,128,512]{2,1,0:T(8,128)(2,1)}, bf16[3,128,512]{2,1,0:T(8,128)(2,1)S(1)}, u32[]{:S(2)}, u32[]{:S(2)}) collective-permute-start(bf16[3,128,512]{2,1,0:T(8,128)(2,1)} %refs_4_.1), channel_id=1, source_target_pairs={{0,2},{2,0},{1,3},{3,1},{4,6},{6,4},{5,7},{7,5},{8,10},{10,8},{9,1... | collective-permute-start | bytes 1179656 | tf_op jit(solution)/shard_map/ppermute | solution.py:192
  5.8 16.3 %all-to-all-start = ((bf16[8,48,512]{2,1,0:T(8,128)(2,1)}), bf16[8,48,512]{2,1,0:T(8,128)(2,1)S(1)}, u32[]{:S(2)}, u32[]{:S(2)}) async-start(bf16[8,48,512]{2,1,0:T(8,128)(2,1)} %pick_halo.1), calls=%async_computation | async-start | bytes 786432 | tf_op jit(solution)/shard_map/all_to_all | solution.py:100
  10.7 8.8 %collective-permute-start.1 = (bf16[128,512]{1,0:T(8,128)(2,1)S(1)}, bf16[128,512]{1,0:T(8,128)(2,1)S(1)}, u32[]{:S(2)}, u32[]{:S(2)}) collective-permute-start(bf16[128,512]{1,0:T(8,128)(2,1)S(1)} %copy-done.11), channel_id=1, source_target_pairs={{0,2},{2,0},{1,3},{3,1},{4,6},{6,4},{5,7},{7,5},{8,10},{10,8},{9,1... | collective-permute-start | bytes 393224 | tf_op jit(solution)/shard_map/ppermute | solution.py:192
  12.7 9.3 %collective-permute-start.2 = (bf16[3,128,512]{2,1,0:T(8,128)(2,1)S(1)}, bf16[3,128,512]{2,1,0:T(8,128)(2,1)S(1)}, u32[]{:S(2)}, u32[]{:S(2)}) collective-permute-start(bf16[3,128,512]{2,1,0:T(8,128)(2,1)S(1)} %copy-done.7), channel_id=1, source_target_pairs={{0,1},{1,0},{2,3},{3,2},{4,5},{5,4},{6,7},{7,6},{8,9},{9,8},{10,11... | collective-permute-start | bytes 1179656 | tf_op jit(solution)/shard_map/ppermute | solution.py:200
  19.5 2.7 %copy-start.12 = (bf16[128,512]{1,0:T(8,128)(2,1)}, bf16[128,512]{1,0:T(8,128)(2,1)S(1)}, u32[]{:S(2)}) copy-start(bf16[128,512]{1,0:T(8,128)(2,1)S(1)} %collective-permute-done.1.refs_10_) | copy-start | bytes 393220
  19.5 2.7 %copy-start.8 = (bf16[3,128,512]{2,1,0:T(8,128)(2,1)}, bf16[3,128,512]{2,1,0:T(8,128)(2,1)S(1)}, u32[]{:S(2)}) copy-start(bf16[3,128,512]{2,1,0:T(8,128)(2,1)S(1)} %collective-permute-done.refs_6_) | copy-start | bytes 1179652
  19.5 2.6 %collective-permute-start.3 = (bf16[3,128,512]{2,1,0:T(8,128)(2,1)S(1)}, bf16[3,128,512]{2,1,0:T(8,128)(2,1)S(1)}, u32[]{:S(2)}, u32[]{:S(2)}) collective-permute-start(bf16[3,128,512]{2,1,0:T(8,128)(2,1)S(1)} %collective-permute-done.refs_6_), channel_id=1, source_target_pairs={{0,1},{1,0},{2,3},{3,2},{4,5},{5,4},{6,7},{7,6},{8,9},{9,8},{10,11... | collective-permute-start | bytes 1179656 | tf_op jit(solution)/shard_map/ppermute | solution.py:200
  19.6 2.3 %collective-permute-start.4 = (bf16[128,512]{1,0:T(8,128)(2,1)S(1)}, bf16[128,512]{1,0:T(8,128)(2,1)S(1)}, u32[]{:S(2)}, u32[]{:S(2)}) collective-permute-start(bf16[128,512]{1,0:T(8,128)(2,1)S(1)} %copy-done.11), channel_id=1, source_target_pairs={{0,1},{1,0},{2,3},{3,2},{4,5},{5,4},{6,7},{7,6},{8,9},{9,8},{10,11... | collective-permute-start | bytes 393224 | tf_op jit(solution)/shard_map/ppermute | solution.py:200
  20.1 2.0 %collective-permute-start.5 = (bf16[128,512]{1,0:T(8,128)(2,1)S(1)}, bf16[128,512]{1,0:T(8,128)(2,1)S(1)}, u32[]{:S(2)}, u32[]{:S(2)}) collective-permute-start(bf16[128,512]{1,0:T(8,128)(2,1)S(1)} %collective-permute-done.1.refs_10_), channel_id=1, source_target_pairs={{0,1},{1,0},{2,3},{3,2},{4,5},{5,4},{6,7},{7,6},{8,9},{9,8},{10,11... | collective-permute-start | bytes 393224 | tf_op jit(solution)/shard_map/ppermute | solution.py:200
  20.1 13.5 %collective-permute-start.8 = (bf16[3,128,512]{2,1,0:T(8,128)(2,1)}, bf16[3,128,512]{2,1,0:T(8,128)(2,1)S(1)}, u32[]{:S(2)}, u32[]{:S(2)}) collective-permute-start(bf16[3,128,512]{2,1,0:T(8,128)(2,1)} %get-tuple-element.17.refs_3_), channel_id=1, source_target_pairs={{0,2},{2,0},{1,3},{3,1},{4,6},{6,4},{5,7},{7,5},{8,10},{10,8},{9,1... | collective-permute-start | bytes 1179656 | tf_op jit(solution)/shard_map/ppermute | solution.py:192
  21.9 11.9 %collective-permute-start.7 = (bf16[3,128,512]{2,1,0:T(8,128)(2,1)}, bf16[3,128,512]{2,1,0:T(8,128)(2,1)S(1)}, u32[]{:S(2)}, u32[]{:S(2)}) collective-permute-start(bf16[3,128,512]{2,1,0:T(8,128)(2,1)} %get-tuple-element.17.refs_3_), channel_id=1, source_target_pairs={{0,1},{1,0},{2,3},{3,2},{4,5},{5,4},{6,7},{7,6},{8,9},{9,8},{10,11... | collective-permute-start | bytes 1179656 | tf_op jit(solution)/shard_map/ppermute | solution.py:200
  22.1 0.8 %copy-start.14 = (bf16[128,512]{1,0:T(8,128)(2,1)}, bf16[128,512]{1,0:T(8,128)(2,1)S(1)}, u32[]{:S(2)}) copy-start(bf16[128,512]{1,0:T(8,128)(2,1)S(1)} %collective-permute-done.5.refs_11_) | copy-start | bytes 393220
  22.1 0.9 %copy-start.6 = (bf16[8,48,512]{2,1,0:T(8,128)(2,1)}, bf16[8,48,512]{2,1,0:T(8,128)(2,1)S(1)}, u32[]{:S(2)}) copy-start(bf16[8,48,512]{2,1,0:T(8,128)(2,1)S(1)} %all-to-all-done.refs_3_) | copy-start | bytes 1179652
  22.1 1.0 %copy-start.10 = (bf16[3,128,512]{2,1,0:T(8,128)(2,1)}, bf16[3,128,512]{2,1,0:T(8,128)(2,1)S(1)}, u32[]{:S(2)}) copy-start(bf16[3,128,512]{2,1,0:T(8,128)(2,1)S(1)} %collective-permute-done.3.refs_7_) | copy-start | bytes 1179652
  23.1 12.4 %copy-start = (bf16[384,512]{1,0:T(8,128)(2,1)S(1)}, bf16[384,512]{1,0:T(8,128)(2,1)}, u32[]{:S(2)}) copy-start(bf16[384,512]{1,0:T(8,128)(2,1)} %refs_0_.3) | copy-start | bytes 1179652
  23.1 12.4 %copy-start.1 = (bf16[3,128,512]{2,1,0:T(8,128)(2,1)S(1)}, bf16[3,128,512]{2,1,0:T(8,128)(2,1)}, u32[]{:S(2)}) copy-start(bf16[3,128,512]{2,1,0:T(8,128)(2,1)} %get-tuple-element.17.refs_3_) | copy-start | bytes 1179652
  23.1 12.4 %copy-start.2 = (f32[512]{0:T(512)S(1)}, f32[512]{0:T(512)}, u32[]{:S(2)}) copy-start(f32[512]{0:T(512)} %param.32) | copy-start | bytes 6148
  23.1 12.4 %copy-start.3 = (f32[512]{0:T(512)S(1)}, f32[512]{0:T(512)}, u32[]{:S(2)}) copy-start(f32[512]{0:T(512)} %param.33) | copy-start | bytes 6148
  23.2 12.4 %copy-start.4 = (f32[512]{0:T(512)S(1)}, f32[512]{0:T(512)}, u32[]{:S(2)}) copy-start(f32[512]{0:T(512)} %param.34) | copy-start | bytes 6148
  23.2 12.4 %copy-start.5 = (f32[512]{0:T(512)S(1)}, f32[512]{0:T(512)}, u32[]{:S(2)}) copy-start(f32[512]{0:T(512)} %param.35) | copy-start | bytes 6148
  33.2 1.8 %collective-permute-start.6 = (bf16[384,512]{1,0:T(8,128)(2,1)S(1)}, bf16[384,512]{1,0:T(8,128)(2,1)S(1)}, u32[]{:S(2)}, u32[]{:S(2)}) collective-permute-start(bf16[384,512]{1,0:T(8,128)(2,1)S(1)} %get-tuple-element.16.refs_1_), channel_id=1, source_target_pairs={{0,1},{1,0},{2,3},{3,2},{4,5},{5,4},{6,7},{7,6},{8,9},{9,8},{10,11... | collective-permute-start | bytes 1179656 | tf_op jit(solution)/shard_map/ppermute | solution.py:453
  33.6 1.9 %collective-permute-start.9 = (bf16[3,128,512]{2,1,0:T(8,128)(2,1)S(1)}, bf16[3,128,512]{2,1,0:T(8,128)(2,1)S(1)}, u32[]{:S(2)}, u32[]{:S(2)}) collective-permute-start(bf16[3,128,512]{2,1,0:T(8,128)(2,1)S(1)} %collective-permute-done.8.refs_5_), channel_id=1, source_target_pairs={{0,1},{1,0},{2,3},{3,2},{4,5},{5,4},{6,7},{7,6},{8,9},{9,8},{10,11... | collective-permute-start | bytes 1179656 | tf_op jit(solution)/shard_map/ppermute | solution.py:200
  (2 other events, 1.4 us)

commit v6 on v5

--- a/solution.py
+++ b/solution.py
@@ -10,7 +10,7 @@
 near_offsets = (1, 2, -1, -2)
 tile_rows = 16
 lanes = 128
-padded_parts = 8
+few_parts = 8
 grant = 32 << 20
 bf16 = jnp.bfloat16
 f32 = jnp.float32
@@ -19,6 +19,10 @@
 
 def in_hbm(array):
     return pltpu.with_memory_space_constraint(array, pltpu.HBM)
+
+
+def in_vmem(array):
+    return pltpu.with_memory_space_constraint(array, pltpu.VMEM)
 
 
 def wrap(value, count):
@@ -62,43 +66,46 @@
     return lax.axis_index("region") * lax.axis_size("feat") + lax.axis_index("feat")
 
 
-def pick_kernel(part_count, near_cap, far_cap, far_ref, near_ref, latent_ref, out_ref):
-    me = my_part()
+def pick_kernel(part_count, near_cap, far_cap, far_ref, near_ref, latent_ref, out_ref, picked):
+    me, sub, subs = my_part(), lax.axis_index("sub"), lax.axis_size("sub")
+    half = near_cap // subs
     columns = [as_columns(near_ref[0])]
     tile_place = lax.broadcasted_iota(jnp.int32, (tile_rows, lanes), 0)
-    far = [as_columns(far_ref[0, slot : slot + 1]) for slot in range(far_cap)]
+    far = as_columns(far_ref[0, 0:1])
+    for slot in range(1, far_cap):
+        far = jnp.where(sub == slot, as_columns(far_ref[0, slot : slot + 1]), far)
     for part in range(part_count):
-        tile = jnp.full((tile_rows, lanes), -1, jnp.int32)
-        for slot in range(far_cap):
-            tile = jnp.where(tile_place == slot, far[slot][part : part + 1], tile)
-        columns.append(tile)
+        columns.append(jnp.where(tile_place == 0, far[part : part + 1], -1))
     hot = one_hot(jnp.concatenate(columns, axis=0), latent_ref.shape[0])
-    picked = jnp.dot(hot, latent_ref[...], preferred_element_type=f32).astype(bf16)
+    picked[...] = jnp.dot(hot, latent_ref[...], preferred_element_type=f32).astype(bf16)
     for which, offset in enumerate(near_offsets):
         target = lax.rem(me + (offset + part_count), part_count)
-        out_ref[target, :near_cap] = picked[which * near_cap : (which + 1) * near_cap]
+        start = pl.multiple_of(which * near_cap + sub * half, half)
+        out_ref[target, :half] = picked[pl.ds(start, half)]
     far_start = len(near_offsets) * near_cap
     for part in range(part_count):
-        out_ref[part, near_cap:] = picked[
-            far_start + part * tile_rows : far_start + (part + 1) * tile_rows
-        ]
-
-
-def exchange_padded(node_latent, near_rows, far_rows, part_count):
+        spot = far_start + part * tile_rows
+        out_ref[part, half:] = picked[spot : spot + tile_rows][:1]
+
+
+def exchange_halves(node_latent, near_rows, far_rows, part_count):
     near_cap, far_cap = near_rows.shape[2], far_rows.shape[2]
-    block = (part_count, near_cap + tile_rows, node_latent.shape[1])
+    subs = lax.axis_size("sub")
+    width = node_latent.shape[1]
+    block = (part_count, near_cap // subs + 1, width)
+    picks = len(near_offsets) * near_cap + part_count * tile_rows
     blocks = pl.pallas_call(
         functools.partial(pick_kernel, part_count, near_cap, far_cap),
         out_shape=pltpu.HBM(block, bf16),
         in_specs=[vmem, vmem, vmem],
         out_specs=vmem,
+        scratch_shapes=[pltpu.VMEM((picks, width), bf16)],
         compiler_params=pltpu.CompilerParams(vmem_limit_bytes=grant),
         cost_estimate=pl.CostEstimate(flops=0, bytes_accessed=0, transcendentals=0),
         name="pick_halo",
     )(in_hbm(jnp.transpose(far_rows, (0, 2, 1))), in_hbm(near_rows), in_hbm(node_latent))
-    return [
-        lax.all_to_all(blocks, ("region", "feat"), split_axis=0, concat_axis=0, tiled=True)
-    ]
+    own = lax.all_to_all(blocks, ("region", "feat"), split_axis=0, concat_axis=0, tiled=True)
+    return blocks, [own] + from_subs([own])
 
 
 def exchange_all(node_latent, near_rows, far_rows, part_count):
@@ -110,14 +117,14 @@
         got.append(lax.ppermute(near_send[which], ("region", "feat"), pairs))
     far = lax.all_to_all(far_send, ("region", "feat"), split_axis=0, concat_axis=0, tiled=True)
     got.append(far.reshape(-1, far.shape[2]))
-    return got
+    return far_send, got
 
 
 def gather_kernel(
     node_count,
     near_cap,
     far_cap,
-    far_stride,
+    halved,
     halo_space,
     source_ref,
     receiver_ref,
@@ -139,9 +146,12 @@
     index_rows = out_ref.shape[0] // lanes
     here = pl.ds(pl.program_id(0) * index_rows, index_rows)
     source = source_ref[here]
-    far = source - (node_count + len(near_offsets) * near_cap)
-    spread = source + lax.div(far, far_cap) * (far_stride - far_cap)
-    columns = as_columns(jnp.where(far >= 0, spread, source))
+    if halved:
+        far = source - (node_count + len(near_offsets) * near_cap)
+        slot = lax.rem(far, far_cap)
+        turned = wrap(slot - lax.axis_index("sub"), far_cap)
+        source = jnp.where(far >= 0, source - slot + turned, source)
+    columns = as_columns(source)
     latent = latent_ref[...]
     sent = one_hot(columns, node_count)
     out_ref[:, :width] = jnp.dot(sent, latent, preferred_element_type=f32).astype(bf16)
@@ -152,23 +162,31 @@
     out_ref[:, halo_start:] = one_hot(columns - node_count, halo_space)
 
 
-def halo_parts(part_count, near_cap, padded, got_refs):
+def place_halo(halo, part_count, near_cap, halved, got):
+    subs = lax.axis_size("sub")
     far_start = len(near_offsets) * near_cap
-    parts = []
-    for which, offset in enumerate(near_offsets):
-        if padded:
+    used = far_start
+    if halved:
+        half = near_cap // subs
+        for which, offset in enumerate(near_offsets):
             origin = lax.rem(my_part() + (part_count - offset), part_count)
-            near = got_refs[0].at[origin, pl.ds(0, near_cap)]
-        else:
-            near = got_refs[which]
-        parts.append((near, pl.ds(which * near_cap, near_cap)))
-    if padded:
-        for part in range(part_count):
-            rows = pl.ds(far_start + part * tile_rows, tile_rows)
-            parts.append((got_refs[0].at[part, pl.ds(near_cap, tile_rows)], rows))
+            for turn in range(subs):
+                owner = wrap(lax.axis_index("sub") - turn, subs)
+                start = pl.multiple_of(which * near_cap + owner * half, half)
+                halo[pl.ds(start, half)] = got[turn][origin, :half]
+        far = [got[turn][part, half:] for part in range(part_count) for turn in range(subs)]
+        used += len(far)
+        halo[far_start:used] = jnp.concatenate(
+            [row.astype(f32) for row in far], axis=0
+        ).astype(bf16)
     else:
-        parts.append((got_refs[-1], pl.ds(far_start, got_refs[-1].shape[0])))
-    return parts
+        for rows in got:
+            start = used - far_start if rows is not got[-1] else far_start
+            halo[start : start + rows.shape[0]] = rows[...]
+            used += rows.shape[0]
+        used -= far_start
+    if used < halo.shape[0]:
+        halo[used:] = jnp.zeros((halo.shape[0] - used, halo.shape[1]), bf16)
 
 
 def place_rows(whole, start, piece, owner):
@@ -203,14 +221,14 @@
     ]
 
 
-def edge_kernel(pieces_count, got_count, part_count, near_cap, padded, block, *refs):
+def edge_kernel(pieces_count, got_count, part_count, near_cap, halved, block, *refs):
     edge_hbm, gathered_hbm, receiver_hbm = refs[:3]
     got_refs = refs[3 : 3 + got_count]
     refs = refs[3 + got_count :]
     in_pieces, out_pieces = refs[:pieces_count], refs[pieces_count : 2 * pieces_count]
     row_refs = refs[2 * pieces_count : 2 * pieces_count + 4]
     new_hbm, sum_ref = refs[2 * pieces_count + 4 : 2 * pieces_count + 6]
-    known, in_weight, out_weight, halo, receiver_ref, rows, new_ref, total, sems = refs[
+    known, in_weight, out_weight, halo, got, receiver_ref, rows, new_ref, total, sems = refs[
         2 * pieces_count + 6 :
     ]
     edge_count, width = edge_hbm.shape
@@ -232,8 +250,7 @@
             target = first if which == 1 else later
             target.append(start(piece.at[which], in_weight.at[spot]))
         if which == 1:
-            for source, spot in halo_parts(part_count, near_cap, padded, got_refs):
-                first.append(start(source, halo.at[spot]))
+            first += [start(source, target) for source, target in zip(got_refs, got)]
     known_copies = []
     for at in range(blocks):
         spot = pl.ds(at * block, block)
@@ -256,13 +273,9 @@
             last.append(start(receiver_hbm, receiver_ref))
     in_bias, out_bias, gain, offset = rows
 
-    used = len(near_offsets) * near_cap + (
-        part_count * tile_rows if padded else got_refs[-1].shape[0]
-    )
-    if used < halo.shape[0]:
-        halo[used:] = jnp.zeros((halo.shape[0] - used, width), bf16)
     for copy in first:
         copy.wait()
+    place_halo(halo, part_count, near_cap, halved, got)
     in_weight[3 * width :] = jnp.dot(
         halo[...], in_weight[width : 2 * width], preferred_element_type=f32
     ).astype(bf16)
@@ -359,11 +372,11 @@
     far_edge = [from_feats(edge_in_weight), from_feats(edge_out_weight)]
     near_edge = [from_subs([edge_in_weight]), from_subs([edge_out_weight])]
 
-    padded = part_count <= padded_parts
-    exchange = exchange_padded if padded else exchange_all
-    got = exchange(node_latent, near_rows, far_rows, part_count)
-    far_stride = tile_rows if padded else far_cap
-    halo_space = len(near_offsets) * near_cap + part_count * far_stride
+    subs = lax.axis_size("sub")
+    halved = part_count <= few_parts and far_cap == subs and near_cap % (tile_rows * subs) == 0
+    exchange = exchange_halves if halved else exchange_all
+    sent, got = exchange(node_latent, near_rows, far_rows, part_count)
+    halo_space = len(near_offsets) * near_cap + part_count * far_cap
     halo_space = -(-halo_space // lanes) * lanes
 
     source_rows = in_hbm(edge_source.reshape(-1, lanes))
@@ -374,11 +387,13 @@
 
     pack_shape = (node_in_weight.shape[0] + 1,) + node_out_weight.shape
     gathered_width = 2 * width + halo_space
+    far_edge[1], sent, latent_after = lax.optimization_barrier((far_edge[1], sent, node_latent))
+    gather_block = block // 2
     gathered, node_weight = pl.pallas_call(
         functools.partial(
-            gather_kernel, node_count, near_cap, far_cap, far_stride, halo_space
+            gather_kernel, node_count, near_cap, far_cap, halved, halo_space
         ),
-        grid=(steps,),
+        grid=(edge_count // gather_block,),
         out_shape=[
             pltpu.HBM((edge_count, gathered_width), bf16),
             pltpu.HBM(pack_shape, bf16),
@@ -388,7 +403,7 @@
             for array in (source_rows, receiver_rows, node_latent, node_in_weight, node_out_weight)
         ],
         out_specs=[
-            pl.BlockSpec((block, gathered_width), lambda step: (step, 0)),
+            pl.BlockSpec((gather_block, gathered_width), lambda step: (step, 0)),
             pl.BlockSpec(pack_shape, lambda step: (0, 0, 0)),
         ],
         compiler_params=pltpu.CompilerParams(vmem_limit_bytes=grant),
@@ -397,7 +412,7 @@
     )(
         source_rows,
         receiver_rows,
-        in_hbm(node_latent),
+        in_hbm(latent_after),
         in_hbm(node_in_weight),
         in_hbm(node_out_weight),
     )
@@ -415,25 +430,30 @@
 
     rows = [value.reshape(1, -1) for value in (edge_in_bias, edge_out_bias, edge_gain, edge_offset)]
     hbm = pl.BlockSpec(memory_space=pltpu.HBM)
-    edge_operands = [edge_latent, gathered, receivers.reshape(-1, lanes)]
-    edge_operands += got + edge_in + edge_out + rows
+    anywhere = pl.BlockSpec(memory_space=pl.ANY)
+    edge_operands = [in_hbm(edge_latent), in_hbm(gathered), in_hbm(receivers.reshape(-1, lanes))]
+    edge_operands += [in_vmem(blocks) for blocks in got]
+    for pieces in (edge_in, edge_out):
+        edge_operands += [in_hbm(pieces[0])] + [in_vmem(piece) for piece in pieces[1:]]
+    edge_operands += [in_hbm(row) for row in rows]
     known_width = 3 * width + halo_space
-    copy_count = 3 * pieces_count + 4 + part_count + 3 * steps + 4 + pieces_count + 1
+    copy_count = 3 * pieces_count + len(got) + 3 * steps + 4 + pieces_count + 1
     edge_new, partial_sums = pl.pallas_call(
         functools.partial(
-            edge_kernel, pieces_count, len(got), part_count, near_cap, padded, block
+            edge_kernel, pieces_count, len(got), part_count, near_cap, halved, block
         ),
         out_shape=[
             pltpu.HBM((edge_count, width), bf16),
             jax.ShapeDtypeStruct((node_count, width), bf16),
         ],
-        in_specs=[hbm] * len(edge_operands),
+        in_specs=[anywhere] * len(edge_operands),
         out_specs=[hbm, vmem],
         scratch_shapes=[
             pltpu.VMEM((edge_count, known_width), bf16),
             pltpu.VMEM((known_width, width), bf16),
             pltpu.VMEM((width, width), bf16),
             pltpu.VMEM((halo_space, width), bf16),
+            [pltpu.VMEM(rows.shape, bf16) for rows in got],
             pltpu.VMEM((edge_count // lanes, lanes), jnp.int32),
             [pltpu.VMEM((1, width), f32)] * 4,
             pltpu.VMEM((edge_count, width), bf16),
@@ -447,7 +467,7 @@
             transcendentals=edge_count * width,
         ),
         name="edge_update",
-    )(*[in_hbm(operand) for operand in edge_operands])
+    )(*edge_operands)
 
     subs = lax.axis_size("sub")
     other_sums = lax.ppermute(partial_sums, "sub", [(at, (at + 1) % subs) for at in range(subs)])

time: 37.9 us -> 53.9 us (1.42)
  waiting for transfers between devices: 3.71 us -> 20.2 us
  Pallas kernels: 19.1 us -> 21.2 us
  starting transfers between devices: 13 us -> 11.6 us
  local copies, waits for them, and re-layouts: 1.05 us -> 0.04 us
    all_to_all x1, waiting for transfers between devices: 0.06 us -> 8.33 us  [exchange_halves(): lax.all_to_all(blocks, ('region', 'feat'), split_axis=0, concat_axis=0, t...]
    ppermute x3, waiting for transfers between devices: 1.87 us -> 9.98 us  [from_feats(): lax.ppermute(weight, 'feat', [(at, (at + shift) % feats) for at in range(...]
    ppermute x3, starting transfers between devices: 6.76 us -> 4.06 us  [from_feats(): lax.ppermute(weight, 'feat', [(at, (at + shift) % feats) for at in range(...]
    pallas_call x1, Pallas kernels: 10 us -> 11.4 us  [shards(): pl.pallas_call(functools.partial(edge_kernel, pieces_count, len(got), par...]
    all_to_all x1, starting transfers between devices: 4.88 us -> 6.05 us  [exchange_halves(): lax.all_to_all(blocks, ('region', 'feat'), split_axis=0, concat_axis=0, t...]
    unnamed x30 -> x14, local copies, waits for them, and re-layouts: 1.05 us -> 0.04 us
    pallas_call x1, Pallas kernels: 4.9 us -> 5.71 us  [shards(): pl.pallas_call(functools.partial(gather_kernel, node_count, near_cap, far...]
  transfers between devices with their start and end apart: 11 -> 12, of which waited for: 4 -> 4; matrix products, arithmetic and copies ran while one was open for 0% -> 0% of each run, Pallas kernels for 45% -> 36%
where the time goes in v6:
time: 53.9 us; the launch traced here: 53.7 us
  Pallas kernels  21.2 us (39%)
  waiting for transfers between devices  20.2 us (37%)
  starting transfers between devices  11.6 us (22%)
  between operations  0.72 us (1%)
    pallas_call x1, Pallas kernels, shards(): pl.pallas_call(functools.partial(edge_kernel, pieces_count, len(got), par...  11.4 us
    ppermute x3, waiting for transfers between devices, from_feats(): lax.ppermute(weight, 'feat', [(at, (at + shift) % feats) for at in range(...  9.98 us
    all_to_all x1, waiting for transfers between devices, exchange_halves(): lax.all_to_all(blocks, ('region', 'feat'), split_axis=0, concat_axis=0, t...  8.33 us
    all_to_all x1, starting transfers between devices, exchange_halves(): lax.all_to_all(blocks, ('region', 'feat'), split_axis=0, concat_axis=0, t...  6.05 us
    pallas_call x1, Pallas kernels, shards(): pl.pallas_call(functools.partial(gather_kernel, node_count, near_cap, far...  5.71 us
    ppermute x3, starting transfers between devices, from_feats(): lax.ppermute(weight, 'feat', [(at, (at + shift) % feats) for at in range(...  4.06 us
    pallas_call x1, Pallas kernels, exchange_halves(): pl.pallas_call(functools.partial(pick_kernel, part_count, near_cap, far_c...  2.08 us
    pallas_call x1, Pallas kernels, shards(): pl.pallas_call(functools.partial(node_kernel, pieces_count), out_shape=ja...  2.01 us
  transfers between devices with their start and end apart: 12, of which 4 were waited for; matrix products, arithmetic and copies ran while one was open for 0% of the time, Pallas kernels for 36%

profile of v6, /device:TPU:0, one launch (start us, length us, event | category | flops | bytes accessed | tf_op | source)
XLA Modules:
  0.0 53.7 jit_solution(17048254604018574034)
XLA Ops:
  0.6 0.0 copy-start.6
  0.6 3.0 %collective-permute-start = (bf16[3,128,512]{2,1,0:T(8,128)(2,1)}, bf16[3,128,512]{2,1,0:T(8,128)(2,1)S(1)}, u32[]{:S(2)}, u32[]{:S(2)}) collective-permute-start(bf16[3,128,512]{2,1,0:T(8,128)(2,1)} %refs_5_.1), channel_id=1, source_target_pairs={{0,2},{2,0},{1,3},{3,1},{4,6},{6,4},{5,7},{7,5},{8,10},{10,8},{9,1... | collective-permute-start | bytes 1179656 | tf_op jit(solution)/shard_map/ppermute | solution.py:210
  3.6 0.1 collective-permute-start.1
  3.7 0.0 collective-permute-start.3
  3.7 2.1 %pick_halo.1 = bf16[8,17,512]{2,1,0:T(8,128)(2,1)} custom-call(s32[1,2,8]{2,1,0:T(2,128)} %bitcast.18, s32[1,4,32]{2,1,0:T(4,128)} %near_ref.1, bf16[384,512]{1,0:T(8,128)(2,1)} %refs_0_.3), custom_call_target="tpu_custom_call" | custom-call | tf_op jit(solution)/shard_map/pick_halo/pallas_call | solution.py:97
  5.8 10.0 %collective-permute-done.1.refs_11_ = bf16[128,512]{1,0:T(8,128)(2,1)S(1)} collective-permute-done((bf16[128,512]{1,0:T(8,128)(2,1)}, bf16[128,512]{1,0:T(8,128)(2,1)S(1)}, u32[]{:S(2)}, u32[]{:S(2)}) %collective-permute-start.1) | collective-permute-done | bytes 131104 | tf_op jit(solution)/shard_map/ppermute | solution.py:210
  15.8 5.7 %gather_latents.1 = (bf16[1536,1280]{1,0:T(8,128)(2,1)}, bf16[3,128,512]{2,1,0:T(8,128)(2,1)}) custom-call(s32[12,128]{1,0:T(8,128)} %bitcast.15, s32[12,128]{1,0:T(8,128)} %bitcast.16, bf16[384,512]{1,0:T(8,128)(2,1)} %refs_0_.3, bf16[2,128,512]{2,1,0:T(8,128)(2,1)} %node_in_ref.1, bf16[128,512]{1,0:T(8,128)(2,1)} %node_out_ref.1), custom_call_target="tpu_custom_call" | custom-call | tf_op jit(solution)/shard_map/gather_latents/pallas_call | solution.py:392
  21.5 6.1 %all-to-all-start = ((bf16[8,17,512]{2,1,0:T(8,128)(2,1)}), bf16[8,17,512]{2,1,0:T(8,128)(2,1)S(1)}, u32[]{:S(2)}, u32[]{:S(2)}) async-start(bf16[8,17,512]{2,1,0:T(8,128)(2,1)} %pick_halo.1), calls=%async_computation | async-start | bytes 393216 | tf_op jit(solution)/shard_map/all_to_all | solution.py:107
  27.6 0.3 collective-permute-start.5
  27.8 8.3 %all-to-all-done.refs_3_ = bf16[8,17,512]{2,1,0:T(8,128)(2,1)S(1)} async-done(((bf16[8,17,512]{2,1,0:T(8,128)(2,1)}), bf16[8,17,512]{2,1,0:T(8,128)(2,1)S(1)}, u32[]{:S(2)}, u32[]{:S(2)}) %all-to-all-start) | async-done | bytes 139296 | tf_op jit(solution)/shard_map/all_to_all | solution.py:107
  36.2 0.0 collective-permute-start.2
  36.2 0.5 collective-permute-start.6
  36.7 1.0 %collective-permute-start.9 = (bf16[3,128,512]{2,1,0:T(8,128)(2,1)}, bf16[3,128,512]{2,1,0:T(8,128)(2,1)S(1)}, u32[]{:S(2)}, u32[]{:S(2)}) collective-permute-start(bf16[3,128,512]{2,1,0:T(8,128)(2,1)} %get-tuple-element.21.refs_3_), channel_id=1, source_target_pairs={{0,2},{2,0},{1,3},{3,1},{4,6},{6,4},{5,7},{7,5},{8,10},{10,8},{9,1... | collective-permute-start | bytes 1179656 | tf_op jit(solution)/shard_map/ppermute | solution.py:210
  37.7 0.1 collective-permute-start.8
  37.8 0.0 collective-permute-done.6.refs_12_
  37.8 0.0 copy-start.3
  37.8 0.0 copy-start.4
  37.8 0.0 copy-start.5
  37.8 11.4 %edge_update.1 = (bf16[1536,512]{1,0:T(8,128)(2,1)}, bf16[384,512]{1,0:T(8,128)(2,1)S(1)}) custom-call(bf16[1536,512]{1,0:T(8,128)(2,1)} %refs_0_.2, bf16[1536,1280]{1,0:T(8,128)(2,1)} %get-tuple-element.16.refs_1_, s32[12,128]{1,0:T(8,128)} %bitcast.17, bf16[8,17,512]{2,1,0:T(8,128)(2,1)S(1)} %all-to-all-done.refs_3_, ...), custom_call_target="tpu_custom_call" | custom-call | flops 3825205248 | bytes 6291456 | tf_op jit(solution)/shard_map/edge_update/pallas_call | solution.py:441
  49.2 0.5 collective-permute-start.7
  49.7 0.1 collective-permute-start.10
  49.8 1.2 %collective-permute-done.7.refs_2_ = bf16[384,512]{1,0:T(8,128)(2,1)S(1)} collective-permute-done((bf16[384,512]{1,0:T(8,128)(2,1)S(1)}, bf16[384,512]{1,0:T(8,128)(2,1)S(1)}, u32[]{:S(2)}, u32[]{:S(2)}) %collective-permute-start.7) | collective-permute-done | bytes 393248 | tf_op jit(solution)/shard_map/ppermute | solution.py:473
  51.1 0.6 %collective-permute-done.10.refs_6_ = bf16[3,128,512]{2,1,0:T(8,128)(2,1)S(1)} collective-permute-done((bf16[3,128,512]{2,1,0:T(8,128)(2,1)S(1)}, bf16[3,128,512]{2,1,0:T(8,128)(2,1)S(1)}, u32[]{:S(2)}, u32[]{:S(2)}) %collective-permute-start.10) | collective-permute-done | bytes 393248 | tf_op jit(solution)/shard_map/ppermute | solution.py:218
  51.7 2.0 %node_update.1 = bf16[384,512]{1,0:T(8,128)(2,1)} custom-call(bf16[384,512]{1,0:T(8,128)(2,1)S(1)} %copy-done, bf16[384,512]{1,0:T(8,128)(2,1)S(1)} %get-tuple-element.20.refs_1_, bf16[384,512]{1,0:T(8,128)(2,1)S(1)} %collective-permute-done.7.refs_2_, bf16[3,128,512]{2,1,0:T(8,128)(2,1)S(1)} %copy-done.1, ...), custom_call_target="tpu_custom_call" | custom-call | flops 603979776 | bytes 1966080 | tf_op jit(solution)/shard_map/node_update/pallas_call | solution.py:476
  (18 shorter events, 0.0 us)
Async XLA Ops:
  0.6 26.9 %copy-start.6 = (bf16[128,512]{1,0:T(8,128)(2,1)S(1)}, bf16[128,512]{1,0:T(8,128)(2,1)}, u32[]{:S(2)}) copy-start(bf16[128,512]{1,0:T(8,128)(2,1)} %refs_9_.1) | copy-start | bytes 393220
  0.6 20.9 %collective-permute-start = (bf16[3,128,512]{2,1,0:T(8,128)(2,1)}, bf16[3,128,512]{2,1,0:T(8,128)(2,1)S(1)}, u32[]{:S(2)}, u32[]{:S(2)}) collective-permute-start(bf16[3,128,512]{2,1,0:T(8,128)(2,1)} %refs_5_.1), channel_id=1, source_target_pairs={{0,2},{2,0},{1,3},{3,1},{4,6},{6,4},{5,7},{7,5},{8,10},{10,8},{9,1... | collective-permute-start | bytes 1179656 | tf_op jit(solution)/shard_map/ppermute | solution.py:210
  3.6 12.1 %collective-permute-start.1 = (bf16[128,512]{1,0:T(8,128)(2,1)}, bf16[128,512]{1,0:T(8,128)(2,1)S(1)}, u32[]{:S(2)}, u32[]{:S(2)}) collective-permute-start(bf16[128,512]{1,0:T(8,128)(2,1)} %refs_9_.1), channel_id=1, source_target_pairs={{0,2},{2,0},{1,3},{3,1},{4,6},{6,4},{5,7},{7,5},{8,10},{10,8},{9,1... | collective-permute-start | bytes 393224 | tf_op jit(solution)/shard_map/ppermute | solution.py:210
  3.7 34.0 %collective-permute-start.3 = (bf16[3,128,512]{2,1,0:T(8,128)(2,1)}, bf16[3,128,512]{2,1,0:T(8,128)(2,1)S(1)}, u32[]{:S(2)}, u32[]{:S(2)}) collective-permute-start(bf16[3,128,512]{2,1,0:T(8,128)(2,1)} %refs_5_.1), channel_id=1, source_target_pairs={{0,1},{1,0},{2,3},{3,2},{4,5},{5,4},{6,7},{7,6},{8,9},{9,8},{10,11... | collective-permute-start | bytes 1179656 | tf_op jit(solution)/shard_map/ppermute | solution.py:218
  21.5 16.3 %collective-permute-start.4 = (bf16[3,128,512]{2,1,0:T(8,128)(2,1)S(1)}, bf16[3,128,512]{2,1,0:T(8,128)(2,1)S(1)}, u32[]{:S(2)}, u32[]{:S(2)}) collective-permute-start(bf16[3,128,512]{2,1,0:T(8,128)(2,1)S(1)} %collective-permute-done.refs_7_), channel_id=1, source_target_pairs={{0,1},{1,0},{2,3},{3,2},{4,5},{5,4},{6,7},{7,6},{8,9},{9,8},{10,11... | collective-permute-start | bytes 1179656 | tf_op jit(solution)/shard_map/ppermute | solution.py:218
  21.5 14.7 %all-to-all-start = ((bf16[8,17,512]{2,1,0:T(8,128)(2,1)}), bf16[8,17,512]{2,1,0:T(8,128)(2,1)S(1)}, u32[]{:S(2)}, u32[]{:S(2)}) async-start(bf16[8,17,512]{2,1,0:T(8,128)(2,1)} %pick_halo.1), calls=%async_computation | async-start | bytes 393216 | tf_op jit(solution)/shard_map/all_to_all | solution.py:107
  27.6 9.1 %collective-permute-start.5 = (bf16[128,512]{1,0:T(8,128)(2,1)S(1)}, bf16[128,512]{1,0:T(8,128)(2,1)S(1)}, u32[]{:S(2)}, u32[]{:S(2)}) collective-permute-start(bf16[128,512]{1,0:T(8,128)(2,1)S(1)} %copy-done.6), channel_id=1, source_target_pairs={{0,1},{1,0},{2,3},{3,2},{4,5},{5,4},{6,7},{7,6},{8,9},{9,8},{10,11... | collective-permute-start | bytes 393224 | tf_op jit(solution)/shard_map/ppermute | solution.py:218
  36.2 1.5 %collective-permute-start.2 = (bf16[8,17,512]{2,1,0:T(8,128)(2,1)S(1)}, bf16[8,17,512]{2,1,0:T(8,128)(2,1)S(1)}, u32[]{:S(2)}, u32[]{:S(2)}) collective-permute-start(bf16[8,17,512]{2,1,0:T(8,128)(2,1)S(1)} %all-to-all-done.refs_3_), channel_id=1, source_target_pairs={{0,1},{1,0},{2,3},{3,2},{4,5},{5,4},{6,7},{7,6},{8,9},{9,8},{10,11... | collective-permute-start | bytes 417800 | tf_op jit(solution)/shard_map/ppermute | solution.py:218
  36.2 1.6 %collective-permute-start.6 = (bf16[128,512]{1,0:T(8,128)(2,1)S(1)}, bf16[128,512]{1,0:T(8,128)(2,1)S(1)}, u32[]{:S(2)}, u32[]{:S(2)}) collective-permute-start(bf16[128,512]{1,0:T(8,128)(2,1)S(1)} %collective-permute-done.1.refs_11_), channel_id=1, source_target_pairs={{0,1},{1,0},{2,3},{3,2},{4,5},{5,4},{6,7},{7,6},{8,9},{9,8},{10,11... | collective-permute-start | bytes 393224 | tf_op jit(solution)/shard_map/ppermute | solution.py:218
  36.7 13.0 %collective-permute-start.9 = (bf16[3,128,512]{2,1,0:T(8,128)(2,1)}, bf16[3,128,512]{2,1,0:T(8,128)(2,1)S(1)}, u32[]{:S(2)}, u32[]{:S(2)}) collective-permute-start(bf16[3,128,512]{2,1,0:T(8,128)(2,1)} %get-tuple-element.21.refs_3_), channel_id=1, source_target_pairs={{0,2},{2,0},{1,3},{3,1},{4,6},{6,4},{5,7},{7,5},{8,10},{10,8},{9,1... | collective-permute-start | bytes 1179656 | tf_op jit(solution)/shard_map/ppermute | solution.py:210
  37.7 12.2 %collective-permute-start.8 = (bf16[3,128,512]{2,1,0:T(8,128)(2,1)}, bf16[3,128,512]{2,1,0:T(8,128)(2,1)S(1)}, u32[]{:S(2)}, u32[]{:S(2)}) collective-permute-start(bf16[3,128,512]{2,1,0:T(8,128)(2,1)} %get-tuple-element.21.refs_3_), channel_id=1, source_target_pairs={{0,1},{1,0},{2,3},{3,2},{4,5},{5,4},{6,7},{7,6},{8,9},{9,8},{10,11... | collective-permute-start | bytes 1179656 | tf_op jit(solution)/shard_map/ppermute | solution.py:218
  37.8 13.8 %copy-start = (bf16[384,512]{1,0:T(8,128)(2,1)S(1)}, bf16[384,512]{1,0:T(8,128)(2,1)}, u32[]{:S(2)}) copy-start(bf16[384,512]{1,0:T(8,128)(2,1)} %refs_0_.3) | copy-start | bytes 1179652
  37.8 13.8 %copy-start.1 = (bf16[3,128,512]{2,1,0:T(8,128)(2,1)S(1)}, bf16[3,128,512]{2,1,0:T(8,128)(2,1)}, u32[]{:S(2)}) copy-start(bf16[3,128,512]{2,1,0:T(8,128)(2,1)} %get-tuple-element.21.refs_3_) | copy-start | bytes 1179652
  37.8 13.8 %copy-start.2 = (f32[512]{0:T(512)S(1)}, f32[512]{0:T(512)}, u32[]{:S(2)}) copy-start(f32[512]{0:T(512)} %param.32) | copy-start | bytes 6148
  37.8 13.8 %copy-start.3 = (f32[512]{0:T(512)S(1)}, f32[512]{0:T(512)}, u32[]{:S(2)}) copy-start(f32[512]{0:T(512)} %param.33) | copy-start | bytes 6148
  37.8 13.8 %copy-start.4 = (f32[512]{0:T(512)S(1)}, f32[512]{0:T(512)}, u32[]{:S(2)}) copy-start(f32[512]{0:T(512)} %param.34) | copy-start | bytes 6148
  37.8 13.8 %copy-start.5 = (f32[512]{0:T(512)S(1)}, f32[512]{0:T(512)}, u32[]{:S(2)}) copy-start(f32[512]{0:T(512)} %param.35) | copy-start | bytes 6148
  49.2 1.8 %collective-permute-start.7 = (bf16[384,512]{1,0:T(8,128)(2,1)S(1)}, bf16[384,512]{1,0:T(8,128)(2,1)S(1)}, u32[]{:S(2)}, u32[]{:S(2)}) collective-permute-start(bf16[384,512]{1,0:T(8,128)(2,1)S(1)} %get-tuple-element.20.refs_1_), channel_id=1, source_target_pairs={{0,1},{1,0},{2,3},{3,2},{4,5},{5,4},{6,7},{7,6},{8,9},{9,8},{10,11... | collective-permute-start | bytes 1179656 | tf_op jit(solution)/shard_map/ppermute | solution.py:473
  49.7 1.9 %collective-permute-start.10 = (bf16[3,128,512]{2,1,0:T(8,128)(2,1)S(1)}, bf16[3,128,512]{2,1,0:T(8,128)(2,1)S(1)}, u32[]{:S(2)}, u32[]{:S(2)}) collective-permute-start(bf16[3,128,512]{2,1,0:T(8,128)(2,1)S(1)} %collective-permute-done.9.refs_5_), channel_id=1, source_target_pairs={{0,1},{1,0},{2,3},{3,2},{4,5},{5,4},{6,7},{7,6},{8,9},{9,8},{10,11... | collective-permute-start | bytes 1179656 | tf_op jit(solution)/shard_map/ppermute | solution.py:218

commit v7 on v6

--- a/solution.py
+++ b/solution.py
@@ -105,7 +105,7 @@
         name="pick_halo",
     )(in_hbm(jnp.transpose(far_rows, (0, 2, 1))), in_hbm(near_rows), in_hbm(node_latent))
     own = lax.all_to_all(blocks, ("region", "feat"), split_axis=0, concat_axis=0, tiled=True)
-    return blocks, [own] + from_subs([own])
+    return [own] + from_subs([own])
 
 
 def exchange_all(node_latent, near_rows, far_rows, part_count):
@@ -117,7 +117,7 @@
         got.append(lax.ppermute(near_send[which], ("region", "feat"), pairs))
     far = lax.all_to_all(far_send, ("region", "feat"), split_axis=0, concat_axis=0, tiled=True)
     got.append(far.reshape(-1, far.shape[2]))
-    return far_send, got
+    return got
 
 
 def gather_kernel(
@@ -366,7 +366,7 @@
     edge_count = edge_latent.shape[0]
     near_cap, far_cap = near_rows.shape[2], far_rows.shape[2]
     part_count = far_rows.shape[1]
-    block = 512
+    block = 256
     steps = edge_count // block
 
     far_edge = [from_feats(edge_in_weight), from_feats(edge_out_weight)]
@@ -375,7 +375,7 @@
     subs = lax.axis_size("sub")
     halved = part_count <= few_parts and far_cap == subs and near_cap % (tile_rows * subs) == 0
     exchange = exchange_halves if halved else exchange_all
-    sent, got = exchange(node_latent, near_rows, far_rows, part_count)
+    got = exchange(node_latent, near_rows, far_rows, part_count)
     halo_space = len(near_offsets) * near_cap + part_count * far_cap
     halo_space = -(-halo_space // lanes) * lanes
 
@@ -387,8 +387,7 @@
 
     pack_shape = (node_in_weight.shape[0] + 1,) + node_out_weight.shape
     gathered_width = 2 * width + halo_space
-    far_edge[1], sent, latent_after = lax.optimization_barrier((far_edge[1], sent, node_latent))
-    gather_block = block // 2
+    gather_block = edge_count // 3
     gathered, node_weight = pl.pallas_call(
         functools.partial(
             gather_kernel, node_count, near_cap, far_cap, halved, halo_space
@@ -412,7 +411,7 @@
     )(
         source_rows,
         receiver_rows,
-        in_hbm(latent_after),
+        in_hbm(node_latent),
         in_hbm(node_in_weight),
         in_hbm(node_out_weight),
     )

time: 53.9 us -> 51.3 us (0.952)
  waiting for transfers between devices: 20.2 us -> 17.4 us
    ppermute x3, waiting for transfers between devices: 9.98 us -> 7.21 us  [from_feats(): lax.ppermute(weight, 'feat', [(at, (at + shift) % feats) for at in range(...]
    pallas_call x1, Pallas kernels: 11.4 us -> 12.4 us  [shards(): pl.pallas_call(functools.partial(edge_kernel, pieces_count, len(got), par...]
    pallas_call x1, Pallas kernels: 5.71 us -> 4.85 us  [shards(): pl.pallas_call(functools.partial(gather_kernel, node_count, near_cap, far...]
  transfers between devices with their start and end apart: 12 -> 12, of which waited for: 4 -> 4; matrix products, arithmetic and copies ran while one was open for 0% -> 0% of each run, Pallas kernels for 36% -> 38%
where the time goes in v7:
time: 51.3 us; the launch traced here: 51 us
  Pallas kernels  21.3 us (42%)
  waiting for transfers between devices  17.4 us (34%)
  starting transfers between devices  11.6 us (23%)
  between operations  0.71 us (1%)
    pallas_call x1, Pallas kernels, shards(): pl.pallas_call(functools.partial(edge_kernel, pieces_count, len(got), par...  12.4 us
    all_to_all x1, waiting for transfers between devices, exchange_halves(): lax.all_to_all(blocks, ('region', 'feat'), split_axis=0, concat_axis=0, t...  8.33 us
    ppermute x3, waiting for transfers between devices, from_feats(): lax.ppermute(weight, 'feat', [(at, (at + shift) % feats) for at in range(...  7.21 us
    all_to_all x1, starting transfers between devices, exchange_halves(): lax.all_to_all(blocks, ('region', 'feat'), split_axis=0, concat_axis=0, t...  6.05 us
    pallas_call x1, Pallas kernels, shards(): pl.pallas_call(functools.partial(gather_kernel, node_count, near_cap, far...  4.85 us
    ppermute x3, starting transfers between devices, from_feats(): lax.ppermute(weight, 'feat', [(at, (at + shift) % feats) for at in range(...  4.06 us
    pallas_call x1, Pallas kernels, exchange_halves(): pl.pallas_call(functools.partial(pick_kernel, part_count, near_cap, far_c...  2.08 us
    pallas_call x1, Pallas kernels, shards(): pl.pallas_call(functools.partial(node_kernel, pieces_count), out_shape=ja...  2.01 us
  transfers between devices with their start and end apart: 12, of which 4 were waited for; matrix products, arithmetic and copies ran while one was open for 0% of the time, Pallas kernels for 38%

profile of v7, /device:TPU:0, one launch (start us, length us, event | category | flops | bytes accessed | tf_op | source)
XLA Modules:
  0.0 51.0 jit_solution(17701923564984893253)
XLA Ops:
  0.6 0.0 copy-start.6
  0.6 3.0 %collective-permute-start = (bf16[3,128,512]{2,1,0:T(8,128)(2,1)}, bf16[3,128,512]{2,1,0:T(8,128)(2,1)S(1)}, u32[]{:S(2)}, u32[]{:S(2)}) collective-permute-start(bf16[3,128,512]{2,1,0:T(8,128)(2,1)} %refs_5_.1), channel_id=1, source_target_pairs={{0,2},{2,0},{1,3},{3,1},{4,6},{6,4},{5,7},{7,5},{8,10},{10,8},{9,1... | collective-permute-start | bytes 1179656 | tf_op jit(solution)/shard_map/ppermute | solution.py:210
  3.6 0.1 collective-permute-start.1
  3.7 4.8 %gather_latents.1 = (bf16[1536,1280]{1,0:T(8,128)(2,1)}, bf16[3,128,512]{2,1,0:T(8,128)(2,1)}) custom-call(s32[12,128]{1,0:T(8,128)} %bitcast.15, s32[12,128]{1,0:T(8,128)} %bitcast.16, bf16[384,512]{1,0:T(8,128)(2,1)} %refs_0_.3, bf16[2,128,512]{2,1,0:T(8,128)(2,1)} %node_in_ref.1, bf16[128,512]{1,0:T(8,128)(2,1)} %node_out_ref.1), custom_call_target="tpu_custom_call" | custom-call | tf_op jit(solution)/shard_map/gather_latents/pallas_call | solution.py:391
  8.6 7.2 %collective-permute-done.1.refs_11_ = bf16[128,512]{1,0:T(8,128)(2,1)S(1)} collective-permute-done((bf16[128,512]{1,0:T(8,128)(2,1)}, bf16[128,512]{1,0:T(8,128)(2,1)S(1)}, u32[]{:S(2)}, u32[]{:S(2)}) %collective-permute-start.1) | collective-permute-done | bytes 131104 | tf_op jit(solution)/shard_map/ppermute | solution.py:210
  15.8 2.1 %pick_halo.1 = bf16[8,17,512]{2,1,0:T(8,128)(2,1)} custom-call(s32[1,2,8]{2,1,0:T(2,128)} %bitcast.18, s32[1,4,32]{2,1,0:T(4,128)} %near_ref.1, bf16[384,512]{1,0:T(8,128)(2,1)} %refs_0_.3), custom_call_target="tpu_custom_call" | custom-call | tf_op jit(solution)/shard_map/pick_halo/pallas_call | solution.py:97
  17.9 6.1 %all-to-all-start = ((bf16[8,17,512]{2,1,0:T(8,128)(2,1)}), bf16[8,17,512]{2,1,0:T(8,128)(2,1)S(1)}, u32[]{:S(2)}, u32[]{:S(2)}) async-start(bf16[8,17,512]{2,1,0:T(8,128)(2,1)} %pick_halo.1), calls=%async_computation | async-start | bytes 393216 | tf_op jit(solution)/shard_map/all_to_all | solution.py:107
  23.9 0.3 collective-permute-start.5
  24.2 8.3 %all-to-all-done.refs_3_ = bf16[8,17,512]{2,1,0:T(8,128)(2,1)S(1)} async-done(((bf16[8,17,512]{2,1,0:T(8,128)(2,1)}), bf16[8,17,512]{2,1,0:T(8,128)(2,1)S(1)}, u32[]{:S(2)}, u32[]{:S(2)}) %all-to-all-start) | async-done | bytes 139296 | tf_op jit(solution)/shard_map/all_to_all | solution.py:107
  32.5 0.0 collective-permute-start.2
  32.6 0.5 collective-permute-start.6
  33.1 1.0 %collective-permute-start.9 = (bf16[3,128,512]{2,1,0:T(8,128)(2,1)}, bf16[3,128,512]{2,1,0:T(8,128)(2,1)S(1)}, u32[]{:S(2)}, u32[]{:S(2)}) collective-permute-start(bf16[3,128,512]{2,1,0:T(8,128)(2,1)} %get-tuple-element.17.refs_3_), channel_id=1, source_target_pairs={{0,2},{2,0},{1,3},{3,1},{4,6},{6,4},{5,7},{7,5},{8,10},{10,8},{9,1... | collective-permute-start | bytes 1179656 | tf_op jit(solution)/shard_map/ppermute | solution.py:210
  34.0 0.1 collective-permute-start.8
  34.1 0.0 collective-permute-done.3.refs_6_
  34.1 0.0 collective-permute-done.6.refs_12_
  34.2 0.0 copy-start.3
  34.2 0.0 copy-start.4
  34.2 0.0 copy-start.5
  34.2 12.4 %edge_update.1 = (bf16[1536,512]{1,0:T(8,128)(2,1)}, bf16[384,512]{1,0:T(8,128)(2,1)S(1)}) custom-call(bf16[1536,512]{1,0:T(8,128)(2,1)} %refs_0_.2, bf16[1536,1280]{1,0:T(8,128)(2,1)} %get-tuple-element.12.refs_1_, s32[12,128]{1,0:T(8,128)} %bitcast.17, bf16[8,17,512]{2,1,0:T(8,128)(2,1)S(1)} %all-to-all-done.refs_3_, ...), custom_call_target="tpu_custom_call" | custom-call | flops 3825205248 | bytes 6291456 | tf_op jit(solution)/shard_map/edge_update/pallas_call | solution.py:440
  46.6 0.5 collective-permute-start.7
  47.1 0.1 collective-permute-start.10
  47.2 1.2 %collective-permute-done.7.refs_2_ = bf16[384,512]{1,0:T(8,128)(2,1)S(1)} collective-permute-done((bf16[384,512]{1,0:T(8,128)(2,1)S(1)}, bf16[384,512]{1,0:T(8,128)(2,1)S(1)}, u32[]{:S(2)}, u32[]{:S(2)}) %collective-permute-start.7) | collective-permute-done | bytes 393248 | tf_op jit(solution)/shard_map/ppermute | solution.py:472
  48.4 0.6 %collective-permute-done.10.refs_6_ = bf16[3,128,512]{2,1,0:T(8,128)(2,1)S(1)} collective-permute-done((bf16[3,128,512]{2,1,0:T(8,128)(2,1)S(1)}, bf16[3,128,512]{2,1,0:T(8,128)(2,1)S(1)}, u32[]{:S(2)}, u32[]{:S(2)}) %collective-permute-start.10) | collective-permute-done | bytes 393248 | tf_op jit(solution)/shard_map/ppermute | solution.py:218
  49.0 2.0 %node_update.1 = bf16[384,512]{1,0:T(8,128)(2,1)} custom-call(bf16[384,512]{1,0:T(8,128)(2,1)S(1)} %copy-done, bf16[384,512]{1,0:T(8,128)(2,1)S(1)} %get-tuple-element.16.refs_1_, bf16[384,512]{1,0:T(8,128)(2,1)S(1)} %collective-permute-done.7.refs_2_, bf16[3,128,512]{2,1,0:T(8,128)(2,1)S(1)} %copy-done.1, ...), custom_call_target="tpu_custom_call" | custom-call | flops 603979776 | bytes 1966080 | tf_op jit(solution)/shard_map/node_update/pallas_call | solution.py:475
  (18 shorter events, 0.0 us)
Async XLA Ops:
  0.6 23.3 %copy-start.6 = (bf16[128,512]{1,0:T(8,128)(2,1)S(1)}, bf16[128,512]{1,0:T(8,128)(2,1)}, u32[]{:S(2)}) copy-start(bf16[128,512]{1,0:T(8,128)(2,1)} %refs_9_.1) | copy-start | bytes 393220
  0.6 15.1 %collective-permute-start = (bf16[3,128,512]{2,1,0:T(8,128)(2,1)}, bf16[3,128,512]{2,1,0:T(8,128)(2,1)S(1)}, u32[]{:S(2)}, u32[]{:S(2)}) collective-permute-start(bf16[3,128,512]{2,1,0:T(8,128)(2,1)} %refs_5_.1), channel_id=1, source_target_pairs={{0,2},{2,0},{1,3},{3,1},{4,6},{6,4},{5,7},{7,5},{8,10},{10,8},{9,1... | collective-permute-start | bytes 1179656 | tf_op jit(solution)/shard_map/ppermute | solution.py:210
  3.6 12.1 %collective-permute-start.1 = (bf16[128,512]{1,0:T(8,128)(2,1)}, bf16[128,512]{1,0:T(8,128)(2,1)S(1)}, u32[]{:S(2)}, u32[]{:S(2)}) collective-permute-start(bf16[128,512]{1,0:T(8,128)(2,1)} %refs_9_.1), channel_id=1, source_target_pairs={{0,2},{2,0},{1,3},{3,1},{4,6},{6,4},{5,7},{7,5},{8,10},{10,8},{9,1... | collective-permute-start | bytes 393224 | tf_op jit(solution)/shard_map/ppermute | solution.py:210
  3.7 30.4 %collective-permute-start.3 = (bf16[3,128,512]{2,1,0:T(8,128)(2,1)}, bf16[3,128,512]{2,1,0:T(8,128)(2,1)S(1)}, u32[]{:S(2)}, u32[]{:S(2)}) collective-permute-start(bf16[3,128,512]{2,1,0:T(8,128)(2,1)} %refs_5_.1), channel_id=1, source_target_pairs={{0,1},{1,0},{2,3},{3,2},{4,5},{5,4},{6,7},{7,6},{8,9},{9,8},{10,11... | collective-permute-start | bytes 1179656 | tf_op jit(solution)/shard_map/ppermute | solution.py:218
  15.8 18.4 %collective-permute-start.4 = (bf16[3,128,512]{2,1,0:T(8,128)(2,1)S(1)}, bf16[3,128,512]{2,1,0:T(8,128)(2,1)S(1)}, u32[]{:S(2)}, u32[]{:S(2)}) collective-permute-start(bf16[3,128,512]{2,1,0:T(8,128)(2,1)S(1)} %collective-permute-done.refs_7_), channel_id=1, source_target_pairs={{0,1},{1,0},{2,3},{3,2},{4,5},{5,4},{6,7},{7,6},{8,9},{9,8},{10,11... | collective-permute-start | bytes 1179656 | tf_op jit(solution)/shard_map/ppermute | solution.py:218
  17.9 14.7 %all-to-all-start = ((bf16[8,17,512]{2,1,0:T(8,128)(2,1)}), bf16[8,17,512]{2,1,0:T(8,128)(2,1)S(1)}, u32[]{:S(2)}, u32[]{:S(2)}) async-start(bf16[8,17,512]{2,1,0:T(8,128)(2,1)} %pick_halo.1), calls=%async_computation | async-start | bytes 393216 | tf_op jit(solution)/shard_map/all_to_all | solution.py:107
  23.9 9.1 %collective-permute-start.5 = (bf16[128,512]{1,0:T(8,128)(2,1)S(1)}, bf16[128,512]{1,0:T(8,128)(2,1)S(1)}, u32[]{:S(2)}, u32[]{:S(2)}) collective-permute-start(bf16[128,512]{1,0:T(8,128)(2,1)S(1)} %copy-done.6), channel_id=1, source_target_pairs={{0,1},{1,0},{2,3},{3,2},{4,5},{5,4},{6,7},{7,6},{8,9},{9,8},{10,11... | collective-permute-start | bytes 393224 | tf_op jit(solution)/shard_map/ppermute | solution.py:218
  32.5 1.5 %collective-permute-start.2 = (bf16[8,17,512]{2,1,0:T(8,128)(2,1)S(1)}, bf16[8,17,512]{2,1,0:T(8,128)(2,1)S(1)}, u32[]{:S(2)}, u32[]{:S(2)}) collective-permute-start(bf16[8,17,512]{2,1,0:T(8,128)(2,1)S(1)} %all-to-all-done.refs_3_), channel_id=1, source_target_pairs={{0,1},{1,0},{2,3},{3,2},{4,5},{5,4},{6,7},{7,6},{8,9},{9,8},{10,11... | collective-permute-start | bytes 417800 | tf_op jit(solution)/shard_map/ppermute | solution.py:218
  32.6 1.6 %collective-permute-start.6 = (bf16[128,512]{1,0:T(8,128)(2,1)S(1)}, bf16[128,512]{1,0:T(8,128)(2,1)S(1)}, u32[]{:S(2)}, u32[]{:S(2)}) collective-permute-start(bf16[128,512]{1,0:T(8,128)(2,1)S(1)} %collective-permute-done.1.refs_11_), channel_id=1, source_target_pairs={{0,1},{1,0},{2,3},{3,2},{4,5},{5,4},{6,7},{7,6},{8,9},{9,8},{10,11... | collective-permute-start | bytes 393224 | tf_op jit(solution)/shard_map/ppermute | solution.py:218
  33.1 14.0 %collective-permute-start.9 = (bf16[3,128,512]{2,1,0:T(8,128)(2,1)}, bf16[3,128,512]{2,1,0:T(8,128)(2,1)S(1)}, u32[]{:S(2)}, u32[]{:S(2)}) collective-permute-start(bf16[3,128,512]{2,1,0:T(8,128)(2,1)} %get-tuple-element.17.refs_3_), channel_id=1, source_target_pairs={{0,2},{2,0},{1,3},{3,1},{4,6},{6,4},{5,7},{7,5},{8,10},{10,8},{9,1... | collective-permute-start | bytes 1179656 | tf_op jit(solution)/shard_map/ppermute | solution.py:210
  34.0 13.1 %collective-permute-start.8 = (bf16[3,128,512]{2,1,0:T(8,128)(2,1)}, bf16[3,128,512]{2,1,0:T(8,128)(2,1)S(1)}, u32[]{:S(2)}, u32[]{:S(2)}) collective-permute-start(bf16[3,128,512]{2,1,0:T(8,128)(2,1)} %get-tuple-element.17.refs_3_), channel_id=1, source_target_pairs={{0,1},{1,0},{2,3},{3,2},{4,5},{5,4},{6,7},{7,6},{8,9},{9,8},{10,11... | collective-permute-start | bytes 1179656 | tf_op jit(solution)/shard_map/ppermute | solution.py:218
  34.2 14.8 %copy-start = (bf16[384,512]{1,0:T(8,128)(2,1)S(1)}, bf16[384,512]{1,0:T(8,128)(2,1)}, u32[]{:S(2)}) copy-start(bf16[384,512]{1,0:T(8,128)(2,1)} %refs_0_.3) | copy-start | bytes 1179652
  34.2 14.8 %copy-start.1 = (bf16[3,128,512]{2,1,0:T(8,128)(2,1)S(1)}, bf16[3,128,512]{2,1,0:T(8,128)(2,1)}, u32[]{:S(2)}) copy-start(bf16[3,128,512]{2,1,0:T(8,128)(2,1)} %get-tuple-element.17.refs_3_) | copy-start | bytes 1179652
  34.2 14.8 %copy-start.2 = (f32[512]{0:T(512)S(1)}, f32[512]{0:T(512)}, u32[]{:S(2)}) copy-start(f32[512]{0:T(512)} %param.32) | copy-start | bytes 6148
  34.2 14.8 %copy-start.3 = (f32[512]{0:T(512)S(1)}, f32[512]{0:T(512)}, u32[]{:S(2)}) copy-start(f32[512]{0:T(512)} %param.33) | copy-start | bytes 6148
  34.2 14.8 %copy-start.4 = (f32[512]{0:T(512)S(1)}, f32[512]{0:T(512)}, u32[]{:S(2)}) copy-start(f32[512]{0:T(512)} %param.34) | copy-start | bytes 6148
  34.2 14.8 %copy-start.5 = (f32[512]{0:T(512)S(1)}, f32[512]{0:T(512)}, u32[]{:S(2)}) copy-start(f32[512]{0:T(512)} %param.35) | copy-start | bytes 6148
  46.6 1.8 %collective-permute-start.7 = (bf16[384,512]{1,0:T(8,128)(2,1)S(1)}, bf16[384,512]{1,0:T(8,128)(2,1)S(1)}, u32[]{:S(2)}, u32[]{:S(2)}) collective-permute-start(bf16[384,512]{1,0:T(8,128)(2,1)S(1)} %get-tuple-element.16.refs_1_), channel_id=1, source_target_pairs={{0,1},{1,0},{2,3},{3,2},{4,5},{5,4},{6,7},{7,6},{8,9},{9,8},{10,11... | collective-permute-start | bytes 1179656 | tf_op jit(solution)/shard_map/ppermute | solution.py:472
  47.1 1.9 %collective-permute-start.10 = (bf16[3,128,512]{2,1,0:T(8,128)(2,1)S(1)}, bf16[3,128,512]{2,1,0:T(8,128)(2,1)S(1)}, u32[]{:S(2)}, u32[]{:S(2)}) collective-permute-start(bf16[3,128,512]{2,1,0:T(8,128)(2,1)S(1)} %collective-permute-done.9.refs_5_), channel_id=1, source_target_pairs={{0,1},{1,0},{2,3},{3,2},{4,5},{5,4},{6,7},{7,6},{8,9},{9,8},{10,11... | collective-permute-start | bytes 1179656 | tf_op jit(solution)/shard_map/ppermute | solution.py:218

commit v8 on v7

--- a/solution.py
+++ b/solution.py
@@ -105,7 +105,7 @@
         name="pick_halo",
     )(in_hbm(jnp.transpose(far_rows, (0, 2, 1))), in_hbm(near_rows), in_hbm(node_latent))
     own = lax.all_to_all(blocks, ("region", "feat"), split_axis=0, concat_axis=0, tiled=True)
-    return [own] + from_subs([own])
+    return [own]
 
 
 def exchange_all(node_latent, near_rows, far_rows, part_count):
@@ -228,7 +228,7 @@
     in_pieces, out_pieces = refs[:pieces_count], refs[pieces_count : 2 * pieces_count]
     row_refs = refs[2 * pieces_count : 2 * pieces_count + 4]
     new_hbm, sum_ref = refs[2 * pieces_count + 4 : 2 * pieces_count + 6]
-    known, in_weight, out_weight, halo, got, receiver_ref, rows, new_ref, total, sems = refs[
+    known, in_weight, out_weight, halo, receiver_ref, rows, new_ref, total, sems = refs[
         2 * pieces_count + 6 :
     ]
     edge_count, width = edge_hbm.shape
@@ -244,13 +244,10 @@
     order = owners()
     first, later, last = [], [], []
     for which in (1, 0, 2):
-        for piece, owner in zip(in_pieces, order):
-            count = piece.shape[1]
-            spot = pl.ds(pl.multiple_of(which * width + owner * count, count), count)
-            target = first if which == 1 else later
-            target.append(start(piece.at[which], in_weight.at[spot]))
-        if which == 1:
-            first += [start(source, target) for source, target in zip(got_refs, got)]
+        count = in_pieces[0].shape[1]
+        spot = pl.ds(pl.multiple_of(which * width + order[0] * count, count), count)
+        target = first if which == 1 else later
+        target.append(start(in_pieces[0].at[which], in_weight.at[spot]))
     known_copies = []
     for at in range(blocks):
         spot = pl.ds(at * block, block)
@@ -266,16 +263,20 @@
         if at == 0:
             for row_ref, row in zip(row_refs, rows):
                 last.append(start(row_ref, row))
-            for piece, owner in zip(out_pieces, order):
-                count = piece.shape[0]
-                spot = pl.ds(pl.multiple_of(owner * count, count), count)
-                last.append(start(piece, out_weight.at[spot]))
+            count = out_pieces[0].shape[0]
+            spot = pl.ds(pl.multiple_of(order[0] * count, count), count)
+            last.append(start(out_pieces[0], out_weight.at[spot]))
             last.append(start(receiver_hbm, receiver_ref))
     in_bias, out_bias, gain, offset = rows
 
+    place_halo(halo, part_count, near_cap, halved, got_refs)
+    for which in (1, 0, 2):
+        for piece, owner in zip(in_pieces[1:], order[1:]):
+            place_rows(in_weight, which * width, piece[which], owner)
+    for piece, owner in zip(out_pieces[1:], order[1:]):
+        place_rows(out_weight, 0, piece[...], owner)
     for copy in first:
         copy.wait()
-    place_halo(halo, part_count, near_cap, halved, got)
     in_weight[3 * width :] = jnp.dot(
         halo[...], in_weight[width : 2 * width], preferred_element_type=f32
     ).astype(bf16)
@@ -366,7 +367,7 @@
     edge_count = edge_latent.shape[0]
     near_cap, far_cap = near_rows.shape[2], far_rows.shape[2]
     part_count = far_rows.shape[1]
-    block = 256
+    block = edge_count // 2
     steps = edge_count // block
 
     far_edge = [from_feats(edge_in_weight), from_feats(edge_out_weight)]
@@ -416,9 +417,11 @@
         in_hbm(node_out_weight),
     )
 
-    far_edge, gathered, node_weight = lax.optimization_barrier(
-        (far_edge, gathered, node_weight)
+    far_edge, got, gathered, node_weight = lax.optimization_barrier(
+        (far_edge, got, gathered, node_weight)
     )
+    if halved:
+        got = got + from_subs(got)
     edge_in, edge_out = [
         [weight] + near + far + from_subs(far)
         for weight, near, far in zip((edge_in_weight, edge_out_weight), near_edge, far_edge)
@@ -429,14 +432,16 @@
 
     rows = [value.reshape(1, -1) for value in (edge_in_bias, edge_out_bias, edge_gain, edge_offset)]
     hbm = pl.BlockSpec(memory_space=pltpu.HBM)
-    anywhere = pl.BlockSpec(memory_space=pl.ANY)
     edge_operands = [in_hbm(edge_latent), in_hbm(gathered), in_hbm(receivers.reshape(-1, lanes))]
     edge_operands += [in_vmem(blocks) for blocks in got]
+    edge_specs = [hbm] * 3 + [vmem] * len(got)
     for pieces in (edge_in, edge_out):
         edge_operands += [in_hbm(pieces[0])] + [in_vmem(piece) for piece in pieces[1:]]
+        edge_specs += [hbm] + [vmem] * (pieces_count - 1)
     edge_operands += [in_hbm(row) for row in rows]
+    edge_specs += [hbm] * len(rows)
     known_width = 3 * width + halo_space
-    copy_count = 3 * pieces_count + len(got) + 3 * steps + 4 + pieces_count + 1
+    copy_count = 3 + 3 * steps + 4 + 1 + 1
     edge_new, partial_sums = pl.pallas_call(
         functools.partial(
             edge_kernel, pieces_count, len(got), part_count, near_cap, halved, block
@@ -445,14 +450,13 @@
             pltpu.HBM((edge_count, width), bf16),
             jax.ShapeDtypeStruct((node_count, width), bf16),
         ],
-        in_specs=[anywhere] * len(edge_operands),
+        in_specs=edge_specs,
         out_specs=[hbm, vmem],
         scratch_shapes=[
             pltpu.VMEM((edge_count, known_width), bf16),
             pltpu.VMEM((known_width, width), bf16),
             pltpu.VMEM((width, width), bf16),
             pltpu.VMEM((halo_space, width), bf16),
-            [pltpu.VMEM(rows.shape, bf16) for rows in got],
             pltpu.VMEM((edge_count // lanes, lanes), jnp.int32),
             [pltpu.VMEM((1, width), f32)] * 4,
             pltpu.VMEM((edge_count, width), bf16),

time: 51.3 us -> 35.9 us (0.70)
  waiting for transfers between devices: 17.4 us -> 3.64 us
  Pallas kernels: 21.3 us -> 18.4 us
  starting transfers between devices: 11.6 us -> 12.8 us
    all_to_all x1, waiting for transfers between devices: 8.33 us -> 0.77 us  [exchange_halves(): lax.all_to_all(blocks, ('region', 'feat'), split_axis=0, concat_axis=0, t...]
    ppermute x3, waiting for transfers between devices: 7.21 us -> 0.16 us  [from_feats(): lax.ppermute(weight, 'feat', [(at, (at + shift) % feats) for at in range(...]
    pallas_call x1, Pallas kernels: 12.4 us -> 9.51 us  [shards(): pl.pallas_call(functools.partial(edge_kernel, pieces_count, len(got), par...]
    ppermute x3, starting transfers between devices: 4.06 us -> 6.26 us  [from_feats(): lax.ppermute(weight, 'feat', [(at, (at + shift) % feats) for at in range(...]
    all_to_all x1, starting transfers between devices: 6.05 us -> 4.88 us  [exchange_halves(): lax.all_to_all(blocks, ('region', 'feat'), split_axis=0, concat_axis=0, t...]
    ppermute x7, waiting for transfers between devices: 0.62 us -> 1.46 us  [from_subs(): lax.ppermute(piece, 'sub', [(at, (at + turn) % subs) for at in range(subs)])]
  transfers between devices with their start and end apart: 12 -> 12, of which waited for: 4 -> 5; matrix products, arithmetic and copies ran while one was open for 0% -> 0% of each run, Pallas kernels for 38% -> 46%
where the time goes in v8:
time: 35.9 us; the launch traced here: 35.7 us
  Pallas kernels  18.4 us (51%)
  starting transfers between devices  12.8 us (36%)
  waiting for transfers between devices  3.64 us (10%)
  between operations  0.75 us (2%)
    pallas_call x1, Pallas kernels, shards(): pl.pallas_call(functools.partial(edge_kernel, pieces_count, len(got), par...  9.51 us
    ppermute x3, starting transfers between devices, from_feats(): lax.ppermute(weight, 'feat', [(at, (at + shift) % feats) for at in range(...  6.26 us
    all_to_all x1, starting transfers between devices, exchange_halves(): lax.all_to_all(blocks, ('region', 'feat'), split_axis=0, concat_axis=0, t...  4.88 us
    pallas_call x1, Pallas kernels, shards(): pl.pallas_call(functools.partial(gather_kernel, node_count, near_cap, far...  4.85 us
    pallas_call x1, Pallas kernels, exchange_halves(): pl.pallas_call(functools.partial(pick_kernel, part_count, near_cap, far_c...  2.08 us
    pallas_call x1, Pallas kernels, shards(): pl.pallas_call(functools.partial(node_kernel, pieces_count), out_shape=ja...  2.01 us
    ppermute x7, waiting for transfers between devices, from_subs(): lax.ppermute(piece, 'sub', [(at, (at + turn) % subs) for at in range(subs)])  1.46 us
    ppermute x1, waiting for transfers between devices, shards(): lax.ppermute(partial_sums, 'sub', [(at, (at + 1) % subs) for at in range(...  1.26 us
  transfers between devices with their start and end apart: 12, of which 5 were waited for; matrix products, arithmetic and copies ran while one was open for 0% of the time, Pallas kernels for 46%

profile of v8, /device:TPU:0, one launch (start us, length us, event | category | flops | bytes accessed | tf_op | source)
XLA Modules:
  0.0 35.7 jit_solution(8561869256702397323)
XLA Ops:
  0.6 0.0 copy-start.6
  0.6 3.0 %collective-permute-start = (bf16[3,128,512]{2,1,0:T(8,128)(2,1)}, bf16[3,128,512]{2,1,0:T(8,128)(2,1)S(1)}, u32[]{:S(2)}, u32[]{:S(2)}) collective-permute-start(bf16[3,128,512]{2,1,0:T(8,128)(2,1)} %refs_5_.1), channel_id=1, source_target_pairs={{0,2},{2,0},{1,3},{3,1},{4,6},{6,4},{5,7},{7,5},{8,10},{10,8},{9,1... | collective-permute-start | bytes 1179656 | tf_op jit(solution)/shard_map/ppermute | solution.py:210
  3.6 2.1 %pick_halo.1 = bf16[8,17,512]{2,1,0:T(8,128)(2,1)} custom-call(s32[1,2,8]{2,1,0:T(2,128)} %bitcast.18, s32[1,4,32]{2,1,0:T(4,128)} %near_ref.1, bf16[384,512]{1,0:T(8,128)(2,1)} %refs_0_.3), custom_call_target="tpu_custom_call" | custom-call | tf_op jit(solution)/shard_map/pick_halo/pallas_call | solution.py:97
  5.7 4.9 %all-to-all-start = ((bf16[8,17,512]{2,1,0:T(8,128)(2,1)}), bf16[8,17,512]{2,1,0:T(8,128)(2,1)S(1)}, u32[]{:S(2)}, u32[]{:S(2)}) async-start(bf16[8,17,512]{2,1,0:T(8,128)(2,1)} %pick_halo.1), calls=%async_computation | async-start | bytes 393216 | tf_op jit(solution)/shard_map/all_to_all | solution.py:107
  10.6 2.0 %collective-permute-start.1 = (bf16[128,512]{1,0:T(8,128)(2,1)}, bf16[128,512]{1,0:T(8,128)(2,1)S(1)}, u32[]{:S(2)}, u32[]{:S(2)}) collective-permute-start(bf16[128,512]{1,0:T(8,128)(2,1)} %refs_9_.1), channel_id=1, source_target_pairs={{0,2},{2,0},{1,3},{3,1},{4,6},{6,4},{5,7},{7,5},{8,10},{10,8},{9,1... | collective-permute-start | bytes 393224 | tf_op jit(solution)/shard_map/ppermute | solution.py:210
  12.6 4.8 %gather_latents.1 = (bf16[1536,1280]{1,0:T(8,128)(2,1)}, bf16[3,128,512]{2,1,0:T(8,128)(2,1)}) custom-call(s32[12,128]{1,0:T(8,128)} %bitcast.15, s32[12,128]{1,0:T(8,128)} %bitcast.16, bf16[384,512]{1,0:T(8,128)(2,1)} %refs_0_.3, bf16[2,128,512]{2,1,0:T(8,128)(2,1)} %node_in_ref.1, bf16[128,512]{1,0:T(8,128)(2,1)} %node_out_ref.1), custom_call_target="tpu_custom_call" | custom-call | tf_op jit(solution)/shard_map/gather_latents/pallas_call | solution.py:392
  17.5 0.2 collective-permute-done.1.refs_11_
  17.6 0.8 %all-to-all-done.refs_3_ = bf16[8,17,512]{2,1,0:T(8,128)(2,1)S(1)} async-done(((bf16[8,17,512]{2,1,0:T(8,128)(2,1)}), bf16[8,17,512]{2,1,0:T(8,128)(2,1)S(1)}, u32[]{:S(2)}, u32[]{:S(2)}) %all-to-all-start) | async-done | bytes 139296 | tf_op jit(solution)/shard_map/all_to_all | solution.py:107
  18.4 0.5 %collective-permute-start.5 = (bf16[128,512]{1,0:T(8,128)(2,1)S(1)}, bf16[128,512]{1,0:T(8,128)(2,1)S(1)}, u32[]{:S(2)}, u32[]{:S(2)}) collective-permute-start(bf16[128,512]{1,0:T(8,128)(2,1)S(1)} %copy-done.6), channel_id=1, source_target_pairs={{0,1},{1,0},{2,3},{3,2},{4,5},{5,4},{6,7},{7,6},{8,9},{9,8},{10,11... | collective-permute-start | bytes 393224 | tf_op jit(solution)/shard_map/ppermute | solution.py:218
  18.9 0.1 collective-permute-start.2
  19.0 0.4 %collective-permute-start.6 = (bf16[128,512]{1,0:T(8,128)(2,1)S(1)}, bf16[128,512]{1,0:T(8,128)(2,1)S(1)}, u32[]{:S(2)}, u32[]{:S(2)}) collective-permute-start(bf16[128,512]{1,0:T(8,128)(2,1)S(1)} %collective-permute-done.1.refs_11_), channel_id=1, source_target_pairs={{0,1},{1,0},{2,3},{3,2},{4,5},{5,4},{6,7},{7,6},{8,9},{9,8},{10,11... | collective-permute-start | bytes 393224 | tf_op jit(solution)/shard_map/ppermute | solution.py:218
  19.4 0.9 %collective-permute-done.5.refs_10_ = bf16[128,512]{1,0:T(8,128)(2,1)S(1)} collective-permute-done((bf16[128,512]{1,0:T(8,128)(2,1)S(1)}, bf16[128,512]{1,0:T(8,128)(2,1)S(1)}, u32[]{:S(2)}, u32[]{:S(2)}) %collective-permute-start.5) | collective-permute-done | bytes 131104 | tf_op jit(solution)/shard_map/ppermute | solution.py:218
  20.3 1.2 %collective-permute-start.9 = (bf16[3,128,512]{2,1,0:T(8,128)(2,1)}, bf16[3,128,512]{2,1,0:T(8,128)(2,1)S(1)}, u32[]{:S(2)}, u32[]{:S(2)}) collective-permute-start(bf16[3,128,512]{2,1,0:T(8,128)(2,1)} %get-tuple-element.19.refs_3_), channel_id=1, source_target_pairs={{0,2},{2,0},{1,3},{3,1},{4,6},{6,4},{5,7},{7,5},{8,10},{10,8},{9,1... | collective-permute-start | bytes 1179656 | tf_op jit(solution)/shard_map/ppermute | solution.py:210
  21.6 0.0 copy-start
  21.6 0.0 copy-start.1
  21.6 0.0 copy-start.2
  21.6 0.0 copy-start.3
  21.6 0.0 copy-start.5
  21.7 9.5 %edge_update.1 = (bf16[1536,512]{1,0:T(8,128)(2,1)}, bf16[384,512]{1,0:T(8,128)(2,1)S(1)}) custom-call(bf16[1536,512]{1,0:T(8,128)(2,1)} %refs_0_.2, bf16[1536,1280]{1,0:T(8,128)(2,1)} %get-tuple-element.13.refs_1_, s32[12,128]{1,0:T(8,128)} %bitcast.17, bf16[8,17,512]{2,1,0:T(8,128)(2,1)S(1)} %all-to-all-done.refs_3_, ...), custom_call_target="tpu_custom_call" | custom-call | flops 3825205248 | bytes 6291456 | tf_op jit(solution)/shard_map/edge_update/pallas_call | solution.py:445
  31.2 0.6 %collective-permute-start.7 = (bf16[384,512]{1,0:T(8,128)(2,1)S(1)}, bf16[384,512]{1,0:T(8,128)(2,1)S(1)}, u32[]{:S(2)}, u32[]{:S(2)}) collective-permute-start(bf16[384,512]{1,0:T(8,128)(2,1)S(1)} %get-tuple-element.18.refs_1_), channel_id=1, source_target_pairs={{0,1},{1,0},{2,3},{3,2},{4,5},{5,4},{6,7},{7,6},{8,9},{9,8},{10,11... | collective-permute-start | bytes 1179656 | tf_op jit(solution)/shard_map/ppermute | solution.py:476
  31.7 0.1 collective-permute-start.10
  31.8 1.3 %collective-permute-done.7.refs_2_ = bf16[384,512]{1,0:T(8,128)(2,1)S(1)} collective-permute-done((bf16[384,512]{1,0:T(8,128)(2,1)S(1)}, bf16[384,512]{1,0:T(8,128)(2,1)S(1)}, u32[]{:S(2)}, u32[]{:S(2)}) %collective-permute-start.7) | collective-permute-done | bytes 393248 | tf_op jit(solution)/shard_map/ppermute | solution.py:476
  33.1 0.6 %collective-permute-done.10.refs_6_ = bf16[3,128,512]{2,1,0:T(8,128)(2,1)S(1)} collective-permute-done((bf16[3,128,512]{2,1,0:T(8,128)(2,1)S(1)}, bf16[3,128,512]{2,1,0:T(8,128)(2,1)S(1)}, u32[]{:S(2)}, u32[]{:S(2)}) %collective-permute-start.10) | collective-permute-done | bytes 393248 | tf_op jit(solution)/shard_map/ppermute | solution.py:218
  33.7 2.0 %node_update.1 = bf16[384,512]{1,0:T(8,128)(2,1)} custom-call(bf16[384,512]{1,0:T(8,128)(2,1)S(1)} %copy-done, bf16[384,512]{1,0:T(8,128)(2,1)S(1)} %get-tuple-element.18.refs_1_, bf16[384,512]{1,0:T(8,128)(2,1)S(1)} %collective-permute-done.7.refs_2_, bf16[3,128,512]{2,1,0:T(8,128)(2,1)S(1)} %copy-done.1, ...), custom_call_target="tpu_custom_call" | custom-call | flops 603979776 | bytes 1966080 | tf_op jit(solution)/shard_map/node_update/pallas_call | solution.py:479
  (18 shorter events, 0.0 us)
Async XLA Ops:
  0.6 17.8 %copy-start.6 = (bf16[128,512]{1,0:T(8,128)(2,1)S(1)}, bf16[128,512]{1,0:T(8,128)(2,1)}, u32[]{:S(2)}) copy-start(bf16[128,512]{1,0:T(8,128)(2,1)} %refs_9_.1) | copy-start | bytes 393220
  0.6 17.8 %collective-permute-start = (bf16[3,128,512]{2,1,0:T(8,128)(2,1)}, bf16[3,128,512]{2,1,0:T(8,128)(2,1)S(1)}, u32[]{:S(2)}, u32[]{:S(2)}) collective-permute-start(bf16[3,128,512]{2,1,0:T(8,128)(2,1)} %refs_5_.1), channel_id=1, source_target_pairs={{0,2},{2,0},{1,3},{3,1},{4,6},{6,4},{5,7},{7,5},{8,10},{10,8},{9,1... | collective-permute-start | bytes 1179656 | tf_op jit(solution)/shard_map/ppermute | solution.py:210
  5.7 12.7 %all-to-all-start = ((bf16[8,17,512]{2,1,0:T(8,128)(2,1)}), bf16[8,17,512]{2,1,0:T(8,128)(2,1)S(1)}, u32[]{:S(2)}, u32[]{:S(2)}) async-start(bf16[8,17,512]{2,1,0:T(8,128)(2,1)} %pick_halo.1), calls=%async_computation | async-start | bytes 393216 | tf_op jit(solution)/shard_map/all_to_all | solution.py:107
  10.6 7.0 %collective-permute-start.1 = (bf16[128,512]{1,0:T(8,128)(2,1)}, bf16[128,512]{1,0:T(8,128)(2,1)S(1)}, u32[]{:S(2)}, u32[]{:S(2)}) collective-permute-start(bf16[128,512]{1,0:T(8,128)(2,1)} %refs_9_.1), channel_id=1, source_target_pairs={{0,2},{2,0},{1,3},{3,1},{4,6},{6,4},{5,7},{7,5},{8,10},{10,8},{9,1... | collective-permute-start | bytes 393224 | tf_op jit(solution)/shard_map/ppermute | solution.py:210
  12.6 8.9 %collective-permute-start.3 = (bf16[3,128,512]{2,1,0:T(8,128)(2,1)}, bf16[3,128,512]{2,1,0:T(8,128)(2,1)S(1)}, u32[]{:S(2)}, u32[]{:S(2)}) collective-permute-start(bf16[3,128,512]{2,1,0:T(8,128)(2,1)} %refs_5_.1), channel_id=1, source_target_pairs={{0,1},{1,0},{2,3},{3,2},{4,5},{5,4},{6,7},{7,6},{8,9},{9,8},{10,11... | collective-permute-start | bytes 1179656 | tf_op jit(solution)/shard_map/ppermute | solution.py:218
  18.4 3.2 %collective-permute-start.4 = (bf16[3,128,512]{2,1,0:T(8,128)(2,1)S(1)}, bf16[3,128,512]{2,1,0:T(8,128)(2,1)S(1)}, u32[]{:S(2)}, u32[]{:S(2)}) collective-permute-start(bf16[3,128,512]{2,1,0:T(8,128)(2,1)S(1)} %collective-permute-done.refs_7_), channel_id=1, source_target_pairs={{0,1},{1,0},{2,3},{3,2},{4,5},{5,4},{6,7},{7,6},{8,9},{9,8},{10,11... | collective-permute-start | bytes 1179656 | tf_op jit(solution)/shard_map/ppermute | solution.py:218
  18.4 1.9 %collective-permute-start.5 = (bf16[128,512]{1,0:T(8,128)(2,1)S(1)}, bf16[128,512]{1,0:T(8,128)(2,1)S(1)}, u32[]{:S(2)}, u32[]{:S(2)}) collective-permute-start(bf16[128,512]{1,0:T(8,128)(2,1)S(1)} %copy-done.6), channel_id=1, source_target_pairs={{0,1},{1,0},{2,3},{3,2},{4,5},{5,4},{6,7},{7,6},{8,9},{9,8},{10,11... | collective-permute-start | bytes 393224 | tf_op jit(solution)/shard_map/ppermute | solution.py:218
  18.9 2.7 %collective-permute-start.2 = (bf16[8,17,512]{2,1,0:T(8,128)(2,1)S(1)}, bf16[8,17,512]{2,1,0:T(8,128)(2,1)S(1)}, u32[]{:S(2)}, u32[]{:S(2)}) collective-permute-start(bf16[8,17,512]{2,1,0:T(8,128)(2,1)S(1)} %all-to-all-done.refs_3_), channel_id=1, source_target_pairs={{0,1},{1,0},{2,3},{3,2},{4,5},{5,4},{6,7},{7,6},{8,9},{9,8},{10,11... | collective-permute-start | bytes 417800 | tf_op jit(solution)/shard_map/ppermute | solution.py:218
  19.0 2.6 %collective-permute-start.6 = (bf16[128,512]{1,0:T(8,128)(2,1)S(1)}, bf16[128,512]{1,0:T(8,128)(2,1)S(1)}, u32[]{:S(2)}, u32[]{:S(2)}) collective-permute-start(bf16[128,512]{1,0:T(8,128)(2,1)S(1)} %collective-permute-done.1.refs_11_), channel_id=1, source_target_pairs={{0,1},{1,0},{2,3},{3,2},{4,5},{5,4},{6,7},{7,6},{8,9},{9,8},{10,11... | collective-permute-start | bytes 393224 | tf_op jit(solution)/shard_map/ppermute | solution.py:218
  20.3 11.4 %collective-permute-start.9 = (bf16[3,128,512]{2,1,0:T(8,128)(2,1)}, bf16[3,128,512]{2,1,0:T(8,128)(2,1)S(1)}, u32[]{:S(2)}, u32[]{:S(2)}) collective-permute-start(bf16[3,128,512]{2,1,0:T(8,128)(2,1)} %get-tuple-element.19.refs_3_), channel_id=1, source_target_pairs={{0,2},{2,0},{1,3},{3,1},{4,6},{6,4},{5,7},{7,5},{8,10},{10,8},{9,1... | collective-permute-start | bytes 1179656 | tf_op jit(solution)/shard_map/ppermute | solution.py:210
  21.5 10.3 %collective-permute-start.8 = (bf16[3,128,512]{2,1,0:T(8,128)(2,1)}, bf16[3,128,512]{2,1,0:T(8,128)(2,1)S(1)}, u32[]{:S(2)}, u32[]{:S(2)}) collective-permute-start(bf16[3,128,512]{2,1,0:T(8,128)(2,1)} %get-tuple-element.19.refs_3_), channel_id=1, source_target_pairs={{0,1},{1,0},{2,3},{3,2},{4,5},{5,4},{6,7},{7,6},{8,9},{9,8},{10,11... | collective-permute-start | bytes 1179656 | tf_op jit(solution)/shard_map/ppermute | solution.py:218
  21.6 12.1 %copy-start = (bf16[384,512]{1,0:T(8,128)(2,1)S(1)}, bf16[384,512]{1,0:T(8,128)(2,1)}, u32[]{:S(2)}) copy-start(bf16[384,512]{1,0:T(8,128)(2,1)} %refs_0_.3) | copy-start | bytes 1179652
  21.6 12.1 %copy-start.1 = (bf16[3,128,512]{2,1,0:T(8,128)(2,1)S(1)}, bf16[3,128,512]{2,1,0:T(8,128)(2,1)}, u32[]{:S(2)}) copy-start(bf16[3,128,512]{2,1,0:T(8,128)(2,1)} %get-tuple-element.19.refs_3_) | copy-start | bytes 1179652
  21.6 12.0 %copy-start.2 = (f32[512]{0:T(512)S(1)}, f32[512]{0:T(512)}, u32[]{:S(2)}) copy-start(f32[512]{0:T(512)} %param.32) | copy-start | bytes 6148
  21.6 12.0 %copy-start.3 = (f32[512]{0:T(512)S(1)}, f32[512]{0:T(512)}, u32[]{:S(2)}) copy-start(f32[512]{0:T(512)} %param.33) | copy-start | bytes 6148
  21.6 12.0 %copy-start.4 = (f32[512]{0:T(512)S(1)}, f32[512]{0:T(512)}, u32[]{:S(2)}) copy-start(f32[512]{0:T(512)} %param.34) | copy-start | bytes 6148
  21.6 12.0 %copy-start.5 = (f32[512]{0:T(512)S(1)}, f32[512]{0:T(512)}, u32[]{:S(2)}) copy-start(f32[512]{0:T(512)} %param.35) | copy-start | bytes 6148
  31.2 1.9 %collective-permute-start.7 = (bf16[384,512]{1,0:T(8,128)(2,1)S(1)}, bf16[384,512]{1,0:T(8,128)(2,1)S(1)}, u32[]{:S(2)}, u32[]{:S(2)}) collective-permute-start(bf16[384,512]{1,0:T(8,128)(2,1)S(1)} %get-tuple-element.18.refs_1_), channel_id=1, source_target_pairs={{0,1},{1,0},{2,3},{3,2},{4,5},{5,4},{6,7},{7,6},{8,9},{9,8},{10,11... | collective-permute-start | bytes 1179656 | tf_op jit(solution)/shard_map/ppermute | solution.py:476
  31.7 1.9 %collective-permute-start.10 = (bf16[3,128,512]{2,1,0:T(8,128)(2,1)S(1)}, bf16[3,128,512]{2,1,0:T(8,128)(2,1)S(1)}, u32[]{:S(2)}, u32[]{:S(2)}) collective-permute-start(bf16[3,128,512]{2,1,0:T(8,128)(2,1)S(1)} %collective-permute-done.9.refs_5_), channel_id=1, source_target_pairs={{0,1},{1,0},{2,3},{3,2},{4,5},{5,4},{6,7},{7,6},{8,9},{9,8},{10,11... | collective-permute-start | bytes 1179656 | tf_op jit(solution)/shard_map/ppermute | solution.py:218

commit v9 on v8

--- a/solution.py
+++ b/solution.py
@@ -12,9 +12,11 @@
 lanes = 128
 few_parts = 8
 grant = 32 << 20
+chunk_rows = 64
 bf16 = jnp.bfloat16
 f32 = jnp.float32
 vmem = pl.BlockSpec(memory_space=pltpu.VMEM)
+hbm = pl.BlockSpec(memory_space=pltpu.HBM)
 
 
 def in_hbm(array):
@@ -121,45 +123,56 @@
 
 
 def gather_kernel(
-    node_count,
     near_cap,
     far_cap,
     halved,
-    halo_space,
+    block,
     source_ref,
     receiver_ref,
     latent_ref,
     node_in_ref,
     node_out_ref,
-    out_ref,
+    edge_hbm,
+    known,
+    to_node,
     pack_ref,
+    sem,
 ):
-    width = latent_ref.shape[1]
-    halo_start = 2 * width
+    node_count, width = latent_ref.shape
+    edge_count = known.shape[0]
+    copy = pltpu.make_async_copy(edge_hbm, known.at[:, pl.ds(0, width)], sem)
+    copy.start()
     count = node_in_ref.shape[0]
-
-    @pl.when(pl.program_id(0) == 0)
-    def _():
-        pack_ref[:count] = node_in_ref[...]
-        pack_ref[count] = node_out_ref[...]
-
-    index_rows = out_ref.shape[0] // lanes
-    here = pl.ds(pl.program_id(0) * index_rows, index_rows)
-    source = source_ref[here]
-    if halved:
-        far = source - (node_count + len(near_offsets) * near_cap)
-        slot = lax.rem(far, far_cap)
-        turned = wrap(slot - lax.axis_index("sub"), far_cap)
-        source = jnp.where(far >= 0, source - slot + turned, source)
-    columns = as_columns(source)
+    pack_ref[:count] = node_in_ref[...]
+    pack_ref[count] = node_out_ref[...]
     latent = latent_ref[...]
-    sent = one_hot(columns, node_count)
-    out_ref[:, :width] = jnp.dot(sent, latent, preferred_element_type=f32).astype(bf16)
-    received = one_hot(as_columns(receiver_ref[here]), node_count)
-    out_ref[:, width:halo_start] = jnp.dot(
-        received, latent, preferred_element_type=f32
-    ).astype(bf16)
-    out_ref[:, halo_start:] = one_hot(columns - node_count, halo_space)
+    index_rows = block // lanes
+    node_place = lax.broadcasted_iota(jnp.int32, (node_count, lanes), 0)
+    for at in range(edge_count // block):
+        spot = slice(at * block, (at + 1) * block)
+        here = slice(at * index_rows, (at + 1) * index_rows)
+        source, receiver = source_ref[here], receiver_ref[here]
+        if halved:
+            far = source - (node_count + len(near_offsets) * near_cap)
+            slot = lax.rem(far, far_cap)
+            turned = wrap(slot - lax.axis_index("sub"), far_cap)
+            source = jnp.where(far >= 0, source - slot + turned, source)
+        columns = as_columns(source)
+        sent = one_hot(columns, node_count)
+        known[spot, width : 2 * width] = jnp.dot(
+            sent, latent, preferred_element_type=f32
+        ).astype(bf16)
+        received = one_hot(as_columns(receiver), node_count)
+        known[spot, 2 * width : 3 * width] = jnp.dot(
+            received, latent, preferred_element_type=f32
+        ).astype(bf16)
+        known[spot, 3 * width :] = one_hot(columns - node_count, known.shape[1] - 3 * width)
+        for row in range(index_rows):
+            start = at * block + row * lanes
+            to_node[:, start : start + lanes] = jnp.where(
+                node_place == receiver[row : row + 1], 1.0, 0.0
+            ).astype(bf16)
+    copy.wait()
 
 
 def place_halo(halo, part_count, near_cap, halved, got):
@@ -222,16 +235,16 @@
 
 
 def edge_kernel(pieces_count, got_count, part_count, near_cap, halved, block, *refs):
-    edge_hbm, gathered_hbm, receiver_hbm = refs[:3]
-    got_refs = refs[3 : 3 + got_count]
-    refs = refs[3 + got_count :]
+    known, to_node = refs[:2]
+    got_refs = refs[2 : 2 + got_count]
+    refs = refs[2 + got_count :]
     in_pieces, out_pieces = refs[:pieces_count], refs[pieces_count : 2 * pieces_count]
     row_refs = refs[2 * pieces_count : 2 * pieces_count + 4]
     new_hbm, sum_ref = refs[2 * pieces_count + 4 : 2 * pieces_count + 6]
-    known, in_weight, out_weight, halo, receiver_ref, rows, new_ref, total, sems = refs[
+    in_weight, out_weight, halo, rows, preact, hidden, output, new_ref, total, sems = refs[
         2 * pieces_count + 6 :
     ]
-    edge_count, width = edge_hbm.shape
+    edge_count, width = new_hbm.shape
     blocks = edge_count // block
     taken = []
 
@@ -242,31 +255,17 @@
         return copy
 
     order = owners()
-    first, later, last = [], [], []
+    first, later = [], []
     for which in (1, 0, 2):
         count = in_pieces[0].shape[1]
         spot = pl.ds(pl.multiple_of(which * width + order[0] * count, count), count)
         target = first if which == 1 else later
         target.append(start(in_pieces[0].at[which], in_weight.at[spot]))
-    known_copies = []
-    for at in range(blocks):
-        spot = pl.ds(at * block, block)
-        known_copies.append(
-            [
-                start(edge_hbm.at[spot], known.at[spot, pl.ds(0, width)]),
-                start(
-                    gathered_hbm.at[spot],
-                    known.at[spot, pl.ds(width, known.shape[1] - width)],
-                ),
-            ]
-        )
-        if at == 0:
-            for row_ref, row in zip(row_refs, rows):
-                last.append(start(row_ref, row))
-            count = out_pieces[0].shape[0]
-            spot = pl.ds(pl.multiple_of(order[0] * count, count), count)
-            last.append(start(out_pieces[0], out_weight.at[spot]))
-            last.append(start(receiver_hbm, receiver_ref))
+    for row_ref, row in zip(row_refs, rows):
+        later.append(start(row_ref, row))
+    count = out_pieces[0].shape[0]
+    spot = pl.ds(pl.multiple_of(order[0] * count, count), count)
+    later.append(start(out_pieces[0], out_weight.at[spot]))
     in_bias, out_bias, gain, offset = rows
 
     place_halo(halo, part_count, near_cap, halved, got_refs)
@@ -283,40 +282,54 @@
     for copy in later:
         copy.wait()
 
-    def first_dot(at):
-        for copy in known_copies[at]:
-            copy.wait()
-        return jnp.dot(
+    def in_dot(at):
+        preact[at][...] = jnp.dot(
             known[at * block : (at + 1) * block], in_weight[...], preferred_element_type=f32
         )
 
-    preact = first_dot(0)
-    for copy in last:
-        copy.wait()
-    out_copies = []
-    for at in range(blocks):
+    def activate(at):
+        for start_row in range(0, block, chunk_rows):
+            here = slice(start_row, start_row + chunk_rows)
+            hidden[at][here] = silu(preact[at][here] + in_bias[...]).astype(bf16)
+
+    def out_dot(at):
+        output[at][...] = jnp.dot(
+            hidden[at][...], out_weight[...], preferred_element_type=f32
+        )
+
+    def normalise(at):
+        for start_row in range(0, block, chunk_rows):
+            here = slice(start_row, start_row + chunk_rows)
+            there = slice(at * block + start_row, at * block + start_row + chunk_rows)
+            normed = layer_norm(output[at][here] + out_bias[...], gain[...], offset[...])
+            new_ref[there] = (known[there, :width].astype(f32) + normed).astype(bf16)
         spot = pl.ds(at * block, block)
-        following = first_dot(at + 1) if at + 1 < blocks else None
-        hidden = silu(preact + in_bias[...]).astype(bf16)
-        output = jnp.dot(hidden, out_weight[...], preferred_element_type=f32) + out_bias[...]
-        edges = known[spot, :width].astype(f32)
-        edge_new = (edges + layer_norm(output, gain[...], offset[...])).astype(bf16)
-        new_ref[spot] = edge_new
-        out_copies.append(start(new_ref.at[spot], new_hbm.at[spot]))
-        index_rows = block // lanes
-        receiver = jnp.concatenate(
-            [receiver_ref[at * index_rows + row][None] for row in range(index_rows)], axis=1
-        )
-        node_place = lax.broadcasted_iota(jnp.int32, (total.shape[0], block), 0)
-        hot = jnp.where(node_place == receiver, 1.0, 0.0).astype(bf16)
-        part = jnp.dot(hot, edge_new, preferred_element_type=f32)
+        taken.append(None)
+        copy = pltpu.make_async_copy(new_ref.at[spot], new_hbm.at[spot], sems.at[len(taken) - 1])
+        copy.start()
+        return copy
+
+    def sum_dot(at):
+        spot = slice(at * block, (at + 1) * block)
+        part = jnp.dot(to_node[:, spot], new_ref[spot], preferred_element_type=f32)
         if at > 0:
             part += total[...]
         if at + 1 < blocks:
             total[...] = part
         else:
             sum_ref[...] = part.astype(bf16)
-        preact = following
+
+    out_copies = []
+    in_dot(0)
+    for at in range(blocks):
+        if at + 1 < blocks:
+            in_dot(at + 1)
+        activate(at)
+        out_dot(at)
+        if at > 0:
+            sum_dot(at - 1)
+        out_copies.append(normalise(at))
+    sum_dot(blocks - 1)
     for copy in out_copies:
         copy.wait()
 
@@ -383,29 +396,18 @@
     source_rows = in_hbm(edge_source.reshape(-1, lanes))
     receiver_rows = in_hbm(receivers.reshape(-1, lanes))
 
-    def whole(array):
-        return pl.BlockSpec(array.shape, lambda step: (0,) * array.ndim)
-
     pack_shape = (node_in_weight.shape[0] + 1,) + node_out_weight.shape
-    gathered_width = 2 * width + halo_space
-    gather_block = edge_count // 3
-    gathered, node_weight = pl.pallas_call(
-        functools.partial(
-            gather_kernel, node_count, near_cap, far_cap, halved, halo_space
-        ),
-        grid=(edge_count // gather_block,),
+    known_width = 3 * width + halo_space
+    known, to_node, node_weight = pl.pallas_call(
+        functools.partial(gather_kernel, near_cap, far_cap, halved, 512),
         out_shape=[
-            pltpu.HBM((edge_count, gathered_width), bf16),
-            pltpu.HBM(pack_shape, bf16),
+            pltpu.VMEM((edge_count, known_width), bf16),
+            pltpu.VMEM((node_count, edge_count), bf16),
+            pltpu.VMEM(pack_shape, bf16),
         ],
-        in_specs=[
-            whole(array)
-            for array in (source_rows, receiver_rows, node_latent, node_in_weight, node_out_weight)
-        ],
-        out_specs=[
-            pl.BlockSpec((gather_block, gathered_width), lambda step: (step, 0)),
-            pl.BlockSpec(pack_shape, lambda step: (0, 0, 0)),
-        ],
+        in_specs=[vmem] * 5 + [hbm],
+        out_specs=[vmem] * 3,
+        scratch_shapes=[pltpu.SemaphoreType.DMA],
         compiler_params=pltpu.CompilerParams(vmem_limit_bytes=grant),
         cost_estimate=pl.CostEstimate(flops=0, bytes_accessed=0, transcendentals=0),
         name="gather_latents",
@@ -415,10 +417,11 @@
         in_hbm(node_latent),
         in_hbm(node_in_weight),
         in_hbm(node_out_weight),
+        in_hbm(edge_latent),
     )
 
-    far_edge, got, gathered, node_weight = lax.optimization_barrier(
-        (far_edge, got, gathered, node_weight)
+    far_edge, got, known, to_node, node_weight = lax.optimization_barrier(
+        (far_edge, got, known, to_node, node_weight)
     )
     if halved:
         got = got + from_subs(got)
@@ -431,17 +434,14 @@
     pieces_count = len(edge_in)
 
     rows = [value.reshape(1, -1) for value in (edge_in_bias, edge_out_bias, edge_gain, edge_offset)]
-    hbm = pl.BlockSpec(memory_space=pltpu.HBM)
-    edge_operands = [in_hbm(edge_latent), in_hbm(gathered), in_hbm(receivers.reshape(-1, lanes))]
-    edge_operands += [in_vmem(blocks) for blocks in got]
-    edge_specs = [hbm] * 3 + [vmem] * len(got)
+    edge_operands = [in_vmem(known), in_vmem(to_node)] + [in_vmem(blocks) for blocks in got]
+    edge_specs = [vmem] * len(edge_operands)
     for pieces in (edge_in, edge_out):
         edge_operands += [in_hbm(pieces[0])] + [in_vmem(piece) for piece in pieces[1:]]
         edge_specs += [hbm] + [vmem] * (pieces_count - 1)
     edge_operands += [in_hbm(row) for row in rows]
     edge_specs += [hbm] * len(rows)
-    known_width = 3 * width + halo_space
-    copy_count = 3 + 3 * steps + 4 + 1 + 1
+    copy_count = 3 + 4 + 1 + steps
     edge_new, partial_sums = pl.pallas_call(
         functools.partial(
             edge_kernel, pieces_count, len(got), part_count, near_cap, halved, block
@@ -453,12 +453,13 @@
         in_specs=edge_specs,
         out_specs=[hbm, vmem],
         scratch_shapes=[
-            pltpu.VMEM((edge_count, known_width), bf16),
             pltpu.VMEM((known_width, width), bf16),
             pltpu.VMEM((width, width), bf16),
             pltpu.VMEM((halo_space, width), bf16),
-            pltpu.VMEM((edge_count // lanes, lanes), jnp.int32),
             [pltpu.VMEM((1, width), f32)] * 4,
+            [pltpu.VMEM((block, width), f32)] * steps,
+            [pltpu.VMEM((block, width), bf16)] * steps,
+            [pltpu.VMEM((block, width), f32)] * steps,
             pltpu.VMEM((edge_count, width), bf16),
             pltpu.VMEM((node_count, width), f32),
             pltpu.SemaphoreType.DMA((copy_count,)),

time: 35.9 us -> 36.2 us (level)
  local copies, waits for them, and re-layouts: 0.04 us -> 4.97 us
  Pallas kernels: 18.4 us -> 14.6 us
  waiting for transfers between devices: 3.64 us -> 2.82 us
    unnamed x14 -> x16, local copies, waits for them, and re-layouts: 0.04 us -> 4.97 us
    pallas_call x1, Pallas kernels: 9.51 us -> 7.21 us  [shards(): pl.pallas_call(functools.partial(edge_kernel, pieces_count, len(got), par...]
    pallas_call x1, Pallas kernels: 4.85 us -> 3.31 us  [shards(): pl.pallas_call(functools.partial(gather_kernel, near_cap, far_cap, halved...]
    all_to_all x1, waiting for transfers between devices: 0.77 us -> 0.04 us  [exchange_halves(): lax.all_to_all(blocks, ('region', 'feat'), split_axis=0, concat_axis=0, t...]
  transfers between devices with their start and end apart: 12 -> 12, of which waited for: 5 -> 3; matrix products, arithmetic and copies ran while one was open for 0% -> 0% of each run, Pallas kernels for 46% -> 35%
where the time goes in v9:
time: 36.2 us; the launch traced here: 35.9 us
  Pallas kernels  14.6 us (40%)
  starting transfers between devices  12.7 us (35%)
  local copies, waits for them, and re-layouts  4.97 us (14%)
  waiting for transfers between devices  2.82 us (8%)
  between operations  0.72 us (2%)
    pallas_call x1, Pallas kernels, shards(): pl.pallas_call(functools.partial(edge_kernel, pieces_count, len(got), par...  7.21 us
    ppermute x3, starting transfers between devices, from_feats(): lax.ppermute(weight, 'feat', [(at, (at + shift) % feats) for at in range(...  6.07 us
    unnamed x16, local copies, waits for them, and re-layouts  4.97 us
    all_to_all x1, starting transfers between devices, exchange_halves(): lax.all_to_all(blocks, ('region', 'feat'), split_axis=0, concat_axis=0, t...  4.88 us
    pallas_call x1, Pallas kernels, shards(): pl.pallas_call(functools.partial(gather_kernel, near_cap, far_cap, halved...  3.31 us
    pallas_call x1, Pallas kernels, exchange_halves(): pl.pallas_call(functools.partial(pick_kernel, part_count, near_cap, far_c...  2.11 us
    pallas_call x1, Pallas kernels, shards(): pl.pallas_call(functools.partial(node_kernel, pieces_count), out_shape=ja...  2.01 us
    ppermute x7, waiting for transfers between devices, from_subs(): lax.ppermute(piece, 'sub', [(at, (at + turn) % subs) for at in range(subs)])  1.51 us
  transfers between devices with their start and end apart: 12, of which 3 were waited for; matrix products, arithmetic and copies ran while one was open for 0% of the time, Pallas kernels for 35%

profile of v9, /device:TPU:0, one launch (start us, length us, event | category | flops | bytes accessed | tf_op | source)
XLA Modules:
  0.0 35.9 jit_solution(14915009496182971451)
XLA Ops:
  0.6 3.0 %collective-permute-start = (bf16[3,128,512]{2,1,0:T(8,128)(2,1)}, bf16[3,128,512]{2,1,0:T(8,128)(2,1)S(1)}, u32[]{:S(2)}, u32[]{:S(2)}) collective-permute-start(bf16[3,128,512]{2,1,0:T(8,128)(2,1)} %refs_4_.1), channel_id=1, source_target_pairs={{0,2},{2,0},{1,3},{3,1},{4,6},{6,4},{5,7},{7,5},{8,10},{10,8},{9,1... | collective-permute-start | bytes 1179656 | tf_op jit(solution)/shard_map/ppermute | solution.py:223
  3.6 2.1 %pick_halo.1 = bf16[8,17,512]{2,1,0:T(8,128)(2,1)} custom-call(s32[1,2,8]{2,1,0:T(2,128)} %bitcast.17, s32[1,4,32]{2,1,0:T(4,128)} %near_ref.1, bf16[384,512]{1,0:T(8,128)(2,1)} %refs_0_.1), custom_call_target="tpu_custom_call" | custom-call | tf_op jit(solution)/shard_map/pick_halo/pallas_call | solution.py:99
  5.8 4.9 %all-to-all-start = ((bf16[8,17,512]{2,1,0:T(8,128)(2,1)}), bf16[8,17,512]{2,1,0:T(8,128)(2,1)S(1)}, u32[]{:S(2)}, u32[]{:S(2)}) async-start(bf16[8,17,512]{2,1,0:T(8,128)(2,1)} %pick_halo.1), calls=%async_computation | async-start | bytes 393216 | tf_op jit(solution)/shard_map/all_to_all | solution.py:109
  10.6 2.0 %collective-permute-start.1 = (bf16[128,512]{1,0:T(8,128)(2,1)}, bf16[128,512]{1,0:T(8,128)(2,1)S(1)}, u32[]{:S(2)}, u32[]{:S(2)}) collective-permute-start(bf16[128,512]{1,0:T(8,128)(2,1)} %refs_8_.1), channel_id=1, source_target_pairs={{0,2},{2,0},{1,3},{3,1},{4,6},{6,4},{5,7},{7,5},{8,10},{10,8},{9,1... | collective-permute-start | bytes 393224 | tf_op jit(solution)/shard_map/ppermute | solution.py:223
  12.7 3.3 %gather_latents.1 = (bf16[1536,1792]{1,0:T(8,128)(2,1)S(1)}, bf16[384,1536]{1,0:T(8,128)(2,1)S(1)}, bf16[3,128,512]{2,1,0:T(8,128)(2,1)S(1)}) custom-call(s32[12,128]{1,0:T(8,128)} %bitcast.15, s32[12,128]{1,0:T(8,128)} %bitcast.16, bf16[384,512]{1,0:T(8,128)(2,1)} %refs_0_.1, bf16[2,128,512]{2,1,0:T(8,128)(2,1)} %node_in_ref.1, ...), custom_call_target="tpu_custom_call" | custom-call | tf_op jit(solution)/shard_map/gather_latents/pallas_call | solution.py:401
  16.0 2.4 %copy-done.5 = bf16[1536,1792]{1,0:T(8,128)(2,1)} copy-done((bf16[1536,1792]{1,0:T(8,128)(2,1)}, bf16[1536,1792]{1,0:T(8,128)(2,1)S(1)}, u32[]{:S(2)}) %copy-start.5) | copy-done | bytes 5505048
  18.4 0.0 collective-permute-done.1.refs_10_
  18.4 0.0 all-to-all-done.refs_2_
  18.4 0.5 %collective-permute-start.4 = (bf16[3,128,512]{2,1,0:T(8,128)(2,1)S(1)}, bf16[3,128,512]{2,1,0:T(8,128)(2,1)S(1)}, u32[]{:S(2)}, u32[]{:S(2)}) collective-permute-start(bf16[3,128,512]{2,1,0:T(8,128)(2,1)S(1)} %collective-permute-done.refs_6_), channel_id=1, source_target_pairs={{0,1},{1,0},{2,3},{3,2},{4,5},{5,4},{6,7},{7,6},{8,9},{9,8},{10,11... | collective-permute-start | bytes 1179656 | tf_op jit(solution)/shard_map/ppermute | solution.py:231
  19.0 0.1 collective-permute-start.5
  19.0 0.4 %collective-permute-start.2 = (bf16[8,17,512]{2,1,0:T(8,128)(2,1)S(1)}, bf16[8,17,512]{2,1,0:T(8,128)(2,1)S(1)}, u32[]{:S(2)}, u32[]{:S(2)}) collective-permute-start(bf16[8,17,512]{2,1,0:T(8,128)(2,1)S(1)} %all-to-all-done.refs_2_), channel_id=1, source_target_pairs={{0,1},{1,0},{2,3},{3,2},{4,5},{5,4},{6,7},{7,6},{8,9},{9,8},{10,11... | collective-permute-start | bytes 417800 | tf_op jit(solution)/shard_map/ppermute | solution.py:231
  19.5 0.1 collective-permute-start.6
  19.6 0.9 %collective-permute-done.5.refs_9_ = bf16[128,512]{1,0:T(8,128)(2,1)S(1)} collective-permute-done((bf16[128,512]{1,0:T(8,128)(2,1)S(1)}, bf16[128,512]{1,0:T(8,128)(2,1)S(1)}, u32[]{:S(2)}, u32[]{:S(2)}) %collective-permute-start.5) | collective-permute-done | bytes 131104 | tf_op jit(solution)/shard_map/ppermute | solution.py:231
  20.5 1.0 %collective-permute-start.9 = (bf16[3,128,512]{2,1,0:T(8,128)(2,1)S(1)}, bf16[3,128,512]{2,1,0:T(8,128)(2,1)S(1)}, u32[]{:S(2)}, u32[]{:S(2)}) collective-permute-start(bf16[3,128,512]{2,1,0:T(8,128)(2,1)S(1)} %get-tuple-element.23.refs_3_), channel_id=1, source_target_pairs={{0,2},{2,0},{1,3},{3,1},{4,6},{6,4},{5,7},{7,5},{8,10},{10,8},{9,1... | collective-permute-start | bytes 1179656 | tf_op jit(solution)/shard_map/ppermute | solution.py:223
  21.5 0.0 collective-permute-done.3.refs_5_
  21.5 0.0 collective-permute-start.8
  21.6 2.6 %copy-done.6 = bf16[1536,1792]{1,0:T(8,128)(2,1)S(1)} copy-done((bf16[1536,1792]{1,0:T(8,128)(2,1)S(1)}, bf16[1536,1792]{1,0:T(8,128)(2,1)}, u32[]{:S(2)}) %copy-start.6) | copy-done | bytes 5505048
  24.1 0.0 copy-start.4
  24.2 7.2 %edge_update.1 = (bf16[1536,512]{1,0:T(8,128)(2,1)}, bf16[384,512]{1,0:T(8,128)(2,1)S(1)}) custom-call(bf16[1536,1792]{1,0:T(8,128)(2,1)S(1)} %copy-done.6, bf16[384,1536]{1,0:T(8,128)(2,1)S(1)} %get-tuple-element.17.refs_1_, bf16[8,17,512]{2,1,0:T(8,128)(2,1)S(1)} %all-to-all-done.refs_2_, bf16[8,17,512]{2,1,0:T(8,128)(2,1)S(1)} %collective-permute-done.2.refs_3_, ...), custom_call_target="tpu_custom_call" | custom-call | flops 3825205248 | bytes 6291456 | tf_op jit(solution)/shard_map/edge_update/pallas_call | solution.py:445
  31.4 0.6 %collective-permute-start.7 = (bf16[384,512]{1,0:T(8,128)(2,1)S(1)}, bf16[384,512]{1,0:T(8,128)(2,1)S(1)}, u32[]{:S(2)}, u32[]{:S(2)}) collective-permute-start(bf16[384,512]{1,0:T(8,128)(2,1)S(1)} %get-tuple-element.22.refs_1_), channel_id=1, source_target_pairs={{0,1},{1,0},{2,3},{3,2},{4,5},{5,4},{6,7},{7,6},{8,9},{9,8},{10,11... | collective-permute-start | bytes 1179656 | tf_op jit(solution)/shard_map/ppermute | solution.py:477
  31.9 0.1 collective-permute-start.10
  32.0 1.3 %collective-permute-done.7.refs_2_ = bf16[384,512]{1,0:T(8,128)(2,1)S(1)} collective-permute-done((bf16[384,512]{1,0:T(8,128)(2,1)S(1)}, bf16[384,512]{1,0:T(8,128)(2,1)S(1)}, u32[]{:S(2)}, u32[]{:S(2)}) %collective-permute-start.7) | collective-permute-done | bytes 393248 | tf_op jit(solution)/shard_map/ppermute | solution.py:477
  33.3 0.6 %collective-permute-done.10.refs_6_ = bf16[3,128,512]{2,1,0:T(8,128)(2,1)S(1)} collective-permute-done((bf16[3,128,512]{2,1,0:T(8,128)(2,1)S(1)}, bf16[3,128,512]{2,1,0:T(8,128)(2,1)S(1)}, u32[]{:S(2)}, u32[]{:S(2)}) %collective-permute-start.10) | collective-permute-done | bytes 393248 | tf_op jit(solution)/shard_map/ppermute | solution.py:231
  33.9 2.0 %node_update.1 = bf16[384,512]{1,0:T(8,128)(2,1)} custom-call(bf16[384,512]{1,0:T(8,128)(2,1)S(1)} %copy-done, bf16[384,512]{1,0:T(8,128)(2,1)S(1)} %get-tuple-element.22.refs_1_, bf16[384,512]{1,0:T(8,128)(2,1)S(1)} %collective-permute-done.7.refs_2_, bf16[3,128,512]{2,1,0:T(8,128)(2,1)S(1)} %get-tuple-element.23.refs_3_, ...), custom_call_target="tpu_custom_call" | custom-call | flops 603979776 | bytes 1966080 | tf_op jit(solution)/shard_map/node_update/pallas_call | solution.py:480
  (20 shorter events, 0.0 us)
Async XLA Ops:
  0.6 17.8 %collective-permute-start = (bf16[3,128,512]{2,1,0:T(8,128)(2,1)}, bf16[3,128,512]{2,1,0:T(8,128)(2,1)S(1)}, u32[]{:S(2)}, u32[]{:S(2)}) collective-permute-start(bf16[3,128,512]{2,1,0:T(8,128)(2,1)} %refs_4_.1), channel_id=1, source_target_pairs={{0,2},{2,0},{1,3},{3,1},{4,6},{6,4},{5,7},{7,5},{8,10},{10,8},{9,1... | collective-permute-start | bytes 1179656 | tf_op jit(solution)/shard_map/ppermute | solution.py:223
  3.6 15.3 %copy-start.7 = (bf16[128,512]{1,0:T(8,128)(2,1)S(1)}, bf16[128,512]{1,0:T(8,128)(2,1)}, u32[]{:S(2)}) copy-start(bf16[128,512]{1,0:T(8,128)(2,1)} %refs_8_.1) | copy-start | bytes 393220
  5.8 12.7 %all-to-all-start = ((bf16[8,17,512]{2,1,0:T(8,128)(2,1)}), bf16[8,17,512]{2,1,0:T(8,128)(2,1)S(1)}, u32[]{:S(2)}, u32[]{:S(2)}) async-start(bf16[8,17,512]{2,1,0:T(8,128)(2,1)} %pick_halo.1), calls=%async_computation | async-start | bytes 393216 | tf_op jit(solution)/shard_map/all_to_all | solution.py:109
  10.6 7.7 %collective-permute-start.1 = (bf16[128,512]{1,0:T(8,128)(2,1)}, bf16[128,512]{1,0:T(8,128)(2,1)S(1)}, u32[]{:S(2)}, u32[]{:S(2)}) collective-permute-start(bf16[128,512]{1,0:T(8,128)(2,1)} %refs_8_.1), channel_id=1, source_target_pairs={{0,2},{2,0},{1,3},{3,1},{4,6},{6,4},{5,7},{7,5},{8,10},{10,8},{9,1... | collective-permute-start | bytes 393224 | tf_op jit(solution)/shard_map/ppermute | solution.py:223
  12.7 8.9 %collective-permute-start.3 = (bf16[3,128,512]{2,1,0:T(8,128)(2,1)}, bf16[3,128,512]{2,1,0:T(8,128)(2,1)S(1)}, u32[]{:S(2)}, u32[]{:S(2)}) collective-permute-start(bf16[3,128,512]{2,1,0:T(8,128)(2,1)} %refs_4_.1), channel_id=1, source_target_pairs={{0,1},{1,0},{2,3},{3,2},{4,5},{5,4},{6,7},{7,6},{8,9},{9,8},{10,11... | collective-permute-start | bytes 1179656 | tf_op jit(solution)/shard_map/ppermute | solution.py:231
  16.0 2.4 %copy-start.5 = (bf16[1536,1792]{1,0:T(8,128)(2,1)}, bf16[1536,1792]{1,0:T(8,128)(2,1)S(1)}, u32[]{:S(2)}) copy-start(bf16[1536,1792]{1,0:T(8,128)(2,1)S(1)} %get-tuple-element.16.refs_0_) | copy-start | bytes 16515076
  18.4 3.1 %collective-permute-start.4 = (bf16[3,128,512]{2,1,0:T(8,128)(2,1)S(1)}, bf16[3,128,512]{2,1,0:T(8,128)(2,1)S(1)}, u32[]{:S(2)}, u32[]{:S(2)}) collective-permute-start(bf16[3,128,512]{2,1,0:T(8,128)(2,1)S(1)} %collective-permute-done.refs_6_), channel_id=1, source_target_pairs={{0,1},{1,0},{2,3},{3,2},{4,5},{5,4},{6,7},{7,6},{8,9},{9,8},{10,11... | collective-permute-start | bytes 1179656 | tf_op jit(solution)/shard_map/ppermute | solution.py:231
  19.0 1.5 %collective-permute-start.5 = (bf16[128,512]{1,0:T(8,128)(2,1)S(1)}, bf16[128,512]{1,0:T(8,128)(2,1)S(1)}, u32[]{:S(2)}, u32[]{:S(2)}) collective-permute-start(bf16[128,512]{1,0:T(8,128)(2,1)S(1)} %copy-done.7), channel_id=1, source_target_pairs={{0,1},{1,0},{2,3},{3,2},{4,5},{5,4},{6,7},{7,6},{8,9},{9,8},{10,11... | collective-permute-start | bytes 393224 | tf_op jit(solution)/shard_map/ppermute | solution.py:231
  19.0 2.5 %collective-permute-start.2 = (bf16[8,17,512]{2,1,0:T(8,128)(2,1)S(1)}, bf16[8,17,512]{2,1,0:T(8,128)(2,1)S(1)}, u32[]{:S(2)}, u32[]{:S(2)}) collective-permute-start(bf16[8,17,512]{2,1,0:T(8,128)(2,1)S(1)} %all-to-all-done.refs_2_), channel_id=1, source_target_pairs={{0,1},{1,0},{2,3},{3,2},{4,5},{5,4},{6,7},{7,6},{8,9},{9,8},{10,11... | collective-permute-start | bytes 417800 | tf_op jit(solution)/shard_map/ppermute | solution.py:231
  19.5 2.1 %collective-permute-start.6 = (bf16[128,512]{1,0:T(8,128)(2,1)S(1)}, bf16[128,512]{1,0:T(8,128)(2,1)S(1)}, u32[]{:S(2)}, u32[]{:S(2)}) collective-permute-start(bf16[128,512]{1,0:T(8,128)(2,1)S(1)} %collective-permute-done.1.refs_10_), channel_id=1, source_target_pairs={{0,1},{1,0},{2,3},{3,2},{4,5},{5,4},{6,7},{7,6},{8,9},{9,8},{10,11... | collective-permute-start | bytes 393224 | tf_op jit(solution)/shard_map/ppermute | solution.py:231
  20.5 11.4 %collective-permute-start.9 = (bf16[3,128,512]{2,1,0:T(8,128)(2,1)S(1)}, bf16[3,128,512]{2,1,0:T(8,128)(2,1)S(1)}, u32[]{:S(2)}, u32[]{:S(2)}) collective-permute-start(bf16[3,128,512]{2,1,0:T(8,128)(2,1)S(1)} %get-tuple-element.23.refs_3_), channel_id=1, source_target_pairs={{0,2},{2,0},{1,3},{3,1},{4,6},{6,4},{5,7},{7,5},{8,10},{10,8},{9,1... | collective-permute-start | bytes 1179656 | tf_op jit(solution)/shard_map/ppermute | solution.py:223
  21.5 10.5 %collective-permute-start.8 = (bf16[3,128,512]{2,1,0:T(8,128)(2,1)S(1)}, bf16[3,128,512]{2,1,0:T(8,128)(2,1)S(1)}, u32[]{:S(2)}, u32[]{:S(2)}) collective-permute-start(bf16[3,128,512]{2,1,0:T(8,128)(2,1)S(1)} %get-tuple-element.23.refs_3_), channel_id=1, source_target_pairs={{0,1},{1,0},{2,3},{3,2},{4,5},{5,4},{6,7},{7,6},{8,9},{9,8},{10,11... | collective-permute-start | bytes 1179656 | tf_op jit(solution)/shard_map/ppermute | solution.py:231
  21.6 2.6 %copy-start.6 = (bf16[1536,1792]{1,0:T(8,128)(2,1)S(1)}, bf16[1536,1792]{1,0:T(8,128)(2,1)}, u32[]{:S(2)}) copy-start(bf16[1536,1792]{1,0:T(8,128)(2,1)} %copy-done.5) | copy-start | bytes 16515076
  24.1 9.7 %copy-start = (bf16[384,512]{1,0:T(8,128)(2,1)S(1)}, bf16[384,512]{1,0:T(8,128)(2,1)}, u32[]{:S(2)}) copy-start(bf16[384,512]{1,0:T(8,128)(2,1)} %refs_0_.1) | copy-start | bytes 1179652
  24.1 9.7 %copy-start.1 = (f32[512]{0:T(512)S(1)}, f32[512]{0:T(512)}, u32[]{:S(2)}) copy-start(f32[512]{0:T(512)} %param.32) | copy-start | bytes 6148
  24.1 9.7 %copy-start.2 = (f32[512]{0:T(512)S(1)}, f32[512]{0:T(512)}, u32[]{:S(2)}) copy-start(f32[512]{0:T(512)} %param.33) | copy-start | bytes 6148
  24.1 9.7 %copy-start.3 = (f32[512]{0:T(512)S(1)}, f32[512]{0:T(512)}, u32[]{:S(2)}) copy-start(f32[512]{0:T(512)} %param.34) | copy-start | bytes 6148
  24.1 9.7 %copy-start.4 = (f32[512]{0:T(512)S(1)}, f32[512]{0:T(512)}, u32[]{:S(2)}) copy-start(f32[512]{0:T(512)} %param.35) | copy-start | bytes 6148
  31.4 1.9 %collective-permute-start.7 = (bf16[384,512]{1,0:T(8,128)(2,1)S(1)}, bf16[384,512]{1,0:T(8,128)(2,1)S(1)}, u32[]{:S(2)}, u32[]{:S(2)}) collective-permute-start(bf16[384,512]{1,0:T(8,128)(2,1)S(1)} %get-tuple-element.22.refs_1_), channel_id=1, source_target_pairs={{0,1},{1,0},{2,3},{3,2},{4,5},{5,4},{6,7},{7,6},{8,9},{9,8},{10,11... | collective-permute-start | bytes 1179656 | tf_op jit(solution)/shard_map/ppermute | solution.py:477
  31.9 1.9 %collective-permute-start.10 = (bf16[3,128,512]{2,1,0:T(8,128)(2,1)S(1)}, bf16[3,128,512]{2,1,0:T(8,128)(2,1)S(1)}, u32[]{:S(2)}, u32[]{:S(2)}) collective-permute-start(bf16[3,128,512]{2,1,0:T(8,128)(2,1)S(1)} %collective-permute-done.9.refs_5_), channel_id=1, source_target_pairs={{0,1},{1,0},{2,3},{3,2},{4,5},{5,4},{6,7},{7,6},{8,9},{9,8},{10,11... | collective-permute-start | bytes 1179656 | tf_op jit(solution)/shard_map/ppermute | solution.py:231

commit v10 on v9

--- a/solution.py
+++ b/solution.py
@@ -132,16 +132,15 @@
     latent_ref,
     node_in_ref,
     node_out_ref,
-    edge_hbm,
-    known,
+    gathered_hbm,
     to_node,
     pack_ref,
-    sem,
+    gathered,
+    sems,
 ):
     node_count, width = latent_ref.shape
-    edge_count = known.shape[0]
-    copy = pltpu.make_async_copy(edge_hbm, known.at[:, pl.ds(0, width)], sem)
-    copy.start()
+    edge_count = gathered.shape[0]
+    copies = []
     count = node_in_ref.shape[0]
     pack_ref[:count] = node_in_ref[...]
     pack_ref[count] = node_out_ref[...]
@@ -159,20 +158,28 @@
             source = jnp.where(far >= 0, source - slot + turned, source)
         columns = as_columns(source)
         sent = one_hot(columns, node_count)
-        known[spot, width : 2 * width] = jnp.dot(
+        gathered[spot, :width] = jnp.dot(
             sent, latent, preferred_element_type=f32
         ).astype(bf16)
         received = one_hot(as_columns(receiver), node_count)
-        known[spot, 2 * width : 3 * width] = jnp.dot(
+        gathered[spot, width : 2 * width] = jnp.dot(
             received, latent, preferred_element_type=f32
         ).astype(bf16)
-        known[spot, 3 * width :] = one_hot(columns - node_count, known.shape[1] - 3 * width)
+        gathered[spot, 2 * width :] = one_hot(
+            columns - node_count, gathered.shape[1] - 2 * width
+        )
+        rows = pl.ds(at * block, block)
+        copies.append(
+            pltpu.make_async_copy(gathered.at[rows], gathered_hbm.at[rows], sems.at[at])
+        )
+        copies[-1].start()
         for row in range(index_rows):
             start = at * block + row * lanes
             to_node[:, start : start + lanes] = jnp.where(
                 node_place == receiver[row : row + 1], 1.0, 0.0
             ).astype(bf16)
-    copy.wait()
+    for copy in copies:
+        copy.wait()
 
 
 def place_halo(halo, part_count, near_cap, halved, got):
@@ -235,13 +242,13 @@
 
 
 def edge_kernel(pieces_count, got_count, part_count, near_cap, halved, block, *refs):
-    known, to_node = refs[:2]
-    got_refs = refs[2 : 2 + got_count]
-    refs = refs[2 + got_count :]
+    edge_hbm, gathered_hbm, to_node = refs[:3]
+    got_refs = refs[3 : 3 + got_count]
+    refs = refs[3 + got_count :]
     in_pieces, out_pieces = refs[:pieces_count], refs[pieces_count : 2 * pieces_count]
     row_refs = refs[2 * pieces_count : 2 * pieces_count + 4]
     new_hbm, sum_ref = refs[2 * pieces_count + 4 : 2 * pieces_count + 6]
-    in_weight, out_weight, halo, rows, preact, hidden, output, new_ref, total, sems = refs[
+    known, in_weight, out_weight, halo, rows, preact, hidden, output, new_ref, total, sems = refs[
         2 * pieces_count + 6 :
     ]
     edge_count, width = new_hbm.shape
@@ -267,6 +274,16 @@
     spot = pl.ds(pl.multiple_of(order[0] * count, count), count)
     later.append(start(out_pieces[0], out_weight.at[spot]))
     in_bias, out_bias, gain, offset = rows
+    known_copies = []
+    for at in range(blocks):
+        spot = pl.ds(at * block, block)
+        others = pl.ds(width, known.shape[1] - width)
+        known_copies.append(
+            [
+                start(edge_hbm.at[spot], known.at[spot, pl.ds(0, width)]),
+                start(gathered_hbm.at[spot], known.at[spot, others]),
+            ]
+        )
 
     place_halo(halo, part_count, near_cap, halved, got_refs)
     for which in (1, 0, 2):
@@ -283,6 +300,8 @@
         copy.wait()
 
     def in_dot(at):
+        for copy in known_copies[at]:
+            copy.wait()
         preact[at][...] = jnp.dot(
             known[at * block : (at + 1) * block], in_weight[...], preferred_element_type=f32
         )
@@ -304,10 +323,7 @@
             normed = layer_norm(output[at][here] + out_bias[...], gain[...], offset[...])
             new_ref[there] = (known[there, :width].astype(f32) + normed).astype(bf16)
         spot = pl.ds(at * block, block)
-        taken.append(None)
-        copy = pltpu.make_async_copy(new_ref.at[spot], new_hbm.at[spot], sems.at[len(taken) - 1])
-        copy.start()
-        return copy
+        return start(new_ref.at[spot], new_hbm.at[spot])
 
     def sum_dot(at):
         spot = slice(at * block, (at + 1) * block)
@@ -397,17 +413,21 @@
     receiver_rows = in_hbm(receivers.reshape(-1, lanes))
 
     pack_shape = (node_in_weight.shape[0] + 1,) + node_out_weight.shape
-    known_width = 3 * width + halo_space
-    known, to_node, node_weight = pl.pallas_call(
-        functools.partial(gather_kernel, near_cap, far_cap, halved, 512),
+    gathered_width = 2 * width + halo_space
+    gather_block = 512
+    gathered, to_node, node_weight = pl.pallas_call(
+        functools.partial(gather_kernel, near_cap, far_cap, halved, gather_block),
         out_shape=[
-            pltpu.VMEM((edge_count, known_width), bf16),
+            pltpu.HBM((edge_count, gathered_width), bf16),
             pltpu.VMEM((node_count, edge_count), bf16),
             pltpu.VMEM(pack_shape, bf16),
         ],
-        in_specs=[vmem] * 5 + [hbm],
-        out_specs=[vmem] * 3,
-        scratch_shapes=[pltpu.SemaphoreType.DMA],
+        in_specs=[vmem] * 5,
+        out_specs=[hbm, vmem, vmem],
+        scratch_shapes=[
+            pltpu.VMEM((edge_count, gathered_width), bf16),
+            pltpu.SemaphoreType.DMA((edge_count // gather_block,)),
+        ],
         compiler_params=pltpu.CompilerParams(vmem_limit_bytes=grant),
         cost_estimate=pl.CostEstimate(flops=0, bytes_accessed=0, transcendentals=0),
         name="gather_latents",
@@ -417,11 +437,13 @@
         in_hbm(node_latent),
         in_hbm(node_in_weight),
         in_hbm(node_out_weight),
-        in_hbm(edge_latent),
-    )
-
-    far_edge, got, known, to_node, node_weight = lax.optimization_barrier(
-        (far_edge, got, known, to_node, node_weight)
+    )
+
+    far_edge[0], got, gathered, to_node = lax.optimization_barrier(
+        (far_edge[0], got, gathered, to_node)
+    )
+    far_edge[1], to_node, node_weight = lax.optimization_barrier(
+        (far_edge[1], to_node, node_weight)
     )
     if halved:
         got = got + from_subs(got)
@@ -434,14 +456,16 @@
     pieces_count = len(edge_in)
 
     rows = [value.reshape(1, -1) for value in (edge_in_bias, edge_out_bias, edge_gain, edge_offset)]
-    edge_operands = [in_vmem(known), in_vmem(to_node)] + [in_vmem(blocks) for blocks in got]
-    edge_specs = [vmem] * len(edge_operands)
+    edge_operands = [in_hbm(edge_latent), in_hbm(gathered), in_vmem(to_node)]
+    edge_operands += [in_vmem(blocks) for blocks in got]
+    edge_specs = [hbm] * 2 + [vmem] * (1 + len(got))
     for pieces in (edge_in, edge_out):
         edge_operands += [in_hbm(pieces[0])] + [in_vmem(piece) for piece in pieces[1:]]
         edge_specs += [hbm] + [vmem] * (pieces_count - 1)
     edge_operands += [in_hbm(row) for row in rows]
     edge_specs += [hbm] * len(rows)
-    copy_count = 3 + 4 + 1 + steps
+    known_width = width + gathered_width
+    copy_count = 3 + 4 + 1 + 3 * steps
     edge_new, partial_sums = pl.pallas_call(
         functools.partial(
             edge_kernel, pieces_count, len(got), part_count, near_cap, halved, block
@@ -453,6 +477,7 @@
         in_specs=edge_specs,
         out_specs=[hbm, vmem],
         scratch_shapes=[
+            pltpu.VMEM((edge_count, known_width), bf16),
             pltpu.VMEM((known_width, width), bf16),
             pltpu.VMEM((width, width), bf16),
             pltpu.VMEM((halo_space, width), bf16),

time: 36.2 us -> 39.9 us (1.10)
  waiting for transfers between devices: 2.82 us -> 10.9 us
  local copies, waits for them, and re-layouts: 4.97 us -> 0.04 us
  Pallas kernels: 14.6 us -> 17 us
  starting transfers between devices: 12.7 us -> 10.9 us
    ppermute x3, waiting for transfers between devices: 0.01 us -> 5.72 us  [from_feats(): lax.ppermute(weight, 'feat', [(at, (at + shift) % feats) for at in range(...]
    unnamed x16 -> x12, local copies, waits for them, and re-layouts: 4.97 us -> 0.04 us
    all_to_all x1, waiting for transfers between devices: 0.04 us -> 3.32 us  [exchange_halves(): lax.all_to_all(blocks, ('region', 'feat'), split_axis=0, concat_axis=0, t...]
    pallas_call x1, Pallas kernels: 7.21 us -> 8.48 us  [shards(): pl.pallas_call(functools.partial(edge_kernel, pieces_count, len(got), par...]
    pallas_call x1, Pallas kernels: 3.31 us -> 4.45 us  [shards(): pl.pallas_call(functools.partial(gather_kernel, near_cap, far_cap, halved...]
    ppermute x1, waiting for transfers between devices: 1.26 us -> 0.14 us  [shards(): lax.ppermute(partial_sums, 'sub', [(at, (at + 1) % subs) for at in range(...]
    ppermute x3, starting transfers between devices: 6.07 us -> 5.02 us  [from_feats(): lax.ppermute(weight, 'feat', [(at, (at + shift) % feats) for at in range(...]
    ppermute x7, starting transfers between devices: 1.22 us -> 0.75 us  [from_subs(): lax.ppermute(piece, 'sub', [(at, (at + turn) % subs) for at in range(subs)])]
  transfers between devices with their start and end apart: 12 -> 12, of which waited for: 3 -> 6; matrix products, arithmetic and copies ran while one was open for 0% -> 0% of each run, Pallas kernels for 35% -> 38%
where the time goes in v10:
time: 39.9 us; the launch traced here: 39.6 us
  Pallas kernels  17 us (43%)
  starting transfers between devices  10.9 us (27%)
  waiting for transfers between devices  10.9 us (27%)
  between operations  0.73 us (2%)
    pallas_call x1, Pallas kernels, shards(): pl.pallas_call(functools.partial(edge_kernel, pieces_count, len(got), par...  8.48 us
    ppermute x3, waiting for transfers between devices, from_feats(): lax.ppermute(weight, 'feat', [(at, (at + shift) % feats) for at in range(...  5.72 us
    ppermute x3, starting transfers between devices, from_feats(): lax.ppermute(weight, 'feat', [(at, (at + shift) % feats) for at in range(...  5.02 us
    all_to_all x1, starting transfers between devices, exchange_halves(): lax.all_to_all(blocks, ('region', 'feat'), split_axis=0, concat_axis=0, t...  4.88 us
    pallas_call x1, Pallas kernels, shards(): pl.pallas_call(functools.partial(gather_kernel, near_cap, far_cap, halved...  4.45 us
    all_to_all x1, waiting for transfers between devices, exchange_halves(): lax.all_to_all(blocks, ('region', 'feat'), split_axis=0, concat_axis=0, t...  3.32 us
    pallas_call x1, Pallas kernels, exchange_halves(): pl.pallas_call(functools.partial(pick_kernel, part_count, near_cap, far_c...  2.08 us
    pallas_call x1, Pallas kernels, shards(): pl.pallas_call(functools.partial(node_kernel, pieces_count), out_shape=ja...  2.01 us
  transfers between devices with their start and end apart: 12, of which 6 were waited for; matrix products, arithmetic and copies ran while one was open for 0% of the time, Pallas kernels for 38%

profile of v10, /device:TPU:0, one launch (start us, length us, event | category | flops | bytes accessed | tf_op | source)
XLA Modules:
  0.0 39.6 jit_solution(9429596358998624348)
XLA Ops:
  0.6 0.0 copy-start.5
  0.6 3.0 %collective-permute-start = (bf16[3,128,512]{2,1,0:T(8,128)(2,1)}, bf16[3,128,512]{2,1,0:T(8,128)(2,1)S(1)}, u32[]{:S(2)}, u32[]{:S(2)}) collective-permute-start(bf16[3,128,512]{2,1,0:T(8,128)(2,1)} %refs_5_.1), channel_id=1, source_target_pairs={{0,2},{2,0},{1,3},{3,1},{4,6},{6,4},{5,7},{7,5},{8,10},{10,8},{9,1... | collective-permute-start | bytes 1179656 | tf_op jit(solution)/shard_map/ppermute | solution.py:230
  3.6 2.1 %pick_halo.1 = bf16[8,17,512]{2,1,0:T(8,128)(2,1)} custom-call(s32[1,2,8]{2,1,0:T(2,128)} %bitcast.17, s32[1,4,32]{2,1,0:T(4,128)} %near_ref.1, bf16[384,512]{1,0:T(8,128)(2,1)} %refs_0_.3), custom_call_target="tpu_custom_call" | custom-call | tf_op jit(solution)/shard_map/pick_halo/pallas_call | solution.py:99
  5.7 4.9 %all-to-all-start = ((bf16[8,17,512]{2,1,0:T(8,128)(2,1)}), bf16[8,17,512]{2,1,0:T(8,128)(2,1)S(1)}, u32[]{:S(2)}, u32[]{:S(2)}) async-start(bf16[8,17,512]{2,1,0:T(8,128)(2,1)} %pick_halo.1), calls=%async_computation | async-start | bytes 393216 | tf_op jit(solution)/shard_map/all_to_all | solution.py:109
  10.6 0.0 collective-permute-start.3
  10.6 4.4 %gather_latents.1 = (bf16[1536,1280]{1,0:T(8,128)(2,1)}, bf16[384,1536]{1,0:T(8,128)(2,1)S(1)}, bf16[3,128,512]{2,1,0:T(8,128)(2,1)S(1)}) custom-call(s32[12,128]{1,0:T(8,128)} %bitcast.15, s32[12,128]{1,0:T(8,128)} %bitcast.16, bf16[384,512]{1,0:T(8,128)(2,1)} %refs_0_.3, bf16[2,128,512]{2,1,0:T(8,128)(2,1)} %node_in_ref.1, bf16[128,512]{1,0:T(8,128)(2,1)} %node_out_ref.1), custom_call_target="tpu_custom_call" | custom-call | tf_op jit(solution)/shard_map/gather_latents/pallas_call | solution.py:418
  15.1 3.3 %all-to-all-done.refs_3_ = bf16[8,17,512]{2,1,0:T(8,128)(2,1)S(1)} async-done(((bf16[8,17,512]{2,1,0:T(8,128)(2,1)}), bf16[8,17,512]{2,1,0:T(8,128)(2,1)S(1)}, u32[]{:S(2)}, u32[]{:S(2)}) %all-to-all-start) | async-done | bytes 139296 | tf_op jit(solution)/shard_map/all_to_all | solution.py:109
  18.4 1.0 %collective-permute-start.1 = (bf16[128,512]{1,0:T(8,128)(2,1)S(1)}, bf16[128,512]{1,0:T(8,128)(2,1)S(1)}, u32[]{:S(2)}, u32[]{:S(2)}) collective-permute-start(bf16[128,512]{1,0:T(8,128)(2,1)S(1)} %copy-done.5), channel_id=1, source_target_pairs={{0,2},{2,0},{1,3},{3,1},{4,6},{6,4},{5,7},{7,5},{8,10},{10,8},{9,1... | collective-permute-start | bytes 393224 | tf_op jit(solution)/shard_map/ppermute | solution.py:230
  19.4 0.2 collective-permute-start.5
  19.6 0.3 collective-permute-start.2
  20.0 4.4 %collective-permute-done.1.refs_11_ = bf16[128,512]{1,0:T(8,128)(2,1)S(1)} collective-permute-done((bf16[128,512]{1,0:T(8,128)(2,1)S(1)}, bf16[128,512]{1,0:T(8,128)(2,1)S(1)}, u32[]{:S(2)}, u32[]{:S(2)}) %collective-permute-start.1) | collective-permute-done | bytes 131104 | tf_op jit(solution)/shard_map/ppermute | solution.py:230
  24.3 1.0 %collective-permute-start.9 = (bf16[3,128,512]{2,1,0:T(8,128)(2,1)S(1)}, bf16[3,128,512]{2,1,0:T(8,128)(2,1)S(1)}, u32[]{:S(2)}, u32[]{:S(2)}) collective-permute-start(bf16[3,128,512]{2,1,0:T(8,128)(2,1)S(1)} %get-tuple-element.25.refs_3_), channel_id=1, source_target_pairs={{0,2},{2,0},{1,3},{3,1},{4,6},{6,4},{5,7},{7,5},{8,10},{10,8},{9,1... | collective-permute-start | bytes 1179656 | tf_op jit(solution)/shard_map/ppermute | solution.py:230
  25.3 0.2 collective-permute-start.8
  25.5 0.1 collective-permute-done.6.refs_12_
  25.7 0.0 copy-start.1
  25.7 0.0 copy-start.2
  25.7 0.0 copy-start.3
  25.7 0.0 copy-start.4
  25.7 8.5 %edge_update.1 = (bf16[1536,512]{1,0:T(8,128)(2,1)}, bf16[384,512]{1,0:T(8,128)(2,1)S(1)}) custom-call(bf16[1536,512]{1,0:T(8,128)(2,1)} %refs_0_.2, bf16[1536,1280]{1,0:T(8,128)(2,1)} %get-tuple-element.16.refs_1_, bf16[384,1536]{1,0:T(8,128)(2,1)S(1)} %get-tuple-element.19.refs_2_, bf16[8,17,512]{2,1,0:T(8,128)(2,1)S(1)} %all-to-all-done.refs_3_, ...), custom_call_target="tpu_custom_call" | custom-call | flops 3825205248 | bytes 6291456 | tf_op jit(solution)/shard_map/edge_update/pallas_call | solution.py:469
  34.2 0.3 collective-permute-start.7
  34.5 1.4 %collective-permute-done.9.refs_5_ = bf16[3,128,512]{2,1,0:T(8,128)(2,1)S(1)} collective-permute-done((bf16[3,128,512]{2,1,0:T(8,128)(2,1)S(1)}, bf16[3,128,512]{2,1,0:T(8,128)(2,1)S(1)}, u32[]{:S(2)}, u32[]{:S(2)}) %collective-permute-start.9) | collective-permute-done | bytes 393248 | tf_op jit(solution)/shard_map/ppermute | solution.py:230
  35.9 0.1 collective-permute-done.7.refs_2_
  36.0 1.6 %collective-permute-done.10.refs_6_ = bf16[3,128,512]{2,1,0:T(8,128)(2,1)S(1)} collective-permute-done((bf16[3,128,512]{2,1,0:T(8,128)(2,1)S(1)}, bf16[3,128,512]{2,1,0:T(8,128)(2,1)S(1)}, u32[]{:S(2)}, u32[]{:S(2)}) %collective-permute-start.10) | collective-permute-done | bytes 393248 | tf_op jit(solution)/shard_map/ppermute | solution.py:238
  37.6 2.0 %node_update.1 = bf16[384,512]{1,0:T(8,128)(2,1)} custom-call(bf16[384,512]{1,0:T(8,128)(2,1)S(1)} %copy-done, bf16[384,512]{1,0:T(8,128)(2,1)S(1)} %get-tuple-element.24.refs_1_, bf16[384,512]{1,0:T(8,128)(2,1)S(1)} %collective-permute-done.7.refs_2_, bf16[3,128,512]{2,1,0:T(8,128)(2,1)S(1)} %get-tuple-element.25.refs_3_, ...), custom_call_target="tpu_custom_call" | custom-call | flops 603979776 | bytes 1966080 | tf_op jit(solution)/shard_map/node_update/pallas_call | solution.py:505
  (16 shorter events, 0.0 us)
Async XLA Ops:
  0.6 17.8 %copy-start.5 = (bf16[128,512]{1,0:T(8,128)(2,1)S(1)}, bf16[128,512]{1,0:T(8,128)(2,1)}, u32[]{:S(2)}) copy-start(bf16[128,512]{1,0:T(8,128)(2,1)} %refs_9_.1) | copy-start | bytes 393220
  0.6 17.8 %collective-permute-start = (bf16[3,128,512]{2,1,0:T(8,128)(2,1)}, bf16[3,128,512]{2,1,0:T(8,128)(2,1)S(1)}, u32[]{:S(2)}, u32[]{:S(2)}) collective-permute-start(bf16[3,128,512]{2,1,0:T(8,128)(2,1)} %refs_5_.1), channel_id=1, source_target_pairs={{0,2},{2,0},{1,3},{3,1},{4,6},{6,4},{5,7},{7,5},{8,10},{10,8},{9,1... | collective-permute-start | bytes 1179656 | tf_op jit(solution)/shard_map/ppermute | solution.py:230
  5.7 12.7 %all-to-all-start = ((bf16[8,17,512]{2,1,0:T(8,128)(2,1)}), bf16[8,17,512]{2,1,0:T(8,128)(2,1)S(1)}, u32[]{:S(2)}, u32[]{:S(2)}) async-start(bf16[8,17,512]{2,1,0:T(8,128)(2,1)} %pick_halo.1), calls=%async_computation | async-start | bytes 393216 | tf_op jit(solution)/shard_map/all_to_all | solution.py:109
  10.6 14.7 %collective-permute-start.3 = (bf16[3,128,512]{2,1,0:T(8,128)(2,1)}, bf16[3,128,512]{2,1,0:T(8,128)(2,1)S(1)}, u32[]{:S(2)}, u32[]{:S(2)}) collective-permute-start(bf16[3,128,512]{2,1,0:T(8,128)(2,1)} %refs_5_.1), channel_id=1, source_target_pairs={{0,1},{1,0},{2,3},{3,2},{4,5},{5,4},{6,7},{7,6},{8,9},{9,8},{10,11... | collective-permute-start | bytes 1179656 | tf_op jit(solution)/shard_map/ppermute | solution.py:238
  18.4 7.3 %collective-permute-start.4 = (bf16[3,128,512]{2,1,0:T(8,128)(2,1)S(1)}, bf16[3,128,512]{2,1,0:T(8,128)(2,1)S(1)}, u32[]{:S(2)}, u32[]{:S(2)}) collective-permute-start(bf16[3,128,512]{2,1,0:T(8,128)(2,1)S(1)} %collective-permute-done.refs_7_), channel_id=1, source_target_pairs={{0,1},{1,0},{2,3},{3,2},{4,5},{5,4},{6,7},{7,6},{8,9},{9,8},{10,11... | collective-permute-start | bytes 1179656 | tf_op jit(solution)/shard_map/ppermute | solution.py:238
  18.4 5.9 %collective-permute-start.1 = (bf16[128,512]{1,0:T(8,128)(2,1)S(1)}, bf16[128,512]{1,0:T(8,128)(2,1)S(1)}, u32[]{:S(2)}, u32[]{:S(2)}) collective-permute-start(bf16[128,512]{1,0:T(8,128)(2,1)S(1)} %copy-done.5), channel_id=1, source_target_pairs={{0,2},{2,0},{1,3},{3,1},{4,6},{6,4},{5,7},{7,5},{8,10},{10,8},{9,1... | collective-permute-start | bytes 393224 | tf_op jit(solution)/shard_map/ppermute | solution.py:230
  19.4 4.9 %collective-permute-start.5 = (bf16[128,512]{1,0:T(8,128)(2,1)S(1)}, bf16[128,512]{1,0:T(8,128)(2,1)S(1)}, u32[]{:S(2)}, u32[]{:S(2)}) collective-permute-start(bf16[128,512]{1,0:T(8,128)(2,1)S(1)} %copy-done.5), channel_id=1, source_target_pairs={{0,1},{1,0},{2,3},{3,2},{4,5},{5,4},{6,7},{7,6},{8,9},{9,8},{10,11... | collective-permute-start | bytes 393224 | tf_op jit(solution)/shard_map/ppermute | solution.py:238
  19.6 6.1 %collective-permute-start.2 = (bf16[8,17,512]{2,1,0:T(8,128)(2,1)S(1)}, bf16[8,17,512]{2,1,0:T(8,128)(2,1)S(1)}, u32[]{:S(2)}, u32[]{:S(2)}) collective-permute-start(bf16[8,17,512]{2,1,0:T(8,128)(2,1)S(1)} %all-to-all-done.refs_3_), channel_id=1, source_target_pairs={{0,1},{1,0},{2,3},{3,2},{4,5},{5,4},{6,7},{7,6},{8,9},{9,8},{10,11... | collective-permute-start | bytes 417800 | tf_op jit(solution)/shard_map/ppermute | solution.py:238
  24.3 1.3 %collective-permute-start.6 = (bf16[128,512]{1,0:T(8,128)(2,1)S(1)}, bf16[128,512]{1,0:T(8,128)(2,1)S(1)}, u32[]{:S(2)}, u32[]{:S(2)}) collective-permute-start(bf16[128,512]{1,0:T(8,128)(2,1)S(1)} %collective-permute-done.1.refs_11_), channel_id=1, source_target_pairs={{0,1},{1,0},{2,3},{3,2},{4,5},{5,4},{6,7},{7,6},{8,9},{9,8},{10,11... | collective-permute-start | bytes 393224 | tf_op jit(solution)/shard_map/ppermute | solution.py:238
  24.3 11.5 %collective-permute-start.9 = (bf16[3,128,512]{2,1,0:T(8,128)(2,1)S(1)}, bf16[3,128,512]{2,1,0:T(8,128)(2,1)S(1)}, u32[]{:S(2)}, u32[]{:S(2)}) collective-permute-start(bf16[3,128,512]{2,1,0:T(8,128)(2,1)S(1)} %get-tuple-element.25.refs_3_), channel_id=1, source_target_pairs={{0,2},{2,0},{1,3},{3,1},{4,6},{6,4},{5,7},{7,5},{8,10},{10,8},{9,1... | collective-permute-start | bytes 1179656 | tf_op jit(solution)/shard_map/ppermute | solution.py:230
  25.3 10.6 %collective-permute-start.8 = (bf16[3,128,512]{2,1,0:T(8,128)(2,1)S(1)}, bf16[3,128,512]{2,1,0:T(8,128)(2,1)S(1)}, u32[]{:S(2)}, u32[]{:S(2)}) collective-permute-start(bf16[3,128,512]{2,1,0:T(8,128)(2,1)S(1)} %get-tuple-element.25.refs_3_), channel_id=1, source_target_pairs={{0,1},{1,0},{2,3},{3,2},{4,5},{5,4},{6,7},{7,6},{8,9},{9,8},{10,11... | collective-permute-start | bytes 1179656 | tf_op jit(solution)/shard_map/ppermute | solution.py:238
  25.7 11.9 %copy-start = (bf16[384,512]{1,0:T(8,128)(2,1)S(1)}, bf16[384,512]{1,0:T(8,128)(2,1)}, u32[]{:S(2)}) copy-start(bf16[384,512]{1,0:T(8,128)(2,1)} %refs_0_.3) | copy-start | bytes 1179652
  25.7 11.9 %copy-start.1 = (f32[512]{0:T(512)S(1)}, f32[512]{0:T(512)}, u32[]{:S(2)}) copy-start(f32[512]{0:T(512)} %param.32) | copy-start | bytes 6148
  25.7 11.9 %copy-start.2 = (f32[512]{0:T(512)S(1)}, f32[512]{0:T(512)}, u32[]{:S(2)}) copy-start(f32[512]{0:T(512)} %param.33) | copy-start | bytes 6148
  25.7 11.9 %copy-start.3 = (f32[512]{0:T(512)S(1)}, f32[512]{0:T(512)}, u32[]{:S(2)}) copy-start(f32[512]{0:T(512)} %param.34) | copy-start | bytes 6148
  25.7 11.9 %copy-start.4 = (f32[512]{0:T(512)S(1)}, f32[512]{0:T(512)}, u32[]{:S(2)}) copy-start(f32[512]{0:T(512)} %param.35) | copy-start | bytes 6148
  34.2 1.8 %collective-permute-start.7 = (bf16[384,512]{1,0:T(8,128)(2,1)S(1)}, bf16[384,512]{1,0:T(8,128)(2,1)S(1)}, u32[]{:S(2)}, u32[]{:S(2)}) collective-permute-start(bf16[384,512]{1,0:T(8,128)(2,1)S(1)} %get-tuple-element.24.refs_1_), channel_id=1, source_target_pairs={{0,1},{1,0},{2,3},{3,2},{4,5},{5,4},{6,7},{7,6},{8,9},{9,8},{10,11... | collective-permute-start | bytes 1179656 | tf_op jit(solution)/shard_map/ppermute | solution.py:502
  35.8 1.7 %collective-permute-start.10 = (bf16[3,128,512]{2,1,0:T(8,128)(2,1)S(1)}, bf16[3,128,512]{2,1,0:T(8,128)(2,1)S(1)}, u32[]{:S(2)}, u32[]{:S(2)}) collective-permute-start(bf16[3,128,512]{2,1,0:T(8,128)(2,1)S(1)} %collective-permute-done.9.refs_5_), channel_id=1, source_target_pairs={{0,1},{1,0},{2,3},{3,2},{4,5},{5,4},{6,7},{7,6},{8,9},{9,8},{10,11... | collective-permute-start | bytes 1179656 | tf_op jit(solution)/shard_map/ppermute | solution.py:238

commit v11 on v9

--- a/solution.py
+++ b/solution.py
@@ -126,7 +126,6 @@
     near_cap,
     far_cap,
     halved,
-    block,
     source_ref,
     receiver_ref,
     latent_ref,
@@ -134,24 +133,38 @@
     node_out_ref,
     edge_hbm,
     known,
+    gathered_hbm,
+    to_node_hbm,
+    pack_ref,
+    gathered,
     to_node,
-    pack_ref,
-    sem,
+    sems,
 ):
     node_count, width = latent_ref.shape
-    edge_count = known.shape[0]
-    copy = pltpu.make_async_copy(edge_hbm, known.at[:, pl.ds(0, width)], sem)
-    copy.start()
+    first = known.shape[0]
+    edge_count = first + gathered.shape[0]
+    block = first // 2
+    copies = []
+
+    def start(source, target):
+        copies.append(pltpu.make_async_copy(source, target, sems.at[len(copies)]))
+        copies[-1].start()
+
+    start(edge_hbm.at[pl.ds(0, first)], known.at[:, pl.ds(0, width)])
     count = node_in_ref.shape[0]
     pack_ref[:count] = node_in_ref[...]
     pack_ref[count] = node_out_ref[...]
     latent = latent_ref[...]
-    index_rows = block // lanes
     node_place = lax.broadcasted_iota(jnp.int32, (node_count, lanes), 0)
-    for at in range(edge_count // block):
-        spot = slice(at * block, (at + 1) * block)
-        here = slice(at * index_rows, (at + 1) * index_rows)
-        source, receiver = source_ref[here], receiver_ref[here]
+    for row in range(edge_count // lanes):
+        to_node[:, row * lanes : (row + 1) * lanes] = jnp.where(
+            node_place == receiver_ref[row : row + 1], 1.0, 0.0
+        ).astype(bf16)
+    start(to_node, to_node_hbm)
+
+    def gather(at, target, rows, begin):
+        here = slice(at * (block // lanes), (at + 1) * (block // lanes))
+        source = source_ref[here]
         if halved:
             far = source - (node_count + len(near_offsets) * near_cap)
             slot = lax.rem(far, far_cap)
@@ -159,20 +172,25 @@
             source = jnp.where(far >= 0, source - slot + turned, source)
         columns = as_columns(source)
         sent = one_hot(columns, node_count)
-        known[spot, width : 2 * width] = jnp.dot(
+        target[rows, begin : begin + width] = jnp.dot(
             sent, latent, preferred_element_type=f32
         ).astype(bf16)
-        received = one_hot(as_columns(receiver), node_count)
-        known[spot, 2 * width : 3 * width] = jnp.dot(
+        received = one_hot(as_columns(receiver_ref[here]), node_count)
+        target[rows, begin + width : begin + 2 * width] = jnp.dot(
             received, latent, preferred_element_type=f32
         ).astype(bf16)
-        known[spot, 3 * width :] = one_hot(columns - node_count, known.shape[1] - 3 * width)
-        for row in range(index_rows):
-            start = at * block + row * lanes
-            to_node[:, start : start + lanes] = jnp.where(
-                node_place == receiver[row : row + 1], 1.0, 0.0
-            ).astype(bf16)
-    copy.wait()
+        slots = target.shape[1] - begin - 2 * width
+        target[rows, begin + 2 * width :] = one_hot(columns - node_count, slots)
+
+    for at in range(first // block, edge_count // block):
+        begin = at * block - first
+        gather(at, gathered, slice(begin, begin + block), 0)
+        rows = pl.ds(begin, block)
+        start(gathered.at[rows], gathered_hbm.at[rows])
+    for at in range(first // block):
+        gather(at, known, slice(at * block, (at + 1) * block), width)
+    for copy in copies:
+        copy.wait()
 
 
 def place_halo(halo, part_count, near_cap, halved, got):
@@ -235,15 +253,15 @@
 
 
 def edge_kernel(pieces_count, got_count, part_count, near_cap, halved, block, *refs):
-    known, to_node = refs[:2]
-    got_refs = refs[2 : 2 + got_count]
-    refs = refs[2 + got_count :]
+    edge_hbm, gathered_hbm, to_node_hbm, known_first = refs[:4]
+    got_refs = refs[4 : 4 + got_count]
+    refs = refs[4 + got_count :]
     in_pieces, out_pieces = refs[:pieces_count], refs[pieces_count : 2 * pieces_count]
     row_refs = refs[2 * pieces_count : 2 * pieces_count + 4]
     new_hbm, sum_ref = refs[2 * pieces_count + 4 : 2 * pieces_count + 6]
-    in_weight, out_weight, halo, rows, preact, hidden, output, new_ref, total, sems = refs[
-        2 * pieces_count + 6 :
-    ]
+    known_rest, to_node, in_weight, out_weight, halo, rows, preact, hidden, output, new_ref, total, sems = (
+        refs[2 * pieces_count + 6 :]
+    )
     edge_count, width = new_hbm.shape
     blocks = edge_count // block
     taken = []
@@ -267,6 +285,15 @@
     spot = pl.ds(pl.multiple_of(order[0] * count, count), count)
     later.append(start(out_pieces[0], out_weight.at[spot]))
     in_bias, out_bias, gain, offset = rows
+    rest = edge_count - block
+    known_copies = [
+        start(edge_hbm.at[pl.ds(block, rest)], known_rest.at[:, pl.ds(0, width)]),
+        start(gathered_hbm, known_rest.at[:, pl.ds(width, known_rest.shape[1] - width)]),
+    ]
+    to_node_copy = start(to_node_hbm, to_node)
+
+    def known(at):
+        return known_first if at == 0 else known_rest.at[pl.ds((at - 1) * block, block)]
 
     place_halo(halo, part_count, near_cap, halved, got_refs)
     for which in (1, 0, 2):
@@ -283,8 +310,11 @@
         copy.wait()
 
     def in_dot(at):
+        if at == 1:
+            for copy in known_copies:
+                copy.wait()
         preact[at][...] = jnp.dot(
-            known[at * block : (at + 1) * block], in_weight[...], preferred_element_type=f32
+            known(at)[...], in_weight[...], preferred_element_type=f32
         )
 
     def activate(at):
@@ -302,14 +332,14 @@
             here = slice(start_row, start_row + chunk_rows)
             there = slice(at * block + start_row, at * block + start_row + chunk_rows)
             normed = layer_norm(output[at][here] + out_bias[...], gain[...], offset[...])
-            new_ref[there] = (known[there, :width].astype(f32) + normed).astype(bf16)
+            edges = known(at)[here, :width].astype(f32)
+            new_ref[there] = (edges + normed).astype(bf16)
         spot = pl.ds(at * block, block)
-        taken.append(None)
-        copy = pltpu.make_async_copy(new_ref.at[spot], new_hbm.at[spot], sems.at[len(taken) - 1])
-        copy.start()
-        return copy
+        return start(new_ref.at[spot], new_hbm.at[spot])
 
     def sum_dot(at):
+        if at == 0:
+            to_node_copy.wait()
         spot = slice(at * block, (at + 1) * block)
         part = jnp.dot(to_node[:, spot], new_ref[spot], preferred_element_type=f32)
         if at > 0:
@@ -397,17 +427,24 @@
     receiver_rows = in_hbm(receivers.reshape(-1, lanes))
 
     pack_shape = (node_in_weight.shape[0] + 1,) + node_out_weight.shape
-    known_width = 3 * width + halo_space
-    known, to_node, node_weight = pl.pallas_call(
-        functools.partial(gather_kernel, near_cap, far_cap, halved, 512),
+    gathered_width = 2 * width + halo_space
+    known_width = width + gathered_width
+    rest = edge_count - block
+    known, gathered, to_node, node_weight = pl.pallas_call(
+        functools.partial(gather_kernel, near_cap, far_cap, halved),
         out_shape=[
-            pltpu.VMEM((edge_count, known_width), bf16),
+            pltpu.VMEM((block, known_width), bf16),
+            pltpu.HBM((rest, gathered_width), bf16),
+            pltpu.HBM((node_count, edge_count), bf16),
+            pltpu.VMEM(pack_shape, bf16),
+        ],
+        in_specs=[vmem] * 5 + [hbm],
+        out_specs=[vmem, hbm, hbm, vmem],
+        scratch_shapes=[
+            pltpu.VMEM((rest, gathered_width), bf16),
             pltpu.VMEM((node_count, edge_count), bf16),
-            pltpu.VMEM(pack_shape, bf16),
-        ],
-        in_specs=[vmem] * 5 + [hbm],
-        out_specs=[vmem] * 3,
-        scratch_shapes=[pltpu.SemaphoreType.DMA],
+            pltpu.SemaphoreType.DMA((2 + 2 * (steps - 1),)),
+        ],
         compiler_params=pltpu.CompilerParams(vmem_limit_bytes=grant),
         cost_estimate=pl.CostEstimate(flops=0, bytes_accessed=0, transcendentals=0),
         name="gather_latents",
@@ -420,8 +457,8 @@
         in_hbm(edge_latent),
     )
 
-    far_edge, got, known, to_node, node_weight = lax.optimization_barrier(
-        (far_edge, got, known, to_node, node_weight)
+    far_edge, got, known, gathered, to_node, node_weight = lax.optimization_barrier(
+        (far_edge, got, known, gathered, to_node, node_weight)
     )
     if halved:
         got = got + from_subs(got)
@@ -434,14 +471,15 @@
     pieces_count = len(edge_in)
 
     rows = [value.reshape(1, -1) for value in (edge_in_bias, edge_out_bias, edge_gain, edge_offset)]
-    edge_operands = [in_vmem(known), in_vmem(to_node)] + [in_vmem(blocks) for blocks in got]
-    edge_specs = [vmem] * len(edge_operands)
+    edge_operands = [in_hbm(edge_latent), in_hbm(gathered), in_hbm(to_node), in_vmem(known)]
+    edge_operands += [in_vmem(blocks) for blocks in got]
+    edge_specs = [hbm] * 3 + [vmem] * (1 + len(got))
     for pieces in (edge_in, edge_out):
         edge_operands += [in_hbm(pieces[0])] + [in_vmem(piece) for piece in pieces[1:]]
         edge_specs += [hbm] + [vmem] * (pieces_count - 1)
     edge_operands += [in_hbm(row) for row in rows]
     edge_specs += [hbm] * len(rows)
-    copy_count = 3 + 4 + 1 + steps
+    copy_count = 3 + 4 + 1 + 2 + 1 + steps
     edge_new, partial_sums = pl.pallas_call(
         functools.partial(
             edge_kernel, pieces_count, len(got), part_count, near_cap, halved, block
@@ -453,6 +491,8 @@
         in_specs=edge_specs,
         out_specs=[hbm, vmem],
         scratch_shapes=[
+            pltpu.VMEM((rest, known_width), bf16),
+            pltpu.VMEM((node_count, edge_count), bf16),
             pltpu.VMEM((known_width, width), bf16),
             pltpu.VMEM((width, width), bf16),
             pltpu.VMEM((halo_space, width), bf16),

time: 36.2 us -> 35.9 us (level)
  local copies, waits for them, and re-layouts: 4.97 us -> 0.03 us
  waiting for transfers between devices: 2.82 us -> 5.17 us
  Pallas kernels: 14.6 us -> 16.9 us
    unnamed x16 -> x10, local copies, waits for them, and re-layouts: 4.97 us -> 0.03 us
    pallas_call x1, Pallas kernels: 7.21 us -> 8.93 us  [shards(): pl.pallas_call(functools.partial(edge_kernel, pieces_count, len(got), par...]
    ppermute x3, waiting for transfers between devices: 0.01 us -> 1.39 us  [from_feats(): lax.ppermute(weight, 'feat', [(at, (at + shift) % feats) for at in range(...]
    all_to_all x1, waiting for transfers between devices: 0.04 us -> 0.76 us  [exchange_halves(): lax.all_to_all(blocks, ('region', 'feat'), split_axis=0, concat_axis=0, t...]
    pallas_call x1, Pallas kernels: 3.31 us -> 3.93 us  [shards(): pl.pallas_call(functools.partial(gather_kernel, near_cap, far_cap, halved...]
    ppermute x7, waiting for transfers between devices: 1.51 us -> 2 us  [from_subs(): lax.ppermute(piece, 'sub', [(at, (at + turn) % subs) for at in range(subs)])]
  transfers between devices with their start and end apart: 12 -> 12, of which waited for: 3 -> 6; matrix products, arithmetic and copies ran while one was open for 0% -> 0% of each run, Pallas kernels for 35% -> 42%
where the time goes in v11:
time: 35.9 us; the launch traced here: 35.6 us
  Pallas kernels  16.9 us (47%)
  starting transfers between devices  12.7 us (35%)
  waiting for transfers between devices  5.17 us (14%)
  between operations  0.74 us (2%)
    pallas_call x1, Pallas kernels, shards(): pl.pallas_call(functools.partial(edge_kernel, pieces_count, len(got), par...  8.93 us
    ppermute x3, starting transfers between devices, from_feats(): lax.ppermute(weight, 'feat', [(at, (at + shift) % feats) for at in range(...  6.26 us
    all_to_all x1, starting transfers between devices, exchange_halves(): lax.all_to_all(blocks, ('region', 'feat'), split_axis=0, concat_axis=0, t...  4.88 us
    pallas_call x1, Pallas kernels, shards(): pl.pallas_call(functools.partial(gather_kernel, near_cap, far_cap, halved...  3.93 us
    pallas_call x1, Pallas kernels, exchange_halves(): pl.pallas_call(functools.partial(pick_kernel, part_count, near_cap, far_c...  2.08 us
    pallas_call x1, Pallas kernels, shards(): pl.pallas_call(functools.partial(node_kernel, pieces_count), out_shape=ja...  2.01 us
    ppermute x7, waiting for transfers between devices, from_subs(): lax.ppermute(piece, 'sub', [(at, (at + turn) % subs) for at in range(subs)])  2 us
    ppermute x3, waiting for transfers between devices, from_feats(): lax.ppermute(weight, 'feat', [(at, (at + shift) % feats) for at in range(...  1.39 us
  transfers between devices with their start and end apart: 12, of which 6 were waited for; matrix products, arithmetic and copies ran while one was open for 0% of the time, Pallas kernels for 42%

profile of v11, /device:TPU:0, one launch (start us, length us, event | category | flops | bytes accessed | tf_op | source)
XLA Modules:
  0.0 35.6 jit_solution(9790857630329383089)
XLA Ops:
  0.6 3.0 %collective-permute-start = (bf16[3,128,512]{2,1,0:T(8,128)(2,1)}, bf16[3,128,512]{2,1,0:T(8,128)(2,1)}, u32[]{:S(2)}, u32[]{:S(2)}) collective-permute-start(bf16[3,128,512]{2,1,0:T(8,128)(2,1)} %refs_6_.1), channel_id=1, source_target_pairs={{0,2},{2,0},{1,3},{3,1},{4,6},{6,4},{5,7},{7,5},{8,10},{10,8},{9,1... | collective-permute-start | bytes 1179656 | tf_op jit(solution)/shard_map/ppermute | solution.py:241
  3.6 2.1 %pick_halo.1 = bf16[8,17,512]{2,1,0:T(8,128)(2,1)} custom-call(s32[1,2,8]{2,1,0:T(2,128)} %bitcast.17, s32[1,4,32]{2,1,0:T(4,128)} %near_ref.1, bf16[384,512]{1,0:T(8,128)(2,1)} %refs_0_.3), custom_call_target="tpu_custom_call" | custom-call | tf_op jit(solution)/shard_map/pick_halo/pallas_call | solution.py:99
  5.7 4.9 %all-to-all-start = ((bf16[8,17,512]{2,1,0:T(8,128)(2,1)}), bf16[8,17,512]{2,1,0:T(8,128)(2,1)S(1)}, u32[]{:S(2)}, u32[]{:S(2)}) async-start(bf16[8,17,512]{2,1,0:T(8,128)(2,1)} %pick_halo.1), calls=%async_computation | async-start | bytes 393216 | tf_op jit(solution)/shard_map/all_to_all | solution.py:109
  10.6 2.0 %collective-permute-start.1 = (bf16[128,512]{1,0:T(8,128)(2,1)}, bf16[128,512]{1,0:T(8,128)(2,1)S(1)}, u32[]{:S(2)}, u32[]{:S(2)}) collective-permute-start(bf16[128,512]{1,0:T(8,128)(2,1)} %refs_10_.1), channel_id=1, source_target_pairs={{0,2},{2,0},{1,3},{3,1},{4,6},{6,4},{5,7},{7,5},{8,10},{10,8},{9,1... | collective-permute-start | bytes 393224 | tf_op jit(solution)/shard_map/ppermute | solution.py:241
  12.6 0.0 collective-permute-start.3
  12.6 3.9 %gather_latents.1 = (bf16[768,1792]{1,0:T(8,128)(2,1)S(1)}, bf16[768,1280]{1,0:T(8,128)(2,1)}, bf16[384,1536]{1,0:T(8,128)(2,1)}, bf16[3,128,512]{2,1,0:T(8,128)(2,1)S(1)}) custom-call(s32[12,128]{1,0:T(8,128)} %bitcast.15, s32[12,128]{1,0:T(8,128)} %bitcast.16, bf16[384,512]{1,0:T(8,128)(2,1)} %refs_0_.3, bf16[2,128,512]{2,1,0:T(8,128)(2,1)} %node_in_ref.1, ...), custom_call_target="tpu_custom_call" | custom-call | tf_op jit(solution)/shard_map/gather_latents/pallas_call | solution.py:433
  16.6 1.1 %collective-permute-done.1.refs_12_ = bf16[128,512]{1,0:T(8,128)(2,1)S(1)} collective-permute-done((bf16[128,512]{1,0:T(8,128)(2,1)}, bf16[128,512]{1,0:T(8,128)(2,1)S(1)}, u32[]{:S(2)}, u32[]{:S(2)}) %collective-permute-start.1) | collective-permute-done | bytes 131104 | tf_op jit(solution)/shard_map/ppermute | solution.py:241
  17.6 0.8 %all-to-all-done.refs_4_ = bf16[8,17,512]{2,1,0:T(8,128)(2,1)S(1)} async-done(((bf16[8,17,512]{2,1,0:T(8,128)(2,1)}), bf16[8,17,512]{2,1,0:T(8,128)(2,1)S(1)}, u32[]{:S(2)}, u32[]{:S(2)}) %all-to-all-start) | async-done | bytes 139296 | tf_op jit(solution)/shard_map/all_to_all | solution.py:109
  18.4 0.5 %collective-permute-start.5 = (bf16[128,512]{1,0:T(8,128)(2,1)}, bf16[128,512]{1,0:T(8,128)(2,1)S(1)}, u32[]{:S(2)}, u32[]{:S(2)}) collective-permute-start(bf16[128,512]{1,0:T(8,128)(2,1)} %refs_10_.1), channel_id=1, source_target_pairs={{0,1},{1,0},{2,3},{3,2},{4,5},{5,4},{6,7},{7,6},{8,9},{9,8},{10,11... | collective-permute-start | bytes 393224 | tf_op jit(solution)/shard_map/ppermute | solution.py:249
  18.9 0.0 collective-permute-start.2
  18.9 0.5 %collective-permute-start.6 = (bf16[128,512]{1,0:T(8,128)(2,1)S(1)}, bf16[128,512]{1,0:T(8,128)(2,1)S(1)}, u32[]{:S(2)}, u32[]{:S(2)}) collective-permute-start(bf16[128,512]{1,0:T(8,128)(2,1)S(1)} %collective-permute-done.1.refs_12_), channel_id=1, source_target_pairs={{0,1},{1,0},{2,3},{3,2},{4,5},{5,4},{6,7},{7,6},{8,9},{9,8},{10,11... | collective-permute-start | bytes 393224 | tf_op jit(solution)/shard_map/ppermute | solution.py:249
  19.4 1.3 %collective-permute-done.5.refs_11_ = bf16[128,512]{1,0:T(8,128)(2,1)S(1)} collective-permute-done((bf16[128,512]{1,0:T(8,128)(2,1)}, bf16[128,512]{1,0:T(8,128)(2,1)S(1)}, u32[]{:S(2)}, u32[]{:S(2)}) %collective-permute-start.5) | collective-permute-done | bytes 131104 | tf_op jit(solution)/shard_map/ppermute | solution.py:249
  20.7 1.2 %collective-permute-start.9 = (bf16[3,128,512]{2,1,0:T(8,128)(2,1)S(1)}, bf16[3,128,512]{2,1,0:T(8,128)(2,1)S(1)}, u32[]{:S(2)}, u32[]{:S(2)}) collective-permute-start(bf16[3,128,512]{2,1,0:T(8,128)(2,1)S(1)} %get-tuple-element.27.refs_3_), channel_id=1, source_target_pairs={{0,2},{2,0},{1,3},{3,1},{4,6},{6,4},{5,7},{7,5},{8,10},{10,8},{9,1... | collective-permute-start | bytes 1179656 | tf_op jit(solution)/shard_map/ppermute | solution.py:241
  22.0 0.0 copy-start
  22.0 0.0 copy-start.1
  22.0 0.0 copy-start.2
  22.0 0.0 copy-start.3
  22.0 0.0 copy-start.4
  22.0 8.9 %edge_update.1 = (bf16[1536,512]{1,0:T(8,128)(2,1)}, bf16[384,512]{1,0:T(8,128)(2,1)S(1)}) custom-call(bf16[1536,512]{1,0:T(8,128)(2,1)} %refs_0_.2, bf16[768,1280]{1,0:T(8,128)(2,1)} %get-tuple-element.19.refs_1_, bf16[384,1536]{1,0:T(8,128)(2,1)} %get-tuple-element.20.refs_2_, bf16[768,1792]{1,0:T(8,128)(2,1)S(1)} %get-tuple-element.21.refs_3_, ...), custom_call_target="tpu_custom_call" | custom-call | flops 3825205248 | bytes 6291456 | tf_op jit(solution)/shard_map/edge_update/pallas_call | solution.py:483
  31.0 0.6 %collective-permute-start.7 = (bf16[384,512]{1,0:T(8,128)(2,1)S(1)}, bf16[384,512]{1,0:T(8,128)(2,1)S(1)}, u32[]{:S(2)}, u32[]{:S(2)}) collective-permute-start(bf16[384,512]{1,0:T(8,128)(2,1)S(1)} %get-tuple-element.26.refs_1_), channel_id=1, source_target_pairs={{0,1},{1,0},{2,3},{3,2},{4,5},{5,4},{6,7},{7,6},{8,9},{9,8},{10,11... | collective-permute-start | bytes 1179656 | tf_op jit(solution)/shard_map/ppermute | solution.py:517
  31.5 0.3 collective-permute-done.9.refs_5_
  31.9 1.0 %collective-permute-done.7.refs_2_ = bf16[384,512]{1,0:T(8,128)(2,1)S(1)} collective-permute-done((bf16[384,512]{1,0:T(8,128)(2,1)S(1)}, bf16[384,512]{1,0:T(8,128)(2,1)S(1)}, u32[]{:S(2)}, u32[]{:S(2)}) %collective-permute-start.7) | collective-permute-done | bytes 393248 | tf_op jit(solution)/shard_map/ppermute | solution.py:517
  32.9 0.7 %collective-permute-done.10.refs_6_ = bf16[3,128,512]{2,1,0:T(8,128)(2,1)S(1)} collective-permute-done((bf16[3,128,512]{2,1,0:T(8,128)(2,1)S(1)}, bf16[3,128,512]{2,1,0:T(8,128)(2,1)S(1)}, u32[]{:S(2)}, u32[]{:S(2)}) %collective-permute-start.10) | collective-permute-done | bytes 393248 | tf_op jit(solution)/shard_map/ppermute | solution.py:249
  33.6 2.0 %node_update.1 = bf16[384,512]{1,0:T(8,128)(2,1)} custom-call(bf16[384,512]{1,0:T(8,128)(2,1)S(1)} %copy-done, bf16[384,512]{1,0:T(8,128)(2,1)S(1)} %get-tuple-element.26.refs_1_, bf16[384,512]{1,0:T(8,128)(2,1)S(1)} %collective-permute-done.7.refs_2_, bf16[3,128,512]{2,1,0:T(8,128)(2,1)S(1)} %get-tuple-element.27.refs_3_, ...), custom_call_target="tpu_custom_call" | custom-call | flops 603979776 | bytes 1966080 | tf_op jit(solution)/shard_map/node_update/pallas_call | solution.py:520
  (14 shorter events, 0.0 us)
Async XLA Ops:
  0.6 17.8 %collective-permute-start = (bf16[3,128,512]{2,1,0:T(8,128)(2,1)}, bf16[3,128,512]{2,1,0:T(8,128)(2,1)}, u32[]{:S(2)}, u32[]{:S(2)}) collective-permute-start(bf16[3,128,512]{2,1,0:T(8,128)(2,1)} %refs_6_.1), channel_id=1, source_target_pairs={{0,2},{2,0},{1,3},{3,1},{4,6},{6,4},{5,7},{7,5},{8,10},{10,8},{9,1... | collective-permute-start | bytes 1179656 | tf_op jit(solution)/shard_map/ppermute | solution.py:241
  5.7 12.7 %all-to-all-start = ((bf16[8,17,512]{2,1,0:T(8,128)(2,1)}), bf16[8,17,512]{2,1,0:T(8,128)(2,1)S(1)}, u32[]{:S(2)}, u32[]{:S(2)}) async-start(bf16[8,17,512]{2,1,0:T(8,128)(2,1)} %pick_halo.1), calls=%async_computation | async-start | bytes 393216 | tf_op jit(solution)/shard_map/all_to_all | solution.py:109
  10.6 7.0 %collective-permute-start.1 = (bf16[128,512]{1,0:T(8,128)(2,1)}, bf16[128,512]{1,0:T(8,128)(2,1)S(1)}, u32[]{:S(2)}, u32[]{:S(2)}) collective-permute-start(bf16[128,512]{1,0:T(8,128)(2,1)} %refs_10_.1), channel_id=1, source_target_pairs={{0,2},{2,0},{1,3},{3,1},{4,6},{6,4},{5,7},{7,5},{8,10},{10,8},{9,1... | collective-permute-start | bytes 393224 | tf_op jit(solution)/shard_map/ppermute | solution.py:241
  12.6 9.3 %collective-permute-start.3 = (bf16[3,128,512]{2,1,0:T(8,128)(2,1)}, bf16[3,128,512]{2,1,0:T(8,128)(2,1)}, u32[]{:S(2)}, u32[]{:S(2)}) collective-permute-start(bf16[3,128,512]{2,1,0:T(8,128)(2,1)} %refs_6_.1), channel_id=1, source_target_pairs={{0,1},{1,0},{2,3},{3,2},{4,5},{5,4},{6,7},{7,6},{8,9},{9,8},{10,11... | collective-permute-start | bytes 1179656 | tf_op jit(solution)/shard_map/ppermute | solution.py:249
  18.4 3.6 %collective-permute-start.4 = (bf16[3,128,512]{2,1,0:T(8,128)(2,1)}, bf16[3,128,512]{2,1,0:T(8,128)(2,1)S(1)}, u32[]{:S(2)}, u32[]{:S(2)}) collective-permute-start(bf16[3,128,512]{2,1,0:T(8,128)(2,1)} %collective-permute-done.refs_8_), channel_id=1, source_target_pairs={{0,1},{1,0},{2,3},{3,2},{4,5},{5,4},{6,7},{7,6},{8,9},{9,8},{10,11... | collective-permute-start | bytes 1179656 | tf_op jit(solution)/shard_map/ppermute | solution.py:249
  18.4 2.3 %collective-permute-start.5 = (bf16[128,512]{1,0:T(8,128)(2,1)}, bf16[128,512]{1,0:T(8,128)(2,1)S(1)}, u32[]{:S(2)}, u32[]{:S(2)}) collective-permute-start(bf16[128,512]{1,0:T(8,128)(2,1)} %refs_10_.1), channel_id=1, source_target_pairs={{0,1},{1,0},{2,3},{3,2},{4,5},{5,4},{6,7},{7,6},{8,9},{9,8},{10,11... | collective-permute-start | bytes 393224 | tf_op jit(solution)/shard_map/ppermute | solution.py:249
  18.9 3.1 %collective-permute-start.2 = (bf16[8,17,512]{2,1,0:T(8,128)(2,1)S(1)}, bf16[8,17,512]{2,1,0:T(8,128)(2,1)S(1)}, u32[]{:S(2)}, u32[]{:S(2)}) collective-permute-start(bf16[8,17,512]{2,1,0:T(8,128)(2,1)S(1)} %all-to-all-done.refs_4_), channel_id=1, source_target_pairs={{0,1},{1,0},{2,3},{3,2},{4,5},{5,4},{6,7},{7,6},{8,9},{9,8},{10,11... | collective-permute-start | bytes 417800 | tf_op jit(solution)/shard_map/ppermute | solution.py:249
  18.9 3.0 %collective-permute-start.6 = (bf16[128,512]{1,0:T(8,128)(2,1)S(1)}, bf16[128,512]{1,0:T(8,128)(2,1)S(1)}, u32[]{:S(2)}, u32[]{:S(2)}) collective-permute-start(bf16[128,512]{1,0:T(8,128)(2,1)S(1)} %collective-permute-done.1.refs_12_), channel_id=1, source_target_pairs={{0,1},{1,0},{2,3},{3,2},{4,5},{5,4},{6,7},{7,6},{8,9},{9,8},{10,11... | collective-permute-start | bytes 393224 | tf_op jit(solution)/shard_map/ppermute | solution.py:249
  20.7 11.2 %collective-permute-start.9 = (bf16[3,128,512]{2,1,0:T(8,128)(2,1)S(1)}, bf16[3,128,512]{2,1,0:T(8,128)(2,1)S(1)}, u32[]{:S(2)}, u32[]{:S(2)}) collective-permute-start(bf16[3,128,512]{2,1,0:T(8,128)(2,1)S(1)} %get-tuple-element.27.refs_3_), channel_id=1, source_target_pairs={{0,2},{2,0},{1,3},{3,1},{4,6},{6,4},{5,7},{7,5},{8,10},{10,8},{9,1... | collective-permute-start | bytes 1179656 | tf_op jit(solution)/shard_map/ppermute | solution.py:241
  21.9 9.9 %collective-permute-start.8 = (bf16[3,128,512]{2,1,0:T(8,128)(2,1)S(1)}, bf16[3,128,512]{2,1,0:T(8,128)(2,1)S(1)}, u32[]{:S(2)}, u32[]{:S(2)}) collective-permute-start(bf16[3,128,512]{2,1,0:T(8,128)(2,1)S(1)} %get-tuple-element.27.refs_3_), channel_id=1, source_target_pairs={{0,1},{1,0},{2,3},{3,2},{4,5},{5,4},{6,7},{7,6},{8,9},{9,8},{10,11... | collective-permute-start | bytes 1179656 | tf_op jit(solution)/shard_map/ppermute | solution.py:249
  22.0 11.6 %copy-start = (bf16[384,512]{1,0:T(8,128)(2,1)S(1)}, bf16[384,512]{1,0:T(8,128)(2,1)}, u32[]{:S(2)}) copy-start(bf16[384,512]{1,0:T(8,128)(2,1)} %refs_0_.3) | copy-start | bytes 1179652
  22.0 11.6 %copy-start.1 = (f32[512]{0:T(512)S(1)}, f32[512]{0:T(512)}, u32[]{:S(2)}) copy-start(f32[512]{0:T(512)} %param.32) | copy-start | bytes 6148
  22.0 11.6 %copy-start.2 = (f32[512]{0:T(512)S(1)}, f32[512]{0:T(512)}, u32[]{:S(2)}) copy-start(f32[512]{0:T(512)} %param.33) | copy-start | bytes 6148
  22.0 11.6 %copy-start.3 = (f32[512]{0:T(512)S(1)}, f32[512]{0:T(512)}, u32[]{:S(2)}) copy-start(f32[512]{0:T(512)} %param.34) | copy-start | bytes 6148
  22.0 11.6 %copy-start.4 = (f32[512]{0:T(512)S(1)}, f32[512]{0:T(512)}, u32[]{:S(2)}) copy-start(f32[512]{0:T(512)} %param.35) | copy-start | bytes 6148
  31.0 1.9 %collective-permute-start.7 = (bf16[384,512]{1,0:T(8,128)(2,1)S(1)}, bf16[384,512]{1,0:T(8,128)(2,1)S(1)}, u32[]{:S(2)}, u32[]{:S(2)}) collective-permute-start(bf16[384,512]{1,0:T(8,128)(2,1)S(1)} %get-tuple-element.26.refs_1_), channel_id=1, source_target_pairs={{0,1},{1,0},{2,3},{3,2},{4,5},{5,4},{6,7},{7,6},{8,9},{9,8},{10,11... | collective-permute-start | bytes 1179656 | tf_op jit(solution)/shard_map/ppermute | solution.py:517
  31.8 1.7 %collective-permute-start.10 = (bf16[3,128,512]{2,1,0:T(8,128)(2,1)S(1)}, bf16[3,128,512]{2,1,0:T(8,128)(2,1)S(1)}, u32[]{:S(2)}, u32[]{:S(2)}) collective-permute-start(bf16[3,128,512]{2,1,0:T(8,128)(2,1)S(1)} %collective-permute-done.9.refs_5_), channel_id=1, source_target_pairs={{0,1},{1,0},{2,3},{3,2},{4,5},{5,4},{6,7},{7,6},{8,9},{9,8},{10,11... | collective-permute-start | bytes 1179656 | tf_op jit(solution)/shard_map/ppermute | solution.py:249

commit v12 on v11

--- a/solution.py
+++ b/solution.py
@@ -134,10 +134,8 @@
     edge_hbm,
     known,
     gathered_hbm,
-    to_node_hbm,
     pack_ref,
     gathered,
-    to_node,
     sems,
 ):
     node_count, width = latent_ref.shape
@@ -155,12 +153,6 @@
     pack_ref[:count] = node_in_ref[...]
     pack_ref[count] = node_out_ref[...]
     latent = latent_ref[...]
-    node_place = lax.broadcasted_iota(jnp.int32, (node_count, lanes), 0)
-    for row in range(edge_count // lanes):
-        to_node[:, row * lanes : (row + 1) * lanes] = jnp.where(
-            node_place == receiver_ref[row : row + 1], 1.0, 0.0
-        ).astype(bf16)
-    start(to_node, to_node_hbm)
 
     def gather(at, target, rows, begin):
         here = slice(at * (block // lanes), (at + 1) * (block // lanes))
@@ -253,7 +245,7 @@
 
 
 def edge_kernel(pieces_count, got_count, part_count, near_cap, halved, block, *refs):
-    edge_hbm, gathered_hbm, to_node_hbm, known_first = refs[:4]
+    edge_hbm, gathered_hbm, receiver_ref, known_first = refs[:4]
     got_refs = refs[4 : 4 + got_count]
     refs = refs[4 + got_count :]
     in_pieces, out_pieces = refs[:pieces_count], refs[pieces_count : 2 * pieces_count]
@@ -290,7 +282,6 @@
         start(edge_hbm.at[pl.ds(block, rest)], known_rest.at[:, pl.ds(0, width)]),
         start(gathered_hbm, known_rest.at[:, pl.ds(width, known_rest.shape[1] - width)]),
     ]
-    to_node_copy = start(to_node_hbm, to_node)
 
     def known(at):
         return known_first if at == 0 else known_rest.at[pl.ds((at - 1) * block, block)]
@@ -338,8 +329,6 @@
         return start(new_ref.at[spot], new_hbm.at[spot])
 
     def sum_dot(at):
-        if at == 0:
-            to_node_copy.wait()
         spot = slice(at * block, (at + 1) * block)
         part = jnp.dot(to_node[:, spot], new_ref[spot], preferred_element_type=f32)
         if at > 0:
@@ -349,16 +338,24 @@
         else:
             sum_ref[...] = part.astype(bf16)
 
+    in_dot(0)
+    node_place = lax.broadcasted_iota(jnp.int32, (to_node.shape[0], lanes), 0)
+    for row in range(edge_count // lanes):
+        to_node[:, row * lanes : (row + 1) * lanes] = jnp.where(
+            node_place == receiver_ref[row : row + 1], 1.0, 0.0
+        ).astype(bf16)
+    for at in range(1, blocks):
+        in_dot(at)
+        activate(at - 1)
+    out_dot(0)
+    activate(blocks - 1)
+    for at in range(1, blocks):
+        out_dot(at)
     out_copies = []
-    in_dot(0)
     for at in range(blocks):
-        if at + 1 < blocks:
-            in_dot(at + 1)
-        activate(at)
-        out_dot(at)
+        out_copies.append(normalise(at))
         if at > 0:
             sum_dot(at - 1)
-        out_copies.append(normalise(at))
     sum_dot(blocks - 1)
     for copy in out_copies:
         copy.wait()
@@ -430,20 +427,18 @@
     gathered_width = 2 * width + halo_space
     known_width = width + gathered_width
     rest = edge_count - block
-    known, gathered, to_node, node_weight = pl.pallas_call(
+    known, gathered, node_weight = pl.pallas_call(
         functools.partial(gather_kernel, near_cap, far_cap, halved),
         out_shape=[
             pltpu.VMEM((block, known_width), bf16),
             pltpu.HBM((rest, gathered_width), bf16),
-            pltpu.HBM((node_count, edge_count), bf16),
             pltpu.VMEM(pack_shape, bf16),
         ],
         in_specs=[vmem] * 5 + [hbm],
-        out_specs=[vmem, hbm, hbm, vmem],
+        out_specs=[vmem, hbm, vmem],
         scratch_shapes=[
             pltpu.VMEM((rest, gathered_width), bf16),
-            pltpu.VMEM((node_count, edge_count), bf16),
-            pltpu.SemaphoreType.DMA((2 + 2 * (steps - 1),)),
+            pltpu.SemaphoreType.DMA((1 + 2 * (steps - 1),)),
         ],
         compiler_params=pltpu.CompilerParams(vmem_limit_bytes=grant),
         cost_estimate=pl.CostEstimate(flops=0, bytes_accessed=0, transcendentals=0),
@@ -457,8 +452,8 @@
         in_hbm(edge_latent),
     )
 
-    far_edge, got, known, gathered, to_node, node_weight = lax.optimization_barrier(
-        (far_edge, got, known, gathered, to_node, node_weight)
+    far_edge, got, known, gathered, node_weight = lax.optimization_barrier(
+        (far_edge, got, known, gathered, node_weight)
     )
     if halved:
         got = got + from_subs(got)
@@ -471,15 +466,15 @@
     pieces_count = len(edge_in)
 
     rows = [value.reshape(1, -1) for value in (edge_in_bias, edge_out_bias, edge_gain, edge_offset)]
-    edge_operands = [in_hbm(edge_latent), in_hbm(gathered), in_hbm(to_node), in_vmem(known)]
+    edge_operands = [in_hbm(edge_latent), in_hbm(gathered), receiver_rows, in_vmem(known)]
     edge_operands += [in_vmem(blocks) for blocks in got]
-    edge_specs = [hbm] * 3 + [vmem] * (1 + len(got))
+    edge_specs = [hbm] * 2 + [vmem] * (2 + len(got))
     for pieces in (edge_in, edge_out):
         edge_operands += [in_hbm(pieces[0])] + [in_vmem(piece) for piece in pieces[1:]]
         edge_specs += [hbm] + [vmem] * (pieces_count - 1)
     edge_operands += [in_hbm(row) for row in rows]
     edge_specs += [hbm] * len(rows)
-    copy_count = 3 + 4 + 1 + 2 + 1 + steps
+    copy_count = 3 + 4 + 1 + 2 + steps
     edge_new, partial_sums = pl.pallas_call(
         functools.partial(
             edge_kernel, pieces_count, len(got), part_count, near_cap, halved, block

time: 35.9 us -> 35.9 us (level)
  waiting for transfers between devices: 5.17 us -> 5.75 us
  Pallas kernels: 16.9 us -> 16.4 us
    pallas_call x1, Pallas kernels: 3.93 us -> 3.23 us  [shards(): pl.pallas_call(functools.partial(gather_kernel, near_cap, far_cap, halved...]
    ppermute x3, waiting for transfers between devices: 1.39 us -> 1.97 us  [from_feats(): lax.ppermute(weight, 'feat', [(at, (at + shift) % feats) for at in range(...]
  transfers between devices with their start and end apart: 12 -> 12, of which waited for: 6 -> 6; matrix products, arithmetic and copies ran while one was open for 0% -> 0% of each run, Pallas kernels for 42% -> 40%
where the time goes in v12:
time: 35.9 us; the launch traced here: 35.6 us
  Pallas kernels  16.4 us (46%)
  starting transfers between devices  12.7 us (35%)
  waiting for transfers between devices  5.75 us (16%)
  between operations  0.74 us (2%)
    pallas_call x1, Pallas kernels, shards(): pl.pallas_call(functools.partial(edge_kernel, pieces_count, len(got), par...  9.05 us
    ppermute x3, starting transfers between devices, from_feats(): lax.ppermute(weight, 'feat', [(at, (at + shift) % feats) for at in range(...  6.26 us
    all_to_all x1, starting transfers between devices, exchange_halves(): lax.all_to_all(blocks, ('region', 'feat'), split_axis=0, concat_axis=0, t...  4.88 us
    pallas_call x1, Pallas kernels, shards(): pl.pallas_call(functools.partial(gather_kernel, near_cap, far_cap, halved...  3.23 us
    pallas_call x1, Pallas kernels, exchange_halves(): pl.pallas_call(functools.partial(pick_kernel, part_count, near_cap, far_c...  2.08 us
    pallas_call x1, Pallas kernels, shards(): pl.pallas_call(functools.partial(node_kernel, pieces_count), out_shape=ja...  2.01 us
    ppermute x3, waiting for transfers between devices, from_feats(): lax.ppermute(weight, 'feat', [(at, (at + shift) % feats) for at in range(...  1.97 us
    ppermute x7, waiting for transfers between devices, from_subs(): lax.ppermute(piece, 'sub', [(at, (at + turn) % subs) for at in range(subs)])  1.88 us
  transfers between devices with their start and end apart: 12, of which 6 were waited for; matrix products, arithmetic and copies ran while one was open for 0% of the time, Pallas kernels for 40%

profile of v12, /device:TPU:0, one launch (start us, length us, event | category | flops | bytes accessed | tf_op | source)
XLA Modules:
  0.0 35.6 jit_solution(1374132558225929078)
XLA Ops:
  0.6 3.0 %collective-permute-start = (bf16[3,128,512]{2,1,0:T(8,128)(2,1)}, bf16[3,128,512]{2,1,0:T(8,128)(2,1)}, u32[]{:S(2)}, u32[]{:S(2)}) collective-permute-start(bf16[3,128,512]{2,1,0:T(8,128)(2,1)} %refs_6_.1), channel_id=1, source_target_pairs={{0,2},{2,0},{1,3},{3,1},{4,6},{6,4},{5,7},{7,5},{8,10},{10,8},{9,1... | collective-permute-start | bytes 1179656 | tf_op jit(solution)/shard_map/ppermute | solution.py:233
  3.6 2.1 %pick_halo.1 = bf16[8,17,512]{2,1,0:T(8,128)(2,1)} custom-call(s32[1,2,8]{2,1,0:T(2,128)} %bitcast.18, s32[1,4,32]{2,1,0:T(4,128)} %near_ref.1, bf16[384,512]{1,0:T(8,128)(2,1)} %refs_0_.3), custom_call_target="tpu_custom_call" | custom-call | tf_op jit(solution)/shard_map/pick_halo/pallas_call | solution.py:99
  5.7 4.9 %all-to-all-start = ((bf16[8,17,512]{2,1,0:T(8,128)(2,1)}), bf16[8,17,512]{2,1,0:T(8,128)(2,1)S(1)}, u32[]{:S(2)}, u32[]{:S(2)}) async-start(bf16[8,17,512]{2,1,0:T(8,128)(2,1)} %pick_halo.1), calls=%async_computation | async-start | bytes 393216 | tf_op jit(solution)/shard_map/all_to_all | solution.py:109
  10.6 2.0 %collective-permute-start.1 = (bf16[128,512]{1,0:T(8,128)(2,1)}, bf16[128,512]{1,0:T(8,128)(2,1)S(1)}, u32[]{:S(2)}, u32[]{:S(2)}) collective-permute-start(bf16[128,512]{1,0:T(8,128)(2,1)} %refs_10_.1), channel_id=1, source_target_pairs={{0,2},{2,0},{1,3},{3,1},{4,6},{6,4},{5,7},{7,5},{8,10},{10,8},{9,1... | collective-permute-start | bytes 393224 | tf_op jit(solution)/shard_map/ppermute | solution.py:233
  12.6 0.0 collective-permute-start.3
  12.6 3.2 %gather_latents.1 = (bf16[768,1792]{1,0:T(8,128)(2,1)S(1)}, bf16[768,1280]{1,0:T(8,128)(2,1)}, bf16[3,128,512]{2,1,0:T(8,128)(2,1)S(1)}) custom-call(s32[12,128]{1,0:T(8,128)} %bitcast.15, s32[12,128]{1,0:T(8,128)} %bitcast.16, bf16[384,512]{1,0:T(8,128)(2,1)} %refs_0_.3, bf16[2,128,512]{2,1,0:T(8,128)(2,1)} %node_in_ref.1, bf16[128,512]{1,0:T(8,128)(2,1)} %node_out_ref.1, ...), custom_call_target="tpu_custom_call" | custom-call | tf_op jit(solution)/shard_map/gather_latents/pallas_call | solution.py:430
  15.9 1.8 %collective-permute-done.1.refs_12_ = bf16[128,512]{1,0:T(8,128)(2,1)S(1)} collective-permute-done((bf16[128,512]{1,0:T(8,128)(2,1)}, bf16[128,512]{1,0:T(8,128)(2,1)S(1)}, u32[]{:S(2)}, u32[]{:S(2)}) %collective-permute-start.1) | collective-permute-done | bytes 131104 | tf_op jit(solution)/shard_map/ppermute | solution.py:233
  17.6 0.8 %all-to-all-done.refs_4_ = bf16[8,17,512]{2,1,0:T(8,128)(2,1)S(1)} async-done(((bf16[8,17,512]{2,1,0:T(8,128)(2,1)}), bf16[8,17,512]{2,1,0:T(8,128)(2,1)S(1)}, u32[]{:S(2)}, u32[]{:S(2)}) %all-to-all-start) | async-done | bytes 139296 | tf_op jit(solution)/shard_map/all_to_all | solution.py:109
  18.4 0.5 %collective-permute-start.5 = (bf16[128,512]{1,0:T(8,128)(2,1)}, bf16[128,512]{1,0:T(8,128)(2,1)S(1)}, u32[]{:S(2)}, u32[]{:S(2)}) collective-permute-start(bf16[128,512]{1,0:T(8,128)(2,1)} %refs_10_.1), channel_id=1, source_target_pairs={{0,1},{1,0},{2,3},{3,2},{4,5},{5,4},{6,7},{7,6},{8,9},{9,8},{10,11... | collective-permute-start | bytes 393224 | tf_op jit(solution)/shard_map/ppermute | solution.py:241
  18.9 0.0 collective-permute-start.2
  18.9 0.5 %collective-permute-start.6 = (bf16[128,512]{1,0:T(8,128)(2,1)S(1)}, bf16[128,512]{1,0:T(8,128)(2,1)S(1)}, u32[]{:S(2)}, u32[]{:S(2)}) collective-permute-start(bf16[128,512]{1,0:T(8,128)(2,1)S(1)} %collective-permute-done.1.refs_12_), channel_id=1, source_target_pairs={{0,1},{1,0},{2,3},{3,2},{4,5},{5,4},{6,7},{7,6},{8,9},{9,8},{10,11... | collective-permute-start | bytes 393224 | tf_op jit(solution)/shard_map/ppermute | solution.py:241
  19.4 1.3 %collective-permute-done.5.refs_11_ = bf16[128,512]{1,0:T(8,128)(2,1)S(1)} collective-permute-done((bf16[128,512]{1,0:T(8,128)(2,1)}, bf16[128,512]{1,0:T(8,128)(2,1)S(1)}, u32[]{:S(2)}, u32[]{:S(2)}) %collective-permute-start.5) | collective-permute-done | bytes 131104 | tf_op jit(solution)/shard_map/ppermute | solution.py:241
  20.7 1.2 %collective-permute-start.9 = (bf16[3,128,512]{2,1,0:T(8,128)(2,1)S(1)}, bf16[3,128,512]{2,1,0:T(8,128)(2,1)S(1)}, u32[]{:S(2)}, u32[]{:S(2)}) collective-permute-start(bf16[3,128,512]{2,1,0:T(8,128)(2,1)S(1)} %get-tuple-element.23.refs_3_), channel_id=1, source_target_pairs={{0,2},{2,0},{1,3},{3,1},{4,6},{6,4},{5,7},{7,5},{8,10},{10,8},{9,1... | collective-permute-start | bytes 1179656 | tf_op jit(solution)/shard_map/ppermute | solution.py:233
  22.0 0.0 copy-start
  22.0 0.0 copy-start.1
  22.0 0.0 copy-start.2
  22.0 0.0 copy-start.3
  22.0 0.0 copy-start.4
  22.0 9.1 %edge_update.1 = (bf16[1536,512]{1,0:T(8,128)(2,1)}, bf16[384,512]{1,0:T(8,128)(2,1)S(1)}) custom-call(bf16[1536,512]{1,0:T(8,128)(2,1)} %refs_0_.2, bf16[768,1280]{1,0:T(8,128)(2,1)} %get-tuple-element.16.refs_1_, s32[12,128]{1,0:T(8,128)} %bitcast.17, bf16[768,1792]{1,0:T(8,128)(2,1)S(1)} %get-tuple-element.17.refs_3_, ...), custom_call_target="tpu_custom_call" | custom-call | flops 3825205248 | bytes 6291456 | tf_op jit(solution)/shard_map/edge_update/pallas_call | solution.py:478
  31.1 0.6 %collective-permute-start.7 = (bf16[384,512]{1,0:T(8,128)(2,1)S(1)}, bf16[384,512]{1,0:T(8,128)(2,1)S(1)}, u32[]{:S(2)}, u32[]{:S(2)}) collective-permute-start(bf16[384,512]{1,0:T(8,128)(2,1)S(1)} %get-tuple-element.22.refs_1_), channel_id=1, source_target_pairs={{0,1},{1,0},{2,3},{3,2},{4,5},{5,4},{6,7},{7,6},{8,9},{9,8},{10,11... | collective-permute-start | bytes 1179656 | tf_op jit(solution)/shard_map/ppermute | solution.py:512
  31.6 0.2 collective-permute-done.9.refs_5_
  31.9 1.1 %collective-permute-done.7.refs_2_ = bf16[384,512]{1,0:T(8,128)(2,1)S(1)} collective-permute-done((bf16[384,512]{1,0:T(8,128)(2,1)S(1)}, bf16[384,512]{1,0:T(8,128)(2,1)S(1)}, u32[]{:S(2)}, u32[]{:S(2)}) %collective-permute-start.7) | collective-permute-done | bytes 393248 | tf_op jit(solution)/shard_map/ppermute | solution.py:512
  33.0 0.6 %collective-permute-done.10.refs_6_ = bf16[3,128,512]{2,1,0:T(8,128)(2,1)S(1)} collective-permute-done((bf16[3,128,512]{2,1,0:T(8,128)(2,1)S(1)}, bf16[3,128,512]{2,1,0:T(8,128)(2,1)S(1)}, u32[]{:S(2)}, u32[]{:S(2)}) %collective-permute-start.10) | collective-permute-done | bytes 393248 | tf_op jit(solution)/shard_map/ppermute | solution.py:241
  33.6 2.0 %node_update.1 = bf16[384,512]{1,0:T(8,128)(2,1)} custom-call(bf16[384,512]{1,0:T(8,128)(2,1)S(1)} %copy-done, bf16[384,512]{1,0:T(8,128)(2,1)S(1)} %get-tuple-element.22.refs_1_, bf16[384,512]{1,0:T(8,128)(2,1)S(1)} %collective-permute-done.7.refs_2_, bf16[3,128,512]{2,1,0:T(8,128)(2,1)S(1)} %get-tuple-element.23.refs_3_, ...), custom_call_target="tpu_custom_call" | custom-call | flops 603979776 | bytes 1966080 | tf_op jit(solution)/shard_map/node_update/pallas_call | solution.py:515
  (14 shorter events, 0.0 us)
Async XLA Ops:
  0.6 17.8 %collective-permute-start = (bf16[3,128,512]{2,1,0:T(8,128)(2,1)}, bf16[3,128,512]{2,1,0:T(8,128)(2,1)}, u32[]{:S(2)}, u32[]{:S(2)}) collective-permute-start(bf16[3,128,512]{2,1,0:T(8,128)(2,1)} %refs_6_.1), channel_id=1, source_target_pairs={{0,2},{2,0},{1,3},{3,1},{4,6},{6,4},{5,7},{7,5},{8,10},{10,8},{9,1... | collective-permute-start | bytes 1179656 | tf_op jit(solution)/shard_map/ppermute | solution.py:233
  5.7 12.7 %all-to-all-start = ((bf16[8,17,512]{2,1,0:T(8,128)(2,1)}), bf16[8,17,512]{2,1,0:T(8,128)(2,1)S(1)}, u32[]{:S(2)}, u32[]{:S(2)}) async-start(bf16[8,17,512]{2,1,0:T(8,128)(2,1)} %pick_halo.1), calls=%async_computation | async-start | bytes 393216 | tf_op jit(solution)/shard_map/all_to_all | solution.py:109
  10.6 7.0 %collective-permute-start.1 = (bf16[128,512]{1,0:T(8,128)(2,1)}, bf16[128,512]{1,0:T(8,128)(2,1)S(1)}, u32[]{:S(2)}, u32[]{:S(2)}) collective-permute-start(bf16[128,512]{1,0:T(8,128)(2,1)} %refs_10_.1), channel_id=1, source_target_pairs={{0,2},{2,0},{1,3},{3,1},{4,6},{6,4},{5,7},{7,5},{8,10},{10,8},{9,1... | collective-permute-start | bytes 393224 | tf_op jit(solution)/shard_map/ppermute | solution.py:233
  12.6 9.3 %collective-permute-start.3 = (bf16[3,128,512]{2,1,0:T(8,128)(2,1)}, bf16[3,128,512]{2,1,0:T(8,128)(2,1)}, u32[]{:S(2)}, u32[]{:S(2)}) collective-permute-start(bf16[3,128,512]{2,1,0:T(8,128)(2,1)} %refs_6_.1), channel_id=1, source_target_pairs={{0,1},{1,0},{2,3},{3,2},{4,5},{5,4},{6,7},{7,6},{8,9},{9,8},{10,11... | collective-permute-start | bytes 1179656 | tf_op jit(solution)/shard_map/ppermute | solution.py:241
  18.4 3.6 %collective-permute-start.4 = (bf16[3,128,512]{2,1,0:T(8,128)(2,1)}, bf16[3,128,512]{2,1,0:T(8,128)(2,1)S(1)}, u32[]{:S(2)}, u32[]{:S(2)}) collective-permute-start(bf16[3,128,512]{2,1,0:T(8,128)(2,1)} %collective-permute-done.refs_8_), channel_id=1, source_target_pairs={{0,1},{1,0},{2,3},{3,2},{4,5},{5,4},{6,7},{7,6},{8,9},{9,8},{10,11... | collective-permute-start | bytes 1179656 | tf_op jit(solution)/shard_map/ppermute | solution.py:241
  18.4 2.3 %collective-permute-start.5 = (bf16[128,512]{1,0:T(8,128)(2,1)}, bf16[128,512]{1,0:T(8,128)(2,1)S(1)}, u32[]{:S(2)}, u32[]{:S(2)}) collective-permute-start(bf16[128,512]{1,0:T(8,128)(2,1)} %refs_10_.1), channel_id=1, source_target_pairs={{0,1},{1,0},{2,3},{3,2},{4,5},{5,4},{6,7},{7,6},{8,9},{9,8},{10,11... | collective-permute-start | bytes 393224 | tf_op jit(solution)/shard_map/ppermute | solution.py:241
  18.9 3.1 %collective-permute-start.2 = (bf16[8,17,512]{2,1,0:T(8,128)(2,1)S(1)}, bf16[8,17,512]{2,1,0:T(8,128)(2,1)S(1)}, u32[]{:S(2)}, u32[]{:S(2)}) collective-permute-start(bf16[8,17,512]{2,1,0:T(8,128)(2,1)S(1)} %all-to-all-done.refs_4_), channel_id=1, source_target_pairs={{0,1},{1,0},{2,3},{3,2},{4,5},{5,4},{6,7},{7,6},{8,9},{9,8},{10,11... | collective-permute-start | bytes 417800 | tf_op jit(solution)/shard_map/ppermute | solution.py:241
  18.9 3.0 %collective-permute-start.6 = (bf16[128,512]{1,0:T(8,128)(2,1)S(1)}, bf16[128,512]{1,0:T(8,128)(2,1)S(1)}, u32[]{:S(2)}, u32[]{:S(2)}) collective-permute-start(bf16[128,512]{1,0:T(8,128)(2,1)S(1)} %collective-permute-done.1.refs_12_), channel_id=1, source_target_pairs={{0,1},{1,0},{2,3},{3,2},{4,5},{5,4},{6,7},{7,6},{8,9},{9,8},{10,11... | collective-permute-start | bytes 393224 | tf_op jit(solution)/shard_map/ppermute | solution.py:241
  20.7 11.2 %collective-permute-start.9 = (bf16[3,128,512]{2,1,0:T(8,128)(2,1)S(1)}, bf16[3,128,512]{2,1,0:T(8,128)(2,1)S(1)}, u32[]{:S(2)}, u32[]{:S(2)}) collective-permute-start(bf16[3,128,512]{2,1,0:T(8,128)(2,1)S(1)} %get-tuple-element.23.refs_3_), channel_id=1, source_target_pairs={{0,2},{2,0},{1,3},{3,1},{4,6},{6,4},{5,7},{7,5},{8,10},{10,8},{9,1... | collective-permute-start | bytes 1179656 | tf_op jit(solution)/shard_map/ppermute | solution.py:233
  21.9 9.9 %collective-permute-start.8 = (bf16[3,128,512]{2,1,0:T(8,128)(2,1)S(1)}, bf16[3,128,512]{2,1,0:T(8,128)(2,1)S(1)}, u32[]{:S(2)}, u32[]{:S(2)}) collective-permute-start(bf16[3,128,512]{2,1,0:T(8,128)(2,1)S(1)} %get-tuple-element.23.refs_3_), channel_id=1, source_target_pairs={{0,1},{1,0},{2,3},{3,2},{4,5},{5,4},{6,7},{7,6},{8,9},{9,8},{10,11... | collective-permute-start | bytes 1179656 | tf_op jit(solution)/shard_map/ppermute | solution.py:241
  22.0 11.6 %copy-start = (bf16[384,512]{1,0:T(8,128)(2,1)S(1)}, bf16[384,512]{1,0:T(8,128)(2,1)}, u32[]{:S(2)}) copy-start(bf16[384,512]{1,0:T(8,128)(2,1)} %refs_0_.3) | copy-start | bytes 1179652
  22.0 11.6 %copy-start.1 = (f32[512]{0:T(512)S(1)}, f32[512]{0:T(512)}, u32[]{:S(2)}) copy-start(f32[512]{0:T(512)} %param.32) | copy-start | bytes 6148
  22.0 11.6 %copy-start.2 = (f32[512]{0:T(512)S(1)}, f32[512]{0:T(512)}, u32[]{:S(2)}) copy-start(f32[512]{0:T(512)} %param.33) | copy-start | bytes 6148
  22.0 11.6 %copy-start.3 = (f32[512]{0:T(512)S(1)}, f32[512]{0:T(512)}, u32[]{:S(2)}) copy-start(f32[512]{0:T(512)} %param.34) | copy-start | bytes 6148
  22.0 11.6 %copy-start.4 = (f32[512]{0:T(512)S(1)}, f32[512]{0:T(512)}, u32[]{:S(2)}) copy-start(f32[512]{0:T(512)} %param.35) | copy-start | bytes 6148
  31.1 1.9 %collective-permute-start.7 = (bf16[384,512]{1,0:T(8,128)(2,1)S(1)}, bf16[384,512]{1,0:T(8,128)(2,1)S(1)}, u32[]{:S(2)}, u32[]{:S(2)}) collective-permute-start(bf16[384,512]{1,0:T(8,128)(2,1)S(1)} %get-tuple-element.22.refs_1_), channel_id=1, source_target_pairs={{0,1},{1,0},{2,3},{3,2},{4,5},{5,4},{6,7},{7,6},{8,9},{9,8},{10,11... | collective-permute-start | bytes 1179656 | tf_op jit(solution)/shard_map/ppermute | solution.py:512
  31.8 1.7 %collective-permute-start.10 = (bf16[3,128,512]{2,1,0:T(8,128)(2,1)S(1)}, bf16[3,128,512]{2,1,0:T(8,128)(2,1)S(1)}, u32[]{:S(2)}, u32[]{:S(2)}) collective-permute-start(bf16[3,128,512]{2,1,0:T(8,128)(2,1)S(1)} %collective-permute-done.9.refs_5_), channel_id=1, source_target_pairs={{0,1},{1,0},{2,3},{3,2},{4,5},{5,4},{6,7},{7,6},{8,9},{9,8},{10,11... | collective-permute-start | bytes 1179656 | tf_op jit(solution)/shard_map/ppermute | solution.py:241

commit v13 on v12

--- a/solution.py
+++ b/solution.py
@@ -286,6 +286,11 @@
     def known(at):
         return known_first if at == 0 else known_rest.at[pl.ds((at - 1) * block, block)]
 
+    node_place = lax.broadcasted_iota(jnp.int32, (to_node.shape[0], lanes), 0)
+    for row in range(edge_count // lanes):
+        to_node[:, row * lanes : (row + 1) * lanes] = jnp.where(
+            node_place == receiver_ref[row : row + 1], 1.0, 0.0
+        ).astype(bf16)
     place_halo(halo, part_count, near_cap, halved, got_refs)
     for which in (1, 0, 2):
         for piece, owner in zip(in_pieces[1:], order[1:]):
@@ -338,24 +343,16 @@
         else:
             sum_ref[...] = part.astype(bf16)
 
+    out_copies = []
     in_dot(0)
-    node_place = lax.broadcasted_iota(jnp.int32, (to_node.shape[0], lanes), 0)
-    for row in range(edge_count // lanes):
-        to_node[:, row * lanes : (row + 1) * lanes] = jnp.where(
-            node_place == receiver_ref[row : row + 1], 1.0, 0.0
-        ).astype(bf16)
-    for at in range(1, blocks):
-        in_dot(at)
-        activate(at - 1)
-    out_dot(0)
-    activate(blocks - 1)
-    for at in range(1, blocks):
+    for at in range(blocks):
+        if at + 1 < blocks:
+            in_dot(at + 1)
+        activate(at)
         out_dot(at)
-    out_copies = []
-    for at in range(blocks):
-        out_copies.append(normalise(at))
         if at > 0:
             sum_dot(at - 1)
+        out_copies.append(normalise(at))
     sum_dot(blocks - 1)
     for copy in out_copies:
         copy.wait()

time: 35.9 us -> 35.9 us (level)
  Pallas kernels: 16.4 us -> 16 us
  transfers between devices with their start and end apart: 12 -> 12, of which waited for: 6 -> 6; matrix products, arithmetic and copies ran while one was open for 0% -> 0% of each run, Pallas kernels for 40% -> 39%
where the time goes in v13:
time: 35.9 us; the launch traced here: 35.6 us
  Pallas kernels  16 us (45%)
  starting transfers between devices  12.7 us (35%)
  waiting for transfers between devices  6.09 us (17%)
  between operations  0.74 us (2%)
    pallas_call x1, Pallas kernels, shards(): pl.pallas_call(functools.partial(edge_kernel, pieces_count, len(got), par...  8.71 us
    ppermute x3, starting transfers between devices, from_feats(): lax.ppermute(weight, 'feat', [(at, (at + shift) % feats) for at in range(...  6.26 us
    all_to_all x1, starting transfers between devices, exchange_halves(): lax.all_to_all(blocks, ('region', 'feat'), split_axis=0, concat_axis=0, t...  4.88 us
    pallas_call x1, Pallas kernels, shards(): pl.pallas_call(functools.partial(gather_kernel, near_cap, far_cap, halved...  3.23 us
    ppermute x3, waiting for transfers between devices, from_feats(): lax.ppermute(weight, 'feat', [(at, (at + shift) % feats) for at in range(...  2.31 us
    ppermute x7, waiting for transfers between devices, from_subs(): lax.ppermute(piece, 'sub', [(at, (at + turn) % subs) for at in range(subs)])  2.22 us
    pallas_call x1, Pallas kernels, exchange_halves(): pl.pallas_call(functools.partial(pick_kernel, part_count, near_cap, far_c...  2.08 us
    pallas_call x1, Pallas kernels, shards(): pl.pallas_call(functools.partial(node_kernel, pieces_count), out_shape=ja...  2.01 us
  transfers between devices with their start and end apart: 12, of which 6 were waited for; matrix products, arithmetic and copies ran while one was open for 0% of the time, Pallas kernels for 39%

profile of v13, /device:TPU:0, one launch (start us, length us, event | category | flops | bytes accessed | tf_op | source)
XLA Modules:
  0.0 35.6 jit_solution(364477830415544342)
XLA Ops:
  0.6 3.0 %collective-permute-start = (bf16[3,128,512]{2,1,0:T(8,128)(2,1)}, bf16[3,128,512]{2,1,0:T(8,128)(2,1)}, u32[]{:S(2)}, u32[]{:S(2)}) collective-permute-start(bf16[3,128,512]{2,1,0:T(8,128)(2,1)} %refs_6_.1), channel_id=1, source_target_pairs={{0,2},{2,0},{1,3},{3,1},{4,6},{6,4},{5,7},{7,5},{8,10},{10,8},{9,1... | collective-permute-start | bytes 1179656 | tf_op jit(solution)/shard_map/ppermute | solution.py:233
  3.6 2.1 %pick_halo.1 = bf16[8,17,512]{2,1,0:T(8,128)(2,1)} custom-call(s32[1,2,8]{2,1,0:T(2,128)} %bitcast.18, s32[1,4,32]{2,1,0:T(4,128)} %near_ref.1, bf16[384,512]{1,0:T(8,128)(2,1)} %refs_0_.3), custom_call_target="tpu_custom_call" | custom-call | tf_op jit(solution)/shard_map/pick_halo/pallas_call | solution.py:99
  5.7 4.9 %all-to-all-start = ((bf16[8,17,512]{2,1,0:T(8,128)(2,1)}), bf16[8,17,512]{2,1,0:T(8,128)(2,1)S(1)}, u32[]{:S(2)}, u32[]{:S(2)}) async-start(bf16[8,17,512]{2,1,0:T(8,128)(2,1)} %pick_halo.1), calls=%async_computation | async-start | bytes 393216 | tf_op jit(solution)/shard_map/all_to_all | solution.py:109
  10.6 2.0 %collective-permute-start.1 = (bf16[128,512]{1,0:T(8,128)(2,1)}, bf16[128,512]{1,0:T(8,128)(2,1)S(1)}, u32[]{:S(2)}, u32[]{:S(2)}) collective-permute-start(bf16[128,512]{1,0:T(8,128)(2,1)} %refs_10_.1), channel_id=1, source_target_pairs={{0,2},{2,0},{1,3},{3,1},{4,6},{6,4},{5,7},{7,5},{8,10},{10,8},{9,1... | collective-permute-start | bytes 393224 | tf_op jit(solution)/shard_map/ppermute | solution.py:233
  12.6 0.0 collective-permute-start.3
  12.6 3.2 %gather_latents.1 = (bf16[768,1792]{1,0:T(8,128)(2,1)S(1)}, bf16[768,1280]{1,0:T(8,128)(2,1)}, bf16[3,128,512]{2,1,0:T(8,128)(2,1)S(1)}) custom-call(s32[12,128]{1,0:T(8,128)} %bitcast.15, s32[12,128]{1,0:T(8,128)} %bitcast.16, bf16[384,512]{1,0:T(8,128)(2,1)} %refs_0_.3, bf16[2,128,512]{2,1,0:T(8,128)(2,1)} %node_in_ref.1, bf16[128,512]{1,0:T(8,128)(2,1)} %node_out_ref.1, ...), custom_call_target="tpu_custom_call" | custom-call | tf_op jit(solution)/shard_map/gather_latents/pallas_call | solution.py:427
  15.9 1.8 %collective-permute-done.1.refs_12_ = bf16[128,512]{1,0:T(8,128)(2,1)S(1)} collective-permute-done((bf16[128,512]{1,0:T(8,128)(2,1)}, bf16[128,512]{1,0:T(8,128)(2,1)S(1)}, u32[]{:S(2)}, u32[]{:S(2)}) %collective-permute-start.1) | collective-permute-done | bytes 131104 | tf_op jit(solution)/shard_map/ppermute | solution.py:233
  17.6 0.8 %all-to-all-done.refs_4_ = bf16[8,17,512]{2,1,0:T(8,128)(2,1)S(1)} async-done(((bf16[8,17,512]{2,1,0:T(8,128)(2,1)}), bf16[8,17,512]{2,1,0:T(8,128)(2,1)S(1)}, u32[]{:S(2)}, u32[]{:S(2)}) %all-to-all-start) | async-done | bytes 139296 | tf_op jit(solution)/shard_map/all_to_all | solution.py:109
  18.4 0.5 %collective-permute-start.5 = (bf16[128,512]{1,0:T(8,128)(2,1)}, bf16[128,512]{1,0:T(8,128)(2,1)S(1)}, u32[]{:S(2)}, u32[]{:S(2)}) collective-permute-start(bf16[128,512]{1,0:T(8,128)(2,1)} %refs_10_.1), channel_id=1, source_target_pairs={{0,1},{1,0},{2,3},{3,2},{4,5},{5,4},{6,7},{7,6},{8,9},{9,8},{10,11... | collective-permute-start | bytes 393224 | tf_op jit(solution)/shard_map/ppermute | solution.py:241
  18.9 0.0 collective-permute-start.2
  18.9 0.5 %collective-permute-start.6 = (bf16[128,512]{1,0:T(8,128)(2,1)S(1)}, bf16[128,512]{1,0:T(8,128)(2,1)S(1)}, u32[]{:S(2)}, u32[]{:S(2)}) collective-permute-start(bf16[128,512]{1,0:T(8,128)(2,1)S(1)} %collective-permute-done.1.refs_12_), channel_id=1, source_target_pairs={{0,1},{1,0},{2,3},{3,2},{4,5},{5,4},{6,7},{7,6},{8,9},{9,8},{10,11... | collective-permute-start | bytes 393224 | tf_op jit(solution)/shard_map/ppermute | solution.py:241
  19.4 1.3 %collective-permute-done.5.refs_11_ = bf16[128,512]{1,0:T(8,128)(2,1)S(1)} collective-permute-done((bf16[128,512]{1,0:T(8,128)(2,1)}, bf16[128,512]{1,0:T(8,128)(2,1)S(1)}, u32[]{:S(2)}, u32[]{:S(2)}) %collective-permute-start.5) | collective-permute-done | bytes 131104 | tf_op jit(solution)/shard_map/ppermute | solution.py:241
  20.7 1.2 %collective-permute-start.9 = (bf16[3,128,512]{2,1,0:T(8,128)(2,1)S(1)}, bf16[3,128,512]{2,1,0:T(8,128)(2,1)S(1)}, u32[]{:S(2)}, u32[]{:S(2)}) collective-permute-start(bf16[3,128,512]{2,1,0:T(8,128)(2,1)S(1)} %get-tuple-element.23.refs_3_), channel_id=1, source_target_pairs={{0,2},{2,0},{1,3},{3,1},{4,6},{6,4},{5,7},{7,5},{8,10},{10,8},{9,1... | collective-permute-start | bytes 1179656 | tf_op jit(solution)/shard_map/ppermute | solution.py:233
  22.0 0.0 copy-start
  22.0 0.0 copy-start.1
  22.0 0.0 copy-start.2
  22.0 0.0 copy-start.3
  22.0 0.0 copy-start.4
  22.0 8.7 %edge_update.1 = (bf16[1536,512]{1,0:T(8,128)(2,1)}, bf16[384,512]{1,0:T(8,128)(2,1)S(1)}) custom-call(bf16[1536,512]{1,0:T(8,128)(2,1)} %refs_0_.2, bf16[768,1280]{1,0:T(8,128)(2,1)} %get-tuple-element.16.refs_1_, s32[12,128]{1,0:T(8,128)} %bitcast.17, bf16[768,1792]{1,0:T(8,128)(2,1)S(1)} %get-tuple-element.17.refs_3_, ...), custom_call_target="tpu_custom_call" | custom-call | flops 3825205248 | bytes 6291456 | tf_op jit(solution)/shard_map/edge_update/pallas_call | solution.py:475
  30.7 0.6 %collective-permute-start.7 = (bf16[384,512]{1,0:T(8,128)(2,1)S(1)}, bf16[384,512]{1,0:T(8,128)(2,1)S(1)}, u32[]{:S(2)}, u32[]{:S(2)}) collective-permute-start(bf16[384,512]{1,0:T(8,128)(2,1)S(1)} %get-tuple-element.22.refs_1_), channel_id=1, source_target_pairs={{0,1},{1,0},{2,3},{3,2},{4,5},{5,4},{6,7},{7,6},{8,9},{9,8},{10,11... | collective-permute-start | bytes 1179656 | tf_op jit(solution)/shard_map/ppermute | solution.py:509
  31.3 0.5 %collective-permute-done.9.refs_5_ = bf16[3,128,512]{2,1,0:T(8,128)(2,1)S(1)} collective-permute-done((bf16[3,128,512]{2,1,0:T(8,128)(2,1)S(1)}, bf16[3,128,512]{2,1,0:T(8,128)(2,1)S(1)}, u32[]{:S(2)}, u32[]{:S(2)}) %collective-permute-start.9) | collective-permute-done | bytes 393248 | tf_op jit(solution)/shard_map/ppermute | solution.py:233
  31.9 0.8 %collective-permute-done.7.refs_2_ = bf16[384,512]{1,0:T(8,128)(2,1)S(1)} collective-permute-done((bf16[384,512]{1,0:T(8,128)(2,1)S(1)}, bf16[384,512]{1,0:T(8,128)(2,1)S(1)}, u32[]{:S(2)}, u32[]{:S(2)}) %collective-permute-start.7) | collective-permute-done | bytes 393248 | tf_op jit(solution)/shard_map/ppermute | solution.py:509
  32.7 0.9 %collective-permute-done.10.refs_6_ = bf16[3,128,512]{2,1,0:T(8,128)(2,1)S(1)} collective-permute-done((bf16[3,128,512]{2,1,0:T(8,128)(2,1)S(1)}, bf16[3,128,512]{2,1,0:T(8,128)(2,1)S(1)}, u32[]{:S(2)}, u32[]{:S(2)}) %collective-permute-start.10) | collective-permute-done | bytes 393248 | tf_op jit(solution)/shard_map/ppermute | solution.py:241
  33.6 2.0 %node_update.1 = bf16[384,512]{1,0:T(8,128)(2,1)} custom-call(bf16[384,512]{1,0:T(8,128)(2,1)S(1)} %copy-done, bf16[384,512]{1,0:T(8,128)(2,1)S(1)} %get-tuple-element.22.refs_1_, bf16[384,512]{1,0:T(8,128)(2,1)S(1)} %collective-permute-done.7.refs_2_, bf16[3,128,512]{2,1,0:T(8,128)(2,1)S(1)} %get-tuple-element.23.refs_3_, ...), custom_call_target="tpu_custom_call" | custom-call | flops 603979776 | bytes 1966080 | tf_op jit(solution)/shard_map/node_update/pallas_call | solution.py:512
  (14 shorter events, 0.0 us)
Async XLA Ops:
  0.6 17.8 %collective-permute-start = (bf16[3,128,512]{2,1,0:T(8,128)(2,1)}, bf16[3,128,512]{2,1,0:T(8,128)(2,1)}, u32[]{:S(2)}, u32[]{:S(2)}) collective-permute-start(bf16[3,128,512]{2,1,0:T(8,128)(2,1)} %refs_6_.1), channel_id=1, source_target_pairs={{0,2},{2,0},{1,3},{3,1},{4,6},{6,4},{5,7},{7,5},{8,10},{10,8},{9,1... | collective-permute-start | bytes 1179656 | tf_op jit(solution)/shard_map/ppermute | solution.py:233
  5.7 12.7 %all-to-all-start = ((bf16[8,17,512]{2,1,0:T(8,128)(2,1)}), bf16[8,17,512]{2,1,0:T(8,128)(2,1)S(1)}, u32[]{:S(2)}, u32[]{:S(2)}) async-start(bf16[8,17,512]{2,1,0:T(8,128)(2,1)} %pick_halo.1), calls=%async_computation | async-start | bytes 393216 | tf_op jit(solution)/shard_map/all_to_all | solution.py:109
  10.6 7.0 %collective-permute-start.1 = (bf16[128,512]{1,0:T(8,128)(2,1)}, bf16[128,512]{1,0:T(8,128)(2,1)S(1)}, u32[]{:S(2)}, u32[]{:S(2)}) collective-permute-start(bf16[128,512]{1,0:T(8,128)(2,1)} %refs_10_.1), channel_id=1, source_target_pairs={{0,2},{2,0},{1,3},{3,1},{4,6},{6,4},{5,7},{7,5},{8,10},{10,8},{9,1... | collective-permute-start | bytes 393224 | tf_op jit(solution)/shard_map/ppermute | solution.py:233
  12.6 9.3 %collective-permute-start.3 = (bf16[3,128,512]{2,1,0:T(8,128)(2,1)}, bf16[3,128,512]{2,1,0:T(8,128)(2,1)}, u32[]{:S(2)}, u32[]{:S(2)}) collective-permute-start(bf16[3,128,512]{2,1,0:T(8,128)(2,1)} %refs_6_.1), channel_id=1, source_target_pairs={{0,1},{1,0},{2,3},{3,2},{4,5},{5,4},{6,7},{7,6},{8,9},{9,8},{10,11... | collective-permute-start | bytes 1179656 | tf_op jit(solution)/shard_map/ppermute | solution.py:241
  18.4 3.6 %collective-permute-start.4 = (bf16[3,128,512]{2,1,0:T(8,128)(2,1)}, bf16[3,128,512]{2,1,0:T(8,128)(2,1)S(1)}, u32[]{:S(2)}, u32[]{:S(2)}) collective-permute-start(bf16[3,128,512]{2,1,0:T(8,128)(2,1)} %collective-permute-done.refs_8_), channel_id=1, source_target_pairs={{0,1},{1,0},{2,3},{3,2},{4,5},{5,4},{6,7},{7,6},{8,9},{9,8},{10,11... | collective-permute-start | bytes 1179656 | tf_op jit(solution)/shard_map/ppermute | solution.py:241
  18.4 2.3 %collective-permute-start.5 = (bf16[128,512]{1,0:T(8,128)(2,1)}, bf16[128,512]{1,0:T(8,128)(2,1)S(1)}, u32[]{:S(2)}, u32[]{:S(2)}) collective-permute-start(bf16[128,512]{1,0:T(8,128)(2,1)} %refs_10_.1), channel_id=1, source_target_pairs={{0,1},{1,0},{2,3},{3,2},{4,5},{5,4},{6,7},{7,6},{8,9},{9,8},{10,11... | collective-permute-start | bytes 393224 | tf_op jit(solution)/shard_map/ppermute | solution.py:241
  18.9 3.1 %collective-permute-start.2 = (bf16[8,17,512]{2,1,0:T(8,128)(2,1)S(1)}, bf16[8,17,512]{2,1,0:T(8,128)(2,1)S(1)}, u32[]{:S(2)}, u32[]{:S(2)}) collective-permute-start(bf16[8,17,512]{2,1,0:T(8,128)(2,1)S(1)} %all-to-all-done.refs_4_), channel_id=1, source_target_pairs={{0,1},{1,0},{2,3},{3,2},{4,5},{5,4},{6,7},{7,6},{8,9},{9,8},{10,11... | collective-permute-start | bytes 417800 | tf_op jit(solution)/shard_map/ppermute | solution.py:241
  18.9 3.0 %collective-permute-start.6 = (bf16[128,512]{1,0:T(8,128)(2,1)S(1)}, bf16[128,512]{1,0:T(8,128)(2,1)S(1)}, u32[]{:S(2)}, u32[]{:S(2)}) collective-permute-start(bf16[128,512]{1,0:T(8,128)(2,1)S(1)} %collective-permute-done.1.refs_12_), channel_id=1, source_target_pairs={{0,1},{1,0},{2,3},{3,2},{4,5},{5,4},{6,7},{7,6},{8,9},{9,8},{10,11... | collective-permute-start | bytes 393224 | tf_op jit(solution)/shard_map/ppermute | solution.py:241
  20.7 11.2 %collective-permute-start.9 = (bf16[3,128,512]{2,1,0:T(8,128)(2,1)S(1)}, bf16[3,128,512]{2,1,0:T(8,128)(2,1)S(1)}, u32[]{:S(2)}, u32[]{:S(2)}) collective-permute-start(bf16[3,128,512]{2,1,0:T(8,128)(2,1)S(1)} %get-tuple-element.23.refs_3_), channel_id=1, source_target_pairs={{0,2},{2,0},{1,3},{3,1},{4,6},{6,4},{5,7},{7,5},{8,10},{10,8},{9,1... | collective-permute-start | bytes 1179656 | tf_op jit(solution)/shard_map/ppermute | solution.py:233
  21.9 9.9 %collective-permute-start.8 = (bf16[3,128,512]{2,1,0:T(8,128)(2,1)S(1)}, bf16[3,128,512]{2,1,0:T(8,128)(2,1)S(1)}, u32[]{:S(2)}, u32[]{:S(2)}) collective-permute-start(bf16[3,128,512]{2,1,0:T(8,128)(2,1)S(1)} %get-tuple-element.23.refs_3_), channel_id=1, source_target_pairs={{0,1},{1,0},{2,3},{3,2},{4,5},{5,4},{6,7},{7,6},{8,9},{9,8},{10,11... | collective-permute-start | bytes 1179656 | tf_op jit(solution)/shard_map/ppermute | solution.py:241
  22.0 11.6 %copy-start = (bf16[384,512]{1,0:T(8,128)(2,1)S(1)}, bf16[384,512]{1,0:T(8,128)(2,1)}, u32[]{:S(2)}) copy-start(bf16[384,512]{1,0:T(8,128)(2,1)} %refs_0_.3) | copy-start | bytes 1179652
  22.0 11.6 %copy-start.1 = (f32[512]{0:T(512)S(1)}, f32[512]{0:T(512)}, u32[]{:S(2)}) copy-start(f32[512]{0:T(512)} %param.32) | copy-start | bytes 6148
  22.0 11.6 %copy-start.2 = (f32[512]{0:T(512)S(1)}, f32[512]{0:T(512)}, u32[]{:S(2)}) copy-start(f32[512]{0:T(512)} %param.33) | copy-start | bytes 6148
  22.0 11.6 %copy-start.3 = (f32[512]{0:T(512)S(1)}, f32[512]{0:T(512)}, u32[]{:S(2)}) copy-start(f32[512]{0:T(512)} %param.34) | copy-start | bytes 6148
  22.0 11.6 %copy-start.4 = (f32[512]{0:T(512)S(1)}, f32[512]{0:T(512)}, u32[]{:S(2)}) copy-start(f32[512]{0:T(512)} %param.35) | copy-start | bytes 6148
  30.7 1.9 %collective-permute-start.7 = (bf16[384,512]{1,0:T(8,128)(2,1)S(1)}, bf16[384,512]{1,0:T(8,128)(2,1)S(1)}, u32[]{:S(2)}, u32[]{:S(2)}) collective-permute-start(bf16[384,512]{1,0:T(8,128)(2,1)S(1)} %get-tuple-element.22.refs_1_), channel_id=1, source_target_pairs={{0,1},{1,0},{2,3},{3,2},{4,5},{5,4},{6,7},{7,6},{8,9},{9,8},{10,11... | collective-permute-start | bytes 1179656 | tf_op jit(solution)/shard_map/ppermute | solution.py:509
  31.8 1.7 %collective-permute-start.10 = (bf16[3,128,512]{2,1,0:T(8,128)(2,1)S(1)}, bf16[3,128,512]{2,1,0:T(8,128)(2,1)S(1)}, u32[]{:S(2)}, u32[]{:S(2)}) collective-permute-start(bf16[3,128,512]{2,1,0:T(8,128)(2,1)S(1)} %collective-permute-done.9.refs_5_), channel_id=1, source_target_pairs={{0,1},{1,0},{2,3},{3,2},{4,5},{5,4},{6,7},{7,6},{8,9},{9,8},{10,11... | collective-permute-start | bytes 1179656 | tf_op jit(solution)/shard_map/ppermute | solution.py:241

commit v14 on v13

--- a/solution.py
+++ b/solution.py
@@ -421,6 +421,7 @@
     receiver_rows = in_hbm(receivers.reshape(-1, lanes))
 
     pack_shape = (node_in_weight.shape[0] + 1,) + node_out_weight.shape
+    near_edge[1], latent_after = lax.optimization_barrier((near_edge[1], node_latent))
     gathered_width = 2 * width + halo_space
     known_width = width + gathered_width
     rest = edge_count - block
@@ -443,15 +444,13 @@
     )(
         source_rows,
         receiver_rows,
-        in_hbm(node_latent),
+        in_hbm(latent_after),
         in_hbm(node_in_weight),
         in_hbm(node_out_weight),
         in_hbm(edge_latent),
     )
 
-    far_edge, got, known, gathered, node_weight = lax.optimization_barrier(
-        (far_edge, got, known, gathered, node_weight)
-    )
+    far_edge, got, known, gathered = lax.optimization_barrier((far_edge, got, known, gathered))
     if halved:
         got = got + from_subs(got)
     edge_in, edge_out = [
@@ -497,11 +496,7 @@
             pltpu.SemaphoreType.DMA((copy_count,)),
         ],
         compiler_params=pltpu.CompilerParams(vmem_limit_bytes=grant),
-        cost_estimate=pl.CostEstimate(
-            flops=2 * edge_count * width * (4 * width + node_count),
-            bytes_accessed=8 * edge_count * width,
-            transcendentals=edge_count * width,
-        ),
+        cost_estimate=pl.CostEstimate(flops=0, bytes_accessed=0, transcendentals=0),
         name="edge_update",
     )(*edge_operands)
 

time: 35.9 us -> 42.6 us (1.19)
  waiting for transfers between devices: 6.09 us -> 10.6 us
  Pallas kernels: 16 us -> 17.8 us
    ppermute x3, waiting for transfers between devices: 2.31 us -> 9.26 us  [from_feats(): lax.ppermute(weight, 'feat', [(at, (at + shift) % feats) for at in range(...]
    ppermute x7, waiting for transfers between devices: 2.22 us -> 0.02 us  [from_subs(): lax.ppermute(piece, 'sub', [(at, (at + turn) % subs) for at in range(subs)])]
    pallas_call x1, Pallas kernels: 2.01 us -> 3.12 us  [shards(): pl.pallas_call(functools.partial(node_kernel, pieces_count), out_shape=ja...]
    all_to_all x1, waiting for transfers between devices: 0.76 us -> 0.01 us  [exchange_halves(): lax.all_to_all(blocks, ('region', 'feat'), split_axis=0, concat_axis=0, t...]
    pallas_call x1, Pallas kernels: 3.23 us -> 3.97 us  [shards(): pl.pallas_call(functools.partial(gather_kernel, near_cap, far_cap, halved...]
    ppermute x1, waiting for transfers between devices: 0.79 us -> 1.34 us  [shards(): lax.ppermute(partial_sums, 'sub', [(at, (at + 1) % subs) for at in range(...]
  transfers between devices with their start and end apart: 12 -> 12, of which waited for: 6 -> 3; matrix products, arithmetic and copies ran while one was open for 0% -> 0% of each run, Pallas kernels for 39% -> 35%
where the time goes in v14:
time: 42.6 us; the launch traced here: 42.3 us
  Pallas kernels  17.8 us (42%)
  starting transfers between devices  13.1 us (31%)
  waiting for transfers between devices  10.6 us (25%)
  between operations  0.74 us (2%)
    ppermute x3, waiting for transfers between devices, from_feats(): lax.ppermute(weight, 'feat', [(at, (at + shift) % feats) for at in range(...  9.26 us
    pallas_call x1, Pallas kernels, shards(): pl.pallas_call(functools.partial(edge_kernel, pieces_count, len(got), par...  8.63 us
    ppermute x3, starting transfers between devices, from_feats(): lax.ppermute(weight, 'feat', [(at, (at + shift) % feats) for at in range(...  6.41 us
    all_to_all x1, starting transfers between devices, exchange_halves(): lax.all_to_all(blocks, ('region', 'feat'), split_axis=0, concat_axis=0, t...  4.88 us
    pallas_call x1, Pallas kernels, shards(): pl.pallas_call(functools.partial(gather_kernel, near_cap, far_cap, halved...  3.97 us
    pallas_call x1, Pallas kernels, shards(): pl.pallas_call(functools.partial(node_kernel, pieces_count), out_shape=ja...  3.12 us
    pallas_call x1, Pallas kernels, exchange_halves(): pl.pallas_call(functools.partial(pick_kernel, part_count, near_cap, far_c...  2.08 us
    ppermute x1, waiting for transfers between devices, shards(): lax.ppermute(partial_sums, 'sub', [(at, (at + 1) % subs) for at in range(...  1.34 us
  transfers between devices with their start and end apart: 12, of which 3 were waited for; matrix products, arithmetic and copies ran while one was open for 0% of the time, Pallas kernels for 35%

profile of v14, /device:TPU:0, one launch (start us, length us, event | category | flops | bytes accessed | tf_op | source)
XLA Modules:
  0.0 42.3 jit_solution(5543114375505994196)
XLA Ops:
  0.6 3.0 %collective-permute-start = (bf16[3,128,512]{2,1,0:T(8,128)(2,1)}, bf16[3,128,512]{2,1,0:T(8,128)(2,1)S(1)}, u32[]{:S(2)}, u32[]{:S(2)}) collective-permute-start(bf16[3,128,512]{2,1,0:T(8,128)(2,1)} %refs_6_.1), channel_id=1, source_target_pairs={{0,2},{2,0},{1,3},{3,1},{4,6},{6,4},{5,7},{7,5},{8,10},{10,8},{9,1... | collective-permute-start | bytes 1179656 | tf_op jit(solution)/shard_map/ppermute | solution.py:233
  3.6 2.1 %pick_halo.1 = bf16[8,17,512]{2,1,0:T(8,128)(2,1)} custom-call(s32[1,2,8]{2,1,0:T(2,128)} %bitcast.22, s32[1,4,32]{2,1,0:T(4,128)} %near_ref.1, bf16[384,512]{1,0:T(8,128)(2,1)} %refs_0_.3), custom_call_target="tpu_custom_call" | custom-call | tf_op jit(solution)/shard_map/pick_halo/pallas_call | solution.py:99
  5.7 4.9 %all-to-all-start = ((bf16[8,17,512]{2,1,0:T(8,128)(2,1)}), bf16[8,17,512]{2,1,0:T(8,128)(2,1)S(1)}, u32[]{:S(2)}, u32[]{:S(2)}) async-start(bf16[8,17,512]{2,1,0:T(8,128)(2,1)} %pick_halo.1), calls=%async_computation | async-start | bytes 393216 | tf_op jit(solution)/shard_map/all_to_all | solution.py:109
  10.6 0.0 collective-permute-start.2
  10.6 2.0 %collective-permute-start.1 = (bf16[128,512]{1,0:T(8,128)(2,1)}, bf16[128,512]{1,0:T(8,128)(2,1)}, u32[]{:S(2)}, u32[]{:S(2)}) collective-permute-start(bf16[128,512]{1,0:T(8,128)(2,1)} %refs_10_.1), channel_id=1, source_target_pairs={{0,2},{2,0},{1,3},{3,1},{4,6},{6,4},{5,7},{7,5},{8,10},{10,8},{9,1... | collective-permute-start | bytes 393224 | tf_op jit(solution)/shard_map/ppermute | solution.py:233
  12.6 0.2 collective-permute-start.4
  12.8 4.0 %gather_latents.1 = (bf16[768,1792]{1,0:T(8,128)(2,1)S(1)}, bf16[768,1280]{1,0:T(8,128)(2,1)}, bf16[3,128,512]{2,1,0:T(8,128)(2,1)}) custom-call(s32[12,128]{1,0:T(8,128)} %bitcast.17, s32[12,128]{1,0:T(8,128)} %bitcast.15, bf16[384,512]{1,0:T(8,128)(2,1)} %refs_0_.3, bf16[2,128,512]{2,1,0:T(8,128)(2,1)} %node_in_ref.1, bf16[128,512]{1,0:T(8,128)(2,1)} %node_out_ref.1, ...), custom_call_target="tpu_custom_call" | custom-call | tf_op jit(solution)/shard_map/gather_latents/pallas_call | solution.py:428
  16.8 1.4 %collective-permute-start.9 = (bf16[3,128,512]{2,1,0:T(8,128)(2,1)}, bf16[3,128,512]{2,1,0:T(8,128)(2,1)}, u32[]{:S(2)}, u32[]{:S(2)}) collective-permute-start(bf16[3,128,512]{2,1,0:T(8,128)(2,1)} %get-tuple-element.25.refs_3_), channel_id=1, source_target_pairs={{0,2},{2,0},{1,3},{3,1},{4,6},{6,4},{5,7},{7,5},{8,10},{10,8},{9,1... | collective-permute-start | bytes 1179656 | tf_op jit(solution)/shard_map/ppermute | solution.py:233
  18.2 0.5 %collective-permute-done.1.refs_12_ = bf16[128,512]{1,0:T(8,128)(2,1)} collective-permute-done((bf16[128,512]{1,0:T(8,128)(2,1)}, bf16[128,512]{1,0:T(8,128)(2,1)}, u32[]{:S(2)}, u32[]{:S(2)}) %collective-permute-start.1) | collective-permute-done | bytes 131104 | tf_op jit(solution)/shard_map/ppermute | solution.py:233
  18.7 0.0 all-to-all-done.refs_4_
  18.7 0.0 collective-permute-done.refs_8_
  18.7 0.5 %collective-permute-start.3 = (bf16[8,17,512]{2,1,0:T(8,128)(2,1)S(1)}, bf16[8,17,512]{2,1,0:T(8,128)(2,1)S(1)}, u32[]{:S(2)}, u32[]{:S(2)}) collective-permute-start(bf16[8,17,512]{2,1,0:T(8,128)(2,1)S(1)} %all-to-all-done.refs_4_), channel_id=1, source_target_pairs={{0,1},{1,0},{2,3},{3,2},{4,5},{5,4},{6,7},{7,6},{8,9},{9,8},{10,11... | collective-permute-start | bytes 417800 | tf_op jit(solution)/shard_map/ppermute | solution.py:241
  19.2 0.1 collective-permute-start.6
  19.3 0.4 %collective-permute-start.8 = (bf16[3,128,512]{2,1,0:T(8,128)(2,1)}, bf16[3,128,512]{2,1,0:T(8,128)(2,1)S(1)}, u32[]{:S(2)}, u32[]{:S(2)}) collective-permute-start(bf16[3,128,512]{2,1,0:T(8,128)(2,1)} %get-tuple-element.25.refs_3_), channel_id=1, source_target_pairs={{0,1},{1,0},{2,3},{3,2},{4,5},{5,4},{6,7},{7,6},{8,9},{9,8},{10,11... | collective-permute-start | bytes 1179656 | tf_op jit(solution)/shard_map/ppermute | solution.py:241
  19.7 8.8 %collective-permute-done.9.refs_5_ = bf16[3,128,512]{2,1,0:T(8,128)(2,1)} collective-permute-done((bf16[3,128,512]{2,1,0:T(8,128)(2,1)}, bf16[3,128,512]{2,1,0:T(8,128)(2,1)}, u32[]{:S(2)}, u32[]{:S(2)}) %collective-permute-start.9) | collective-permute-done | bytes 393248 | tf_op jit(solution)/shard_map/ppermute | solution.py:233
  28.5 0.0 copy-start
  28.5 0.0 copy-start.1
  28.6 0.0 copy-start.2
  28.6 0.0 copy-start.3
  28.6 0.0 copy-start.4
  28.6 8.6 %edge_update.1 = (bf16[1536,512]{1,0:T(8,128)(2,1)}, bf16[384,512]{1,0:T(8,128)(2,1)S(1)}) custom-call(bf16[1536,512]{1,0:T(8,128)(2,1)} %refs_0_.2, bf16[768,1280]{1,0:T(8,128)(2,1)} %get-tuple-element.17.refs_1_, s32[12,128]{1,0:T(8,128)} %bitcast.16, bf16[768,1792]{1,0:T(8,128)(2,1)S(1)} %get-tuple-element.18.refs_3_, ...), custom_call_target="tpu_custom_call" | custom-call | tf_op jit(solution)/shard_map/edge_update/pallas_call | solution.py:474
  37.2 0.6 %collective-permute-start.7 = (bf16[384,512]{1,0:T(8,128)(2,1)S(1)}, bf16[384,512]{1,0:T(8,128)(2,1)S(1)}, u32[]{:S(2)}, u32[]{:S(2)}) collective-permute-start(bf16[384,512]{1,0:T(8,128)(2,1)S(1)} %get-tuple-element.24.refs_1_), channel_id=1, source_target_pairs={{0,1},{1,0},{2,3},{3,2},{4,5},{5,4},{6,7},{7,6},{8,9},{9,8},{10,11... | collective-permute-start | bytes 1179656 | tf_op jit(solution)/shard_map/ppermute | solution.py:504
  37.8 1.3 %collective-permute-done.7.refs_2_ = bf16[384,512]{1,0:T(8,128)(2,1)S(1)} collective-permute-done((bf16[384,512]{1,0:T(8,128)(2,1)S(1)}, bf16[384,512]{1,0:T(8,128)(2,1)S(1)}, u32[]{:S(2)}, u32[]{:S(2)}) %collective-permute-start.7) | collective-permute-done | bytes 393248 | tf_op jit(solution)/shard_map/ppermute | solution.py:504
  39.2 3.1 %node_update.1 = bf16[384,512]{1,0:T(8,128)(2,1)} custom-call(bf16[384,512]{1,0:T(8,128)(2,1)S(1)} %copy-done, bf16[384,512]{1,0:T(8,128)(2,1)S(1)} %get-tuple-element.24.refs_1_, bf16[384,512]{1,0:T(8,128)(2,1)S(1)} %collective-permute-done.7.refs_2_, bf16[3,128,512]{2,1,0:T(8,128)(2,1)} %get-tuple-element.25.refs_3_, ...), custom_call_target="tpu_custom_call" | custom-call | flops 603979776 | bytes 1966080 | tf_op jit(solution)/shard_map/node_update/pallas_call | solution.py:507
  (14 shorter events, 0.0 us)
Async XLA Ops:
  0.6 18.1 %collective-permute-start = (bf16[3,128,512]{2,1,0:T(8,128)(2,1)}, bf16[3,128,512]{2,1,0:T(8,128)(2,1)S(1)}, u32[]{:S(2)}, u32[]{:S(2)}) collective-permute-start(bf16[3,128,512]{2,1,0:T(8,128)(2,1)} %refs_6_.1), channel_id=1, source_target_pairs={{0,2},{2,0},{1,3},{3,1},{4,6},{6,4},{5,7},{7,5},{8,10},{10,8},{9,1... | collective-permute-start | bytes 1179656 | tf_op jit(solution)/shard_map/ppermute | solution.py:233
  5.7 13.0 %all-to-all-start = ((bf16[8,17,512]{2,1,0:T(8,128)(2,1)}), bf16[8,17,512]{2,1,0:T(8,128)(2,1)S(1)}, u32[]{:S(2)}, u32[]{:S(2)}) async-start(bf16[8,17,512]{2,1,0:T(8,128)(2,1)} %pick_halo.1), calls=%async_computation | async-start | bytes 393216 | tf_op jit(solution)/shard_map/all_to_all | solution.py:109
  10.6 2.3 %collective-permute-start.2 = (bf16[128,512]{1,0:T(8,128)(2,1)}, bf16[128,512]{1,0:T(8,128)(2,1)S(1)}, u32[]{:S(2)}, u32[]{:S(2)}) collective-permute-start(bf16[128,512]{1,0:T(8,128)(2,1)} %refs_10_.1), channel_id=1, source_target_pairs={{0,1},{1,0},{2,3},{3,2},{4,5},{5,4},{6,7},{7,6},{8,9},{9,8},{10,11... | collective-permute-start | bytes 393224 | tf_op jit(solution)/shard_map/ppermute | solution.py:241
  10.6 8.1 %collective-permute-start.1 = (bf16[128,512]{1,0:T(8,128)(2,1)}, bf16[128,512]{1,0:T(8,128)(2,1)}, u32[]{:S(2)}, u32[]{:S(2)}) collective-permute-start(bf16[128,512]{1,0:T(8,128)(2,1)} %refs_10_.1), channel_id=1, source_target_pairs={{0,2},{2,0},{1,3},{3,1},{4,6},{6,4},{5,7},{7,5},{8,10},{10,8},{9,1... | collective-permute-start | bytes 393224 | tf_op jit(solution)/shard_map/ppermute | solution.py:233
  12.6 6.7 %collective-permute-start.4 = (bf16[3,128,512]{2,1,0:T(8,128)(2,1)}, bf16[3,128,512]{2,1,0:T(8,128)(2,1)}, u32[]{:S(2)}, u32[]{:S(2)}) collective-permute-start(bf16[3,128,512]{2,1,0:T(8,128)(2,1)} %refs_6_.1), channel_id=1, source_target_pairs={{0,1},{1,0},{2,3},{3,2},{4,5},{5,4},{6,7},{7,6},{8,9},{9,8},{10,11... | collective-permute-start | bytes 1179656 | tf_op jit(solution)/shard_map/ppermute | solution.py:241
  16.8 11.7 %collective-permute-start.9 = (bf16[3,128,512]{2,1,0:T(8,128)(2,1)}, bf16[3,128,512]{2,1,0:T(8,128)(2,1)}, u32[]{:S(2)}, u32[]{:S(2)}) collective-permute-start(bf16[3,128,512]{2,1,0:T(8,128)(2,1)} %get-tuple-element.25.refs_3_), channel_id=1, source_target_pairs={{0,2},{2,0},{1,3},{3,1},{4,6},{6,4},{5,7},{7,5},{8,10},{10,8},{9,1... | collective-permute-start | bytes 1179656 | tf_op jit(solution)/shard_map/ppermute | solution.py:233
  18.7 9.8 %collective-permute-start.5 = (bf16[3,128,512]{2,1,0:T(8,128)(2,1)S(1)}, bf16[3,128,512]{2,1,0:T(8,128)(2,1)S(1)}, u32[]{:S(2)}, u32[]{:S(2)}) collective-permute-start(bf16[3,128,512]{2,1,0:T(8,128)(2,1)S(1)} %collective-permute-done.refs_8_), channel_id=1, source_target_pairs={{0,1},{1,0},{2,3},{3,2},{4,5},{5,4},{6,7},{7,6},{8,9},{9,8},{10,11... | collective-permute-start | bytes 1179656 | tf_op jit(solution)/shard_map/ppermute | solution.py:241
  18.7 9.8 %collective-permute-start.3 = (bf16[8,17,512]{2,1,0:T(8,128)(2,1)S(1)}, bf16[8,17,512]{2,1,0:T(8,128)(2,1)S(1)}, u32[]{:S(2)}, u32[]{:S(2)}) collective-permute-start(bf16[8,17,512]{2,1,0:T(8,128)(2,1)S(1)} %all-to-all-done.refs_4_), channel_id=1, source_target_pairs={{0,1},{1,0},{2,3},{3,2},{4,5},{5,4},{6,7},{7,6},{8,9},{9,8},{10,11... | collective-permute-start | bytes 417800 | tf_op jit(solution)/shard_map/ppermute | solution.py:241
  19.2 9.3 %collective-permute-start.6 = (bf16[128,512]{1,0:T(8,128)(2,1)}, bf16[128,512]{1,0:T(8,128)(2,1)S(1)}, u32[]{:S(2)}, u32[]{:S(2)}) collective-permute-start(bf16[128,512]{1,0:T(8,128)(2,1)} %collective-permute-done.1.refs_12_), channel_id=1, source_target_pairs={{0,1},{1,0},{2,3},{3,2},{4,5},{5,4},{6,7},{7,6},{8,9},{9,8},{10,11... | collective-permute-start | bytes 393224 | tf_op jit(solution)/shard_map/ppermute | solution.py:241
  19.3 18.5 %collective-permute-start.8 = (bf16[3,128,512]{2,1,0:T(8,128)(2,1)}, bf16[3,128,512]{2,1,0:T(8,128)(2,1)S(1)}, u32[]{:S(2)}, u32[]{:S(2)}) collective-permute-start(bf16[3,128,512]{2,1,0:T(8,128)(2,1)} %get-tuple-element.25.refs_3_), channel_id=1, source_target_pairs={{0,1},{1,0},{2,3},{3,2},{4,5},{5,4},{6,7},{7,6},{8,9},{9,8},{10,11... | collective-permute-start | bytes 1179656 | tf_op jit(solution)/shard_map/ppermute | solution.py:241
  28.5 9.3 %collective-permute-start.10 = (bf16[3,128,512]{2,1,0:T(8,128)(2,1)}, bf16[3,128,512]{2,1,0:T(8,128)(2,1)S(1)}, u32[]{:S(2)}, u32[]{:S(2)}) collective-permute-start(bf16[3,128,512]{2,1,0:T(8,128)(2,1)} %collective-permute-done.9.refs_5_), channel_id=1, source_target_pairs={{0,1},{1,0},{2,3},{3,2},{4,5},{5,4},{6,7},{7,6},{8,9},{9,8},{10,11... | collective-permute-start | bytes 1179656 | tf_op jit(solution)/shard_map/ppermute | solution.py:241
  28.5 10.6 %copy-start = (bf16[384,512]{1,0:T(8,128)(2,1)S(1)}, bf16[384,512]{1,0:T(8,128)(2,1)}, u32[]{:S(2)}) copy-start(bf16[384,512]{1,0:T(8,128)(2,1)} %refs_0_.3) | copy-start | bytes 1179652
  28.5 10.6 %copy-start.1 = (f32[512]{0:T(512)S(1)}, f32[512]{0:T(512)}, u32[]{:S(2)}) copy-start(f32[512]{0:T(512)} %param.32) | copy-start | bytes 6148
  28.6 10.6 %copy-start.2 = (f32[512]{0:T(512)S(1)}, f32[512]{0:T(512)}, u32[]{:S(2)}) copy-start(f32[512]{0:T(512)} %param.33) | copy-start | bytes 6148
  28.6 10.6 %copy-start.3 = (f32[512]{0:T(512)S(1)}, f32[512]{0:T(512)}, u32[]{:S(2)}) copy-start(f32[512]{0:T(512)} %param.34) | copy-start | bytes 6148
  28.6 10.6 %copy-start.4 = (f32[512]{0:T(512)S(1)}, f32[512]{0:T(512)}, u32[]{:S(2)}) copy-start(f32[512]{0:T(512)} %param.35) | copy-start | bytes 6148
  37.2 1.9 %collective-permute-start.7 = (bf16[384,512]{1,0:T(8,128)(2,1)S(1)}, bf16[384,512]{1,0:T(8,128)(2,1)S(1)}, u32[]{:S(2)}, u32[]{:S(2)}) collective-permute-start(bf16[384,512]{1,0:T(8,128)(2,1)S(1)} %get-tuple-element.24.refs_1_), channel_id=1, source_target_pairs={{0,1},{1,0},{2,3},{3,2},{4,5},{5,4},{6,7},{7,6},{8,9},{9,8},{10,11... | collective-permute-start | bytes 1179656 | tf_op jit(solution)/shard_map/ppermute | solution.py:504

commit v15 on v13

--- a/solution.py
+++ b/solution.py
@@ -132,29 +132,26 @@
     node_in_ref,
     node_out_ref,
     edge_hbm,
-    known,
-    gathered_hbm,
-    pack_ref,
-    gathered,
-    sems,
+    *refs,
 ):
+    known, pack_ref, sems = refs[:-2], refs[-2], refs[-1]
     node_count, width = latent_ref.shape
-    first = known.shape[0]
-    edge_count = first + gathered.shape[0]
-    block = first // 2
+    rows = known[0].shape[0]
+    block = rows // 2
     copies = []
 
     def start(source, target):
         copies.append(pltpu.make_async_copy(source, target, sems.at[len(copies)]))
         copies[-1].start()
 
-    start(edge_hbm.at[pl.ds(0, first)], known.at[:, pl.ds(0, width)])
+    for at, target in enumerate(known):
+        start(edge_hbm.at[pl.ds(at * rows, rows)], target.at[:, pl.ds(0, width)])
     count = node_in_ref.shape[0]
     pack_ref[:count] = node_in_ref[...]
     pack_ref[count] = node_out_ref[...]
     latent = latent_ref[...]
 
-    def gather(at, target, rows, begin):
+    def gather(at, target, spot, begin):
         here = slice(at * (block // lanes), (at + 1) * (block // lanes))
         source = source_ref[here]
         if halved:
@@ -164,23 +161,20 @@
             source = jnp.where(far >= 0, source - slot + turned, source)
         columns = as_columns(source)
         sent = one_hot(columns, node_count)
-        target[rows, begin : begin + width] = jnp.dot(
+        target[spot, begin : begin + width] = jnp.dot(
             sent, latent, preferred_element_type=f32
         ).astype(bf16)
         received = one_hot(as_columns(receiver_ref[here]), node_count)
-        target[rows, begin + width : begin + 2 * width] = jnp.dot(
+        target[spot, begin + width : begin + 2 * width] = jnp.dot(
             received, latent, preferred_element_type=f32
         ).astype(bf16)
         slots = target.shape[1] - begin - 2 * width
-        target[rows, begin + 2 * width :] = one_hot(columns - node_count, slots)
-
-    for at in range(first // block, edge_count // block):
-        begin = at * block - first
-        gather(at, gathered, slice(begin, begin + block), 0)
-        rows = pl.ds(begin, block)
-        start(gathered.at[rows], gathered_hbm.at[rows])
-    for at in range(first // block):
-        gather(at, known, slice(at * block, (at + 1) * block), width)
+        target[spot, begin + 2 * width :] = one_hot(columns - node_count, slots)
+
+    for at, target in enumerate(known):
+        for part in range(rows // block):
+            spot = slice(part * block, (part + 1) * block)
+            gather(at * (rows // block) + part, target, spot, width)
     for copy in copies:
         copy.wait()
 
@@ -244,18 +238,18 @@
     ]
 
 
-def edge_kernel(pieces_count, got_count, part_count, near_cap, halved, block, *refs):
-    edge_hbm, gathered_hbm, receiver_ref, known_first = refs[:4]
-    got_refs = refs[4 : 4 + got_count]
-    refs = refs[4 + got_count :]
+def edge_kernel(pieces_count, got_count, part_count, near_cap, halved, blocks, *refs):
+    receiver_ref, known = refs[0], refs[1 : 1 + blocks]
+    got_refs = refs[1 + blocks : 1 + blocks + got_count]
+    refs = refs[1 + blocks + got_count :]
     in_pieces, out_pieces = refs[:pieces_count], refs[pieces_count : 2 * pieces_count]
     row_refs = refs[2 * pieces_count : 2 * pieces_count + 4]
     new_hbm, sum_ref = refs[2 * pieces_count + 4 : 2 * pieces_count + 6]
-    known_rest, to_node, in_weight, out_weight, halo, rows, preact, hidden, output, new_ref, total, sems = (
+    to_node, in_weight, out_weight, halo, rows, preact, hidden, output, new_ref, total, sems = (
         refs[2 * pieces_count + 6 :]
     )
     edge_count, width = new_hbm.shape
-    blocks = edge_count // block
+    block = edge_count // blocks
     taken = []
 
     def start(source, target):
@@ -277,15 +271,6 @@
     spot = pl.ds(pl.multiple_of(order[0] * count, count), count)
     later.append(start(out_pieces[0], out_weight.at[spot]))
     in_bias, out_bias, gain, offset = rows
-    rest = edge_count - block
-    known_copies = [
-        start(edge_hbm.at[pl.ds(block, rest)], known_rest.at[:, pl.ds(0, width)]),
-        start(gathered_hbm, known_rest.at[:, pl.ds(width, known_rest.shape[1] - width)]),
-    ]
-
-    def known(at):
-        return known_first if at == 0 else known_rest.at[pl.ds((at - 1) * block, block)]
-
     node_place = lax.broadcasted_iota(jnp.int32, (to_node.shape[0], lanes), 0)
     for row in range(edge_count // lanes):
         to_node[:, row * lanes : (row + 1) * lanes] = jnp.where(
@@ -306,11 +291,8 @@
         copy.wait()
 
     def in_dot(at):
-        if at == 1:
-            for copy in known_copies:
-                copy.wait()
         preact[at][...] = jnp.dot(
-            known(at)[...], in_weight[...], preferred_element_type=f32
+            known[at][...], in_weight[...], preferred_element_type=f32
         )
 
     def activate(at):
@@ -328,7 +310,7 @@
             here = slice(start_row, start_row + chunk_rows)
             there = slice(at * block + start_row, at * block + start_row + chunk_rows)
             normed = layer_norm(output[at][here] + out_bias[...], gain[...], offset[...])
-            edges = known(at)[here, :width].astype(f32)
+            edges = known[at][here, :width].astype(f32)
             new_ref[there] = (edges + normed).astype(bf16)
         spot = pl.ds(at * block, block)
         return start(new_ref.at[spot], new_hbm.at[spot])
@@ -421,36 +403,29 @@
     receiver_rows = in_hbm(receivers.reshape(-1, lanes))
 
     pack_shape = (node_in_weight.shape[0] + 1,) + node_out_weight.shape
-    gathered_width = 2 * width + halo_space
-    known_width = width + gathered_width
-    rest = edge_count - block
-    known, gathered, node_weight = pl.pallas_call(
+    near_edge[1], latent_after = lax.optimization_barrier((near_edge[1], node_latent))
+    known_width = 3 * width + halo_space
+    *known, node_weight = pl.pallas_call(
         functools.partial(gather_kernel, near_cap, far_cap, halved),
-        out_shape=[
-            pltpu.VMEM((block, known_width), bf16),
-            pltpu.HBM((rest, gathered_width), bf16),
-            pltpu.VMEM(pack_shape, bf16),
-        ],
+        out_shape=[pltpu.VMEM((block, known_width), bf16)] * steps
+        + [pltpu.HBM(pack_shape, bf16)],
         in_specs=[vmem] * 5 + [hbm],
-        out_specs=[vmem, hbm, vmem],
-        scratch_shapes=[
-            pltpu.VMEM((rest, gathered_width), bf16),
-            pltpu.SemaphoreType.DMA((1 + 2 * (steps - 1),)),
-        ],
+        out_specs=[vmem] * (steps + 1),
+        scratch_shapes=[pltpu.SemaphoreType.DMA((steps,))],
         compiler_params=pltpu.CompilerParams(vmem_limit_bytes=grant),
         cost_estimate=pl.CostEstimate(flops=0, bytes_accessed=0, transcendentals=0),
         name="gather_latents",
     )(
         source_rows,
         receiver_rows,
-        in_hbm(node_latent),
+        in_hbm(latent_after),
         in_hbm(node_in_weight),
         in_hbm(node_out_weight),
         in_hbm(edge_latent),
     )
 
-    far_edge, got, known, gathered, node_weight = lax.optimization_barrier(
-        (far_edge, got, known, gathered, node_weight)
+    far_edge, got, known, node_weight = lax.optimization_barrier(
+        (far_edge, got, known, node_weight)
     )
     if halved:
         got = got + from_subs(got)
@@ -463,18 +438,17 @@
     pieces_count = len(edge_in)
 
     rows = [value.reshape(1, -1) for value in (edge_in_bias, edge_out_bias, edge_gain, edge_offset)]
-    edge_operands = [in_hbm(edge_latent), in_hbm(gathered), receiver_rows, in_vmem(known)]
-    edge_operands += [in_vmem(blocks) for blocks in got]
-    edge_specs = [hbm] * 2 + [vmem] * (2 + len(got))
+    edge_operands = [receiver_rows] + [in_vmem(array) for array in known + got]
+    edge_specs = [vmem] * len(edge_operands)
     for pieces in (edge_in, edge_out):
         edge_operands += [in_hbm(pieces[0])] + [in_vmem(piece) for piece in pieces[1:]]
         edge_specs += [hbm] + [vmem] * (pieces_count - 1)
     edge_operands += [in_hbm(row) for row in rows]
     edge_specs += [hbm] * len(rows)
-    copy_count = 3 + 4 + 1 + 2 + steps
+    copy_count = 3 + 4 + 1 + steps
     edge_new, partial_sums = pl.pallas_call(
         functools.partial(
-            edge_kernel, pieces_count, len(got), part_count, near_cap, halved, block
+            edge_kernel, pieces_count, len(got), part_count, near_cap, halved, steps
         ),
         out_shape=[
             pltpu.HBM((edge_count, width), bf16),
@@ -483,7 +457,6 @@
         in_specs=edge_specs,
         out_specs=[hbm, vmem],
         scratch_shapes=[
-            pltpu.VMEM((rest, known_width), bf16),
             pltpu.VMEM((node_count, edge_count), bf16),
             pltpu.VMEM((known_width, width), bf16),
             pltpu.VMEM((width, width), bf16),

time: 35.9 us -> 35.8 us (level)
  waiting for transfers between devices: 6.09 us -> 2.56 us
  local copies, waits for them, and re-layouts: 0.03 us -> 3.35 us
    unnamed x10 -> x16, local copies, waits for them, and re-layouts: 0.03 us -> 3.35 us
    ppermute x3, waiting for transfers between devices: 2.31 us -> 0.43 us  [from_feats(): lax.ppermute(weight, 'feat', [(at, (at + shift) % feats) for at in range(...]
    ppermute x7, waiting for transfers between devices: 2.22 us -> 0.93 us  [from_subs(): lax.ppermute(piece, 'sub', [(at, (at + turn) % subs) for at in range(subs)])]
    all_to_all x1, waiting for transfers between devices: 0.76 us -> 0.01 us  [exchange_halves(): lax.all_to_all(blocks, ('region', 'feat'), split_axis=0, concat_axis=0, t...]
    pallas_call x1, Pallas kernels: 3.23 us -> 3.84 us  [shards(): pl.pallas_call(functools.partial(gather_kernel, near_cap, far_cap, halved...]
    pallas_call x1, Pallas kernels: 8.71 us -> 8.26 us  [shards(): pl.pallas_call(functools.partial(edge_kernel, pieces_count, len(got), par...]
    ppermute x1, waiting for transfers between devices: 0.79 us -> 1.21 us  [shards(): lax.ppermute(partial_sums, 'sub', [(at, (at + 1) % subs) for at in range(...]
    ppermute x1, starting transfers between devices: 0.56 us -> 0.2 us  [shards(): lax.ppermute(partial_sums, 'sub', [(at, (at + 1) % subs) for at in range(...]
  transfers between devices with their start and end apart: 12 -> 12, of which waited for: 6 -> 4; matrix products, arithmetic and copies ran while one was open for 0% -> 0% of each run, Pallas kernels for 39% -> 40%
where the time goes in v15:
time: 35.8 us; the launch traced here: 35.5 us
  Pallas kernels  16.2 us (45%)
  starting transfers between devices  12.6 us (35%)
  local copies, waits for them, and re-layouts  3.35 us (9%)
  waiting for transfers between devices  2.56 us (7%)
  between operations  0.73 us (2%)
    pallas_call x1, Pallas kernels, shards(): pl.pallas_call(functools.partial(edge_kernel, pieces_count, len(got), par...  8.26 us
    ppermute x3, starting transfers between devices, from_feats(): lax.ppermute(weight, 'feat', [(at, (at + shift) % feats) for at in range(...  6.23 us
    all_to_all x1, starting transfers between devices, exchange_halves(): lax.all_to_all(blocks, ('region', 'feat'), split_axis=0, concat_axis=0, t...  4.88 us
    pallas_call x1, Pallas kernels, shards(): pl.pallas_call(functools.partial(gather_kernel, near_cap, far_cap, halved...  3.84 us
    unnamed x16, local copies, waits for them, and re-layouts  3.35 us
    pallas_call x1, Pallas kernels, exchange_halves(): pl.pallas_call(functools.partial(pick_kernel, part_count, near_cap, far_c...  2.08 us
    pallas_call x1, Pallas kernels, shards(): pl.pallas_call(functools.partial(node_kernel, pieces_count), out_shape=ja...  2.01 us
    ppermute x7, starting transfers between devices, from_subs(): lax.ppermute(piece, 'sub', [(at, (at + turn) % subs) for at in range(subs)])  1.35 us
  transfers between devices with their start and end apart: 12, of which 4 were waited for; matrix products, arithmetic and copies ran while one was open for 0% of the time, Pallas kernels for 40%

profile of v15, /device:TPU:0, one launch (start us, length us, event | category | flops | bytes accessed | tf_op | source)
XLA Modules:
  0.0 35.5 jit_solution(4034932350682738185)
XLA Ops:
  0.6 3.0 %collective-permute-start = (bf16[3,128,512]{2,1,0:T(8,128)(2,1)}, bf16[3,128,512]{2,1,0:T(8,128)(2,1)S(1)}, u32[]{:S(2)}, u32[]{:S(2)}) collective-permute-start(bf16[3,128,512]{2,1,0:T(8,128)(2,1)} %refs_5_.1), channel_id=1, source_target_pairs={{0,2},{2,0},{1,3},{3,1},{4,6},{6,4},{5,7},{7,5},{8,10},{10,8},{9,1... | collective-permute-start | bytes 1179656 | tf_op jit(solution)/shard_map/ppermute | solution.py:227
  3.6 2.1 %pick_halo.1 = bf16[8,17,512]{2,1,0:T(8,128)(2,1)} custom-call(s32[1,2,8]{2,1,0:T(2,128)} %bitcast.18, s32[1,4,32]{2,1,0:T(4,128)} %near_ref.1, bf16[384,512]{1,0:T(8,128)(2,1)} %refs_0_.1), custom_call_target="tpu_custom_call" | custom-call | tf_op jit(solution)/shard_map/pick_halo/pallas_call | solution.py:99
  5.7 4.9 %all-to-all-start = ((bf16[8,17,512]{2,1,0:T(8,128)(2,1)}), bf16[8,17,512]{2,1,0:T(8,128)(2,1)S(1)}, u32[]{:S(2)}, u32[]{:S(2)}) async-start(bf16[8,17,512]{2,1,0:T(8,128)(2,1)} %pick_halo.1), calls=%async_computation | async-start | bytes 393216 | tf_op jit(solution)/shard_map/all_to_all | solution.py:109
  10.6 0.0 collective-permute-start.2
  10.6 2.0 %collective-permute-start.1 = (bf16[128,512]{1,0:T(8,128)(2,1)}, bf16[128,512]{1,0:T(8,128)(2,1)}, u32[]{:S(2)}, u32[]{:S(2)}) collective-permute-start(bf16[128,512]{1,0:T(8,128)(2,1)} %refs_9_.1), channel_id=1, source_target_pairs={{0,2},{2,0},{1,3},{3,1},{4,6},{6,4},{5,7},{7,5},{8,10},{10,8},{9,1... | collective-permute-start | bytes 393224 | tf_op jit(solution)/shard_map/ppermute | solution.py:227
  12.6 0.2 collective-permute-start.4
  12.8 0.0 collective-permute-done.2.refs_10_
  12.8 3.8 %gather_latents.1 = (bf16[768,1792]{1,0:T(8,128)(2,1)S(1)}, bf16[768,1792]{1,0:T(8,128)(2,1)S(1)}, bf16[3,128,512]{2,1,0:T(8,128)(2,1)}) custom-call(s32[12,128]{1,0:T(8,128)} %bitcast.15, s32[12,128]{1,0:T(8,128)} %bitcast.16, bf16[384,512]{1,0:T(8,128)(2,1)} %refs_0_.1, bf16[2,128,512]{2,1,0:T(8,128)(2,1)} %node_in_ref.1, bf16[128,512]{1,0:T(8,128)(2,1)} %node_out_ref.1, ...), custom_call_target="tpu_custom_call" | custom-call | tf_op jit(solution)/shard_map/gather_latents/pallas_call | solution.py:408
  16.7 1.5 %copy-done.6 = bf16[768,1792]{1,0:T(8,128)(2,1)} copy-done((bf16[768,1792]{1,0:T(8,128)(2,1)}, bf16[768,1792]{1,0:T(8,128)(2,1)S(1)}, u32[]{:S(2)}) %copy-start.6) | copy-done | bytes 2752536
  18.3 0.4 %collective-permute-done.1.refs_11_ = bf16[128,512]{1,0:T(8,128)(2,1)} collective-permute-done((bf16[128,512]{1,0:T(8,128)(2,1)}, bf16[128,512]{1,0:T(8,128)(2,1)}, u32[]{:S(2)}, u32[]{:S(2)}) %collective-permute-start.1) | collective-permute-done | bytes 131104 | tf_op jit(solution)/shard_map/ppermute | solution.py:227
  18.7 0.5 %collective-permute-start.3 = (bf16[8,17,512]{2,1,0:T(8,128)(2,1)S(1)}, bf16[8,17,512]{2,1,0:T(8,128)(2,1)S(1)}, u32[]{:S(2)}, u32[]{:S(2)}) collective-permute-start(bf16[8,17,512]{2,1,0:T(8,128)(2,1)S(1)} %all-to-all-done.refs_3_), channel_id=1, source_target_pairs={{0,1},{1,0},{2,3},{3,2},{4,5},{5,4},{6,7},{7,6},{8,9},{9,8},{10,11... | collective-permute-start | bytes 417800 | tf_op jit(solution)/shard_map/ppermute | solution.py:235
  19.2 0.1 collective-permute-start.6
  19.3 1.2 %collective-permute-start.9 = (bf16[3,128,512]{2,1,0:T(8,128)(2,1)}, bf16[3,128,512]{2,1,0:T(8,128)(2,1)S(1)}, u32[]{:S(2)}, u32[]{:S(2)}) collective-permute-start(bf16[3,128,512]{2,1,0:T(8,128)(2,1)} %get-tuple-element.27.refs_3_), channel_id=1, source_target_pairs={{0,2},{2,0},{1,3},{3,1},{4,6},{6,4},{5,7},{7,5},{8,10},{10,8},{9,1... | collective-permute-start | bytes 1179656 | tf_op jit(solution)/shard_map/ppermute | solution.py:227
  20.5 0.2 collective-permute-start.8
  20.6 0.4 collective-permute-done.6.refs_12_
  21.0 1.8 %copy-done.7 = bf16[768,1792]{1,0:T(8,128)(2,1)S(1)} copy-done((bf16[768,1792]{1,0:T(8,128)(2,1)S(1)}, bf16[768,1792]{1,0:T(8,128)(2,1)}, u32[]{:S(2)}) %copy-start.7) | copy-done | bytes 2752536
  22.8 0.0 copy-start.4
  22.8 0.0 copy-start.5
  22.8 8.3 %edge_update.1 = (bf16[1536,512]{1,0:T(8,128)(2,1)}, bf16[384,512]{1,0:T(8,128)(2,1)S(1)}) custom-call(s32[12,128]{1,0:T(8,128)} %bitcast.17, bf16[768,1792]{1,0:T(8,128)(2,1)S(1)} %get-tuple-element.19.refs_1_, bf16[768,1792]{1,0:T(8,128)(2,1)S(1)} %copy-done.7, bf16[8,17,512]{2,1,0:T(8,128)(2,1)S(1)} %all-to-all-done.refs_3_, ...), custom_call_target="tpu_custom_call" | custom-call | flops 3825205248 | bytes 6291456 | tf_op jit(solution)/shard_map/edge_update/pallas_call | solution.py:449
  31.1 0.2 collective-permute-start.7
  31.3 0.4 %collective-permute-start.10 = (bf16[3,128,512]{2,1,0:T(8,128)(2,1)S(1)}, bf16[3,128,512]{2,1,0:T(8,128)(2,1)S(1)}, u32[]{:S(2)}, u32[]{:S(2)}) collective-permute-start(bf16[3,128,512]{2,1,0:T(8,128)(2,1)S(1)} %collective-permute-done.9.refs_5_), channel_id=1, source_target_pairs={{0,1},{1,0},{2,3},{3,2},{4,5},{5,4},{6,7},{7,6},{8,9},{9,8},{10,11... | collective-permute-start | bytes 1179656 | tf_op jit(solution)/shard_map/ppermute | solution.py:235
  31.7 1.2 %collective-permute-done.7.refs_2_ = bf16[384,512]{1,0:T(8,128)(2,1)S(1)} collective-permute-done((bf16[384,512]{1,0:T(8,128)(2,1)S(1)}, bf16[384,512]{1,0:T(8,128)(2,1)S(1)}, u32[]{:S(2)}, u32[]{:S(2)}) %collective-permute-start.7) | collective-permute-done | bytes 393248 | tf_op jit(solution)/shard_map/ppermute | solution.py:482
  32.9 0.6 %collective-permute-done.10.refs_6_ = bf16[3,128,512]{2,1,0:T(8,128)(2,1)S(1)} collective-permute-done((bf16[3,128,512]{2,1,0:T(8,128)(2,1)S(1)}, bf16[3,128,512]{2,1,0:T(8,128)(2,1)S(1)}, u32[]{:S(2)}, u32[]{:S(2)}) %collective-permute-start.10) | collective-permute-done | bytes 393248 | tf_op jit(solution)/shard_map/ppermute | solution.py:235
  33.5 2.0 %node_update.1 = bf16[384,512]{1,0:T(8,128)(2,1)} custom-call(bf16[384,512]{1,0:T(8,128)(2,1)S(1)} %copy-done, bf16[384,512]{1,0:T(8,128)(2,1)S(1)} %get-tuple-element.26.refs_1_, bf16[384,512]{1,0:T(8,128)(2,1)S(1)} %collective-permute-done.7.refs_2_, bf16[3,128,512]{2,1,0:T(8,128)(2,1)S(1)} %copy-done.1, ...), custom_call_target="tpu_custom_call" | custom-call | flops 603979776 | bytes 1966080 | tf_op jit(solution)/shard_map/node_update/pallas_call | solution.py:485
  (20 shorter events, 0.0 us)
Async XLA Ops:
  0.6 18.1 %collective-permute-start = (bf16[3,128,512]{2,1,0:T(8,128)(2,1)}, bf16[3,128,512]{2,1,0:T(8,128)(2,1)S(1)}, u32[]{:S(2)}, u32[]{:S(2)}) collective-permute-start(bf16[3,128,512]{2,1,0:T(8,128)(2,1)} %refs_5_.1), channel_id=1, source_target_pairs={{0,2},{2,0},{1,3},{3,1},{4,6},{6,4},{5,7},{7,5},{8,10},{10,8},{9,1... | collective-permute-start | bytes 1179656 | tf_op jit(solution)/shard_map/ppermute | solution.py:227
  5.7 13.0 %all-to-all-start = ((bf16[8,17,512]{2,1,0:T(8,128)(2,1)}), bf16[8,17,512]{2,1,0:T(8,128)(2,1)S(1)}, u32[]{:S(2)}, u32[]{:S(2)}) async-start(bf16[8,17,512]{2,1,0:T(8,128)(2,1)} %pick_halo.1), calls=%async_computation | async-start | bytes 393216 | tf_op jit(solution)/shard_map/all_to_all | solution.py:109
  10.6 2.3 %collective-permute-start.2 = (bf16[128,512]{1,0:T(8,128)(2,1)}, bf16[128,512]{1,0:T(8,128)(2,1)S(1)}, u32[]{:S(2)}, u32[]{:S(2)}) collective-permute-start(bf16[128,512]{1,0:T(8,128)(2,1)} %refs_9_.1), channel_id=1, source_target_pairs={{0,1},{1,0},{2,3},{3,2},{4,5},{5,4},{6,7},{7,6},{8,9},{9,8},{10,11... | collective-permute-start | bytes 393224 | tf_op jit(solution)/shard_map/ppermute | solution.py:235
  10.6 8.1 %collective-permute-start.1 = (bf16[128,512]{1,0:T(8,128)(2,1)}, bf16[128,512]{1,0:T(8,128)(2,1)}, u32[]{:S(2)}, u32[]{:S(2)}) collective-permute-start(bf16[128,512]{1,0:T(8,128)(2,1)} %refs_9_.1), channel_id=1, source_target_pairs={{0,2},{2,0},{1,3},{3,1},{4,6},{6,4},{5,7},{7,5},{8,10},{10,8},{9,1... | collective-permute-start | bytes 393224 | tf_op jit(solution)/shard_map/ppermute | solution.py:227
  12.6 7.9 %collective-permute-start.4 = (bf16[3,128,512]{2,1,0:T(8,128)(2,1)}, bf16[3,128,512]{2,1,0:T(8,128)(2,1)}, u32[]{:S(2)}, u32[]{:S(2)}) collective-permute-start(bf16[3,128,512]{2,1,0:T(8,128)(2,1)} %refs_5_.1), channel_id=1, source_target_pairs={{0,1},{1,0},{2,3},{3,2},{4,5},{5,4},{6,7},{7,6},{8,9},{9,8},{10,11... | collective-permute-start | bytes 1179656 | tf_op jit(solution)/shard_map/ppermute | solution.py:235
  16.7 1.6 %copy-start.6 = (bf16[768,1792]{1,0:T(8,128)(2,1)}, bf16[768,1792]{1,0:T(8,128)(2,1)S(1)}, u32[]{:S(2)}) copy-start(bf16[768,1792]{1,0:T(8,128)(2,1)S(1)} %get-tuple-element.20.refs_2_) | copy-start | bytes 8257540
  18.7 2.3 %collective-permute-start.5 = (bf16[3,128,512]{2,1,0:T(8,128)(2,1)S(1)}, bf16[3,128,512]{2,1,0:T(8,128)(2,1)S(1)}, u32[]{:S(2)}, u32[]{:S(2)}) collective-permute-start(bf16[3,128,512]{2,1,0:T(8,128)(2,1)S(1)} %collective-permute-done.refs_7_), channel_id=1, source_target_pairs={{0,1},{1,0},{2,3},{3,2},{4,5},{5,4},{6,7},{7,6},{8,9},{9,8},{10,11... | collective-permute-start | bytes 1179656 | tf_op jit(solution)/shard_map/ppermute | solution.py:235
  18.7 2.3 %collective-permute-start.3 = (bf16[8,17,512]{2,1,0:T(8,128)(2,1)S(1)}, bf16[8,17,512]{2,1,0:T(8,128)(2,1)S(1)}, u32[]{:S(2)}, u32[]{:S(2)}) collective-permute-start(bf16[8,17,512]{2,1,0:T(8,128)(2,1)S(1)} %all-to-all-done.refs_3_), channel_id=1, source_target_pairs={{0,1},{1,0},{2,3},{3,2},{4,5},{5,4},{6,7},{7,6},{8,9},{9,8},{10,11... | collective-permute-start | bytes 417800 | tf_op jit(solution)/shard_map/ppermute | solution.py:235
  19.2 1.8 %collective-permute-start.6 = (bf16[128,512]{1,0:T(8,128)(2,1)}, bf16[128,512]{1,0:T(8,128)(2,1)S(1)}, u32[]{:S(2)}, u32[]{:S(2)}) collective-permute-start(bf16[128,512]{1,0:T(8,128)(2,1)} %collective-permute-done.1.refs_11_), channel_id=1, source_target_pairs={{0,1},{1,0},{2,3},{3,2},{4,5},{5,4},{6,7},{7,6},{8,9},{9,8},{10,11... | collective-permute-start | bytes 393224 | tf_op jit(solution)/shard_map/ppermute | solution.py:235
  19.3 12.0 %collective-permute-start.9 = (bf16[3,128,512]{2,1,0:T(8,128)(2,1)}, bf16[3,128,512]{2,1,0:T(8,128)(2,1)S(1)}, u32[]{:S(2)}, u32[]{:S(2)}) collective-permute-start(bf16[3,128,512]{2,1,0:T(8,128)(2,1)} %get-tuple-element.27.refs_3_), channel_id=1, source_target_pairs={{0,2},{2,0},{1,3},{3,1},{4,6},{6,4},{5,7},{7,5},{8,10},{10,8},{9,1... | collective-permute-start | bytes 1179656 | tf_op jit(solution)/shard_map/ppermute | solution.py:227
  20.5 11.2 %collective-permute-start.8 = (bf16[3,128,512]{2,1,0:T(8,128)(2,1)}, bf16[3,128,512]{2,1,0:T(8,128)(2,1)S(1)}, u32[]{:S(2)}, u32[]{:S(2)}) collective-permute-start(bf16[3,128,512]{2,1,0:T(8,128)(2,1)} %get-tuple-element.27.refs_3_), channel_id=1, source_target_pairs={{0,1},{1,0},{2,3},{3,2},{4,5},{5,4},{6,7},{7,6},{8,9},{9,8},{10,11... | collective-permute-start | bytes 1179656 | tf_op jit(solution)/shard_map/ppermute | solution.py:235
  21.0 1.8 %copy-start.7 = (bf16[768,1792]{1,0:T(8,128)(2,1)S(1)}, bf16[768,1792]{1,0:T(8,128)(2,1)}, u32[]{:S(2)}) copy-start(bf16[768,1792]{1,0:T(8,128)(2,1)} %copy-done.6) | copy-start | bytes 8257540
  22.8 10.7 %copy-start = (bf16[384,512]{1,0:T(8,128)(2,1)S(1)}, bf16[384,512]{1,0:T(8,128)(2,1)}, u32[]{:S(2)}) copy-start(bf16[384,512]{1,0:T(8,128)(2,1)} %refs_0_.1) | copy-start | bytes 1179652
  22.8 10.7 %copy-start.1 = (bf16[3,128,512]{2,1,0:T(8,128)(2,1)S(1)}, bf16[3,128,512]{2,1,0:T(8,128)(2,1)}, u32[]{:S(2)}) copy-start(bf16[3,128,512]{2,1,0:T(8,128)(2,1)} %get-tuple-element.27.refs_3_) | copy-start | bytes 1179652
  22.8 10.7 %copy-start.2 = (f32[512]{0:T(512)S(1)}, f32[512]{0:T(512)}, u32[]{:S(2)}) copy-start(f32[512]{0:T(512)} %param.32) | copy-start | bytes 6148
  22.8 10.7 %copy-start.3 = (f32[512]{0:T(512)S(1)}, f32[512]{0:T(512)}, u32[]{:S(2)}) copy-start(f32[512]{0:T(512)} %param.33) | copy-start | bytes 6148
  22.8 10.7 %copy-start.4 = (f32[512]{0:T(512)S(1)}, f32[512]{0:T(512)}, u32[]{:S(2)}) copy-start(f32[512]{0:T(512)} %param.34) | copy-start | bytes 6148
  22.8 10.7 %copy-start.5 = (f32[512]{0:T(512)S(1)}, f32[512]{0:T(512)}, u32[]{:S(2)}) copy-start(f32[512]{0:T(512)} %param.35) | copy-start | bytes 6148
  31.1 1.8 %collective-permute-start.7 = (bf16[384,512]{1,0:T(8,128)(2,1)S(1)}, bf16[384,512]{1,0:T(8,128)(2,1)S(1)}, u32[]{:S(2)}, u32[]{:S(2)}) collective-permute-start(bf16[384,512]{1,0:T(8,128)(2,1)S(1)} %get-tuple-element.26.refs_1_), channel_id=1, source_target_pairs={{0,1},{1,0},{2,3},{3,2},{4,5},{5,4},{6,7},{7,6},{8,9},{9,8},{10,11... | collective-permute-start | bytes 1179656 | tf_op jit(solution)/shard_map/ppermute | solution.py:482
  31.3 2.2 %collective-permute-start.10 = (bf16[3,128,512]{2,1,0:T(8,128)(2,1)S(1)}, bf16[3,128,512]{2,1,0:T(8,128)(2,1)S(1)}, u32[]{:S(2)}, u32[]{:S(2)}) collective-permute-start(bf16[3,128,512]{2,1,0:T(8,128)(2,1)S(1)} %collective-permute-done.9.refs_5_), channel_id=1, source_target_pairs={{0,1},{1,0},{2,3},{3,2},{4,5},{5,4},{6,7},{7,6},{8,9},{9,8},{10,11... | collective-permute-start | bytes 1179656 | tf_op jit(solution)/shard_map/ppermute | solution.py:235

commit v16 on v11

--- a/solution.py
+++ b/solution.py
@@ -155,12 +155,6 @@
     pack_ref[:count] = node_in_ref[...]
     pack_ref[count] = node_out_ref[...]
     latent = latent_ref[...]
-    node_place = lax.broadcasted_iota(jnp.int32, (node_count, lanes), 0)
-    for row in range(edge_count // lanes):
-        to_node[:, row * lanes : (row + 1) * lanes] = jnp.where(
-            node_place == receiver_ref[row : row + 1], 1.0, 0.0
-        ).astype(bf16)
-    start(to_node, to_node_hbm)
 
     def gather(at, target, rows, begin):
         here = slice(at * (block // lanes), (at + 1) * (block // lanes))
@@ -187,6 +181,12 @@
         gather(at, gathered, slice(begin, begin + block), 0)
         rows = pl.ds(begin, block)
         start(gathered.at[rows], gathered_hbm.at[rows])
+    node_place = lax.broadcasted_iota(jnp.int32, (to_node.shape[0], lanes), 0)
+    for row in range(edge_count // lanes):
+        to_node[:, row * lanes : (row + 1) * lanes] = jnp.where(
+            node_place == receiver_ref[row : row + 1], 1.0, 0.0
+        ).astype(bf16)
+    start(to_node, to_node_hbm)
     for at in range(first // block):
         gather(at, known, slice(at * block, (at + 1) * block), width)
     for copy in copies:
@@ -289,8 +289,8 @@
     known_copies = [
         start(edge_hbm.at[pl.ds(block, rest)], known_rest.at[:, pl.ds(0, width)]),
         start(gathered_hbm, known_rest.at[:, pl.ds(width, known_rest.shape[1] - width)]),
+        start(to_node_hbm, to_node),
     ]
-    to_node_copy = start(to_node_hbm, to_node)
 
     def known(at):
         return known_first if at == 0 else known_rest.at[pl.ds((at - 1) * block, block)]
@@ -338,8 +338,6 @@
         return start(new_ref.at[spot], new_hbm.at[spot])
 
     def sum_dot(at):
-        if at == 0:
-            to_node_copy.wait()
         spot = slice(at * block, (at + 1) * block)
         part = jnp.dot(to_node[:, spot], new_ref[spot], preferred_element_type=f32)
         if at > 0:
@@ -427,6 +425,7 @@
     receiver_rows = in_hbm(receivers.reshape(-1, lanes))
 
     pack_shape = (node_in_weight.shape[0] + 1,) + node_out_weight.shape
+    near_edge[1], latent_after = lax.optimization_barrier((near_edge[1], node_latent))
     gathered_width = 2 * width + halo_space
     known_width = width + gathered_width
     rest = edge_count - block
@@ -451,7 +450,7 @@
     )(
         source_rows,
         receiver_rows,
-        in_hbm(node_latent),
+        in_hbm(latent_after),
         in_hbm(node_in_weight),
         in_hbm(node_out_weight),
         in_hbm(edge_latent),
@@ -479,7 +478,7 @@
         edge_specs += [hbm] + [vmem] * (pieces_count - 1)
     edge_operands += [in_hbm(row) for row in rows]
     edge_specs += [hbm] * len(rows)
-    copy_count = 3 + 4 + 1 + 2 + 1 + steps
+    copy_count = 3 + 4 + 1 + 3 + steps
     edge_new, partial_sums = pl.pallas_call(
         functools.partial(
             edge_kernel, pieces_count, len(got), part_count, near_cap, halved, block

time: 35.9 us -> 34.8 us (0.969)
  waiting for transfers between devices: 5.17 us -> 4.1 us
  Pallas kernels: 16.9 us -> 17.4 us
  starting transfers between devices: 12.7 us -> 12.3 us
    ppermute x7, waiting for transfers between devices: 2 us -> 1.2 us  [from_subs(): lax.ppermute(piece, 'sub', [(at, (at + turn) % subs) for at in range(subs)])]
    all_to_all x1, waiting for transfers between devices: 0.76 us -> 0.01 us  [exchange_halves(): lax.all_to_all(blocks, ('region', 'feat'), split_axis=0, concat_axis=0, t...]
    ppermute x3, waiting for transfers between devices: 1.39 us -> 2.02 us  [from_feats(): lax.ppermute(weight, 'feat', [(at, (at + shift) % feats) for at in range(...]
    pallas_call x1, Pallas kernels: 3.93 us -> 4.51 us  [shards(): pl.pallas_call(functools.partial(gather_kernel, near_cap, far_cap, halved...]
    ppermute x1, starting transfers between devices: 0.56 us -> 0.2 us  [shards(): lax.ppermute(partial_sums, 'sub', [(at, (at + 1) % subs) for at in range(...]
  transfers between devices with their start and end apart: 12 -> 12, of which waited for: 6 -> 5; matrix products, arithmetic and copies ran while one was open for 0% -> 0% of each run, Pallas kernels for 42% -> 44%
where the time goes in v16:
time: 34.8 us; the launch traced here: 34.5 us
  Pallas kernels  17.4 us (50%)
  starting transfers between devices  12.3 us (35%)
  waiting for transfers between devices  4.1 us (12%)
  between operations  0.73 us (2%)
    pallas_call x1, Pallas kernels, shards(): pl.pallas_call(functools.partial(edge_kernel, pieces_count, len(got), par...  8.76 us
    ppermute x3, starting transfers between devices, from_feats(): lax.ppermute(weight, 'feat', [(at, (at + shift) % feats) for at in range(...  6.23 us
    all_to_all x1, starting transfers between devices, exchange_halves(): lax.all_to_all(blocks, ('region', 'feat'), split_axis=0, concat_axis=0, t...  4.88 us
    pallas_call x1, Pallas kernels, shards(): pl.pallas_call(functools.partial(gather_kernel, near_cap, far_cap, halved...  4.51 us
    pallas_call x1, Pallas kernels, exchange_halves(): pl.pallas_call(functools.partial(pick_kernel, part_count, near_cap, far_c...  2.08 us
    ppermute x3, waiting for transfers between devices, from_feats(): lax.ppermute(weight, 'feat', [(at, (at + shift) % feats) for at in range(...  2.02 us
    pallas_call x1, Pallas kernels, shards(): pl.pallas_call(functools.partial(node_kernel, pieces_count), out_shape=ja...  2.01 us
    ppermute x7, waiting for transfers between devices, from_subs(): lax.ppermute(piece, 'sub', [(at, (at + turn) % subs) for at in range(subs)])  1.2 us
  transfers between devices with their start and end apart: 12, of which 5 were waited for; matrix products, arithmetic and copies ran while one was open for 0% of the time, Pallas kernels for 44%

profile of v16, /device:TPU:0, one launch (start us, length us, event | category | flops | bytes accessed | tf_op | source)
XLA Modules:
  0.0 34.5 jit_solution(15683755569160188038)
XLA Ops:
  0.6 3.0 %collective-permute-start = (bf16[3,128,512]{2,1,0:T(8,128)(2,1)}, bf16[3,128,512]{2,1,0:T(8,128)(2,1)}, u32[]{:S(2)}, u32[]{:S(2)}) collective-permute-start(bf16[3,128,512]{2,1,0:T(8,128)(2,1)} %refs_6_.1), channel_id=1, source_target_pairs={{0,2},{2,0},{1,3},{3,1},{4,6},{6,4},{5,7},{7,5},{8,10},{10,8},{9,1... | collective-permute-start | bytes 1179656 | tf_op jit(solution)/shard_map/ppermute | solution.py:241
  3.6 2.1 %pick_halo.1 = bf16[8,17,512]{2,1,0:T(8,128)(2,1)} custom-call(s32[1,2,8]{2,1,0:T(2,128)} %bitcast.17, s32[1,4,32]{2,1,0:T(4,128)} %near_ref.1, bf16[384,512]{1,0:T(8,128)(2,1)} %refs_0_.3), custom_call_target="tpu_custom_call" | custom-call | tf_op jit(solution)/shard_map/pick_halo/pallas_call | solution.py:99
  5.7 4.9 %all-to-all-start = ((bf16[8,17,512]{2,1,0:T(8,128)(2,1)}), bf16[8,17,512]{2,1,0:T(8,128)(2,1)S(1)}, u32[]{:S(2)}, u32[]{:S(2)}) async-start(bf16[8,17,512]{2,1,0:T(8,128)(2,1)} %pick_halo.1), calls=%async_computation | async-start | bytes 393216 | tf_op jit(solution)/shard_map/all_to_all | solution.py:109
  10.6 0.0 collective-permute-start.2
  10.6 2.0 %collective-permute-start.1 = (bf16[128,512]{1,0:T(8,128)(2,1)}, bf16[128,512]{1,0:T(8,128)(2,1)}, u32[]{:S(2)}, u32[]{:S(2)}) collective-permute-start(bf16[128,512]{1,0:T(8,128)(2,1)} %refs_10_.1), channel_id=1, source_target_pairs={{0,2},{2,0},{1,3},{3,1},{4,6},{6,4},{5,7},{7,5},{8,10},{10,8},{9,1... | collective-permute-start | bytes 393224 | tf_op jit(solution)/shard_map/ppermute | solution.py:241
  12.6 0.2 collective-permute-start.4
  12.8 4.5 %gather_latents.1 = (bf16[768,1792]{1,0:T(8,128)(2,1)S(1)}, bf16[768,1280]{1,0:T(8,128)(2,1)}, bf16[384,1536]{1,0:T(8,128)(2,1)}, bf16[3,128,512]{2,1,0:T(8,128)(2,1)S(1)}) custom-call(s32[12,128]{1,0:T(8,128)} %bitcast.15, s32[12,128]{1,0:T(8,128)} %bitcast.16, bf16[384,512]{1,0:T(8,128)(2,1)} %refs_0_.3, bf16[2,128,512]{2,1,0:T(8,128)(2,1)} %node_in_ref.1, ...), custom_call_target="tpu_custom_call" | custom-call | tf_op jit(solution)/shard_map/gather_latents/pallas_call | solution.py:432
  17.4 1.3 %collective-permute-done.1.refs_12_ = bf16[128,512]{1,0:T(8,128)(2,1)} collective-permute-done((bf16[128,512]{1,0:T(8,128)(2,1)}, bf16[128,512]{1,0:T(8,128)(2,1)}, u32[]{:S(2)}, u32[]{:S(2)}) %collective-permute-start.1) | collective-permute-done | bytes 131104 | tf_op jit(solution)/shard_map/ppermute | solution.py:241
  18.7 0.0 all-to-all-done.refs_4_
  18.7 0.5 %collective-permute-start.3 = (bf16[8,17,512]{2,1,0:T(8,128)(2,1)S(1)}, bf16[8,17,512]{2,1,0:T(8,128)(2,1)S(1)}, u32[]{:S(2)}, u32[]{:S(2)}) collective-permute-start(bf16[8,17,512]{2,1,0:T(8,128)(2,1)S(1)} %all-to-all-done.refs_4_), channel_id=1, source_target_pairs={{0,1},{1,0},{2,3},{3,2},{4,5},{5,4},{6,7},{7,6},{8,9},{9,8},{10,11... | collective-permute-start | bytes 417800 | tf_op jit(solution)/shard_map/ppermute | solution.py:249
  19.2 0.1 collective-permute-start.6
  19.3 1.2 %collective-permute-start.9 = (bf16[3,128,512]{2,1,0:T(8,128)(2,1)S(1)}, bf16[3,128,512]{2,1,0:T(8,128)(2,1)S(1)}, u32[]{:S(2)}, u32[]{:S(2)}) collective-permute-start(bf16[3,128,512]{2,1,0:T(8,128)(2,1)S(1)} %get-tuple-element.31.refs_3_), channel_id=1, source_target_pairs={{0,2},{2,0},{1,3},{3,1},{4,6},{6,4},{5,7},{7,5},{8,10},{10,8},{9,1... | collective-permute-start | bytes 1179656 | tf_op jit(solution)/shard_map/ppermute | solution.py:241
  20.5 0.2 collective-permute-start.8
  20.6 0.4 %collective-permute-done.6.refs_13_ = bf16[128,512]{1,0:T(8,128)(2,1)S(1)} collective-permute-done((bf16[128,512]{1,0:T(8,128)(2,1)}, bf16[128,512]{1,0:T(8,128)(2,1)S(1)}, u32[]{:S(2)}, u32[]{:S(2)}) %collective-permute-start.6) | collective-permute-done | bytes 131104 | tf_op jit(solution)/shard_map/ppermute | solution.py:249
  21.0 0.0 copy-start.1
  21.0 0.0 copy-start.2
  21.0 0.0 copy-start.3
  21.0 0.0 copy-start.4
  21.1 8.8 %edge_update.1 = (bf16[1536,512]{1,0:T(8,128)(2,1)}, bf16[384,512]{1,0:T(8,128)(2,1)S(1)}) custom-call(bf16[1536,512]{1,0:T(8,128)(2,1)} %refs_0_.2, bf16[768,1280]{1,0:T(8,128)(2,1)} %get-tuple-element.22.refs_1_, bf16[384,1536]{1,0:T(8,128)(2,1)} %get-tuple-element.23.refs_2_, bf16[768,1792]{1,0:T(8,128)(2,1)S(1)} %get-tuple-element.24.refs_3_, ...), custom_call_target="tpu_custom_call" | custom-call | flops 3825205248 | bytes 6291456 | tf_op jit(solution)/shard_map/edge_update/pallas_call | solution.py:482
  29.8 0.2 collective-permute-start.7
  30.0 0.7 %collective-permute-done.9.refs_5_ = bf16[3,128,512]{2,1,0:T(8,128)(2,1)S(1)} collective-permute-done((bf16[3,128,512]{2,1,0:T(8,128)(2,1)S(1)}, bf16[3,128,512]{2,1,0:T(8,128)(2,1)S(1)}, u32[]{:S(2)}, u32[]{:S(2)}) %collective-permute-start.9) | collective-permute-done | bytes 393248 | tf_op jit(solution)/shard_map/ppermute | solution.py:241
  30.7 0.9 %collective-permute-done.7.refs_2_ = bf16[384,512]{1,0:T(8,128)(2,1)S(1)} collective-permute-done((bf16[384,512]{1,0:T(8,128)(2,1)S(1)}, bf16[384,512]{1,0:T(8,128)(2,1)S(1)}, u32[]{:S(2)}, u32[]{:S(2)}) %collective-permute-start.7) | collective-permute-done | bytes 393248 | tf_op jit(solution)/shard_map/ppermute | solution.py:516
  31.6 0.8 %collective-permute-done.10.refs_6_ = bf16[3,128,512]{2,1,0:T(8,128)(2,1)S(1)} collective-permute-done((bf16[3,128,512]{2,1,0:T(8,128)(2,1)S(1)}, bf16[3,128,512]{2,1,0:T(8,128)(2,1)S(1)}, u32[]{:S(2)}, u32[]{:S(2)}) %collective-permute-start.10) | collective-permute-done | bytes 393248 | tf_op jit(solution)/shard_map/ppermute | solution.py:249
  32.5 2.0 %node_update.1 = bf16[384,512]{1,0:T(8,128)(2,1)} custom-call(bf16[384,512]{1,0:T(8,128)(2,1)S(1)} %copy-done, bf16[384,512]{1,0:T(8,128)(2,1)S(1)} %get-tuple-element.30.refs_1_, bf16[384,512]{1,0:T(8,128)(2,1)S(1)} %collective-permute-done.7.refs_2_, bf16[3,128,512]{2,1,0:T(8,128)(2,1)S(1)} %get-tuple-element.31.refs_3_, ...), custom_call_target="tpu_custom_call" | custom-call | flops 603979776 | bytes 1966080 | tf_op jit(solution)/shard_map/node_update/pallas_call | solution.py:519
  (14 shorter events, 0.0 us)
Async XLA Ops:
  0.6 18.1 %collective-permute-start = (bf16[3,128,512]{2,1,0:T(8,128)(2,1)}, bf16[3,128,512]{2,1,0:T(8,128)(2,1)}, u32[]{:S(2)}, u32[]{:S(2)}) collective-permute-start(bf16[3,128,512]{2,1,0:T(8,128)(2,1)} %refs_6_.1), channel_id=1, source_target_pairs={{0,2},{2,0},{1,3},{3,1},{4,6},{6,4},{5,7},{7,5},{8,10},{10,8},{9,1... | collective-permute-start | bytes 1179656 | tf_op jit(solution)/shard_map/ppermute | solution.py:241
  5.7 13.0 %all-to-all-start = ((bf16[8,17,512]{2,1,0:T(8,128)(2,1)}), bf16[8,17,512]{2,1,0:T(8,128)(2,1)S(1)}, u32[]{:S(2)}, u32[]{:S(2)}) async-start(bf16[8,17,512]{2,1,0:T(8,128)(2,1)} %pick_halo.1), calls=%async_computation | async-start | bytes 393216 | tf_op jit(solution)/shard_map/all_to_all | solution.py:109
  10.6 2.3 %collective-permute-start.2 = (bf16[128,512]{1,0:T(8,128)(2,1)}, bf16[128,512]{1,0:T(8,128)(2,1)S(1)}, u32[]{:S(2)}, u32[]{:S(2)}) collective-permute-start(bf16[128,512]{1,0:T(8,128)(2,1)} %refs_10_.1), channel_id=1, source_target_pairs={{0,1},{1,0},{2,3},{3,2},{4,5},{5,4},{6,7},{7,6},{8,9},{9,8},{10,11... | collective-permute-start | bytes 393224 | tf_op jit(solution)/shard_map/ppermute | solution.py:249
  10.6 8.1 %collective-permute-start.1 = (bf16[128,512]{1,0:T(8,128)(2,1)}, bf16[128,512]{1,0:T(8,128)(2,1)}, u32[]{:S(2)}, u32[]{:S(2)}) collective-permute-start(bf16[128,512]{1,0:T(8,128)(2,1)} %refs_10_.1), channel_id=1, source_target_pairs={{0,2},{2,0},{1,3},{3,1},{4,6},{6,4},{5,7},{7,5},{8,10},{10,8},{9,1... | collective-permute-start | bytes 393224 | tf_op jit(solution)/shard_map/ppermute | solution.py:241
  12.6 7.9 %collective-permute-start.4 = (bf16[3,128,512]{2,1,0:T(8,128)(2,1)}, bf16[3,128,512]{2,1,0:T(8,128)(2,1)}, u32[]{:S(2)}, u32[]{:S(2)}) collective-permute-start(bf16[3,128,512]{2,1,0:T(8,128)(2,1)} %refs_6_.1), channel_id=1, source_target_pairs={{0,1},{1,0},{2,3},{3,2},{4,5},{5,4},{6,7},{7,6},{8,9},{9,8},{10,11... | collective-permute-start | bytes 1179656 | tf_op jit(solution)/shard_map/ppermute | solution.py:249
  18.7 2.3 %collective-permute-start.5 = (bf16[3,128,512]{2,1,0:T(8,128)(2,1)}, bf16[3,128,512]{2,1,0:T(8,128)(2,1)S(1)}, u32[]{:S(2)}, u32[]{:S(2)}) collective-permute-start(bf16[3,128,512]{2,1,0:T(8,128)(2,1)} %collective-permute-done.refs_8_), channel_id=1, source_target_pairs={{0,1},{1,0},{2,3},{3,2},{4,5},{5,4},{6,7},{7,6},{8,9},{9,8},{10,11... | collective-permute-start | bytes 1179656 | tf_op jit(solution)/shard_map/ppermute | solution.py:249
  18.7 2.3 %collective-permute-start.3 = (bf16[8,17,512]{2,1,0:T(8,128)(2,1)S(1)}, bf16[8,17,512]{2,1,0:T(8,128)(2,1)S(1)}, u32[]{:S(2)}, u32[]{:S(2)}) collective-permute-start(bf16[8,17,512]{2,1,0:T(8,128)(2,1)S(1)} %all-to-all-done.refs_4_), channel_id=1, source_target_pairs={{0,1},{1,0},{2,3},{3,2},{4,5},{5,4},{6,7},{7,6},{8,9},{9,8},{10,11... | collective-permute-start | bytes 417800 | tf_op jit(solution)/shard_map/ppermute | solution.py:249
  19.2 1.8 %collective-permute-start.6 = (bf16[128,512]{1,0:T(8,128)(2,1)}, bf16[128,512]{1,0:T(8,128)(2,1)S(1)}, u32[]{:S(2)}, u32[]{:S(2)}) collective-permute-start(bf16[128,512]{1,0:T(8,128)(2,1)} %collective-permute-done.1.refs_12_), channel_id=1, source_target_pairs={{0,1},{1,0},{2,3},{3,2},{4,5},{5,4},{6,7},{7,6},{8,9},{9,8},{10,11... | collective-permute-start | bytes 393224 | tf_op jit(solution)/shard_map/ppermute | solution.py:249
  19.3 11.5 %collective-permute-start.9 = (bf16[3,128,512]{2,1,0:T(8,128)(2,1)S(1)}, bf16[3,128,512]{2,1,0:T(8,128)(2,1)S(1)}, u32[]{:S(2)}, u32[]{:S(2)}) collective-permute-start(bf16[3,128,512]{2,1,0:T(8,128)(2,1)S(1)} %get-tuple-element.31.refs_3_), channel_id=1, source_target_pairs={{0,2},{2,0},{1,3},{3,1},{4,6},{6,4},{5,7},{7,5},{8,10},{10,8},{9,1... | collective-permute-start | bytes 1179656 | tf_op jit(solution)/shard_map/ppermute | solution.py:241
  20.5 10.2 %collective-permute-start.8 = (bf16[3,128,512]{2,1,0:T(8,128)(2,1)S(1)}, bf16[3,128,512]{2,1,0:T(8,128)(2,1)S(1)}, u32[]{:S(2)}, u32[]{:S(2)}) collective-permute-start(bf16[3,128,512]{2,1,0:T(8,128)(2,1)S(1)} %get-tuple-element.31.refs_3_), channel_id=1, source_target_pairs={{0,1},{1,0},{2,3},{3,2},{4,5},{5,4},{6,7},{7,6},{8,9},{9,8},{10,11... | collective-permute-start | bytes 1179656 | tf_op jit(solution)/shard_map/ppermute | solution.py:249
  21.0 11.5 %copy-start = (bf16[384,512]{1,0:T(8,128)(2,1)S(1)}, bf16[384,512]{1,0:T(8,128)(2,1)}, u32[]{:S(2)}) copy-start(bf16[384,512]{1,0:T(8,128)(2,1)} %refs_0_.3) | copy-start | bytes 1179652
  21.0 11.5 %copy-start.1 = (f32[512]{0:T(512)S(1)}, f32[512]{0:T(512)}, u32[]{:S(2)}) copy-start(f32[512]{0:T(512)} %param.32) | copy-start | bytes 6148
  21.0 11.4 %copy-start.2 = (f32[512]{0:T(512)S(1)}, f32[512]{0:T(512)}, u32[]{:S(2)}) copy-start(f32[512]{0:T(512)} %param.33) | copy-start | bytes 6148
  21.0 11.4 %copy-start.3 = (f32[512]{0:T(512)S(1)}, f32[512]{0:T(512)}, u32[]{:S(2)}) copy-start(f32[512]{0:T(512)} %param.34) | copy-start | bytes 6148
  21.0 11.4 %copy-start.4 = (f32[512]{0:T(512)S(1)}, f32[512]{0:T(512)}, u32[]{:S(2)}) copy-start(f32[512]{0:T(512)} %param.35) | copy-start | bytes 6148
  29.8 1.8 %collective-permute-start.7 = (bf16[384,512]{1,0:T(8,128)(2,1)S(1)}, bf16[384,512]{1,0:T(8,128)(2,1)S(1)}, u32[]{:S(2)}, u32[]{:S(2)}) collective-permute-start(bf16[384,512]{1,0:T(8,128)(2,1)S(1)} %get-tuple-element.30.refs_1_), channel_id=1, source_target_pairs={{0,1},{1,0},{2,3},{3,2},{4,5},{5,4},{6,7},{7,6},{8,9},{9,8},{10,11... | collective-permute-start | bytes 1179656 | tf_op jit(solution)/shard_map/ppermute | solution.py:516
  30.7 1.7 %collective-permute-start.10 = (bf16[3,128,512]{2,1,0:T(8,128)(2,1)S(1)}, bf16[3,128,512]{2,1,0:T(8,128)(2,1)S(1)}, u32[]{:S(2)}, u32[]{:S(2)}) collective-permute-start(bf16[3,128,512]{2,1,0:T(8,128)(2,1)S(1)} %collective-permute-done.9.refs_5_), channel_id=1, source_target_pairs={{0,1},{1,0},{2,3},{3,2},{4,5},{5,4},{6,7},{7,6},{8,9},{9,8},{10,11... | collective-permute-start | bytes 1179656 | tf_op jit(solution)/shard_map/ppermute | solution.py:249

commit v17 on v16

--- a/solution.py
+++ b/solution.py
@@ -13,6 +13,8 @@
 few_parts = 8
 grant = 32 << 20
 chunk_rows = 64
+first_rows = 512
+gather_rows = 512
 bf16 = jnp.bfloat16
 f32 = jnp.float32
 vmem = pl.BlockSpec(memory_space=pltpu.VMEM)
@@ -134,16 +136,15 @@
     edge_hbm,
     known,
     gathered_hbm,
-    to_node_hbm,
+    to_node,
     pack_ref,
     gathered,
-    to_node,
     sems,
 ):
     node_count, width = latent_ref.shape
     first = known.shape[0]
     edge_count = first + gathered.shape[0]
-    block = first // 2
+    block = gather_rows
     copies = []
 
     def start(source, target):
@@ -186,7 +187,6 @@
         to_node[:, row * lanes : (row + 1) * lanes] = jnp.where(
             node_place == receiver_ref[row : row + 1], 1.0, 0.0
         ).astype(bf16)
-    start(to_node, to_node_hbm)
     for at in range(first // block):
         gather(at, known, slice(at * block, (at + 1) * block), width)
     for copy in copies:
@@ -252,18 +252,20 @@
     ]
 
 
-def edge_kernel(pieces_count, got_count, part_count, near_cap, halved, block, *refs):
-    edge_hbm, gathered_hbm, to_node_hbm, known_first = refs[:4]
+def edge_kernel(pieces_count, got_count, part_count, near_cap, halved, *refs):
+    edge_hbm, gathered_hbm, to_node, known_first = refs[:4]
     got_refs = refs[4 : 4 + got_count]
     refs = refs[4 + got_count :]
     in_pieces, out_pieces = refs[:pieces_count], refs[pieces_count : 2 * pieces_count]
     row_refs = refs[2 * pieces_count : 2 * pieces_count + 4]
     new_hbm, sum_ref = refs[2 * pieces_count + 4 : 2 * pieces_count + 6]
-    known_rest, to_node, in_weight, out_weight, halo, rows, preact, hidden, output, new_ref, total, sems = (
+    known_rest, in_weight, out_weight, halo, rows, preact, hidden, output, new_ref, total, sems = (
         refs[2 * pieces_count + 6 :]
     )
     edge_count, width = new_hbm.shape
-    blocks = edge_count // block
+    known = [known_first, known_rest]
+    starts = [0, known_first.shape[0]]
+    blocks = len(known)
     taken = []
 
     def start(source, target):
@@ -285,15 +287,10 @@
     spot = pl.ds(pl.multiple_of(order[0] * count, count), count)
     later.append(start(out_pieces[0], out_weight.at[spot]))
     in_bias, out_bias, gain, offset = rows
-    rest = edge_count - block
     known_copies = [
-        start(edge_hbm.at[pl.ds(block, rest)], known_rest.at[:, pl.ds(0, width)]),
+        start(edge_hbm.at[pl.ds(starts[1], known_rest.shape[0])], known_rest.at[:, pl.ds(0, width)]),
         start(gathered_hbm, known_rest.at[:, pl.ds(width, known_rest.shape[1] - width)]),
-        start(to_node_hbm, to_node),
     ]
-
-    def known(at):
-        return known_first if at == 0 else known_rest.at[pl.ds((at - 1) * block, block)]
 
     place_halo(halo, part_count, near_cap, halved, got_refs)
     for which in (1, 0, 2):
@@ -314,11 +311,11 @@
             for copy in known_copies:
                 copy.wait()
         preact[at][...] = jnp.dot(
-            known(at)[...], in_weight[...], preferred_element_type=f32
+            known[at][...], in_weight[...], preferred_element_type=f32
         )
 
     def activate(at):
-        for start_row in range(0, block, chunk_rows):
+        for start_row in range(0, known[at].shape[0], chunk_rows):
             here = slice(start_row, start_row + chunk_rows)
             hidden[at][here] = silu(preact[at][here] + in_bias[...]).astype(bf16)
 
@@ -328,17 +325,17 @@
         )
 
     def normalise(at):
-        for start_row in range(0, block, chunk_rows):
+        for start_row in range(0, known[at].shape[0], chunk_rows):
             here = slice(start_row, start_row + chunk_rows)
-            there = slice(at * block + start_row, at * block + start_row + chunk_rows)
+            there = slice(starts[at] + start_row, starts[at] + start_row + chunk_rows)
             normed = layer_norm(output[at][here] + out_bias[...], gain[...], offset[...])
-            edges = known(at)[here, :width].astype(f32)
+            edges = known[at][here, :width].astype(f32)
             new_ref[there] = (edges + normed).astype(bf16)
-        spot = pl.ds(at * block, block)
+        spot = pl.ds(starts[at], known[at].shape[0])
         return start(new_ref.at[spot], new_hbm.at[spot])
 
     def sum_dot(at):
-        spot = slice(at * block, (at + 1) * block)
+        spot = slice(starts[at], starts[at] + known[at].shape[0])
         part = jnp.dot(to_node[:, spot], new_ref[spot], preferred_element_type=f32)
         if at > 0:
             part += total[...]
@@ -408,8 +405,6 @@
     edge_count = edge_latent.shape[0]
     near_cap, far_cap = near_rows.shape[2], far_rows.shape[2]
     part_count = far_rows.shape[1]
-    block = edge_count // 2
-    steps = edge_count // block
 
     far_edge = [from_feats(edge_in_weight), from_feats(edge_out_weight)]
     near_edge = [from_subs([edge_in_weight]), from_subs([edge_out_weight])]
@@ -428,21 +423,20 @@
     near_edge[1], latent_after = lax.optimization_barrier((near_edge[1], node_latent))
     gathered_width = 2 * width + halo_space
     known_width = width + gathered_width
-    rest = edge_count - block
+    sizes = [first_rows, edge_count - first_rows]
     known, gathered, to_node, node_weight = pl.pallas_call(
         functools.partial(gather_kernel, near_cap, far_cap, halved),
         out_shape=[
-            pltpu.VMEM((block, known_width), bf16),
-            pltpu.HBM((rest, gathered_width), bf16),
-            pltpu.HBM((node_count, edge_count), bf16),
-            pltpu.VMEM(pack_shape, bf16),
+            pltpu.VMEM((sizes[0], known_width), bf16),
+            pltpu.HBM((sizes[1], gathered_width), bf16),
+            pltpu.VMEM((node_count, edge_count), bf16),
+            pltpu.HBM(pack_shape, bf16),
         ],
         in_specs=[vmem] * 5 + [hbm],
-        out_specs=[vmem, hbm, hbm, vmem],
+        out_specs=[vmem, hbm, vmem, vmem],
         scratch_shapes=[
-            pltpu.VMEM((rest, gathered_width), bf16),
-            pltpu.VMEM((node_count, edge_count), bf16),
-            pltpu.SemaphoreType.DMA((2 + 2 * (steps - 1),)),
+            pltpu.VMEM((sizes[1], gathered_width), bf16),
+            pltpu.SemaphoreType.DMA((1 + sizes[1] // gather_rows,)),
         ],
         compiler_params=pltpu.CompilerParams(vmem_limit_bytes=grant),
         cost_estimate=pl.CostEstimate(flops=0, bytes_accessed=0, transcendentals=0),
@@ -470,19 +464,17 @@
     pieces_count = len(edge_in)
 
     rows = [value.reshape(1, -1) for value in (edge_in_bias, edge_out_bias, edge_gain, edge_offset)]
-    edge_operands = [in_hbm(edge_latent), in_hbm(gathered), in_hbm(to_node), in_vmem(known)]
+    edge_operands = [in_hbm(edge_latent), in_hbm(gathered), in_vmem(to_node), in_vmem(known)]
     edge_operands += [in_vmem(blocks) for blocks in got]
-    edge_specs = [hbm] * 3 + [vmem] * (1 + len(got))
+    edge_specs = [hbm] * 2 + [vmem] * (2 + len(got))
     for pieces in (edge_in, edge_out):
         edge_operands += [in_hbm(pieces[0])] + [in_vmem(piece) for piece in pieces[1:]]
         edge_specs += [hbm] + [vmem] * (pieces_count - 1)
     edge_operands += [in_hbm(row) for row in rows]
     edge_specs += [hbm] * len(rows)
-    copy_count = 3 + 4 + 1 + 3 + steps
+    copy_count = 3 + 4 + 1 + 2 + len(sizes)
     edge_new, partial_sums = pl.pallas_call(
-        functools.partial(
-            edge_kernel, pieces_count, len(got), part_count, near_cap, halved, block
-        ),
+        functools.partial(edge_kernel, pieces_count, len(got), part_count, near_cap, halved),
         out_shape=[
             pltpu.HBM((edge_count, width), bf16),
             jax.ShapeDtypeStruct((node_count, width), bf16),
@@ -490,15 +482,14 @@
         in_specs=edge_specs,
         out_specs=[hbm, vmem],
         scratch_shapes=[
-            pltpu.VMEM((rest, known_width), bf16),
-            pltpu.VMEM((node_count, edge_count), bf16),
+            pltpu.VMEM((sizes[1], known_width), bf16),
             pltpu.VMEM((known_width, width), bf16),
             pltpu.VMEM((width, width), bf16),
             pltpu.VMEM((halo_space, width), bf16),
             [pltpu.VMEM((1, width), f32)] * 4,
-            [pltpu.VMEM((block, width), f32)] * steps,
-            [pltpu.VMEM((block, width), bf16)] * steps,
-            [pltpu.VMEM((block, width), f32)] * steps,
+            [pltpu.VMEM((size, width), f32) for size in sizes],
+            [pltpu.VMEM((size, width), bf16) for size in sizes],
+            [pltpu.VMEM((size, width), f32) for size in sizes],
             pltpu.VMEM((edge_count, width), bf16),
             pltpu.VMEM((node_count, width), f32),
             pltpu.SemaphoreType.DMA((copy_count,)),

time: 34.8 us -> 34.9 us (level)
  transfers between devices with their start and end apart: 12 -> 12, of which waited for: 5 -> 5; matrix products, arithmetic and copies ran while one was open for 0% -> 0% of each run, Pallas kernels for 44% -> 45%
where the time goes in v17:
time: 34.9 us; the launch traced here: 34.6 us
  Pallas kernels  17.7 us (51%)
  starting transfers between devices  12.3 us (35%)
  waiting for transfers between devices  3.84 us (11%)
  between operations  0.74 us (2%)
    pallas_call x1, Pallas kernels, shards(): pl.pallas_call(functools.partial(edge_kernel, pieces_count, len(got), par...  8.86 us
    ppermute x3, starting transfers between devices, from_feats(): lax.ppermute(weight, 'feat', [(at, (at + shift) % feats) for at in range(...  6.23 us
    all_to_all x1, starting transfers between devices, exchange_halves(): lax.all_to_all(blocks, ('region', 'feat'), split_axis=0, concat_axis=0, t...  4.88 us
    pallas_call x1, Pallas kernels, shards(): pl.pallas_call(functools.partial(gather_kernel, near_cap, far_cap, halved...  4.77 us
    pallas_call x1, Pallas kernels, exchange_halves(): pl.pallas_call(functools.partial(pick_kernel, part_count, near_cap, far_c...  2.08 us
    pallas_call x1, Pallas kernels, shards(): pl.pallas_call(functools.partial(node_kernel, pieces_count), out_shape=ja...  2.01 us
    ppermute x3, waiting for transfers between devices, from_feats(): lax.ppermute(weight, 'feat', [(at, (at + shift) % feats) for at in range(...  1.87 us
    ppermute x7, waiting for transfers between devices, from_subs(): lax.ppermute(piece, 'sub', [(at, (at + turn) % subs) for at in range(subs)])  1.3 us
  transfers between devices with their start and end apart: 12, of which 5 were waited for; matrix products, arithmetic and copies ran while one was open for 0% of the time, Pallas kernels for 45%

profile of v17, /device:TPU:0, one launch (start us, length us, event | category | flops | bytes accessed | tf_op | source)
XLA Modules:
  0.0 34.6 jit_solution(1567806437986083807)
XLA Ops:
  0.6 3.0 %collective-permute-start = (bf16[3,128,512]{2,1,0:T(8,128)(2,1)}, bf16[3,128,512]{2,1,0:T(8,128)(2,1)}, u32[]{:S(2)}, u32[]{:S(2)}) collective-permute-start(bf16[3,128,512]{2,1,0:T(8,128)(2,1)} %refs_6_.1), channel_id=1, source_target_pairs={{0,2},{2,0},{1,3},{3,1},{4,6},{6,4},{5,7},{7,5},{8,10},{10,8},{9,1... | collective-permute-start | bytes 1179656 | tf_op jit(solution)/shard_map/ppermute | solution.py:241
  3.6 2.1 %pick_halo.1 = bf16[8,17,512]{2,1,0:T(8,128)(2,1)} custom-call(s32[1,2,8]{2,1,0:T(2,128)} %bitcast.17, s32[1,4,32]{2,1,0:T(4,128)} %near_ref.1, bf16[384,512]{1,0:T(8,128)(2,1)} %refs_0_.3), custom_call_target="tpu_custom_call" | custom-call | tf_op jit(solution)/shard_map/pick_halo/pallas_call | solution.py:101
  5.7 4.9 %all-to-all-start = ((bf16[8,17,512]{2,1,0:T(8,128)(2,1)}), bf16[8,17,512]{2,1,0:T(8,128)(2,1)S(1)}, u32[]{:S(2)}, u32[]{:S(2)}) async-start(bf16[8,17,512]{2,1,0:T(8,128)(2,1)} %pick_halo.1), calls=%async_computation | async-start | bytes 393216 | tf_op jit(solution)/shard_map/all_to_all | solution.py:111
  10.6 0.0 collective-permute-start.2
  10.6 2.0 %collective-permute-start.1 = (bf16[128,512]{1,0:T(8,128)(2,1)}, bf16[128,512]{1,0:T(8,128)(2,1)S(1)}, u32[]{:S(2)}, u32[]{:S(2)}) collective-permute-start(bf16[128,512]{1,0:T(8,128)(2,1)} %refs_10_.1), channel_id=1, source_target_pairs={{0,2},{2,0},{1,3},{3,1},{4,6},{6,4},{5,7},{7,5},{8,10},{10,8},{9,1... | collective-permute-start | bytes 393224 | tf_op jit(solution)/shard_map/ppermute | solution.py:241
  12.6 0.2 collective-permute-start.4
  12.8 4.8 %gather_latents.1 = (bf16[512,1792]{1,0:T(8,128)(2,1)S(1)}, bf16[1024,1280]{1,0:T(8,128)(2,1)}, bf16[384,1536]{1,0:T(8,128)(2,1)S(1)}, bf16[3,128,512]{2,1,0:T(8,128)(2,1)}) custom-call(s32[12,128]{1,0:T(8,128)} %bitcast.15, s32[12,128]{1,0:T(8,128)} %bitcast.16, bf16[384,512]{1,0:T(8,128)(2,1)} %refs_0_.3, bf16[2,128,512]{2,1,0:T(8,128)(2,1)} %node_in_ref.1, ...), custom_call_target="tpu_custom_call" | custom-call | tf_op jit(solution)/shard_map/gather_latents/pallas_call | solution.py:427
  17.6 0.9 %collective-permute-done.1.refs_12_ = bf16[128,512]{1,0:T(8,128)(2,1)S(1)} collective-permute-done((bf16[128,512]{1,0:T(8,128)(2,1)}, bf16[128,512]{1,0:T(8,128)(2,1)S(1)}, u32[]{:S(2)}, u32[]{:S(2)}) %collective-permute-start.1) | collective-permute-done | bytes 131104 | tf_op jit(solution)/shard_map/ppermute | solution.py:241
  18.6 0.5 %collective-permute-start.3 = (bf16[8,17,512]{2,1,0:T(8,128)(2,1)S(1)}, bf16[8,17,512]{2,1,0:T(8,128)(2,1)S(1)}, u32[]{:S(2)}, u32[]{:S(2)}) collective-permute-start(bf16[8,17,512]{2,1,0:T(8,128)(2,1)S(1)} %all-to-all-done.refs_4_), channel_id=1, source_target_pairs={{0,1},{1,0},{2,3},{3,2},{4,5},{5,4},{6,7},{7,6},{8,9},{9,8},{10,11... | collective-permute-start | bytes 417800 | tf_op jit(solution)/shard_map/ppermute | solution.py:249
  19.1 0.1 collective-permute-start.6
  19.2 1.2 %collective-permute-start.9 = (bf16[3,128,512]{2,1,0:T(8,128)(2,1)}, bf16[3,128,512]{2,1,0:T(8,128)(2,1)S(1)}, u32[]{:S(2)}, u32[]{:S(2)}) collective-permute-start(bf16[3,128,512]{2,1,0:T(8,128)(2,1)} %get-tuple-element.31.refs_3_), channel_id=1, source_target_pairs={{0,2},{2,0},{1,3},{3,1},{4,6},{6,4},{5,7},{7,5},{8,10},{10,8},{9,1... | collective-permute-start | bytes 1179656 | tf_op jit(solution)/shard_map/ppermute | solution.py:241
  20.4 0.2 collective-permute-start.8
  20.5 0.2 collective-permute-done.6.refs_13_
  20.8 0.0 copy-start.1
  20.8 0.0 copy-start.2
  20.8 0.0 copy-start.3
  20.8 0.0 copy-start.4
  20.8 0.0 copy-start.5
  20.8 8.9 %edge_update.1 = (bf16[1536,512]{1,0:T(8,128)(2,1)}, bf16[384,512]{1,0:T(8,128)(2,1)S(1)}) custom-call(bf16[1536,512]{1,0:T(8,128)(2,1)} %refs_0_.2, bf16[1024,1280]{1,0:T(8,128)(2,1)} %get-tuple-element.22.refs_1_, bf16[384,1536]{1,0:T(8,128)(2,1)S(1)} %get-tuple-element.23.refs_2_, bf16[512,1792]{1,0:T(8,128)(2,1)S(1)} %get-tuple-element.24.refs_3_, ...), custom_call_target="tpu_custom_call" | custom-call | flops 3825205248 | bytes 6291456 | tf_op jit(solution)/shard_map/edge_update/pallas_call | solution.py:476
  29.7 0.2 collective-permute-start.7
  29.9 0.9 %collective-permute-done.9.refs_5_ = bf16[3,128,512]{2,1,0:T(8,128)(2,1)S(1)} collective-permute-done((bf16[3,128,512]{2,1,0:T(8,128)(2,1)}, bf16[3,128,512]{2,1,0:T(8,128)(2,1)S(1)}, u32[]{:S(2)}, u32[]{:S(2)}) %collective-permute-start.9) | collective-permute-done | bytes 393248 | tf_op jit(solution)/shard_map/ppermute | solution.py:241
  30.8 0.7 %collective-permute-done.7.refs_2_ = bf16[384,512]{1,0:T(8,128)(2,1)S(1)} collective-permute-done((bf16[384,512]{1,0:T(8,128)(2,1)S(1)}, bf16[384,512]{1,0:T(8,128)(2,1)S(1)}, u32[]{:S(2)}, u32[]{:S(2)}) %collective-permute-start.7) | collective-permute-done | bytes 393248 | tf_op jit(solution)/shard_map/ppermute | solution.py:507
  31.5 1.1 %collective-permute-done.10.refs_6_ = bf16[3,128,512]{2,1,0:T(8,128)(2,1)S(1)} collective-permute-done((bf16[3,128,512]{2,1,0:T(8,128)(2,1)S(1)}, bf16[3,128,512]{2,1,0:T(8,128)(2,1)S(1)}, u32[]{:S(2)}, u32[]{:S(2)}) %collective-permute-start.10) | collective-permute-done | bytes 393248 | tf_op jit(solution)/shard_map/ppermute | solution.py:249
  32.6 2.0 %node_update.1 = bf16[384,512]{1,0:T(8,128)(2,1)} custom-call(bf16[384,512]{1,0:T(8,128)(2,1)S(1)} %copy-done, bf16[384,512]{1,0:T(8,128)(2,1)S(1)} %get-tuple-element.30.refs_1_, bf16[384,512]{1,0:T(8,128)(2,1)S(1)} %collective-permute-done.7.refs_2_, bf16[3,128,512]{2,1,0:T(8,128)(2,1)S(1)} %copy-done.1, ...), custom_call_target="tpu_custom_call" | custom-call | flops 603979776 | bytes 1966080 | tf_op jit(solution)/shard_map/node_update/pallas_call | solution.py:510
  (16 shorter events, 0.0 us)
Async XLA Ops:
  0.6 17.9 %collective-permute-start = (bf16[3,128,512]{2,1,0:T(8,128)(2,1)}, bf16[3,128,512]{2,1,0:T(8,128)(2,1)}, u32[]{:S(2)}, u32[]{:S(2)}) collective-permute-start(bf16[3,128,512]{2,1,0:T(8,128)(2,1)} %refs_6_.1), channel_id=1, source_target_pairs={{0,2},{2,0},{1,3},{3,1},{4,6},{6,4},{5,7},{7,5},{8,10},{10,8},{9,1... | collective-permute-start | bytes 1179656 | tf_op jit(solution)/shard_map/ppermute | solution.py:241
  5.7 12.9 %all-to-all-start = ((bf16[8,17,512]{2,1,0:T(8,128)(2,1)}), bf16[8,17,512]{2,1,0:T(8,128)(2,1)S(1)}, u32[]{:S(2)}, u32[]{:S(2)}) async-start(bf16[8,17,512]{2,1,0:T(8,128)(2,1)} %pick_halo.1), calls=%async_computation | async-start | bytes 393216 | tf_op jit(solution)/shard_map/all_to_all | solution.py:111
  10.6 2.3 %collective-permute-start.2 = (bf16[128,512]{1,0:T(8,128)(2,1)}, bf16[128,512]{1,0:T(8,128)(2,1)S(1)}, u32[]{:S(2)}, u32[]{:S(2)}) collective-permute-start(bf16[128,512]{1,0:T(8,128)(2,1)} %refs_10_.1), channel_id=1, source_target_pairs={{0,1},{1,0},{2,3},{3,2},{4,5},{5,4},{6,7},{7,6},{8,9},{9,8},{10,11... | collective-permute-start | bytes 393224 | tf_op jit(solution)/shard_map/ppermute | solution.py:249
  10.6 8.0 %collective-permute-start.1 = (bf16[128,512]{1,0:T(8,128)(2,1)}, bf16[128,512]{1,0:T(8,128)(2,1)S(1)}, u32[]{:S(2)}, u32[]{:S(2)}) collective-permute-start(bf16[128,512]{1,0:T(8,128)(2,1)} %refs_10_.1), channel_id=1, source_target_pairs={{0,2},{2,0},{1,3},{3,1},{4,6},{6,4},{5,7},{7,5},{8,10},{10,8},{9,1... | collective-permute-start | bytes 393224 | tf_op jit(solution)/shard_map/ppermute | solution.py:241
  12.6 7.8 %collective-permute-start.4 = (bf16[3,128,512]{2,1,0:T(8,128)(2,1)}, bf16[3,128,512]{2,1,0:T(8,128)(2,1)}, u32[]{:S(2)}, u32[]{:S(2)}) collective-permute-start(bf16[3,128,512]{2,1,0:T(8,128)(2,1)} %refs_6_.1), channel_id=1, source_target_pairs={{0,1},{1,0},{2,3},{3,2},{4,5},{5,4},{6,7},{7,6},{8,9},{9,8},{10,11... | collective-permute-start | bytes 1179656 | tf_op jit(solution)/shard_map/ppermute | solution.py:249
  18.6 2.2 %collective-permute-start.5 = (bf16[3,128,512]{2,1,0:T(8,128)(2,1)}, bf16[3,128,512]{2,1,0:T(8,128)(2,1)S(1)}, u32[]{:S(2)}, u32[]{:S(2)}) collective-permute-start(bf16[3,128,512]{2,1,0:T(8,128)(2,1)} %collective-permute-done.refs_8_), channel_id=1, source_target_pairs={{0,1},{1,0},{2,3},{3,2},{4,5},{5,4},{6,7},{7,6},{8,9},{9,8},{10,11... | collective-permute-start | bytes 1179656 | tf_op jit(solution)/shard_map/ppermute | solution.py:249
  18.6 2.2 %collective-permute-start.3 = (bf16[8,17,512]{2,1,0:T(8,128)(2,1)S(1)}, bf16[8,17,512]{2,1,0:T(8,128)(2,1)S(1)}, u32[]{:S(2)}, u32[]{:S(2)}) collective-permute-start(bf16[8,17,512]{2,1,0:T(8,128)(2,1)S(1)} %all-to-all-done.refs_4_), channel_id=1, source_target_pairs={{0,1},{1,0},{2,3},{3,2},{4,5},{5,4},{6,7},{7,6},{8,9},{9,8},{10,11... | collective-permute-start | bytes 417800 | tf_op jit(solution)/shard_map/ppermute | solution.py:249
  19.1 1.7 %collective-permute-start.6 = (bf16[128,512]{1,0:T(8,128)(2,1)S(1)}, bf16[128,512]{1,0:T(8,128)(2,1)S(1)}, u32[]{:S(2)}, u32[]{:S(2)}) collective-permute-start(bf16[128,512]{1,0:T(8,128)(2,1)S(1)} %collective-permute-done.1.refs_12_), channel_id=1, source_target_pairs={{0,1},{1,0},{2,3},{3,2},{4,5},{5,4},{6,7},{7,6},{8,9},{9,8},{10,11... | collective-permute-start | bytes 393224 | tf_op jit(solution)/shard_map/ppermute | solution.py:249
  19.2 11.7 %collective-permute-start.9 = (bf16[3,128,512]{2,1,0:T(8,128)(2,1)}, bf16[3,128,512]{2,1,0:T(8,128)(2,1)S(1)}, u32[]{:S(2)}, u32[]{:S(2)}) collective-permute-start(bf16[3,128,512]{2,1,0:T(8,128)(2,1)} %get-tuple-element.31.refs_3_), channel_id=1, source_target_pairs={{0,2},{2,0},{1,3},{3,1},{4,6},{6,4},{5,7},{7,5},{8,10},{10,8},{9,1... | collective-permute-start | bytes 1179656 | tf_op jit(solution)/shard_map/ppermute | solution.py:241
  20.4 10.5 %collective-permute-start.8 = (bf16[3,128,512]{2,1,0:T(8,128)(2,1)}, bf16[3,128,512]{2,1,0:T(8,128)(2,1)S(1)}, u32[]{:S(2)}, u32[]{:S(2)}) collective-permute-start(bf16[3,128,512]{2,1,0:T(8,128)(2,1)} %get-tuple-element.31.refs_3_), channel_id=1, source_target_pairs={{0,1},{1,0},{2,3},{3,2},{4,5},{5,4},{6,7},{7,6},{8,9},{9,8},{10,11... | collective-permute-start | bytes 1179656 | tf_op jit(solution)/shard_map/ppermute | solution.py:249
  20.8 11.8 %copy-start = (bf16[384,512]{1,0:T(8,128)(2,1)S(1)}, bf16[384,512]{1,0:T(8,128)(2,1)}, u32[]{:S(2)}) copy-start(bf16[384,512]{1,0:T(8,128)(2,1)} %refs_0_.3) | copy-start | bytes 1179652
  20.8 11.8 %copy-start.1 = (bf16[3,128,512]{2,1,0:T(8,128)(2,1)S(1)}, bf16[3,128,512]{2,1,0:T(8,128)(2,1)}, u32[]{:S(2)}) copy-start(bf16[3,128,512]{2,1,0:T(8,128)(2,1)} %get-tuple-element.31.refs_3_) | copy-start | bytes 1179652
  20.8 11.8 %copy-start.2 = (f32[512]{0:T(512)S(1)}, f32[512]{0:T(512)}, u32[]{:S(2)}) copy-start(f32[512]{0:T(512)} %param.32) | copy-start | bytes 6148
  20.8 11.8 %copy-start.3 = (f32[512]{0:T(512)S(1)}, f32[512]{0:T(512)}, u32[]{:S(2)}) copy-start(f32[512]{0:T(512)} %param.33) | copy-start | bytes 6148
  20.8 11.8 %copy-start.4 = (f32[512]{0:T(512)S(1)}, f32[512]{0:T(512)}, u32[]{:S(2)}) copy-start(f32[512]{0:T(512)} %param.34) | copy-start | bytes 6148
  20.8 11.8 %copy-start.5 = (f32[512]{0:T(512)S(1)}, f32[512]{0:T(512)}, u32[]{:S(2)}) copy-start(f32[512]{0:T(512)} %param.35) | copy-start | bytes 6148
  29.7 1.8 %collective-permute-start.7 = (bf16[384,512]{1,0:T(8,128)(2,1)S(1)}, bf16[384,512]{1,0:T(8,128)(2,1)S(1)}, u32[]{:S(2)}, u32[]{:S(2)}) collective-permute-start(bf16[384,512]{1,0:T(8,128)(2,1)S(1)} %get-tuple-element.30.refs_1_), channel_id=1, source_target_pairs={{0,1},{1,0},{2,3},{3,2},{4,5},{5,4},{6,7},{7,6},{8,9},{9,8},{10,11... | collective-permute-start | bytes 1179656 | tf_op jit(solution)/shard_map/ppermute | solution.py:507
  30.8 1.7 %collective-permute-start.10 = (bf16[3,128,512]{2,1,0:T(8,128)(2,1)S(1)}, bf16[3,128,512]{2,1,0:T(8,128)(2,1)S(1)}, u32[]{:S(2)}, u32[]{:S(2)}) collective-permute-start(bf16[3,128,512]{2,1,0:T(8,128)(2,1)S(1)} %collective-permute-done.9.refs_5_), channel_id=1, source_target_pairs={{0,1},{1,0},{2,3},{3,2},{4,5},{5,4},{6,7},{7,6},{8,9},{9,8},{10,11... | collective-permute-start | bytes 1179656 | tf_op jit(solution)/shard_map/ppermute | solution.py:249

commit v18 on v17

--- a/solution.py
+++ b/solution.py
@@ -13,8 +13,7 @@
 few_parts = 8
 grant = 32 << 20
 chunk_rows = 64
-first_rows = 512
-gather_rows = 512
+block_rows = 512
 bf16 = jnp.bfloat16
 f32 = jnp.float32
 vmem = pl.BlockSpec(memory_space=pltpu.VMEM)
@@ -144,7 +143,7 @@
     node_count, width = latent_ref.shape
     first = known.shape[0]
     edge_count = first + gathered.shape[0]
-    block = gather_rows
+    block = block_rows
     copies = []
 
     def start(source, target):
@@ -263,9 +262,9 @@
         refs[2 * pieces_count + 6 :]
     )
     edge_count, width = new_hbm.shape
-    known = [known_first, known_rest]
-    starts = [0, known_first.shape[0]]
-    blocks = len(known)
+    block = known_first.shape[0]
+    blocks = edge_count // block
+    known = [known_first]
     taken = []
 
     def start(source, target):
@@ -287,10 +286,19 @@
     spot = pl.ds(pl.multiple_of(order[0] * count, count), count)
     later.append(start(out_pieces[0], out_weight.at[spot]))
     in_bias, out_bias, gain, offset = rows
-    known_copies = [
-        start(edge_hbm.at[pl.ds(starts[1], known_rest.shape[0])], known_rest.at[:, pl.ds(0, width)]),
-        start(gathered_hbm, known_rest.at[:, pl.ds(width, known_rest.shape[1] - width)]),
-    ]
+    known_copies = [[]]
+    for at in range(1, blocks):
+        spot, rows_here = pl.ds(at * block, block), pl.ds((at - 1) * block, block)
+        view = known_rest.at[rows_here]
+        known.append(view)
+        known_copies.append(
+            [
+                start(edge_hbm.at[spot], view.at[:, pl.ds(0, width)]),
+                start(
+                    gathered_hbm.at[rows_here], view.at[:, pl.ds(width, view.shape[1] - width)]
+                ),
+            ]
+        )
 
     place_halo(halo, part_count, near_cap, halved, got_refs)
     for which in (1, 0, 2):
@@ -307,15 +315,14 @@
         copy.wait()
 
     def in_dot(at):
-        if at == 1:
-            for copy in known_copies:
-                copy.wait()
+        for copy in known_copies[at]:
+            copy.wait()
         preact[at][...] = jnp.dot(
             known[at][...], in_weight[...], preferred_element_type=f32
         )
 
     def activate(at):
-        for start_row in range(0, known[at].shape[0], chunk_rows):
+        for start_row in range(0, block, chunk_rows):
             here = slice(start_row, start_row + chunk_rows)
             hidden[at][here] = silu(preact[at][here] + in_bias[...]).astype(bf16)
 
@@ -325,17 +332,17 @@
         )
 
     def normalise(at):
-        for start_row in range(0, known[at].shape[0], chunk_rows):
+        for start_row in range(0, block, chunk_rows):
             here = slice(start_row, start_row + chunk_rows)
-            there = slice(starts[at] + start_row, starts[at] + start_row + chunk_rows)
+            there = slice(at * block + start_row, at * block + start_row + chunk_rows)
             normed = layer_norm(output[at][here] + out_bias[...], gain[...], offset[...])
             edges = known[at][here, :width].astype(f32)
             new_ref[there] = (edges + normed).astype(bf16)
-        spot = pl.ds(starts[at], known[at].shape[0])
+        spot = pl.ds(at * block, block)
         return start(new_ref.at[spot], new_hbm.at[spot])
 
     def sum_dot(at):
-        spot = slice(starts[at], starts[at] + known[at].shape[0])
+        spot = slice(at * block, (at + 1) * block)
         part = jnp.dot(to_node[:, spot], new_ref[spot], preferred_element_type=f32)
         if at > 0:
             part += total[...]
@@ -423,20 +430,21 @@
     near_edge[1], latent_after = lax.optimization_barrier((near_edge[1], node_latent))
     gathered_width = 2 * width + halo_space
     known_width = width + gathered_width
-    sizes = [first_rows, edge_count - first_rows]
+    steps = edge_count // block_rows
+    rest = edge_count - block_rows
     known, gathered, to_node, node_weight = pl.pallas_call(
         functools.partial(gather_kernel, near_cap, far_cap, halved),
         out_shape=[
-            pltpu.VMEM((sizes[0], known_width), bf16),
-            pltpu.HBM((sizes[1], gathered_width), bf16),
+            pltpu.VMEM((block_rows, known_width), bf16),
+            pltpu.HBM((rest, gathered_width), bf16),
             pltpu.VMEM((node_count, edge_count), bf16),
             pltpu.HBM(pack_shape, bf16),
         ],
         in_specs=[vmem] * 5 + [hbm],
         out_specs=[vmem, hbm, vmem, vmem],
         scratch_shapes=[
-            pltpu.VMEM((sizes[1], gathered_width), bf16),
-            pltpu.SemaphoreType.DMA((1 + sizes[1] // gather_rows,)),
+            pltpu.VMEM((rest, gathered_width), bf16),
+            pltpu.SemaphoreType.DMA((steps,)),
         ],
         compiler_params=pltpu.CompilerParams(vmem_limit_bytes=grant),
         cost_estimate=pl.CostEstimate(flops=0, bytes_accessed=0, transcendentals=0),
@@ -472,7 +480,7 @@
         edge_specs += [hbm] + [vmem] * (pieces_count - 1)
     edge_operands += [in_hbm(row) for row in rows]
     edge_specs += [hbm] * len(rows)
-    copy_count = 3 + 4 + 1 + 2 + len(sizes)
+    copy_count = 3 + 4 + 1 + 3 * steps
     edge_new, partial_sums = pl.pallas_call(
         functools.partial(edge_kernel, pieces_count, len(got), part_count, near_cap, halved),
         out_shape=[
@@ -482,14 +490,14 @@
         in_specs=edge_specs,
         out_specs=[hbm, vmem],
         scratch_shapes=[
-            pltpu.VMEM((sizes[1], known_width), bf16),
+            pltpu.VMEM((rest, known_width), bf16),
             pltpu.VMEM((known_width, width), bf16),
             pltpu.VMEM((width, width), bf16),
             pltpu.VMEM((halo_space, width), bf16),
             [pltpu.VMEM((1, width), f32)] * 4,
-            [pltpu.VMEM((size, width), f32) for size in sizes],
-            [pltpu.VMEM((size, width), bf16) for size in sizes],
-            [pltpu.VMEM((size, width), f32) for size in sizes],
+            [pltpu.VMEM((block_rows, width), f32) for _ in range(steps)],
+            [pltpu.VMEM((block_rows, width), bf16) for _ in range(steps)],
+            [pltpu.VMEM((block_rows, width), f32) for _ in range(steps)],
             pltpu.VMEM((edge_count, width), bf16),
             pltpu.VMEM((node_count, width), f32),
             pltpu.SemaphoreType.DMA((copy_count,)),

time: 34.9 us -> 34.9 us (level)
  no operation moved by 1% of the time
where the time goes in v18:
time: 34.9 us; the launch traced here: 34.6 us
  Pallas kernels  17.6 us (50%)
  starting transfers between devices  12.3 us (35%)
  waiting for transfers between devices  3.92 us (11%)
  between operations  0.74 us (2%)
    pallas_call x1, Pallas kernels, shards(): pl.pallas_call(functools.partial(edge_kernel, pieces_count, len(got), par...  8.79 us
    ppermute x3, starting transfers between devices, from_feats(): lax.ppermute(weight, 'feat', [(at, (at + shift) % feats) for at in range(...  6.23 us
    all_to_all x1, starting transfers between devices, exchange_halves(): lax.all_to_all(blocks, ('region', 'feat'), split_axis=0, concat_axis=0, t...  4.88 us
    pallas_call x1, Pallas kernels, shards(): pl.pallas_call(functools.partial(gather_kernel, near_cap, far_cap, halved...  4.77 us
    pallas_call x1, Pallas kernels, exchange_halves(): pl.pallas_call(functools.partial(pick_kernel, part_count, near_cap, far_c...  2.08 us
    pallas_call x1, Pallas kernels, shards(): pl.pallas_call(functools.partial(node_kernel, pieces_count), out_shape=ja...  2.01 us
    ppermute x3, waiting for transfers between devices, from_feats(): lax.ppermute(weight, 'feat', [(at, (at + shift) % feats) for at in range(...  1.95 us
    ppermute x7, waiting for transfers between devices, from_subs(): lax.ppermute(piece, 'sub', [(at, (at + turn) % subs) for at in range(subs)])  1.38 us
  transfers between devices with their start and end apart: 12, of which 5 were waited for; matrix products, arithmetic and copies ran while one was open for 0% of the time, Pallas kernels for 45%

profile of v18, /device:TPU:0, one launch (start us, length us, event | category | flops | bytes accessed | tf_op | source)
XLA Modules:
  0.0 34.6 jit_solution(5197571590986326994)
XLA Ops:
  0.6 3.0 %collective-permute-start = (bf16[3,128,512]{2,1,0:T(8,128)(2,1)}, bf16[3,128,512]{2,1,0:T(8,128)(2,1)}, u32[]{:S(2)}, u32[]{:S(2)}) collective-permute-start(bf16[3,128,512]{2,1,0:T(8,128)(2,1)} %refs_6_.1), channel_id=1, source_target_pairs={{0,2},{2,0},{1,3},{3,1},{4,6},{6,4},{5,7},{7,5},{8,10},{10,8},{9,1... | collective-permute-start | bytes 1179656 | tf_op jit(solution)/shard_map/ppermute | solution.py:240
  3.6 2.1 %pick_halo.1 = bf16[8,17,512]{2,1,0:T(8,128)(2,1)} custom-call(s32[1,2,8]{2,1,0:T(2,128)} %bitcast.17, s32[1,4,32]{2,1,0:T(4,128)} %near_ref.1, bf16[384,512]{1,0:T(8,128)(2,1)} %refs_0_.3), custom_call_target="tpu_custom_call" | custom-call | tf_op jit(solution)/shard_map/pick_halo/pallas_call | solution.py:100
  5.7 4.9 %all-to-all-start = ((bf16[8,17,512]{2,1,0:T(8,128)(2,1)}), bf16[8,17,512]{2,1,0:T(8,128)(2,1)S(1)}, u32[]{:S(2)}, u32[]{:S(2)}) async-start(bf16[8,17,512]{2,1,0:T(8,128)(2,1)} %pick_halo.1), calls=%async_computation | async-start | bytes 393216 | tf_op jit(solution)/shard_map/all_to_all | solution.py:110
  10.6 0.0 collective-permute-start.2
  10.6 2.0 %collective-permute-start.1 = (bf16[128,512]{1,0:T(8,128)(2,1)}, bf16[128,512]{1,0:T(8,128)(2,1)S(1)}, u32[]{:S(2)}, u32[]{:S(2)}) collective-permute-start(bf16[128,512]{1,0:T(8,128)(2,1)} %refs_10_.1), channel_id=1, source_target_pairs={{0,2},{2,0},{1,3},{3,1},{4,6},{6,4},{5,7},{7,5},{8,10},{10,8},{9,1... | collective-permute-start | bytes 393224 | tf_op jit(solution)/shard_map/ppermute | solution.py:240
  12.6 0.2 collective-permute-start.4
  12.8 4.8 %gather_latents.1 = (bf16[512,1792]{1,0:T(8,128)(2,1)S(1)}, bf16[1024,1280]{1,0:T(8,128)(2,1)}, bf16[384,1536]{1,0:T(8,128)(2,1)S(1)}, bf16[3,128,512]{2,1,0:T(8,128)(2,1)}) custom-call(s32[12,128]{1,0:T(8,128)} %bitcast.15, s32[12,128]{1,0:T(8,128)} %bitcast.16, bf16[384,512]{1,0:T(8,128)(2,1)} %refs_0_.3, bf16[2,128,512]{2,1,0:T(8,128)(2,1)} %node_in_ref.1, ...), custom_call_target="tpu_custom_call" | custom-call | tf_op jit(solution)/shard_map/gather_latents/pallas_call | solution.py:435
  17.6 0.9 %collective-permute-done.1.refs_12_ = bf16[128,512]{1,0:T(8,128)(2,1)S(1)} collective-permute-done((bf16[128,512]{1,0:T(8,128)(2,1)}, bf16[128,512]{1,0:T(8,128)(2,1)S(1)}, u32[]{:S(2)}, u32[]{:S(2)}) %collective-permute-start.1) | collective-permute-done | bytes 131104 | tf_op jit(solution)/shard_map/ppermute | solution.py:240
  18.6 0.5 %collective-permute-start.3 = (bf16[8,17,512]{2,1,0:T(8,128)(2,1)S(1)}, bf16[8,17,512]{2,1,0:T(8,128)(2,1)S(1)}, u32[]{:S(2)}, u32[]{:S(2)}) collective-permute-start(bf16[8,17,512]{2,1,0:T(8,128)(2,1)S(1)} %all-to-all-done.refs_4_), channel_id=1, source_target_pairs={{0,1},{1,0},{2,3},{3,2},{4,5},{5,4},{6,7},{7,6},{8,9},{9,8},{10,11... | collective-permute-start | bytes 417800 | tf_op jit(solution)/shard_map/ppermute | solution.py:248
  19.1 0.1 collective-permute-start.6
  19.2 1.2 %collective-permute-start.9 = (bf16[3,128,512]{2,1,0:T(8,128)(2,1)}, bf16[3,128,512]{2,1,0:T(8,128)(2,1)S(1)}, u32[]{:S(2)}, u32[]{:S(2)}) collective-permute-start(bf16[3,128,512]{2,1,0:T(8,128)(2,1)} %get-tuple-element.31.refs_3_), channel_id=1, source_target_pairs={{0,2},{2,0},{1,3},{3,1},{4,6},{6,4},{5,7},{7,5},{8,10},{10,8},{9,1... | collective-permute-start | bytes 1179656 | tf_op jit(solution)/shard_map/ppermute | solution.py:240
  20.4 0.2 collective-permute-start.8
  20.5 0.2 collective-permute-done.6.refs_13_
  20.8 0.0 copy-start.1
  20.8 0.0 copy-start.2
  20.8 0.0 copy-start.3
  20.8 0.0 copy-start.4
  20.8 0.0 copy-start.5
  20.8 8.8 %edge_update.1 = (bf16[1536,512]{1,0:T(8,128)(2,1)}, bf16[384,512]{1,0:T(8,128)(2,1)S(1)}) custom-call(bf16[1536,512]{1,0:T(8,128)(2,1)} %refs_0_.2, bf16[1024,1280]{1,0:T(8,128)(2,1)} %get-tuple-element.22.refs_1_, bf16[384,1536]{1,0:T(8,128)(2,1)S(1)} %get-tuple-element.23.refs_2_, bf16[512,1792]{1,0:T(8,128)(2,1)S(1)} %get-tuple-element.24.refs_3_, ...), custom_call_target="tpu_custom_call" | custom-call | flops 3825205248 | bytes 6291456 | tf_op jit(solution)/shard_map/edge_update/pallas_call | solution.py:484
  29.6 0.2 collective-permute-start.7
  29.8 1.0 %collective-permute-done.9.refs_5_ = bf16[3,128,512]{2,1,0:T(8,128)(2,1)S(1)} collective-permute-done((bf16[3,128,512]{2,1,0:T(8,128)(2,1)}, bf16[3,128,512]{2,1,0:T(8,128)(2,1)S(1)}, u32[]{:S(2)}, u32[]{:S(2)}) %collective-permute-start.9) | collective-permute-done | bytes 393248 | tf_op jit(solution)/shard_map/ppermute | solution.py:240
  30.8 0.6 %collective-permute-done.7.refs_2_ = bf16[384,512]{1,0:T(8,128)(2,1)S(1)} collective-permute-done((bf16[384,512]{1,0:T(8,128)(2,1)S(1)}, bf16[384,512]{1,0:T(8,128)(2,1)S(1)}, u32[]{:S(2)}, u32[]{:S(2)}) %collective-permute-start.7) | collective-permute-done | bytes 393248 | tf_op jit(solution)/shard_map/ppermute | solution.py:515
  31.4 1.1 %collective-permute-done.10.refs_6_ = bf16[3,128,512]{2,1,0:T(8,128)(2,1)S(1)} collective-permute-done((bf16[3,128,512]{2,1,0:T(8,128)(2,1)S(1)}, bf16[3,128,512]{2,1,0:T(8,128)(2,1)S(1)}, u32[]{:S(2)}, u32[]{:S(2)}) %collective-permute-start.10) | collective-permute-done | bytes 393248 | tf_op jit(solution)/shard_map/ppermute | solution.py:248
  32.6 2.0 %node_update.1 = bf16[384,512]{1,0:T(8,128)(2,1)} custom-call(bf16[384,512]{1,0:T(8,128)(2,1)S(1)} %copy-done, bf16[384,512]{1,0:T(8,128)(2,1)S(1)} %get-tuple-element.30.refs_1_, bf16[384,512]{1,0:T(8,128)(2,1)S(1)} %collective-permute-done.7.refs_2_, bf16[3,128,512]{2,1,0:T(8,128)(2,1)S(1)} %copy-done.1, ...), custom_call_target="tpu_custom_call" | custom-call | flops 603979776 | bytes 1966080 | tf_op jit(solution)/shard_map/node_update/pallas_call | solution.py:518
  (16 shorter events, 0.0 us)
Async XLA Ops:
  0.6 17.9 %collective-permute-start = (bf16[3,128,512]{2,1,0:T(8,128)(2,1)}, bf16[3,128,512]{2,1,0:T(8,128)(2,1)}, u32[]{:S(2)}, u32[]{:S(2)}) collective-permute-start(bf16[3,128,512]{2,1,0:T(8,128)(2,1)} %refs_6_.1), channel_id=1, source_target_pairs={{0,2},{2,0},{1,3},{3,1},{4,6},{6,4},{5,7},{7,5},{8,10},{10,8},{9,1... | collective-permute-start | bytes 1179656 | tf_op jit(solution)/shard_map/ppermute | solution.py:240
  5.7 12.9 %all-to-all-start = ((bf16[8,17,512]{2,1,0:T(8,128)(2,1)}), bf16[8,17,512]{2,1,0:T(8,128)(2,1)S(1)}, u32[]{:S(2)}, u32[]{:S(2)}) async-start(bf16[8,17,512]{2,1,0:T(8,128)(2,1)} %pick_halo.1), calls=%async_computation | async-start | bytes 393216 | tf_op jit(solution)/shard_map/all_to_all | solution.py:110
  10.6 2.3 %collective-permute-start.2 = (bf16[128,512]{1,0:T(8,128)(2,1)}, bf16[128,512]{1,0:T(8,128)(2,1)S(1)}, u32[]{:S(2)}, u32[]{:S(2)}) collective-permute-start(bf16[128,512]{1,0:T(8,128)(2,1)} %refs_10_.1), channel_id=1, source_target_pairs={{0,1},{1,0},{2,3},{3,2},{4,5},{5,4},{6,7},{7,6},{8,9},{9,8},{10,11... | collective-permute-start | bytes 393224 | tf_op jit(solution)/shard_map/ppermute | solution.py:248
  10.6 8.0 %collective-permute-start.1 = (bf16[128,512]{1,0:T(8,128)(2,1)}, bf16[128,512]{1,0:T(8,128)(2,1)S(1)}, u32[]{:S(2)}, u32[]{:S(2)}) collective-permute-start(bf16[128,512]{1,0:T(8,128)(2,1)} %refs_10_.1), channel_id=1, source_target_pairs={{0,2},{2,0},{1,3},{3,1},{4,6},{6,4},{5,7},{7,5},{8,10},{10,8},{9,1... | collective-permute-start | bytes 393224 | tf_op jit(solution)/shard_map/ppermute | solution.py:240
  12.6 7.8 %collective-permute-start.4 = (bf16[3,128,512]{2,1,0:T(8,128)(2,1)}, bf16[3,128,512]{2,1,0:T(8,128)(2,1)}, u32[]{:S(2)}, u32[]{:S(2)}) collective-permute-start(bf16[3,128,512]{2,1,0:T(8,128)(2,1)} %refs_6_.1), channel_id=1, source_target_pairs={{0,1},{1,0},{2,3},{3,2},{4,5},{5,4},{6,7},{7,6},{8,9},{9,8},{10,11... | collective-permute-start | bytes 1179656 | tf_op jit(solution)/shard_map/ppermute | solution.py:248
  18.6 2.2 %collective-permute-start.5 = (bf16[3,128,512]{2,1,0:T(8,128)(2,1)}, bf16[3,128,512]{2,1,0:T(8,128)(2,1)S(1)}, u32[]{:S(2)}, u32[]{:S(2)}) collective-permute-start(bf16[3,128,512]{2,1,0:T(8,128)(2,1)} %collective-permute-done.refs_8_), channel_id=1, source_target_pairs={{0,1},{1,0},{2,3},{3,2},{4,5},{5,4},{6,7},{7,6},{8,9},{9,8},{10,11... | collective-permute-start | bytes 1179656 | tf_op jit(solution)/shard_map/ppermute | solution.py:248
  18.6 2.2 %collective-permute-start.3 = (bf16[8,17,512]{2,1,0:T(8,128)(2,1)S(1)}, bf16[8,17,512]{2,1,0:T(8,128)(2,1)S(1)}, u32[]{:S(2)}, u32[]{:S(2)}) collective-permute-start(bf16[8,17,512]{2,1,0:T(8,128)(2,1)S(1)} %all-to-all-done.refs_4_), channel_id=1, source_target_pairs={{0,1},{1,0},{2,3},{3,2},{4,5},{5,4},{6,7},{7,6},{8,9},{9,8},{10,11... | collective-permute-start | bytes 417800 | tf_op jit(solution)/shard_map/ppermute | solution.py:248
  19.1 1.7 %collective-permute-start.6 = (bf16[128,512]{1,0:T(8,128)(2,1)S(1)}, bf16[128,512]{1,0:T(8,128)(2,1)S(1)}, u32[]{:S(2)}, u32[]{:S(2)}) collective-permute-start(bf16[128,512]{1,0:T(8,128)(2,1)S(1)} %collective-permute-done.1.refs_12_), channel_id=1, source_target_pairs={{0,1},{1,0},{2,3},{3,2},{4,5},{5,4},{6,7},{7,6},{8,9},{9,8},{10,11... | collective-permute-start | bytes 393224 | tf_op jit(solution)/shard_map/ppermute | solution.py:248
  19.2 11.7 %collective-permute-start.9 = (bf16[3,128,512]{2,1,0:T(8,128)(2,1)}, bf16[3,128,512]{2,1,0:T(8,128)(2,1)S(1)}, u32[]{:S(2)}, u32[]{:S(2)}) collective-permute-start(bf16[3,128,512]{2,1,0:T(8,128)(2,1)} %get-tuple-element.31.refs_3_), channel_id=1, source_target_pairs={{0,2},{2,0},{1,3},{3,1},{4,6},{6,4},{5,7},{7,5},{8,10},{10,8},{9,1... | collective-permute-start | bytes 1179656 | tf_op jit(solution)/shard_map/ppermute | solution.py:240
  20.4 10.5 %collective-permute-start.8 = (bf16[3,128,512]{2,1,0:T(8,128)(2,1)}, bf16[3,128,512]{2,1,0:T(8,128)(2,1)S(1)}, u32[]{:S(2)}, u32[]{:S(2)}) collective-permute-start(bf16[3,128,512]{2,1,0:T(8,128)(2,1)} %get-tuple-element.31.refs_3_), channel_id=1, source_target_pairs={{0,1},{1,0},{2,3},{3,2},{4,5},{5,4},{6,7},{7,6},{8,9},{9,8},{10,11... | collective-permute-start | bytes 1179656 | tf_op jit(solution)/shard_map/ppermute | solution.py:248
  20.8 11.8 %copy-start = (bf16[384,512]{1,0:T(8,128)(2,1)S(1)}, bf16[384,512]{1,0:T(8,128)(2,1)}, u32[]{:S(2)}) copy-start(bf16[384,512]{1,0:T(8,128)(2,1)} %refs_0_.3) | copy-start | bytes 1179652
  20.8 11.8 %copy-start.1 = (bf16[3,128,512]{2,1,0:T(8,128)(2,1)S(1)}, bf16[3,128,512]{2,1,0:T(8,128)(2,1)}, u32[]{:S(2)}) copy-start(bf16[3,128,512]{2,1,0:T(8,128)(2,1)} %get-tuple-element.31.refs_3_) | copy-start | bytes 1179652
  20.8 11.8 %copy-start.2 = (f32[512]{0:T(512)S(1)}, f32[512]{0:T(512)}, u32[]{:S(2)}) copy-start(f32[512]{0:T(512)} %param.32) | copy-start | bytes 6148
  20.8 11.8 %copy-start.3 = (f32[512]{0:T(512)S(1)}, f32[512]{0:T(512)}, u32[]{:S(2)}) copy-start(f32[512]{0:T(512)} %param.33) | copy-start | bytes 6148
  20.8 11.8 %copy-start.4 = (f32[512]{0:T(512)S(1)}, f32[512]{0:T(512)}, u32[]{:S(2)}) copy-start(f32[512]{0:T(512)} %param.34) | copy-start | bytes 6148
  20.8 11.8 %copy-start.5 = (f32[512]{0:T(512)S(1)}, f32[512]{0:T(512)}, u32[]{:S(2)}) copy-start(f32[512]{0:T(512)} %param.35) | copy-start | bytes 6148
  29.6 1.8 %collective-permute-start.7 = (bf16[384,512]{1,0:T(8,128)(2,1)S(1)}, bf16[384,512]{1,0:T(8,128)(2,1)S(1)}, u32[]{:S(2)}, u32[]{:S(2)}) collective-permute-start(bf16[384,512]{1,0:T(8,128)(2,1)S(1)} %get-tuple-element.30.refs_1_), channel_id=1, source_target_pairs={{0,1},{1,0},{2,3},{3,2},{4,5},{5,4},{6,7},{7,6},{8,9},{9,8},{10,11... | collective-permute-start | bytes 1179656 | tf_op jit(solution)/shard_map/ppermute | solution.py:515
  30.8 1.7 %collective-permute-start.10 = (bf16[3,128,512]{2,1,0:T(8,128)(2,1)S(1)}, bf16[3,128,512]{2,1,0:T(8,128)(2,1)S(1)}, u32[]{:S(2)}, u32[]{:S(2)}) collective-permute-start(bf16[3,128,512]{2,1,0:T(8,128)(2,1)S(1)} %collective-permute-done.9.refs_5_), channel_id=1, source_target_pairs={{0,1},{1,0},{2,3},{3,2},{4,5},{5,4},{6,7},{7,6},{8,9},{9,8},{10,11... | collective-permute-start | bytes 1179656 | tf_op jit(solution)/shard_map/ppermute | solution.py:248

commit v19 on v18

--- a/solution.py
+++ b/solution.py
@@ -12,8 +12,8 @@
 lanes = 128
 few_parts = 8
 grant = 32 << 20
-chunk_rows = 64
-block_rows = 512
+chunk_rows = 32
+gather_rows = 512
 bf16 = jnp.bfloat16
 f32 = jnp.float32
 vmem = pl.BlockSpec(memory_space=pltpu.VMEM)
@@ -132,8 +132,6 @@
     latent_ref,
     node_in_ref,
     node_out_ref,
-    edge_hbm,
-    known,
     gathered_hbm,
     to_node,
     pack_ref,
@@ -141,16 +139,14 @@
     sems,
 ):
     node_count, width = latent_ref.shape
-    first = known.shape[0]
-    edge_count = first + gathered.shape[0]
-    block = block_rows
+    edge_count = gathered.shape[0]
+    block = gather_rows
     copies = []
 
     def start(source, target):
         copies.append(pltpu.make_async_copy(source, target, sems.at[len(copies)]))
         copies[-1].start()
 
-    start(edge_hbm.at[pl.ds(0, first)], known.at[:, pl.ds(0, width)])
     count = node_in_ref.shape[0]
     pack_ref[:count] = node_in_ref[...]
     pack_ref[count] = node_out_ref[...]
@@ -176,18 +172,15 @@
         slots = target.shape[1] - begin - 2 * width
         target[rows, begin + 2 * width :] = one_hot(columns - node_count, slots)
 
-    for at in range(first // block, edge_count // block):
-        begin = at * block - first
-        gather(at, gathered, slice(begin, begin + block), 0)
-        rows = pl.ds(begin, block)
+    for at in range(edge_count // block):
+        gather(at, gathered, slice(at * block, (at + 1) * block), 0)
+        rows = pl.ds(at * block, block)
         start(gathered.at[rows], gathered_hbm.at[rows])
     node_place = lax.broadcasted_iota(jnp.int32, (to_node.shape[0], lanes), 0)
     for row in range(edge_count // lanes):
         to_node[:, row * lanes : (row + 1) * lanes] = jnp.where(
             node_place == receiver_ref[row : row + 1], 1.0, 0.0
         ).astype(bf16)
-    for at in range(first // block):
-        gather(at, known, slice(at * block, (at + 1) * block), width)
     for copy in copies:
         copy.wait()
 
@@ -252,19 +245,19 @@
 
 
 def edge_kernel(pieces_count, got_count, part_count, near_cap, halved, *refs):
-    edge_hbm, gathered_hbm, to_node, known_first = refs[:4]
-    got_refs = refs[4 : 4 + got_count]
-    refs = refs[4 + got_count :]
+    edge_hbm, gathered_hbm, to_node = refs[:3]
+    got_refs = refs[3 : 3 + got_count]
+    refs = refs[3 + got_count :]
     in_pieces, out_pieces = refs[:pieces_count], refs[pieces_count : 2 * pieces_count]
     row_refs = refs[2 * pieces_count : 2 * pieces_count + 4]
     new_hbm, sum_ref = refs[2 * pieces_count + 4 : 2 * pieces_count + 6]
-    known_rest, in_weight, out_weight, halo, rows, preact, hidden, output, new_ref, total, sems = (
+    known_rows, in_weight, out_weight, halo, rows, preact, hidden, output, new_ref, total, sems = (
         refs[2 * pieces_count + 6 :]
     )
     edge_count, width = new_hbm.shape
-    block = known_first.shape[0]
-    blocks = edge_count // block
-    known = [known_first]
+    blocks = len(preact)
+    block = edge_count // blocks
+    known = []
     taken = []
 
     def start(source, target):
@@ -286,16 +279,16 @@
     spot = pl.ds(pl.multiple_of(order[0] * count, count), count)
     later.append(start(out_pieces[0], out_weight.at[spot]))
     in_bias, out_bias, gain, offset = rows
-    known_copies = [[]]
-    for at in range(1, blocks):
-        spot, rows_here = pl.ds(at * block, block), pl.ds((at - 1) * block, block)
-        view = known_rest.at[rows_here]
+    known_copies = []
+    for at in range(blocks):
+        spot = pl.ds(at * block, block)
+        view = known_rows.at[spot]
         known.append(view)
         known_copies.append(
             [
                 start(edge_hbm.at[spot], view.at[:, pl.ds(0, width)]),
                 start(
-                    gathered_hbm.at[rows_here], view.at[:, pl.ds(width, view.shape[1] - width)]
+                    gathered_hbm.at[spot], view.at[:, pl.ds(width, view.shape[1] - width)]
                 ),
             ]
         )
@@ -430,21 +423,20 @@
     near_edge[1], latent_after = lax.optimization_barrier((near_edge[1], node_latent))
     gathered_width = 2 * width + halo_space
     known_width = width + gathered_width
-    steps = edge_count // block_rows
-    rest = edge_count - block_rows
-    known, gathered, to_node, node_weight = pl.pallas_call(
+    steps = 2
+    block = edge_count // steps
+    gathered, to_node, node_weight = pl.pallas_call(
         functools.partial(gather_kernel, near_cap, far_cap, halved),
         out_shape=[
-            pltpu.VMEM((block_rows, known_width), bf16),
-            pltpu.HBM((rest, gathered_width), bf16),
+            pltpu.HBM((edge_count, gathered_width), bf16),
             pltpu.VMEM((node_count, edge_count), bf16),
             pltpu.HBM(pack_shape, bf16),
         ],
-        in_specs=[vmem] * 5 + [hbm],
-        out_specs=[vmem, hbm, vmem, vmem],
+        in_specs=[vmem] * 5,
+        out_specs=[hbm, vmem, vmem],
         scratch_shapes=[
-            pltpu.VMEM((rest, gathered_width), bf16),
-            pltpu.SemaphoreType.DMA((steps,)),
+            pltpu.VMEM((edge_count, gathered_width), bf16),
+            pltpu.SemaphoreType.DMA((edge_count // gather_rows,)),
         ],
         compiler_params=pltpu.CompilerParams(vmem_limit_bytes=grant),
         cost_estimate=pl.CostEstimate(flops=0, bytes_accessed=0, transcendentals=0),
@@ -455,11 +447,10 @@
         in_hbm(latent_after),
         in_hbm(node_in_weight),
         in_hbm(node_out_weight),
-        in_hbm(edge_latent),
-    )
-
-    far_edge, got, known, gathered, to_node, node_weight = lax.optimization_barrier(
-        (far_edge, got, known, gathered, to_node, node_weight)
+    )
+
+    far_edge, got, gathered, to_node, node_weight = lax.optimization_barrier(
+        (far_edge, got, gathered, to_node, node_weight)
     )
     if halved:
         got = got + from_subs(got)
@@ -472,9 +463,9 @@
     pieces_count = len(edge_in)
 
     rows = [value.reshape(1, -1) for value in (edge_in_bias, edge_out_bias, edge_gain, edge_offset)]
-    edge_operands = [in_hbm(edge_latent), in_hbm(gathered), in_vmem(to_node), in_vmem(known)]
+    edge_operands = [in_hbm(edge_latent), in_hbm(gathered), in_vmem(to_node)]
     edge_operands += [in_vmem(blocks) for blocks in got]
-    edge_specs = [hbm] * 2 + [vmem] * (2 + len(got))
+    edge_specs = [hbm] * 2 + [vmem] * (1 + len(got))
     for pieces in (edge_in, edge_out):
         edge_operands += [in_hbm(pieces[0])] + [in_vmem(piece) for piece in pieces[1:]]
         edge_specs += [hbm] + [vmem] * (pieces_count - 1)
@@ -490,14 +481,14 @@
         in_specs=edge_specs,
         out_specs=[hbm, vmem],
         scratch_shapes=[
-            pltpu.VMEM((rest, known_width), bf16),
+            pltpu.VMEM((edge_count, known_width), bf16),
             pltpu.VMEM((known_width, width), bf16),
             pltpu.VMEM((width, width), bf16),
             pltpu.VMEM((halo_space, width), bf16),
             [pltpu.VMEM((1, width), f32)] * 4,
-            [pltpu.VMEM((block_rows, width), f32) for _ in range(steps)],
-            [pltpu.VMEM((block_rows, width), bf16) for _ in range(steps)],
-            [pltpu.VMEM((block_rows, width), f32) for _ in range(steps)],
+            [pltpu.VMEM((block, width), f32) for _ in range(steps)],
+            [pltpu.VMEM((block, width), bf16) for _ in range(steps)],
+            [pltpu.VMEM((block, width), f32) for _ in range(steps)],
             pltpu.VMEM((edge_count, width), bf16),
             pltpu.VMEM((node_count, width), f32),
             pltpu.SemaphoreType.DMA((copy_count,)),

time: 34.9 us -> 34.9 us (level)
  Pallas kernels: 17.6 us -> 18 us
    pallas_call x1, Pallas kernels: 4.77 us -> 5.36 us  [shards(): pl.pallas_call(functools.partial(gather_kernel, near_cap, far_cap, halved...]
  transfers between devices with their start and end apart: 12 -> 12, of which waited for: 5 -> 5; matrix products, arithmetic and copies ran while one was open for 0% -> 0% of each run, Pallas kernels for 45% -> 46%
where the time goes in v19:
time: 34.9 us; the launch traced here: 34.6 us
  Pallas kernels  18 us (52%)
  starting transfers between devices  12.3 us (35%)
  waiting for transfers between devices  3.59 us (10%)
  between operations  0.74 us (2%)
    pallas_call x1, Pallas kernels, shards(): pl.pallas_call(functools.partial(edge_kernel, pieces_count, len(got), par...  8.53 us
    ppermute x3, starting transfers between devices, from_feats(): lax.ppermute(weight, 'feat', [(at, (at + shift) % feats) for at in range(...  6.23 us
    pallas_call x1, Pallas kernels, shards(): pl.pallas_call(functools.partial(gather_kernel, near_cap, far_cap, halved...  5.36 us
    all_to_all x1, starting transfers between devices, exchange_halves(): lax.all_to_all(blocks, ('region', 'feat'), split_axis=0, concat_axis=0, t...  4.88 us
    pallas_call x1, Pallas kernels, exchange_halves(): pl.pallas_call(functools.partial(pick_kernel, part_count, near_cap, far_c...  2.08 us
    pallas_call x1, Pallas kernels, shards(): pl.pallas_call(functools.partial(node_kernel, pieces_count), out_shape=ja...  2.01 us
    ppermute x7, waiting for transfers between devices, from_subs(): lax.ppermute(piece, 'sub', [(at, (at + turn) % subs) for at in range(subs)])  1.64 us
    ppermute x3, waiting for transfers between devices, from_feats(): lax.ppermute(weight, 'feat', [(at, (at + shift) % feats) for at in range(...  1.62 us
  transfers between devices with their start and end apart: 12, of which 5 were waited for; matrix products, arithmetic and copies ran while one was open for 0% of the time, Pallas kernels for 46%

profile of v19, /device:TPU:0, one launch (start us, length us, event | category | flops | bytes accessed | tf_op | source)
XLA Modules:
  0.0 34.6 jit_solution(5110747108384726397)
XLA Ops:
  0.6 3.0 %collective-permute-start = (bf16[3,128,512]{2,1,0:T(8,128)(2,1)}, bf16[3,128,512]{2,1,0:T(8,128)(2,1)S(1)}, u32[]{:S(2)}, u32[]{:S(2)}) collective-permute-start(bf16[3,128,512]{2,1,0:T(8,128)(2,1)} %refs_5_.1), channel_id=1, source_target_pairs={{0,2},{2,0},{1,3},{3,1},{4,6},{6,4},{5,7},{7,5},{8,10},{10,8},{9,1... | collective-permute-start | bytes 1179656 | tf_op jit(solution)/shard_map/ppermute | solution.py:233
  3.6 2.1 %pick_halo.1 = bf16[8,17,512]{2,1,0:T(8,128)(2,1)} custom-call(s32[1,2,8]{2,1,0:T(2,128)} %bitcast.17, s32[1,4,32]{2,1,0:T(4,128)} %near_ref.1, bf16[384,512]{1,0:T(8,128)(2,1)} %refs_0_.3), custom_call_target="tpu_custom_call" | custom-call | tf_op jit(solution)/shard_map/pick_halo/pallas_call | solution.py:100
  5.7 4.9 %all-to-all-start = ((bf16[8,17,512]{2,1,0:T(8,128)(2,1)}), bf16[8,17,512]{2,1,0:T(8,128)(2,1)S(1)}, u32[]{:S(2)}, u32[]{:S(2)}) async-start(bf16[8,17,512]{2,1,0:T(8,128)(2,1)} %pick_halo.1), calls=%async_computation | async-start | bytes 393216 | tf_op jit(solution)/shard_map/all_to_all | solution.py:110
  10.6 2.0 %collective-permute-start.1 = (bf16[128,512]{1,0:T(8,128)(2,1)}, bf16[128,512]{1,0:T(8,128)(2,1)S(1)}, u32[]{:S(2)}, u32[]{:S(2)}) collective-permute-start(bf16[128,512]{1,0:T(8,128)(2,1)} %refs_9_.1), channel_id=1, source_target_pairs={{0,2},{2,0},{1,3},{3,1},{4,6},{6,4},{5,7},{7,5},{8,10},{10,8},{9,1... | collective-permute-start | bytes 393224 | tf_op jit(solution)/shard_map/ppermute | solution.py:233
  12.6 0.2 collective-permute-start.4
  12.8 5.4 %gather_latents.1 = (bf16[1536,1280]{1,0:T(8,128)(2,1)}, bf16[384,1536]{1,0:T(8,128)(2,1)S(1)}, bf16[3,128,512]{2,1,0:T(8,128)(2,1)}) custom-call(s32[12,128]{1,0:T(8,128)} %bitcast.15, s32[12,128]{1,0:T(8,128)} %bitcast.16, bf16[384,512]{1,0:T(8,128)(2,1)} %refs_0_.3, bf16[2,128,512]{2,1,0:T(8,128)(2,1)} %node_in_ref.1, bf16[128,512]{1,0:T(8,128)(2,1)} %node_out_ref.1), custom_call_target="tpu_custom_call" | custom-call | tf_op jit(solution)/shard_map/gather_latents/pallas_call | solution.py:428
  18.2 0.4 %collective-permute-done.1.refs_11_ = bf16[128,512]{1,0:T(8,128)(2,1)S(1)} collective-permute-done((bf16[128,512]{1,0:T(8,128)(2,1)}, bf16[128,512]{1,0:T(8,128)(2,1)S(1)}, u32[]{:S(2)}, u32[]{:S(2)}) %collective-permute-start.1) | collective-permute-done | bytes 131104 | tf_op jit(solution)/shard_map/ppermute | solution.py:233
  18.6 0.0 collective-permute-start.5
  18.6 0.5 %collective-permute-start.3 = (bf16[8,17,512]{2,1,0:T(8,128)(2,1)S(1)}, bf16[8,17,512]{2,1,0:T(8,128)(2,1)S(1)}, u32[]{:S(2)}, u32[]{:S(2)}) collective-permute-start(bf16[8,17,512]{2,1,0:T(8,128)(2,1)S(1)} %all-to-all-done.refs_3_), channel_id=1, source_target_pairs={{0,1},{1,0},{2,3},{3,2},{4,5},{5,4},{6,7},{7,6},{8,9},{9,8},{10,11... | collective-permute-start | bytes 417800 | tf_op jit(solution)/shard_map/ppermute | solution.py:241
  19.1 0.1 collective-permute-start.6
  19.2 1.2 %collective-permute-start.9 = (bf16[3,128,512]{2,1,0:T(8,128)(2,1)}, bf16[3,128,512]{2,1,0:T(8,128)(2,1)S(1)}, u32[]{:S(2)}, u32[]{:S(2)}) collective-permute-start(bf16[3,128,512]{2,1,0:T(8,128)(2,1)} %get-tuple-element.27.refs_3_), channel_id=1, source_target_pairs={{0,2},{2,0},{1,3},{3,1},{4,6},{6,4},{5,7},{7,5},{8,10},{10,8},{9,1... | collective-permute-start | bytes 1179656 | tf_op jit(solution)/shard_map/ppermute | solution.py:233
  20.4 0.2 collective-permute-start.8
  20.5 0.2 collective-permute-done.6.refs_12_
  20.8 0.0 copy-start.1
  20.8 0.0 copy-start.2
  20.8 0.0 copy-start.3
  20.8 0.0 copy-start.4
  20.8 0.0 copy-start.5
  20.8 8.5 %edge_update.1 = (bf16[1536,512]{1,0:T(8,128)(2,1)}, bf16[384,512]{1,0:T(8,128)(2,1)S(1)}) custom-call(bf16[1536,512]{1,0:T(8,128)(2,1)} %refs_0_.2, bf16[1536,1280]{1,0:T(8,128)(2,1)} %get-tuple-element.19.refs_1_, bf16[384,1536]{1,0:T(8,128)(2,1)S(1)} %get-tuple-element.20.refs_2_, bf16[8,17,512]{2,1,0:T(8,128)(2,1)S(1)} %all-to-all-done.refs_3_, ...), custom_call_target="tpu_custom_call" | custom-call | flops 3825205248 | bytes 6291456 | tf_op jit(solution)/shard_map/edge_update/pallas_call | solution.py:475
  29.4 0.2 collective-permute-start.7
  29.6 1.3 %collective-permute-done.9.refs_5_ = bf16[3,128,512]{2,1,0:T(8,128)(2,1)S(1)} collective-permute-done((bf16[3,128,512]{2,1,0:T(8,128)(2,1)}, bf16[3,128,512]{2,1,0:T(8,128)(2,1)S(1)}, u32[]{:S(2)}, u32[]{:S(2)}) %collective-permute-start.9) | collective-permute-done | bytes 393248 | tf_op jit(solution)/shard_map/ppermute | solution.py:233
  30.8 0.3 collective-permute-done.7.refs_2_
  31.2 1.4 %collective-permute-done.10.refs_6_ = bf16[3,128,512]{2,1,0:T(8,128)(2,1)S(1)} collective-permute-done((bf16[3,128,512]{2,1,0:T(8,128)(2,1)S(1)}, bf16[3,128,512]{2,1,0:T(8,128)(2,1)S(1)}, u32[]{:S(2)}, u32[]{:S(2)}) %collective-permute-start.10) | collective-permute-done | bytes 393248 | tf_op jit(solution)/shard_map/ppermute | solution.py:241
  32.6 2.0 %node_update.1 = bf16[384,512]{1,0:T(8,128)(2,1)} custom-call(bf16[384,512]{1,0:T(8,128)(2,1)S(1)} %copy-done, bf16[384,512]{1,0:T(8,128)(2,1)S(1)} %get-tuple-element.26.refs_1_, bf16[384,512]{1,0:T(8,128)(2,1)S(1)} %collective-permute-done.7.refs_2_, bf16[3,128,512]{2,1,0:T(8,128)(2,1)S(1)} %copy-done.1, ...), custom_call_target="tpu_custom_call" | custom-call | flops 603979776 | bytes 1966080 | tf_op jit(solution)/shard_map/node_update/pallas_call | solution.py:509
  (16 shorter events, 0.0 us)
Async XLA Ops:
  0.6 17.9 %collective-permute-start = (bf16[3,128,512]{2,1,0:T(8,128)(2,1)}, bf16[3,128,512]{2,1,0:T(8,128)(2,1)S(1)}, u32[]{:S(2)}, u32[]{:S(2)}) collective-permute-start(bf16[3,128,512]{2,1,0:T(8,128)(2,1)} %refs_5_.1), channel_id=1, source_target_pairs={{0,2},{2,0},{1,3},{3,1},{4,6},{6,4},{5,7},{7,5},{8,10},{10,8},{9,1... | collective-permute-start | bytes 1179656 | tf_op jit(solution)/shard_map/ppermute | solution.py:233
  5.7 12.9 %all-to-all-start = ((bf16[8,17,512]{2,1,0:T(8,128)(2,1)}), bf16[8,17,512]{2,1,0:T(8,128)(2,1)S(1)}, u32[]{:S(2)}, u32[]{:S(2)}) async-start(bf16[8,17,512]{2,1,0:T(8,128)(2,1)} %pick_halo.1), calls=%async_computation | async-start | bytes 393216 | tf_op jit(solution)/shard_map/all_to_all | solution.py:110
  10.6 2.3 %collective-permute-start.2 = (bf16[128,512]{1,0:T(8,128)(2,1)}, bf16[128,512]{1,0:T(8,128)(2,1)S(1)}, u32[]{:S(2)}, u32[]{:S(2)}) collective-permute-start(bf16[128,512]{1,0:T(8,128)(2,1)} %refs_9_.1), channel_id=1, source_target_pairs={{0,1},{1,0},{2,3},{3,2},{4,5},{5,4},{6,7},{7,6},{8,9},{9,8},{10,11... | collective-permute-start | bytes 393224 | tf_op jit(solution)/shard_map/ppermute | solution.py:241
  10.6 8.0 %collective-permute-start.1 = (bf16[128,512]{1,0:T(8,128)(2,1)}, bf16[128,512]{1,0:T(8,128)(2,1)S(1)}, u32[]{:S(2)}, u32[]{:S(2)}) collective-permute-start(bf16[128,512]{1,0:T(8,128)(2,1)} %refs_9_.1), channel_id=1, source_target_pairs={{0,2},{2,0},{1,3},{3,1},{4,6},{6,4},{5,7},{7,5},{8,10},{10,8},{9,1... | collective-permute-start | bytes 393224 | tf_op jit(solution)/shard_map/ppermute | solution.py:233
  12.6 7.8 %collective-permute-start.4 = (bf16[3,128,512]{2,1,0:T(8,128)(2,1)}, bf16[3,128,512]{2,1,0:T(8,128)(2,1)S(1)}, u32[]{:S(2)}, u32[]{:S(2)}) collective-permute-start(bf16[3,128,512]{2,1,0:T(8,128)(2,1)} %refs_5_.1), channel_id=1, source_target_pairs={{0,1},{1,0},{2,3},{3,2},{4,5},{5,4},{6,7},{7,6},{8,9},{9,8},{10,11... | collective-permute-start | bytes 1179656 | tf_op jit(solution)/shard_map/ppermute | solution.py:241
  18.6 2.2 %collective-permute-start.5 = (bf16[3,128,512]{2,1,0:T(8,128)(2,1)S(1)}, bf16[3,128,512]{2,1,0:T(8,128)(2,1)S(1)}, u32[]{:S(2)}, u32[]{:S(2)}) collective-permute-start(bf16[3,128,512]{2,1,0:T(8,128)(2,1)S(1)} %collective-permute-done.refs_7_), channel_id=1, source_target_pairs={{0,1},{1,0},{2,3},{3,2},{4,5},{5,4},{6,7},{7,6},{8,9},{9,8},{10,11... | collective-permute-start | bytes 1179656 | tf_op jit(solution)/shard_map/ppermute | solution.py:241
  18.6 2.2 %collective-permute-start.3 = (bf16[8,17,512]{2,1,0:T(8,128)(2,1)S(1)}, bf16[8,17,512]{2,1,0:T(8,128)(2,1)S(1)}, u32[]{:S(2)}, u32[]{:S(2)}) collective-permute-start(bf16[8,17,512]{2,1,0:T(8,128)(2,1)S(1)} %all-to-all-done.refs_3_), channel_id=1, source_target_pairs={{0,1},{1,0},{2,3},{3,2},{4,5},{5,4},{6,7},{7,6},{8,9},{9,8},{10,11... | collective-permute-start | bytes 417800 | tf_op jit(solution)/shard_map/ppermute | solution.py:241
  19.1 1.7 %collective-permute-start.6 = (bf16[128,512]{1,0:T(8,128)(2,1)S(1)}, bf16[128,512]{1,0:T(8,128)(2,1)S(1)}, u32[]{:S(2)}, u32[]{:S(2)}) collective-permute-start(bf16[128,512]{1,0:T(8,128)(2,1)S(1)} %collective-permute-done.1.refs_11_), channel_id=1, source_target_pairs={{0,1},{1,0},{2,3},{3,2},{4,5},{5,4},{6,7},{7,6},{8,9},{9,8},{10,11... | collective-permute-start | bytes 393224 | tf_op jit(solution)/shard_map/ppermute | solution.py:241
  19.2 11.7 %collective-permute-start.9 = (bf16[3,128,512]{2,1,0:T(8,128)(2,1)}, bf16[3,128,512]{2,1,0:T(8,128)(2,1)S(1)}, u32[]{:S(2)}, u32[]{:S(2)}) collective-permute-start(bf16[3,128,512]{2,1,0:T(8,128)(2,1)} %get-tuple-element.27.refs_3_), channel_id=1, source_target_pairs={{0,2},{2,0},{1,3},{3,1},{4,6},{6,4},{5,7},{7,5},{8,10},{10,8},{9,1... | collective-permute-start | bytes 1179656 | tf_op jit(solution)/shard_map/ppermute | solution.py:233
  20.4 10.5 %collective-permute-start.8 = (bf16[3,128,512]{2,1,0:T(8,128)(2,1)}, bf16[3,128,512]{2,1,0:T(8,128)(2,1)S(1)}, u32[]{:S(2)}, u32[]{:S(2)}) collective-permute-start(bf16[3,128,512]{2,1,0:T(8,128)(2,1)} %get-tuple-element.27.refs_3_), channel_id=1, source_target_pairs={{0,1},{1,0},{2,3},{3,2},{4,5},{5,4},{6,7},{7,6},{8,9},{9,8},{10,11... | collective-permute-start | bytes 1179656 | tf_op jit(solution)/shard_map/ppermute | solution.py:241
  20.8 11.8 %copy-start = (bf16[384,512]{1,0:T(8,128)(2,1)S(1)}, bf16[384,512]{1,0:T(8,128)(2,1)}, u32[]{:S(2)}) copy-start(bf16[384,512]{1,0:T(8,128)(2,1)} %refs_0_.3) | copy-start | bytes 1179652
  20.8 11.8 %copy-start.1 = (bf16[3,128,512]{2,1,0:T(8,128)(2,1)S(1)}, bf16[3,128,512]{2,1,0:T(8,128)(2,1)}, u32[]{:S(2)}) copy-start(bf16[3,128,512]{2,1,0:T(8,128)(2,1)} %get-tuple-element.27.refs_3_) | copy-start | bytes 1179652
  20.8 11.8 %copy-start.2 = (f32[512]{0:T(512)S(1)}, f32[512]{0:T(512)}, u32[]{:S(2)}) copy-start(f32[512]{0:T(512)} %param.32) | copy-start | bytes 6148
  20.8 11.8 %copy-start.3 = (f32[512]{0:T(512)S(1)}, f32[512]{0:T(512)}, u32[]{:S(2)}) copy-start(f32[512]{0:T(512)} %param.33) | copy-start | bytes 6148
  20.8 11.8 %copy-start.4 = (f32[512]{0:T(512)S(1)}, f32[512]{0:T(512)}, u32[]{:S(2)}) copy-start(f32[512]{0:T(512)} %param.34) | copy-start | bytes 6148
  20.8 11.8 %copy-start.5 = (f32[512]{0:T(512)S(1)}, f32[512]{0:T(512)}, u32[]{:S(2)}) copy-start(f32[512]{0:T(512)} %param.35) | copy-start | bytes 6148
  29.4 1.8 %collective-permute-start.7 = (bf16[384,512]{1,0:T(8,128)(2,1)S(1)}, bf16[384,512]{1,0:T(8,128)(2,1)S(1)}, u32[]{:S(2)}, u32[]{:S(2)}) collective-permute-start(bf16[384,512]{1,0:T(8,128)(2,1)S(1)} %get-tuple-element.26.refs_1_), channel_id=1, source_target_pairs={{0,1},{1,0},{2,3},{3,2},{4,5},{5,4},{6,7},{7,6},{8,9},{9,8},{10,11... | collective-permute-start | bytes 1179656 | tf_op jit(solution)/shard_map/ppermute | solution.py:506
  30.8 1.7 %collective-permute-start.10 = (bf16[3,128,512]{2,1,0:T(8,128)(2,1)S(1)}, bf16[3,128,512]{2,1,0:T(8,128)(2,1)S(1)}, u32[]{:S(2)}, u32[]{:S(2)}) collective-permute-start(bf16[3,128,512]{2,1,0:T(8,128)(2,1)S(1)} %collective-permute-done.9.refs_5_), channel_id=1, source_target_pairs={{0,1},{1,0},{2,3},{3,2},{4,5},{5,4},{6,7},{7,6},{8,9},{9,8},{10,11... | collective-permute-start | bytes 1179656 | tf_op jit(solution)/shard_map/ppermute | solution.py:241

commit v20 on v19

--- a/solution.py
+++ b/solution.py
@@ -130,11 +130,8 @@
     source_ref,
     receiver_ref,
     latent_ref,
-    node_in_ref,
-    node_out_ref,
     gathered_hbm,
     to_node,
-    pack_ref,
     gathered,
     sems,
 ):
@@ -147,9 +144,6 @@
         copies.append(pltpu.make_async_copy(source, target, sems.at[len(copies)]))
         copies[-1].start()
 
-    count = node_in_ref.shape[0]
-    pack_ref[:count] = node_in_ref[...]
-    pack_ref[count] = node_out_ref[...]
     latent = latent_ref[...]
 
     def gather(at, target, rows, begin):
@@ -361,24 +355,26 @@
 
 def node_kernel(pieces_count, *refs):
     latent_ref, own_ref, other_ref = refs[:3]
-    pieces = refs[3 : 3 + pieces_count]
-    in_bias, out_bias, gain, offset, new_ref, weights = refs[3 + pieces_count :]
-    width = latent_ref.shape[1]
-    for piece, owner in zip(pieces, owners()):
-        for which in range(piece.shape[0]):
-            place_rows(weights, which * width, piece[which], owner)
-    latent = latent_ref[...]
-    summed = (own_ref[...].astype(f32) + other_ref[...].astype(f32)).astype(bf16)
-    preact = jnp.dot(
-        jnp.concatenate([latent, summed], axis=1),
-        weights[: 2 * width],
-        preferred_element_type=f32,
-    )
-    hidden = silu(preact + in_bias[...]).astype(bf16)
-    output = jnp.dot(hidden, weights[2 * width :], preferred_element_type=f32) + out_bias[...]
-    new_ref[...] = (
-        latent.astype(f32) + layer_norm(output, gain[...], offset[...])
-    ).astype(bf16)
+    in_pieces = refs[3 : 3 + pieces_count]
+    out_pieces = refs[3 + pieces_count : 3 + 2 * pieces_count]
+    in_bias, out_bias, gain, offset, new_ref, weights, known, preact, hidden, output = refs[
+        3 + 2 * pieces_count :
+    ]
+    node_count, width = latent_ref.shape
+    known[:, :width] = latent_ref[...]
+    known[:, width:] = (own_ref[...].astype(f32) + other_ref[...].astype(f32)).astype(bf16)
+    for in_piece, out_piece, owner in zip(in_pieces, out_pieces, owners()):
+        for which in range(in_piece.shape[0]):
+            place_rows(weights, which * width, in_piece[which], owner)
+        place_rows(weights, 2 * width, out_piece[...], owner)
+    preact[...] = jnp.dot(known[...], weights[: 2 * width], preferred_element_type=f32)
+    chunks = [slice(at, at + chunk_rows) for at in range(0, node_count, chunk_rows)]
+    for here in chunks:
+        hidden[here] = silu(preact[here] + in_bias[...]).astype(bf16)
+    output[...] = jnp.dot(hidden[...], weights[2 * width :], preferred_element_type=f32)
+    for here in chunks:
+        normed = layer_norm(output[here] + out_bias[...], gain[...], offset[...])
+        new_ref[here] = (latent_ref[here].astype(f32) + normed).astype(bf16)
 
 
 def shards(
@@ -419,21 +415,19 @@
     source_rows = in_hbm(edge_source.reshape(-1, lanes))
     receiver_rows = in_hbm(receivers.reshape(-1, lanes))
 
-    pack_shape = (node_in_weight.shape[0] + 1,) + node_out_weight.shape
     near_edge[1], latent_after = lax.optimization_barrier((near_edge[1], node_latent))
     gathered_width = 2 * width + halo_space
     known_width = width + gathered_width
     steps = 2
     block = edge_count // steps
-    gathered, to_node, node_weight = pl.pallas_call(
+    gathered, to_node = pl.pallas_call(
         functools.partial(gather_kernel, near_cap, far_cap, halved),
         out_shape=[
             pltpu.HBM((edge_count, gathered_width), bf16),
             pltpu.VMEM((node_count, edge_count), bf16),
-            pltpu.HBM(pack_shape, bf16),
-        ],
-        in_specs=[vmem] * 5,
-        out_specs=[hbm, vmem, vmem],
+        ],
+        in_specs=[vmem] * 3,
+        out_specs=[hbm, vmem],
         scratch_shapes=[
             pltpu.VMEM((edge_count, gathered_width), bf16),
             pltpu.SemaphoreType.DMA((edge_count // gather_rows,)),
@@ -445,12 +439,11 @@
         source_rows,
         receiver_rows,
         in_hbm(latent_after),
-        in_hbm(node_in_weight),
-        in_hbm(node_out_weight),
     )
 
-    far_edge, got, gathered, to_node, node_weight = lax.optimization_barrier(
-        (far_edge, got, gathered, to_node, node_weight)
+    node_weights = [node_in_weight, node_out_weight]
+    far_edge, got, gathered, to_node, node_weights = lax.optimization_barrier(
+        (far_edge, got, gathered, to_node, node_weights)
     )
     if halved:
         got = got + from_subs(got)
@@ -458,8 +451,10 @@
         [weight] + near + far + from_subs(far)
         for weight, near, far in zip((edge_in_weight, edge_out_weight), near_edge, far_edge)
     ]
-    far_node = from_feats(node_weight)
-    node_pieces = [node_weight] + from_subs([node_weight]) + far_node + from_subs(far_node)
+    node_in, node_out = [
+        [weight] + from_subs([weight]) + far + from_subs(far)
+        for weight, far in zip(node_weights, [from_feats(weight) for weight in node_weights])
+    ]
     pieces_count = len(edge_in)
 
     rows = [value.reshape(1, -1) for value in (edge_in_bias, edge_out_bias, edge_gain, edge_offset)]
@@ -509,10 +504,14 @@
     node_new = pl.pallas_call(
         functools.partial(node_kernel, pieces_count),
         out_shape=jax.ShapeDtypeStruct((node_count, width), bf16),
-        in_specs=[vmem] * (3 + pieces_count + 4),
+        in_specs=[vmem] * (3 + 2 * pieces_count + 4),
         out_specs=vmem,
         scratch_shapes=[
             pltpu.VMEM((3 * width, width), bf16),
+            pltpu.VMEM((node_count, 2 * width), bf16),
+            pltpu.VMEM((node_count, width), f32),
+            pltpu.VMEM((node_count, width), bf16),
+            pltpu.VMEM((node_count, width), f32),
         ],
         compiler_params=pltpu.CompilerParams(vmem_limit_bytes=grant),
         cost_estimate=pl.CostEstimate(
@@ -521,7 +520,7 @@
             transcendentals=node_count * width,
         ),
         name="node_update",
-    )(node_latent, partial_sums, other_sums, *node_pieces, *rows)
+    )(node_latent, partial_sums, other_sums, *node_in, *node_out, *rows)
     return (edge_new, node_new)
 
 

time: 34.9 us -> 39.1 us (1.12)
  waiting for transfers between devices: 3.59 us -> 7 us
  starting transfers between devices: 12.3 us -> 13.9 us
  Pallas kernels: 18 us -> 17.1 us
    ppermute x3 -> x4, waiting for transfers between devices: 1.62 us -> 5.24 us  [from_feats(): lax.ppermute(weight, 'feat', [(at, (at + shift) % feats) for at in range(...]
    ppermute x3 -> x4, starting transfers between devices: 6.23 us -> 7.46 us  [from_feats(): lax.ppermute(weight, 'feat', [(at, (at + shift) % feats) for at in range(...]
    pallas_call x1, Pallas kernels: 5.36 us -> 4.48 us  [shards(): pl.pallas_call(functools.partial(gather_kernel, near_cap, far_cap, halved...]
    ppermute x7 -> x9, starting transfers between devices: 0.98 us -> 1.4 us  [from_subs(): lax.ppermute(piece, 'sub', [(at, (at + turn) % subs) for at in range(subs)])]
    ppermute x7 -> x9, waiting for transfers between devices: 1.64 us -> 1.75 us  [from_subs(): lax.ppermute(piece, 'sub', [(at, (at + turn) % subs) for at in range(subs)])]
  transfers between devices with their start and end apart: 12 -> 15, of which waited for: 5 -> 4; matrix products, arithmetic and copies ran while one was open for 0% -> 0% of each run, Pallas kernels for 46% -> 39%
where the time goes in v20:
time: 39.1 us; the launch traced here: 38.9 us
  Pallas kernels  17.1 us (44%)
  starting transfers between devices  13.9 us (36%)
  waiting for transfers between devices  7 us (18%)
  between operations  0.77 us (2%)
    pallas_call x1, Pallas kernels, shards(): pl.pallas_call(functools.partial(edge_kernel, pieces_count, len(got), par...  8.55 us
    ppermute x4, starting transfers between devices, from_feats(): lax.ppermute(weight, 'feat', [(at, (at + shift) % feats) for at in range(...  7.46 us
    ppermute x4, waiting for transfers between devices, from_feats(): lax.ppermute(weight, 'feat', [(at, (at + shift) % feats) for at in range(...  5.24 us
    all_to_all x1, starting transfers between devices, exchange_halves(): lax.all_to_all(blocks, ('region', 'feat'), split_axis=0, concat_axis=0, t...  4.88 us
    pallas_call x1, Pallas kernels, shards(): pl.pallas_call(functools.partial(gather_kernel, near_cap, far_cap, halved...  4.48 us
    pallas_call x1, Pallas kernels, exchange_halves(): pl.pallas_call(functools.partial(pick_kernel, part_count, near_cap, far_c...  2.08 us
    pallas_call x1, Pallas kernels, shards(): pl.pallas_call(functools.partial(node_kernel, pieces_count), out_shape=ja...  2.02 us
    ppermute x9, waiting for transfers between devices, from_subs(): lax.ppermute(piece, 'sub', [(at, (at + turn) % subs) for at in range(subs)])  1.75 us
  transfers between devices with their start and end apart: 15, of which 4 were waited for; matrix products, arithmetic and copies ran while one was open for 0% of the time, Pallas kernels for 39%

profile of v20, /device:TPU:0, one launch (start us, length us, event | category | flops | bytes accessed | tf_op | source)
XLA Modules:
  0.0 38.9 jit_solution(12358728353231568437)
XLA Ops:
  0.6 3.0 %collective-permute-start = (bf16[3,128,512]{2,1,0:T(8,128)(2,1)}, bf16[3,128,512]{2,1,0:T(8,128)(2,1)S(1)}, u32[]{:S(2)}, u32[]{:S(2)}) collective-permute-start(bf16[3,128,512]{2,1,0:T(8,128)(2,1)} %refs_5_.1), channel_id=1, source_target_pairs={{0,2},{2,0},{1,3},{3,1},{4,6},{6,4},{5,7},{7,5},{8,10},{10,8},{9,1... | collective-permute-start | bytes 1179656 | tf_op jit(solution)/shard_map/ppermute | solution.py:227
  3.6 2.1 %pick_halo.1 = bf16[8,17,512]{2,1,0:T(8,128)(2,1)} custom-call(s32[1,2,8]{2,1,0:T(2,128)} %bitcast.17, s32[1,4,32]{2,1,0:T(4,128)} %near_ref.1, bf16[384,512]{1,0:T(8,128)(2,1)} %refs_0_.3), custom_call_target="tpu_custom_call" | custom-call | tf_op jit(solution)/shard_map/pick_halo/pallas_call | solution.py:100
  5.7 4.9 %all-to-all-start = ((bf16[8,17,512]{2,1,0:T(8,128)(2,1)}), bf16[8,17,512]{2,1,0:T(8,128)(2,1)S(1)}, u32[]{:S(2)}, u32[]{:S(2)}) async-start(bf16[8,17,512]{2,1,0:T(8,128)(2,1)} %pick_halo.1), calls=%async_computation | async-start | bytes 393216 | tf_op jit(solution)/shard_map/all_to_all | solution.py:110
  10.6 2.0 %collective-permute-start.1 = (bf16[128,512]{1,0:T(8,128)(2,1)}, bf16[128,512]{1,0:T(8,128)(2,1)S(1)}, u32[]{:S(2)}, u32[]{:S(2)}) collective-permute-start(bf16[128,512]{1,0:T(8,128)(2,1)} %refs_9_.1), channel_id=1, source_target_pairs={{0,2},{2,0},{1,3},{3,1},{4,6},{6,4},{5,7},{7,5},{8,10},{10,8},{9,1... | collective-permute-start | bytes 393224 | tf_op jit(solution)/shard_map/ppermute | solution.py:227
  12.6 0.2 collective-permute-start.4
  12.8 4.5 %gather_latents.1 = (bf16[1536,1280]{1,0:T(8,128)(2,1)}, bf16[384,1536]{1,0:T(8,128)(2,1)S(1)}) custom-call(s32[12,128]{1,0:T(8,128)} %bitcast.15, s32[12,128]{1,0:T(8,128)} %bitcast.16, bf16[384,512]{1,0:T(8,128)(2,1)} %refs_0_.3), custom_call_target="tpu_custom_call" | custom-call | tf_op jit(solution)/shard_map/gather_latents/pallas_call | solution.py:423
  17.3 1.2 %collective-permute-done.1.refs_11_ = bf16[128,512]{1,0:T(8,128)(2,1)S(1)} collective-permute-done((bf16[128,512]{1,0:T(8,128)(2,1)}, bf16[128,512]{1,0:T(8,128)(2,1)S(1)}, u32[]{:S(2)}, u32[]{:S(2)}) %collective-permute-start.1) | collective-permute-done | bytes 131104 | tf_op jit(solution)/shard_map/ppermute | solution.py:227
  18.6 0.5 %collective-permute-start.3 = (bf16[8,17,512]{2,1,0:T(8,128)(2,1)S(1)}, bf16[8,17,512]{2,1,0:T(8,128)(2,1)S(1)}, u32[]{:S(2)}, u32[]{:S(2)}) collective-permute-start(bf16[8,17,512]{2,1,0:T(8,128)(2,1)S(1)} %all-to-all-done.refs_3_), channel_id=1, source_target_pairs={{0,1},{1,0},{2,3},{3,2},{4,5},{5,4},{6,7},{7,6},{8,9},{9,8},{10,11... | collective-permute-start | bytes 417800 | tf_op jit(solution)/shard_map/ppermute | solution.py:235
  19.1 0.1 collective-permute-start.6
  19.2 1.2 %collective-permute-start.9 = (bf16[2,128,512]{2,1,0:T(8,128)(2,1)}, bf16[2,128,512]{2,1,0:T(8,128)(2,1)S(1)}, u32[]{:S(2)}, u32[]{:S(2)}) collective-permute-start(bf16[2,128,512]{2,1,0:T(8,128)(2,1)} %refs_3_), channel_id=1, source_target_pairs={{0,2},{2,0},{1,3},{3,1},{4,6},{6,4},{5,7},{7,5},{8,10},{10,8},{9,1... | collective-permute-start | bytes 786440 | tf_op jit(solution)/shard_map/ppermute | solution.py:227
  20.4 0.4 %collective-permute-done.6.refs_12_ = bf16[128,512]{1,0:T(8,128)(2,1)S(1)} collective-permute-done((bf16[128,512]{1,0:T(8,128)(2,1)S(1)}, bf16[128,512]{1,0:T(8,128)(2,1)S(1)}, u32[]{:S(2)}, u32[]{:S(2)}) %collective-permute-start.6) | collective-permute-done | bytes 131104 | tf_op jit(solution)/shard_map/ppermute | solution.py:235
  20.8 0.0 copy-start
  20.8 0.0 copy-start.3
  20.8 0.0 copy-start.4
  20.8 0.0 copy-start.5
  20.9 8.6 %edge_update.1 = (bf16[1536,512]{1,0:T(8,128)(2,1)}, bf16[384,512]{1,0:T(8,128)(2,1)S(1)}) custom-call(bf16[1536,512]{1,0:T(8,128)(2,1)} %refs_0_.2, bf16[1536,1280]{1,0:T(8,128)(2,1)} %get-tuple-element.18.refs_1_, bf16[384,1536]{1,0:T(8,128)(2,1)S(1)} %get-tuple-element.19.refs_2_, bf16[8,17,512]{2,1,0:T(8,128)(2,1)S(1)} %all-to-all-done.refs_3_, ...), custom_call_target="tpu_custom_call" | custom-call | flops 3825205248 | bytes 6291456 | tf_op jit(solution)/shard_map/edge_update/pallas_call | solution.py:470
  29.4 0.2 collective-permute-start.7
  29.6 1.2 %collective-permute-start.12 = (bf16[128,512]{1,0:T(8,128)(2,1)S(1)}, bf16[128,512]{1,0:T(8,128)(2,1)S(1)}, u32[]{:S(2)}, u32[]{:S(2)}) collective-permute-start(bf16[128,512]{1,0:T(8,128)(2,1)S(1)} %copy-done.2), channel_id=1, source_target_pairs={{0,2},{2,0},{1,3},{3,1},{4,6},{6,4},{5,7},{7,5},{8,10},{10,8},{9,1... | collective-permute-start | bytes 393224 | tf_op jit(solution)/shard_map/ppermute | solution.py:227
  30.8 0.1 collective-permute-start.8
  30.9 0.4 %collective-permute-start.10 = (bf16[2,128,512]{2,1,0:T(8,128)(2,1)S(1)}, bf16[2,128,512]{2,1,0:T(8,128)(2,1)S(1)}, u32[]{:S(2)}, u32[]{:S(2)}) collective-permute-start(bf16[2,128,512]{2,1,0:T(8,128)(2,1)S(1)} %collective-permute-done.9.refs_5_), channel_id=1, source_target_pairs={{0,1},{1,0},{2,3},{3,2},{4,5},{5,4},{6,7},{7,6},{8,9},{9,8},{10,11... | collective-permute-start | bytes 786440 | tf_op jit(solution)/shard_map/ppermute | solution.py:235
  31.3 0.1 collective-permute-start.11
  31.4 4.0 %collective-permute-done.12.refs_9_ = bf16[128,512]{1,0:T(8,128)(2,1)S(1)} collective-permute-done((bf16[128,512]{1,0:T(8,128)(2,1)S(1)}, bf16[128,512]{1,0:T(8,128)(2,1)S(1)}, u32[]{:S(2)}, u32[]{:S(2)}) %collective-permute-start.12) | collective-permute-done | bytes 131104 | tf_op jit(solution)/shard_map/ppermute | solution.py:227
  35.4 1.3 %collective-permute-done.13.refs_10_ = bf16[128,512]{1,0:T(8,128)(2,1)S(1)} collective-permute-done((bf16[128,512]{1,0:T(8,128)(2,1)S(1)}, bf16[128,512]{1,0:T(8,128)(2,1)S(1)}, u32[]{:S(2)}, u32[]{:S(2)}) %collective-permute-start.13) | collective-permute-done | bytes 131104 | tf_op jit(solution)/shard_map/ppermute | solution.py:235
  36.8 2.0 %node_update.1 = bf16[384,512]{1,0:T(8,128)(2,1)} custom-call(bf16[384,512]{1,0:T(8,128)(2,1)S(1)} %copy-done, bf16[384,512]{1,0:T(8,128)(2,1)S(1)} %get-tuple-element.25.refs_1_, bf16[384,512]{1,0:T(8,128)(2,1)S(1)} %collective-permute-done.7.refs_2_, bf16[2,128,512]{2,1,0:T(8,128)(2,1)S(1)} %copy-done.1, ...), custom_call_target="tpu_custom_call" | custom-call | flops 603979776 | bytes 1966080 | tf_op jit(solution)/shard_map/node_update/pallas_call | solution.py:504
  (24 shorter events, 0.1 us)
Async XLA Ops:
  0.6 17.9 %collective-permute-start = (bf16[3,128,512]{2,1,0:T(8,128)(2,1)}, bf16[3,128,512]{2,1,0:T(8,128)(2,1)S(1)}, u32[]{:S(2)}, u32[]{:S(2)}) collective-permute-start(bf16[3,128,512]{2,1,0:T(8,128)(2,1)} %refs_5_.1), channel_id=1, source_target_pairs={{0,2},{2,0},{1,3},{3,1},{4,6},{6,4},{5,7},{7,5},{8,10},{10,8},{9,1... | collective-permute-start | bytes 1179656 | tf_op jit(solution)/shard_map/ppermute | solution.py:227
  5.7 12.9 %all-to-all-start = ((bf16[8,17,512]{2,1,0:T(8,128)(2,1)}), bf16[8,17,512]{2,1,0:T(8,128)(2,1)S(1)}, u32[]{:S(2)}, u32[]{:S(2)}) async-start(bf16[8,17,512]{2,1,0:T(8,128)(2,1)} %pick_halo.1), calls=%async_computation | async-start | bytes 393216 | tf_op jit(solution)/shard_map/all_to_all | solution.py:110
  10.6 2.3 %collective-permute-start.2 = (bf16[128,512]{1,0:T(8,128)(2,1)}, bf16[128,512]{1,0:T(8,128)(2,1)S(1)}, u32[]{:S(2)}, u32[]{:S(2)}) collective-permute-start(bf16[128,512]{1,0:T(8,128)(2,1)} %refs_9_.1), channel_id=1, source_target_pairs={{0,1},{1,0},{2,3},{3,2},{4,5},{5,4},{6,7},{7,6},{8,9},{9,8},{10,11... | collective-permute-start | bytes 393224 | tf_op jit(solution)/shard_map/ppermute | solution.py:235
  10.6 8.0 %collective-permute-start.1 = (bf16[128,512]{1,0:T(8,128)(2,1)}, bf16[128,512]{1,0:T(8,128)(2,1)S(1)}, u32[]{:S(2)}, u32[]{:S(2)}) collective-permute-start(bf16[128,512]{1,0:T(8,128)(2,1)} %refs_9_.1), channel_id=1, source_target_pairs={{0,2},{2,0},{1,3},{3,1},{4,6},{6,4},{5,7},{7,5},{8,10},{10,8},{9,1... | collective-permute-start | bytes 393224 | tf_op jit(solution)/shard_map/ppermute | solution.py:227
  12.6 7.8 %collective-permute-start.4 = (bf16[3,128,512]{2,1,0:T(8,128)(2,1)}, bf16[3,128,512]{2,1,0:T(8,128)(2,1)S(1)}, u32[]{:S(2)}, u32[]{:S(2)}) collective-permute-start(bf16[3,128,512]{2,1,0:T(8,128)(2,1)} %refs_5_.1), channel_id=1, source_target_pairs={{0,1},{1,0},{2,3},{3,2},{4,5},{5,4},{6,7},{7,6},{8,9},{9,8},{10,11... | collective-permute-start | bytes 1179656 | tf_op jit(solution)/shard_map/ppermute | solution.py:235
  18.6 2.2 %collective-permute-start.5 = (bf16[3,128,512]{2,1,0:T(8,128)(2,1)S(1)}, bf16[3,128,512]{2,1,0:T(8,128)(2,1)S(1)}, u32[]{:S(2)}, u32[]{:S(2)}) collective-permute-start(bf16[3,128,512]{2,1,0:T(8,128)(2,1)S(1)} %collective-permute-done.refs_7_), channel_id=1, source_target_pairs={{0,1},{1,0},{2,3},{3,2},{4,5},{5,4},{6,7},{7,6},{8,9},{9,8},{10,11... | collective-permute-start | bytes 1179656 | tf_op jit(solution)/shard_map/ppermute | solution.py:235
  18.6 2.2 %collective-permute-start.3 = (bf16[8,17,512]{2,1,0:T(8,128)(2,1)S(1)}, bf16[8,17,512]{2,1,0:T(8,128)(2,1)S(1)}, u32[]{:S(2)}, u32[]{:S(2)}) collective-permute-start(bf16[8,17,512]{2,1,0:T(8,128)(2,1)S(1)} %all-to-all-done.refs_3_), channel_id=1, source_target_pairs={{0,1},{1,0},{2,3},{3,2},{4,5},{5,4},{6,7},{7,6},{8,9},{9,8},{10,11... | collective-permute-start | bytes 417800 | tf_op jit(solution)/shard_map/ppermute | solution.py:235
  19.1 1.7 %collective-permute-start.6 = (bf16[128,512]{1,0:T(8,128)(2,1)S(1)}, bf16[128,512]{1,0:T(8,128)(2,1)S(1)}, u32[]{:S(2)}, u32[]{:S(2)}) collective-permute-start(bf16[128,512]{1,0:T(8,128)(2,1)S(1)} %collective-permute-done.1.refs_11_), channel_id=1, source_target_pairs={{0,1},{1,0},{2,3},{3,2},{4,5},{5,4},{6,7},{7,6},{8,9},{9,8},{10,11... | collective-permute-start | bytes 393224 | tf_op jit(solution)/shard_map/ppermute | solution.py:235
  19.2 11.7 %collective-permute-start.9 = (bf16[2,128,512]{2,1,0:T(8,128)(2,1)}, bf16[2,128,512]{2,1,0:T(8,128)(2,1)S(1)}, u32[]{:S(2)}, u32[]{:S(2)}) collective-permute-start(bf16[2,128,512]{2,1,0:T(8,128)(2,1)} %refs_3_), channel_id=1, source_target_pairs={{0,2},{2,0},{1,3},{3,1},{4,6},{6,4},{5,7},{7,5},{8,10},{10,8},{9,1... | collective-permute-start | bytes 786440 | tf_op jit(solution)/shard_map/ppermute | solution.py:227
  20.8 8.8 %copy-start.2 = (bf16[128,512]{1,0:T(8,128)(2,1)S(1)}, bf16[128,512]{1,0:T(8,128)(2,1)}, u32[]{:S(2)}) copy-start(bf16[128,512]{1,0:T(8,128)(2,1)} %refs_7_) | copy-start | bytes 393220
  20.8 10.1 %copy-start.1 = (bf16[2,128,512]{2,1,0:T(8,128)(2,1)S(1)}, bf16[2,128,512]{2,1,0:T(8,128)(2,1)}, u32[]{:S(2)}) copy-start(bf16[2,128,512]{2,1,0:T(8,128)(2,1)} %refs_3_) | copy-start | bytes 786436
  20.8 16.0 %copy-start = (bf16[384,512]{1,0:T(8,128)(2,1)S(1)}, bf16[384,512]{1,0:T(8,128)(2,1)}, u32[]{:S(2)}) copy-start(bf16[384,512]{1,0:T(8,128)(2,1)} %refs_0_.3) | copy-start | bytes 1179652
  20.8 16.0 %copy-start.3 = (f32[512]{0:T(512)S(1)}, f32[512]{0:T(512)}, u32[]{:S(2)}) copy-start(f32[512]{0:T(512)} %param.32) | copy-start | bytes 6148
  20.8 16.0 %copy-start.4 = (f32[512]{0:T(512)S(1)}, f32[512]{0:T(512)}, u32[]{:S(2)}) copy-start(f32[512]{0:T(512)} %param.33) | copy-start | bytes 6148
  20.8 16.0 %copy-start.5 = (f32[512]{0:T(512)S(1)}, f32[512]{0:T(512)}, u32[]{:S(2)}) copy-start(f32[512]{0:T(512)} %param.34) | copy-start | bytes 6148
  20.8 16.0 %copy-start.6 = (f32[512]{0:T(512)S(1)}, f32[512]{0:T(512)}, u32[]{:S(2)}) copy-start(f32[512]{0:T(512)} %param.35) | copy-start | bytes 6148
  29.4 7.4 %collective-permute-start.7 = (bf16[384,512]{1,0:T(8,128)(2,1)S(1)}, bf16[384,512]{1,0:T(8,128)(2,1)S(1)}, u32[]{:S(2)}, u32[]{:S(2)}) collective-permute-start(bf16[384,512]{1,0:T(8,128)(2,1)S(1)} %get-tuple-element.25.refs_1_), channel_id=1, source_target_pairs={{0,1},{1,0},{2,3},{3,2},{4,5},{5,4},{6,7},{7,6},{8,9},{9,8},{10,11... | collective-permute-start | bytes 1179656 | tf_op jit(solution)/shard_map/ppermute | solution.py:501
  29.6 5.8 %collective-permute-start.12 = (bf16[128,512]{1,0:T(8,128)(2,1)S(1)}, bf16[128,512]{1,0:T(8,128)(2,1)S(1)}, u32[]{:S(2)}, u32[]{:S(2)}) collective-permute-start(bf16[128,512]{1,0:T(8,128)(2,1)S(1)} %copy-done.2), channel_id=1, source_target_pairs={{0,2},{2,0},{1,3},{3,1},{4,6},{6,4},{5,7},{7,5},{8,10},{10,8},{9,1... | collective-permute-start | bytes 393224 | tf_op jit(solution)/shard_map/ppermute | solution.py:227
  30.8 5.9 %collective-permute-start.8 = (bf16[2,128,512]{2,1,0:T(8,128)(2,1)S(1)}, bf16[2,128,512]{2,1,0:T(8,128)(2,1)S(1)}, u32[]{:S(2)}, u32[]{:S(2)}) collective-permute-start(bf16[2,128,512]{2,1,0:T(8,128)(2,1)S(1)} %copy-done.1), channel_id=1, source_target_pairs={{0,1},{1,0},{2,3},{3,2},{4,5},{5,4},{6,7},{7,6},{8,9},{9,8},{10,11... | collective-permute-start | bytes 786440 | tf_op jit(solution)/shard_map/ppermute | solution.py:235
  30.9 5.9 %collective-permute-start.10 = (bf16[2,128,512]{2,1,0:T(8,128)(2,1)S(1)}, bf16[2,128,512]{2,1,0:T(8,128)(2,1)S(1)}, u32[]{:S(2)}, u32[]{:S(2)}) collective-permute-start(bf16[2,128,512]{2,1,0:T(8,128)(2,1)S(1)} %collective-permute-done.9.refs_5_), channel_id=1, source_target_pairs={{0,1},{1,0},{2,3},{3,2},{4,5},{5,4},{6,7},{7,6},{8,9},{9,8},{10,11... | collective-permute-start | bytes 786440 | tf_op jit(solution)/shard_map/ppermute | solution.py:235
  31.3 4.1 %collective-permute-start.11 = (bf16[128,512]{1,0:T(8,128)(2,1)S(1)}, bf16[128,512]{1,0:T(8,128)(2,1)S(1)}, u32[]{:S(2)}, u32[]{:S(2)}) collective-permute-start(bf16[128,512]{1,0:T(8,128)(2,1)S(1)} %copy-done.2), channel_id=1, source_target_pairs={{0,1},{1,0},{2,3},{3,2},{4,5},{5,4},{6,7},{7,6},{8,9},{9,8},{10,11... | collective-permute-start | bytes 393224 | tf_op jit(solution)/shard_map/ppermute | solution.py:235
  35.4 1.3 %collective-permute-start.13 = (bf16[128,512]{1,0:T(8,128)(2,1)S(1)}, bf16[128,512]{1,0:T(8,128)(2,1)S(1)}, u32[]{:S(2)}, u32[]{:S(2)}) collective-permute-start(bf16[128,512]{1,0:T(8,128)(2,1)S(1)} %collective-permute-done.12.refs_9_), channel_id=1, source_target_pairs={{0,1},{1,0},{2,3},{3,2},{4,5},{5,4},{6,7},{7,6},{8,9},{9,8},{10,11... | collective-permute-start | bytes 393224 | tf_op jit(solution)/shard_map/ppermute | solution.py:235

commit v21 on v13

--- a/solution.py
+++ b/solution.py
@@ -90,7 +90,7 @@
         out_ref[part, half:] = picked[spot : spot + tile_rows][:1]
 
 
-def exchange_halves(node_latent, near_rows, far_rows, part_count):
+def exchange_halves(node_latent, near_rows, far_rows, part_count, earlier):
     near_cap, far_cap = near_rows.shape[2], far_rows.shape[2]
     subs = lax.axis_size("sub")
     width = node_latent.shape[1]
@@ -106,11 +106,12 @@
         cost_estimate=pl.CostEstimate(flops=0, bytes_accessed=0, transcendentals=0),
         name="pick_halo",
     )(in_hbm(jnp.transpose(far_rows, (0, 2, 1))), in_hbm(near_rows), in_hbm(node_latent))
+    blocks, earlier = lax.optimization_barrier((blocks, earlier))
     own = lax.all_to_all(blocks, ("region", "feat"), split_axis=0, concat_axis=0, tiled=True)
-    return [own]
-
-
-def exchange_all(node_latent, near_rows, far_rows, part_count):
+    return [own], earlier
+
+
+def exchange_all(node_latent, near_rows, far_rows, part_count, earlier):
     near_send = jnp.take(node_latent, near_rows[0], axis=0, mode="clip")
     far_send = jnp.take(node_latent, far_rows[0], axis=0, mode="clip")
     got = []
@@ -119,7 +120,7 @@
         got.append(lax.ppermute(near_send[which], ("region", "feat"), pairs))
     far = lax.all_to_all(far_send, ("region", "feat"), split_axis=0, concat_axis=0, tiled=True)
     got.append(far.reshape(-1, far.shape[2]))
-    return got
+    return got, earlier
 
 
 def gather_kernel(
@@ -413,7 +414,9 @@
     subs = lax.axis_size("sub")
     halved = part_count <= few_parts and far_cap == subs and near_cap % (tile_rows * subs) == 0
     exchange = exchange_halves if halved else exchange_all
-    got = exchange(node_latent, near_rows, far_rows, part_count)
+    got, near_edge[1] = exchange(
+        node_latent, near_rows, far_rows, part_count, near_edge[1]
+    )
     halo_space = len(near_offsets) * near_cap + part_count * far_cap
     halo_space = -(-halo_space // lanes) * lanes
 

time: 35.9 us -> 35.3 us (0.983)
  starting transfers between devices: 12.7 us -> 11.8 us
    ppermute x3, waiting for transfers between devices: 2.31 us -> 3.15 us  [from_feats(): lax.ppermute(weight, 'feat', [(at, (at + shift) % feats) for at in range(...]
    ppermute x7, waiting for transfers between devices: 2.22 us -> 1.45 us  [from_subs(): lax.ppermute(piece, 'sub', [(at, (at + turn) % subs) for at in range(subs)])]
    ppermute x1, starting transfers between devices: 0.56 us -> 0.2 us  [shards(): lax.ppermute(partial_sums, 'sub', [(at, (at + 1) % subs) for at in range(...]
  transfers between devices with their start and end apart: 12 -> 12, of which waited for: 6 -> 6; matrix products, arithmetic and copies ran while one was open for 0% -> 0% of each run, Pallas kernels for 39% -> 40%
where the time goes in v21:
time: 35.3 us; the launch traced here: 35 us
  Pallas kernels  16.1 us (46%)
  starting transfers between devices  11.8 us (33%)
  waiting for transfers between devices  6.4 us (18%)
  between operations  0.71 us (2%)
    pallas_call x1, Pallas kernels, shards(): pl.pallas_call(functools.partial(edge_kernel, pieces_count, len(got), par...  8.75 us
    ppermute x3, starting transfers between devices, from_feats(): lax.ppermute(weight, 'feat', [(at, (at + shift) % feats) for at in range(...  6 us
    all_to_all x1, starting transfers between devices, exchange_halves(): lax.all_to_all(blocks, ('region', 'feat'), split_axis=0, concat_axis=0, t...  4.88 us
    pallas_call x1, Pallas kernels, shards(): pl.pallas_call(functools.partial(gather_kernel, near_cap, far_cap, halved...  3.22 us
    ppermute x3, waiting for transfers between devices, from_feats(): lax.ppermute(weight, 'feat', [(at, (at + shift) % feats) for at in range(...  3.15 us
    pallas_call x1, Pallas kernels, exchange_halves(): pl.pallas_call(functools.partial(pick_kernel, part_count, near_cap, far_c...  2.08 us
    pallas_call x1, Pallas kernels, shards(): pl.pallas_call(functools.partial(node_kernel, pieces_count), out_shape=ja...  2.01 us
    ppermute x7, waiting for transfers between devices, from_subs(): lax.ppermute(piece, 'sub', [(at, (at + turn) % subs) for at in range(subs)])  1.45 us
  transfers between devices with their start and end apart: 12, of which 6 were waited for; matrix products, arithmetic and copies ran while one was open for 0% of the time, Pallas kernels for 40%

profile of v21, /device:TPU:0, one launch (start us, length us, event | category | flops | bytes accessed | tf_op | source)
XLA Modules:
  0.0 35.0 jit_solution(6766773385379081587)
XLA Ops:
  0.6 3.0 %collective-permute-start = (bf16[3,128,512]{2,1,0:T(8,128)(2,1)}, bf16[3,128,512]{2,1,0:T(8,128)(2,1)}, u32[]{:S(2)}, u32[]{:S(2)}) collective-permute-start(bf16[3,128,512]{2,1,0:T(8,128)(2,1)} %refs_6_.1), channel_id=1, source_target_pairs={{0,2},{2,0},{1,3},{3,1},{4,6},{6,4},{5,7},{7,5},{8,10},{10,8},{9,1... | collective-permute-start | bytes 1179656 | tf_op jit(solution)/shard_map/ppermute | solution.py:234
  3.6 0.0 collective-permute-start.2
  3.6 2.1 %pick_halo.1 = bf16[8,17,512]{2,1,0:T(8,128)(2,1)} custom-call(s32[1,2,8]{2,1,0:T(2,128)} %bitcast.18, s32[1,4,32]{2,1,0:T(4,128)} %near_ref.1, bf16[384,512]{1,0:T(8,128)(2,1)} %refs_0_.3), custom_call_target="tpu_custom_call" | custom-call | tf_op jit(solution)/shard_map/pick_halo/pallas_call | solution.py:99
  5.7 4.9 %all-to-all-start = ((bf16[8,17,512]{2,1,0:T(8,128)(2,1)}), bf16[8,17,512]{2,1,0:T(8,128)(2,1)S(1)}, u32[]{:S(2)}, u32[]{:S(2)}) async-start(bf16[8,17,512]{2,1,0:T(8,128)(2,1)} %pick_halo.1), calls=%async_computation | async-start | bytes 393216 | tf_op jit(solution)/shard_map/all_to_all | solution.py:110
  10.6 2.0 %collective-permute-start.1 = (bf16[128,512]{1,0:T(8,128)(2,1)}, bf16[128,512]{1,0:T(8,128)(2,1)}, u32[]{:S(2)}, u32[]{:S(2)}) collective-permute-start(bf16[128,512]{1,0:T(8,128)(2,1)} %refs_10_.1), channel_id=1, source_target_pairs={{0,2},{2,0},{1,3},{3,1},{4,6},{6,4},{5,7},{7,5},{8,10},{10,8},{9,1... | collective-permute-start | bytes 393224 | tf_op jit(solution)/shard_map/ppermute | solution.py:234
  12.6 0.0 collective-permute-start.4
  12.6 3.2 %gather_latents.1 = (bf16[768,1792]{1,0:T(8,128)(2,1)S(1)}, bf16[768,1280]{1,0:T(8,128)(2,1)}, bf16[3,128,512]{2,1,0:T(8,128)(2,1)S(1)}) custom-call(s32[12,128]{1,0:T(8,128)} %bitcast.15, s32[12,128]{1,0:T(8,128)} %bitcast.16, bf16[384,512]{1,0:T(8,128)(2,1)} %refs_0_.3, bf16[2,128,512]{2,1,0:T(8,128)(2,1)} %node_in_ref.1, bf16[128,512]{1,0:T(8,128)(2,1)} %node_out_ref.1, ...), custom_call_target="tpu_custom_call" | custom-call | tf_op jit(solution)/shard_map/gather_latents/pallas_call | solution.py:430
  15.9 2.5 %collective-permute-done.1.refs_12_ = bf16[128,512]{1,0:T(8,128)(2,1)} collective-permute-done((bf16[128,512]{1,0:T(8,128)(2,1)}, bf16[128,512]{1,0:T(8,128)(2,1)}, u32[]{:S(2)}, u32[]{:S(2)}) %collective-permute-start.1) | collective-permute-done | bytes 131104 | tf_op jit(solution)/shard_map/ppermute | solution.py:234
  18.4 0.8 %all-to-all-done.refs_4_ = bf16[8,17,512]{2,1,0:T(8,128)(2,1)S(1)} async-done(((bf16[8,17,512]{2,1,0:T(8,128)(2,1)}), bf16[8,17,512]{2,1,0:T(8,128)(2,1)S(1)}, u32[]{:S(2)}, u32[]{:S(2)}) %all-to-all-start) | async-done | bytes 139296 | tf_op jit(solution)/shard_map/all_to_all | solution.py:110
  19.2 0.5 %collective-permute-start.3 = (bf16[8,17,512]{2,1,0:T(8,128)(2,1)S(1)}, bf16[8,17,512]{2,1,0:T(8,128)(2,1)S(1)}, u32[]{:S(2)}, u32[]{:S(2)}) collective-permute-start(bf16[8,17,512]{2,1,0:T(8,128)(2,1)S(1)} %all-to-all-done.refs_4_), channel_id=1, source_target_pairs={{0,1},{1,0},{2,3},{3,2},{4,5},{5,4},{6,7},{7,6},{8,9},{9,8},{10,11... | collective-permute-start | bytes 417800 | tf_op jit(solution)/shard_map/ppermute | solution.py:242
  19.7 0.0 collective-permute-start.6
  19.7 1.0 %collective-permute-start.9 = (bf16[3,128,512]{2,1,0:T(8,128)(2,1)S(1)}, bf16[3,128,512]{2,1,0:T(8,128)(2,1)S(1)}, u32[]{:S(2)}, u32[]{:S(2)}) collective-permute-start(bf16[3,128,512]{2,1,0:T(8,128)(2,1)S(1)} %get-tuple-element.27.refs_3_), channel_id=1, source_target_pairs={{0,2},{2,0},{1,3},{3,1},{4,6},{6,4},{5,7},{7,5},{8,10},{10,8},{9,1... | collective-permute-start | bytes 1179656 | tf_op jit(solution)/shard_map/ppermute | solution.py:234
  20.7 0.2 collective-permute-start.8
  20.9 0.7 %collective-permute-done.6.refs_13_ = bf16[128,512]{1,0:T(8,128)(2,1)S(1)} collective-permute-done((bf16[128,512]{1,0:T(8,128)(2,1)}, bf16[128,512]{1,0:T(8,128)(2,1)S(1)}, u32[]{:S(2)}, u32[]{:S(2)}) %collective-permute-start.6) | collective-permute-done | bytes 131104 | tf_op jit(solution)/shard_map/ppermute | solution.py:242
  21.6 0.0 copy-start.1
  21.7 0.0 copy-start.2
  21.7 0.0 copy-start.3
  21.7 0.0 copy-start.4
  21.7 8.8 %edge_update.1 = (bf16[1536,512]{1,0:T(8,128)(2,1)}, bf16[384,512]{1,0:T(8,128)(2,1)S(1)}) custom-call(bf16[1536,512]{1,0:T(8,128)(2,1)} %refs_0_.2, bf16[768,1280]{1,0:T(8,128)(2,1)} %get-tuple-element.19.refs_1_, s32[12,128]{1,0:T(8,128)} %bitcast.17, bf16[768,1792]{1,0:T(8,128)(2,1)S(1)} %get-tuple-element.20.refs_3_, ...), custom_call_target="tpu_custom_call" | custom-call | flops 3825205248 | bytes 6291456 | tf_op jit(solution)/shard_map/edge_update/pallas_call | solution.py:478
  30.5 0.2 collective-permute-start.7
  30.6 0.6 %collective-permute-done.9.refs_5_ = bf16[3,128,512]{2,1,0:T(8,128)(2,1)S(1)} collective-permute-done((bf16[3,128,512]{2,1,0:T(8,128)(2,1)S(1)}, bf16[3,128,512]{2,1,0:T(8,128)(2,1)S(1)}, u32[]{:S(2)}, u32[]{:S(2)}) %collective-permute-start.9) | collective-permute-done | bytes 393248 | tf_op jit(solution)/shard_map/ppermute | solution.py:234
  31.3 1.0 %collective-permute-done.7.refs_2_ = bf16[384,512]{1,0:T(8,128)(2,1)S(1)} collective-permute-done((bf16[384,512]{1,0:T(8,128)(2,1)S(1)}, bf16[384,512]{1,0:T(8,128)(2,1)S(1)}, u32[]{:S(2)}, u32[]{:S(2)}) %collective-permute-start.7) | collective-permute-done | bytes 393248 | tf_op jit(solution)/shard_map/ppermute | solution.py:512
  32.2 0.8 %collective-permute-done.10.refs_6_ = bf16[3,128,512]{2,1,0:T(8,128)(2,1)S(1)} collective-permute-done((bf16[3,128,512]{2,1,0:T(8,128)(2,1)S(1)}, bf16[3,128,512]{2,1,0:T(8,128)(2,1)S(1)}, u32[]{:S(2)}, u32[]{:S(2)}) %collective-permute-start.10) | collective-permute-done | bytes 393248 | tf_op jit(solution)/shard_map/ppermute | solution.py:242
  33.0 2.0 %node_update.1 = bf16[384,512]{1,0:T(8,128)(2,1)} custom-call(bf16[384,512]{1,0:T(8,128)(2,1)S(1)} %copy-done, bf16[384,512]{1,0:T(8,128)(2,1)S(1)} %get-tuple-element.26.refs_1_, bf16[384,512]{1,0:T(8,128)(2,1)S(1)} %collective-permute-done.7.refs_2_, bf16[3,128,512]{2,1,0:T(8,128)(2,1)S(1)} %get-tuple-element.27.refs_3_, ...), custom_call_target="tpu_custom_call" | custom-call | flops 603979776 | bytes 1966080 | tf_op jit(solution)/shard_map/node_update/pallas_call | solution.py:515
  (14 shorter events, 0.0 us)
Async XLA Ops:
  0.6 18.6 %collective-permute-start = (bf16[3,128,512]{2,1,0:T(8,128)(2,1)}, bf16[3,128,512]{2,1,0:T(8,128)(2,1)}, u32[]{:S(2)}, u32[]{:S(2)}) collective-permute-start(bf16[3,128,512]{2,1,0:T(8,128)(2,1)} %refs_6_.1), channel_id=1, source_target_pairs={{0,2},{2,0},{1,3},{3,1},{4,6},{6,4},{5,7},{7,5},{8,10},{10,8},{9,1... | collective-permute-start | bytes 1179656 | tf_op jit(solution)/shard_map/ppermute | solution.py:234
  3.6 2.1 %collective-permute-start.2 = (bf16[128,512]{1,0:T(8,128)(2,1)}, bf16[128,512]{1,0:T(8,128)(2,1)S(1)}, u32[]{:S(2)}, u32[]{:S(2)}) collective-permute-start(bf16[128,512]{1,0:T(8,128)(2,1)} %refs_10_.1), channel_id=1, source_target_pairs={{0,1},{1,0},{2,3},{3,2},{4,5},{5,4},{6,7},{7,6},{8,9},{9,8},{10,11... | collective-permute-start | bytes 393224 | tf_op jit(solution)/shard_map/ppermute | solution.py:242
  5.7 13.5 %all-to-all-start = ((bf16[8,17,512]{2,1,0:T(8,128)(2,1)}), bf16[8,17,512]{2,1,0:T(8,128)(2,1)S(1)}, u32[]{:S(2)}, u32[]{:S(2)}) async-start(bf16[8,17,512]{2,1,0:T(8,128)(2,1)} %pick_halo.1), calls=%async_computation | async-start | bytes 393216 | tf_op jit(solution)/shard_map/all_to_all | solution.py:110
  10.6 7.8 %collective-permute-start.1 = (bf16[128,512]{1,0:T(8,128)(2,1)}, bf16[128,512]{1,0:T(8,128)(2,1)}, u32[]{:S(2)}, u32[]{:S(2)}) collective-permute-start(bf16[128,512]{1,0:T(8,128)(2,1)} %refs_10_.1), channel_id=1, source_target_pairs={{0,2},{2,0},{1,3},{3,1},{4,6},{6,4},{5,7},{7,5},{8,10},{10,8},{9,1... | collective-permute-start | bytes 393224 | tf_op jit(solution)/shard_map/ppermute | solution.py:234
  12.6 8.1 %collective-permute-start.4 = (bf16[3,128,512]{2,1,0:T(8,128)(2,1)}, bf16[3,128,512]{2,1,0:T(8,128)(2,1)}, u32[]{:S(2)}, u32[]{:S(2)}) collective-permute-start(bf16[3,128,512]{2,1,0:T(8,128)(2,1)} %refs_6_.1), channel_id=1, source_target_pairs={{0,1},{1,0},{2,3},{3,2},{4,5},{5,4},{6,7},{7,6},{8,9},{9,8},{10,11... | collective-permute-start | bytes 1179656 | tf_op jit(solution)/shard_map/ppermute | solution.py:242
  19.2 2.4 %collective-permute-start.5 = (bf16[3,128,512]{2,1,0:T(8,128)(2,1)}, bf16[3,128,512]{2,1,0:T(8,128)(2,1)S(1)}, u32[]{:S(2)}, u32[]{:S(2)}) collective-permute-start(bf16[3,128,512]{2,1,0:T(8,128)(2,1)} %collective-permute-done.refs_8_), channel_id=1, source_target_pairs={{0,1},{1,0},{2,3},{3,2},{4,5},{5,4},{6,7},{7,6},{8,9},{9,8},{10,11... | collective-permute-start | bytes 1179656 | tf_op jit(solution)/shard_map/ppermute | solution.py:242
  19.2 2.4 %collective-permute-start.3 = (bf16[8,17,512]{2,1,0:T(8,128)(2,1)S(1)}, bf16[8,17,512]{2,1,0:T(8,128)(2,1)S(1)}, u32[]{:S(2)}, u32[]{:S(2)}) collective-permute-start(bf16[8,17,512]{2,1,0:T(8,128)(2,1)S(1)} %all-to-all-done.refs_4_), channel_id=1, source_target_pairs={{0,1},{1,0},{2,3},{3,2},{4,5},{5,4},{6,7},{7,6},{8,9},{9,8},{10,11... | collective-permute-start | bytes 417800 | tf_op jit(solution)/shard_map/ppermute | solution.py:242
  19.7 1.9 %collective-permute-start.6 = (bf16[128,512]{1,0:T(8,128)(2,1)}, bf16[128,512]{1,0:T(8,128)(2,1)S(1)}, u32[]{:S(2)}, u32[]{:S(2)}) collective-permute-start(bf16[128,512]{1,0:T(8,128)(2,1)} %collective-permute-done.1.refs_12_), channel_id=1, source_target_pairs={{0,1},{1,0},{2,3},{3,2},{4,5},{5,4},{6,7},{7,6},{8,9},{9,8},{10,11... | collective-permute-start | bytes 393224 | tf_op jit(solution)/shard_map/ppermute | solution.py:242
  19.7 11.5 %collective-permute-start.9 = (bf16[3,128,512]{2,1,0:T(8,128)(2,1)S(1)}, bf16[3,128,512]{2,1,0:T(8,128)(2,1)S(1)}, u32[]{:S(2)}, u32[]{:S(2)}) collective-permute-start(bf16[3,128,512]{2,1,0:T(8,128)(2,1)S(1)} %get-tuple-element.27.refs_3_), channel_id=1, source_target_pairs={{0,2},{2,0},{1,3},{3,1},{4,6},{6,4},{5,7},{7,5},{8,10},{10,8},{9,1... | collective-permute-start | bytes 1179656 | tf_op jit(solution)/shard_map/ppermute | solution.py:234
  20.7 10.6 %collective-permute-start.8 = (bf16[3,128,512]{2,1,0:T(8,128)(2,1)S(1)}, bf16[3,128,512]{2,1,0:T(8,128)(2,1)S(1)}, u32[]{:S(2)}, u32[]{:S(2)}) collective-permute-start(bf16[3,128,512]{2,1,0:T(8,128)(2,1)S(1)} %get-tuple-element.27.refs_3_), channel_id=1, source_target_pairs={{0,1},{1,0},{2,3},{3,2},{4,5},{5,4},{6,7},{7,6},{8,9},{9,8},{10,11... | collective-permute-start | bytes 1179656 | tf_op jit(solution)/shard_map/ppermute | solution.py:242
  21.6 11.4 %copy-start = (bf16[384,512]{1,0:T(8,128)(2,1)S(1)}, bf16[384,512]{1,0:T(8,128)(2,1)}, u32[]{:S(2)}) copy-start(bf16[384,512]{1,0:T(8,128)(2,1)} %refs_0_.3) | copy-start | bytes 1179652
  21.6 11.4 %copy-start.1 = (f32[512]{0:T(512)S(1)}, f32[512]{0:T(512)}, u32[]{:S(2)}) copy-start(f32[512]{0:T(512)} %param.32) | copy-start | bytes 6148
  21.7 11.3 %copy-start.2 = (f32[512]{0:T(512)S(1)}, f32[512]{0:T(512)}, u32[]{:S(2)}) copy-start(f32[512]{0:T(512)} %param.33) | copy-start | bytes 6148
  21.7 11.3 %copy-start.3 = (f32[512]{0:T(512)S(1)}, f32[512]{0:T(512)}, u32[]{:S(2)}) copy-start(f32[512]{0:T(512)} %param.34) | copy-start | bytes 6148
  21.7 11.3 %copy-start.4 = (f32[512]{0:T(512)S(1)}, f32[512]{0:T(512)}, u32[]{:S(2)}) copy-start(f32[512]{0:T(512)} %param.35) | copy-start | bytes 6148
  30.5 1.8 %collective-permute-start.7 = (bf16[384,512]{1,0:T(8,128)(2,1)S(1)}, bf16[384,512]{1,0:T(8,128)(2,1)S(1)}, u32[]{:S(2)}, u32[]{:S(2)}) collective-permute-start(bf16[384,512]{1,0:T(8,128)(2,1)S(1)} %get-tuple-element.26.refs_1_), channel_id=1, source_target_pairs={{0,1},{1,0},{2,3},{3,2},{4,5},{5,4},{6,7},{7,6},{8,9},{9,8},{10,11... | collective-permute-start | bytes 1179656 | tf_op jit(solution)/shard_map/ppermute | solution.py:512
  31.3 1.7 %collective-permute-start.10 = (bf16[3,128,512]{2,1,0:T(8,128)(2,1)S(1)}, bf16[3,128,512]{2,1,0:T(8,128)(2,1)S(1)}, u32[]{:S(2)}, u32[]{:S(2)}) collective-permute-start(bf16[3,128,512]{2,1,0:T(8,128)(2,1)S(1)} %collective-permute-done.9.refs_5_), channel_id=1, source_target_pairs={{0,1},{1,0},{2,3},{3,2},{4,5},{5,4},{6,7},{7,6},{8,9},{9,8},{10,11... | collective-permute-start | bytes 1179656 | tf_op jit(solution)/shard_map/ppermute | solution.py:242

commit v22 on v17

--- a/solution.py
+++ b/solution.py
@@ -72,7 +72,7 @@
 
 def pick_kernel(part_count, near_cap, far_cap, far_ref, near_ref, latent_ref, out_ref, picked):
     me, sub, subs = my_part(), lax.axis_index("sub"), lax.axis_size("sub")
-    half = near_cap // subs
+    half, width = near_cap // subs, latent_ref.shape[1]
     columns = [as_columns(near_ref[0])]
     tile_place = lax.broadcasted_iota(jnp.int32, (tile_rows, lanes), 0)
     far = as_columns(far_ref[0, 0:1])
@@ -81,23 +81,27 @@
     for part in range(part_count):
         columns.append(jnp.where(tile_place == 0, far[part : part + 1], -1))
     hot = one_hot(jnp.concatenate(columns, axis=0), latent_ref.shape[0])
-    picked[...] = jnp.dot(hot, latent_ref[...], preferred_element_type=f32).astype(bf16)
+    rows = jnp.dot(hot, latent_ref[...], preferred_element_type=f32)
+    far_start = len(near_offsets) * near_cap
+    picked[...] = rows[:far_start].astype(bf16)
     for which, offset in enumerate(near_offsets):
         target = lax.rem(me + (offset + part_count), part_count)
         start = pl.multiple_of(which * near_cap + sub * half, half)
-        out_ref[target, :half] = picked[pl.ds(start, half)]
-    far_start = len(near_offsets) * near_cap
+        out_ref[target, :, :width] = picked[pl.ds(start, half)]
     for part in range(part_count):
         spot = far_start + part * tile_rows
-        out_ref[part, half:] = picked[spot : spot + tile_rows][:1]
+        far_row = rows[spot : spot + 1]
+        pieces = [far_row[:, at : at + lanes] for at in range(0, width, lanes)]
+        pieces.append(jnp.zeros((half - len(pieces), lanes), f32))
+        out_ref[part, :, width:] = jnp.concatenate(pieces, axis=0).astype(bf16)
 
 
 def exchange_halves(node_latent, near_rows, far_rows, part_count):
     near_cap, far_cap = near_rows.shape[2], far_rows.shape[2]
     subs = lax.axis_size("sub")
     width = node_latent.shape[1]
-    block = (part_count, near_cap // subs + 1, width)
-    picks = len(near_offsets) * near_cap + part_count * tile_rows
+    block = (part_count, near_cap // subs, width + lanes)
+    picks = len(near_offsets) * near_cap
     blocks = pl.pallas_call(
         functools.partial(pick_kernel, part_count, near_cap, far_cap),
         out_shape=pltpu.HBM(block, bf16),
@@ -194,7 +198,7 @@
 
 
 def place_halo(halo, part_count, near_cap, halved, got):
-    subs = lax.axis_size("sub")
+    subs, width = lax.axis_size("sub"), halo.shape[1]
     far_start = len(near_offsets) * near_cap
     used = far_start
     if halved:
@@ -204,12 +208,15 @@
             for turn in range(subs):
                 owner = wrap(lax.axis_index("sub") - turn, subs)
                 start = pl.multiple_of(which * near_cap + owner * half, half)
-                halo[pl.ds(start, half)] = got[turn][origin, :half]
-        far = [got[turn][part, half:] for part in range(part_count) for turn in range(subs)]
+                halo[pl.ds(start, half)] = got[turn][origin, :, :width]
+        far = []
+        for part in range(part_count):
+            for turn in range(subs):
+                tile = got[turn][part, :, width:].astype(f32)
+                pieces = [tile[at : at + 1] for at in range(width // lanes)]
+                far.append(jnp.concatenate(pieces, axis=1))
         used += len(far)
-        halo[far_start:used] = jnp.concatenate(
-            [row.astype(f32) for row in far], axis=0
-        ).astype(bf16)
+        halo[far_start:used] = jnp.concatenate(far, axis=0).astype(bf16)
     else:
         for rows in got:
             start = used - far_start if rows is not got[-1] else far_start

time: 34.9 us -> 34.6 us (level)
  waiting for transfers between devices: 3.84 us -> 3.41 us
  transfers between devices with their start and end apart: 12 -> 12, of which waited for: 5 -> 5; matrix products, arithmetic and copies ran while one was open for 0% -> 0% of each run, Pallas kernels for 45% -> 46%
where the time goes in v22:
time: 34.6 us; the launch traced here: 34.3 us
  Pallas kernels  17.7 us (51%)
  starting transfers between devices  12.4 us (36%)
  waiting for transfers between devices  3.41 us (10%)
  between operations  0.74 us (2%)
    pallas_call x1, Pallas kernels, shards(): pl.pallas_call(functools.partial(edge_kernel, pieces_count, len(got), par...  8.86 us
    ppermute x3, starting transfers between devices, from_feats(): lax.ppermute(weight, 'feat', [(at, (at + shift) % feats) for at in range(...  6.3 us
    all_to_all x1, starting transfers between devices, exchange_halves(): lax.all_to_all(blocks, ('region', 'feat'), split_axis=0, concat_axis=0, t...  4.88 us
    pallas_call x1, Pallas kernels, shards(): pl.pallas_call(functools.partial(gather_kernel, near_cap, far_cap, halved...  4.77 us
    pallas_call x1, Pallas kernels, exchange_halves(): pl.pallas_call(functools.partial(pick_kernel, part_count, near_cap, far_c...  2.07 us
    pallas_call x1, Pallas kernels, shards(): pl.pallas_call(functools.partial(node_kernel, pieces_count), out_shape=ja...  2.01 us
    ppermute x3, waiting for transfers between devices, from_feats(): lax.ppermute(weight, 'feat', [(at, (at + shift) % feats) for at in range(...  1.56 us
    ppermute x7, waiting for transfers between devices, from_subs(): lax.ppermute(piece, 'sub', [(at, (at + turn) % subs) for at in range(subs)])  1.23 us
  transfers between devices with their start and end apart: 12, of which 5 were waited for; matrix products, arithmetic and copies ran while one was open for 0% of the time, Pallas kernels for 46%

profile of v22, /device:TPU:0, one launch (start us, length us, event | category | flops | bytes accessed | tf_op | source)
XLA Modules:
  0.0 34.3 jit_solution(2580453762207629089)
XLA Ops:
  0.6 3.0 %collective-permute-start = (bf16[3,128,512]{2,1,0:T(8,128)(2,1)}, bf16[3,128,512]{2,1,0:T(8,128)(2,1)}, u32[]{:S(2)}, u32[]{:S(2)}) collective-permute-start(bf16[3,128,512]{2,1,0:T(8,128)(2,1)} %refs_6_.1), channel_id=1, source_target_pairs={{0,2},{2,0},{1,3},{3,1},{4,6},{6,4},{5,7},{7,5},{8,10},{10,8},{9,1... | collective-permute-start | bytes 1179656 | tf_op jit(solution)/shard_map/ppermute | solution.py:248
  3.6 2.1 %pick_halo.1 = bf16[8,16,640]{2,1,0:T(8,128)(2,1)} custom-call(s32[1,2,8]{2,1,0:T(2,128)} %bitcast.17, s32[1,4,32]{2,1,0:T(4,128)} %near_ref.1, bf16[384,512]{1,0:T(8,128)(2,1)} %refs_0_.3), custom_call_target="tpu_custom_call" | custom-call | tf_op jit(solution)/shard_map/pick_halo/pallas_call | solution.py:105
  5.7 4.9 %all-to-all-start = ((bf16[8,16,640]{2,1,0:T(8,128)(2,1)}), bf16[8,16,640]{2,1,0:T(8,128)(2,1)S(1)}, u32[]{:S(2)}, u32[]{:S(2)}) async-start(bf16[8,16,640]{2,1,0:T(8,128)(2,1)} %pick_halo.1), calls=%async_computation | async-start | bytes 327680 | tf_op jit(solution)/shard_map/all_to_all | solution.py:115
  10.6 0.0 collective-permute-start.2
  10.6 2.0 %collective-permute-start.1 = (bf16[128,512]{1,0:T(8,128)(2,1)}, bf16[128,512]{1,0:T(8,128)(2,1)S(1)}, u32[]{:S(2)}, u32[]{:S(2)}) collective-permute-start(bf16[128,512]{1,0:T(8,128)(2,1)} %refs_10_.1), channel_id=1, source_target_pairs={{0,2},{2,0},{1,3},{3,1},{4,6},{6,4},{5,7},{7,5},{8,10},{10,8},{9,1... | collective-permute-start | bytes 393224 | tf_op jit(solution)/shard_map/ppermute | solution.py:248
  12.6 0.2 collective-permute-start.4
  12.8 4.8 %gather_latents.1 = (bf16[512,1792]{1,0:T(8,128)(2,1)S(1)}, bf16[1024,1280]{1,0:T(8,128)(2,1)}, bf16[384,1536]{1,0:T(8,128)(2,1)S(1)}, bf16[3,128,512]{2,1,0:T(8,128)(2,1)}) custom-call(s32[12,128]{1,0:T(8,128)} %bitcast.15, s32[12,128]{1,0:T(8,128)} %bitcast.16, bf16[384,512]{1,0:T(8,128)(2,1)} %refs_0_.3, bf16[2,128,512]{2,1,0:T(8,128)(2,1)} %node_in_ref.1, ...), custom_call_target="tpu_custom_call" | custom-call | tf_op jit(solution)/shard_map/gather_latents/pallas_call | solution.py:434
  17.6 0.7 %collective-permute-done.1.refs_12_ = bf16[128,512]{1,0:T(8,128)(2,1)S(1)} collective-permute-done((bf16[128,512]{1,0:T(8,128)(2,1)}, bf16[128,512]{1,0:T(8,128)(2,1)S(1)}, u32[]{:S(2)}, u32[]{:S(2)}) %collective-permute-start.1) | collective-permute-done | bytes 131104 | tf_op jit(solution)/shard_map/ppermute | solution.py:248
  18.3 0.5 %collective-permute-start.3 = (bf16[8,16,640]{2,1,0:T(8,128)(2,1)S(1)}, bf16[8,16,640]{2,1,0:T(8,128)(2,1)S(1)}, u32[]{:S(2)}, u32[]{:S(2)}) collective-permute-start(bf16[8,16,640]{2,1,0:T(8,128)(2,1)S(1)} %all-to-all-done.refs_4_), channel_id=1, source_target_pairs={{0,1},{1,0},{2,3},{3,2},{4,5},{5,4},{6,7},{7,6},{8,9},{9,8},{10,11... | collective-permute-start | bytes 491528 | tf_op jit(solution)/shard_map/ppermute | solution.py:256
  18.8 0.1 collective-permute-start.6
  18.9 1.3 %collective-permute-start.9 = (bf16[3,128,512]{2,1,0:T(8,128)(2,1)}, bf16[3,128,512]{2,1,0:T(8,128)(2,1)S(1)}, u32[]{:S(2)}, u32[]{:S(2)}) collective-permute-start(bf16[3,128,512]{2,1,0:T(8,128)(2,1)} %get-tuple-element.31.refs_3_), channel_id=1, source_target_pairs={{0,2},{2,0},{1,3},{3,1},{4,6},{6,4},{5,7},{7,5},{8,10},{10,8},{9,1... | collective-permute-start | bytes 1179656 | tf_op jit(solution)/shard_map/ppermute | solution.py:248
  20.2 0.2 collective-permute-start.8
  20.3 0.1 collective-permute-done.6.refs_13_
  20.5 0.0 copy-start.1
  20.5 0.0 copy-start.2
  20.5 0.0 copy-start.3
  20.5 0.0 copy-start.4
  20.5 0.0 copy-start.5
  20.5 8.9 %edge_update.1 = (bf16[1536,512]{1,0:T(8,128)(2,1)}, bf16[384,512]{1,0:T(8,128)(2,1)S(1)}) custom-call(bf16[1536,512]{1,0:T(8,128)(2,1)} %refs_0_.2, bf16[1024,1280]{1,0:T(8,128)(2,1)} %get-tuple-element.22.refs_1_, bf16[384,1536]{1,0:T(8,128)(2,1)S(1)} %get-tuple-element.23.refs_2_, bf16[512,1792]{1,0:T(8,128)(2,1)S(1)} %get-tuple-element.24.refs_3_, ...), custom_call_target="tpu_custom_call" | custom-call | flops 3825205248 | bytes 6291456 | tf_op jit(solution)/shard_map/edge_update/pallas_call | solution.py:483
  29.4 0.3 collective-permute-start.7
  29.7 0.9 %collective-permute-done.9.refs_5_ = bf16[3,128,512]{2,1,0:T(8,128)(2,1)S(1)} collective-permute-done((bf16[3,128,512]{2,1,0:T(8,128)(2,1)}, bf16[3,128,512]{2,1,0:T(8,128)(2,1)S(1)}, u32[]{:S(2)}, u32[]{:S(2)}) %collective-permute-start.9) | collective-permute-done | bytes 393248 | tf_op jit(solution)/shard_map/ppermute | solution.py:248
  30.6 0.6 %collective-permute-done.7.refs_2_ = bf16[384,512]{1,0:T(8,128)(2,1)S(1)} collective-permute-done((bf16[384,512]{1,0:T(8,128)(2,1)S(1)}, bf16[384,512]{1,0:T(8,128)(2,1)S(1)}, u32[]{:S(2)}, u32[]{:S(2)}) %collective-permute-start.7) | collective-permute-done | bytes 393248 | tf_op jit(solution)/shard_map/ppermute | solution.py:514
  31.2 1.1 %collective-permute-done.10.refs_6_ = bf16[3,128,512]{2,1,0:T(8,128)(2,1)S(1)} collective-permute-done((bf16[3,128,512]{2,1,0:T(8,128)(2,1)S(1)}, bf16[3,128,512]{2,1,0:T(8,128)(2,1)S(1)}, u32[]{:S(2)}, u32[]{:S(2)}) %collective-permute-start.10) | collective-permute-done | bytes 393248 | tf_op jit(solution)/shard_map/ppermute | solution.py:256
  32.3 2.0 %node_update.1 = bf16[384,512]{1,0:T(8,128)(2,1)} custom-call(bf16[384,512]{1,0:T(8,128)(2,1)S(1)} %copy-done, bf16[384,512]{1,0:T(8,128)(2,1)S(1)} %get-tuple-element.30.refs_1_, bf16[384,512]{1,0:T(8,128)(2,1)S(1)} %collective-permute-done.7.refs_2_, bf16[3,128,512]{2,1,0:T(8,128)(2,1)S(1)} %copy-done.1, ...), custom_call_target="tpu_custom_call" | custom-call | flops 603979776 | bytes 1966080 | tf_op jit(solution)/shard_map/node_update/pallas_call | solution.py:517
  (16 shorter events, 0.0 us)
Async XLA Ops:
  0.6 17.7 %collective-permute-start = (bf16[3,128,512]{2,1,0:T(8,128)(2,1)}, bf16[3,128,512]{2,1,0:T(8,128)(2,1)}, u32[]{:S(2)}, u32[]{:S(2)}) collective-permute-start(bf16[3,128,512]{2,1,0:T(8,128)(2,1)} %refs_6_.1), channel_id=1, source_target_pairs={{0,2},{2,0},{1,3},{3,1},{4,6},{6,4},{5,7},{7,5},{8,10},{10,8},{9,1... | collective-permute-start | bytes 1179656 | tf_op jit(solution)/shard_map/ppermute | solution.py:248
  5.7 12.6 %all-to-all-start = ((bf16[8,16,640]{2,1,0:T(8,128)(2,1)}), bf16[8,16,640]{2,1,0:T(8,128)(2,1)S(1)}, u32[]{:S(2)}, u32[]{:S(2)}) async-start(bf16[8,16,640]{2,1,0:T(8,128)(2,1)} %pick_halo.1), calls=%async_computation | async-start | bytes 327680 | tf_op jit(solution)/shard_map/all_to_all | solution.py:115
  10.6 2.3 %collective-permute-start.2 = (bf16[128,512]{1,0:T(8,128)(2,1)}, bf16[128,512]{1,0:T(8,128)(2,1)S(1)}, u32[]{:S(2)}, u32[]{:S(2)}) collective-permute-start(bf16[128,512]{1,0:T(8,128)(2,1)} %refs_10_.1), channel_id=1, source_target_pairs={{0,1},{1,0},{2,3},{3,2},{4,5},{5,4},{6,7},{7,6},{8,9},{9,8},{10,11... | collective-permute-start | bytes 393224 | tf_op jit(solution)/shard_map/ppermute | solution.py:256
  10.6 7.7 %collective-permute-start.1 = (bf16[128,512]{1,0:T(8,128)(2,1)}, bf16[128,512]{1,0:T(8,128)(2,1)S(1)}, u32[]{:S(2)}, u32[]{:S(2)}) collective-permute-start(bf16[128,512]{1,0:T(8,128)(2,1)} %refs_10_.1), channel_id=1, source_target_pairs={{0,2},{2,0},{1,3},{3,1},{4,6},{6,4},{5,7},{7,5},{8,10},{10,8},{9,1... | collective-permute-start | bytes 393224 | tf_op jit(solution)/shard_map/ppermute | solution.py:248
  12.6 7.6 %collective-permute-start.4 = (bf16[3,128,512]{2,1,0:T(8,128)(2,1)}, bf16[3,128,512]{2,1,0:T(8,128)(2,1)}, u32[]{:S(2)}, u32[]{:S(2)}) collective-permute-start(bf16[3,128,512]{2,1,0:T(8,128)(2,1)} %refs_6_.1), channel_id=1, source_target_pairs={{0,1},{1,0},{2,3},{3,2},{4,5},{5,4},{6,7},{7,6},{8,9},{9,8},{10,11... | collective-permute-start | bytes 1179656 | tf_op jit(solution)/shard_map/ppermute | solution.py:256
  18.3 2.2 %collective-permute-start.5 = (bf16[3,128,512]{2,1,0:T(8,128)(2,1)}, bf16[3,128,512]{2,1,0:T(8,128)(2,1)S(1)}, u32[]{:S(2)}, u32[]{:S(2)}) collective-permute-start(bf16[3,128,512]{2,1,0:T(8,128)(2,1)} %collective-permute-done.refs_8_), channel_id=1, source_target_pairs={{0,1},{1,0},{2,3},{3,2},{4,5},{5,4},{6,7},{7,6},{8,9},{9,8},{10,11... | collective-permute-start | bytes 1179656 | tf_op jit(solution)/shard_map/ppermute | solution.py:256
  18.3 2.1 %collective-permute-start.3 = (bf16[8,16,640]{2,1,0:T(8,128)(2,1)S(1)}, bf16[8,16,640]{2,1,0:T(8,128)(2,1)S(1)}, u32[]{:S(2)}, u32[]{:S(2)}) collective-permute-start(bf16[8,16,640]{2,1,0:T(8,128)(2,1)S(1)} %all-to-all-done.refs_4_), channel_id=1, source_target_pairs={{0,1},{1,0},{2,3},{3,2},{4,5},{5,4},{6,7},{7,6},{8,9},{9,8},{10,11... | collective-permute-start | bytes 491528 | tf_op jit(solution)/shard_map/ppermute | solution.py:256
  18.8 1.6 %collective-permute-start.6 = (bf16[128,512]{1,0:T(8,128)(2,1)S(1)}, bf16[128,512]{1,0:T(8,128)(2,1)S(1)}, u32[]{:S(2)}, u32[]{:S(2)}) collective-permute-start(bf16[128,512]{1,0:T(8,128)(2,1)S(1)} %collective-permute-done.1.refs_12_), channel_id=1, source_target_pairs={{0,1},{1,0},{2,3},{3,2},{4,5},{5,4},{6,7},{7,6},{8,9},{9,8},{10,11... | collective-permute-start | bytes 393224 | tf_op jit(solution)/shard_map/ppermute | solution.py:256
  18.9 11.7 %collective-permute-start.9 = (bf16[3,128,512]{2,1,0:T(8,128)(2,1)}, bf16[3,128,512]{2,1,0:T(8,128)(2,1)S(1)}, u32[]{:S(2)}, u32[]{:S(2)}) collective-permute-start(bf16[3,128,512]{2,1,0:T(8,128)(2,1)} %get-tuple-element.31.refs_3_), channel_id=1, source_target_pairs={{0,2},{2,0},{1,3},{3,1},{4,6},{6,4},{5,7},{7,5},{8,10},{10,8},{9,1... | collective-permute-start | bytes 1179656 | tf_op jit(solution)/shard_map/ppermute | solution.py:248
  20.2 10.4 %collective-permute-start.8 = (bf16[3,128,512]{2,1,0:T(8,128)(2,1)}, bf16[3,128,512]{2,1,0:T(8,128)(2,1)S(1)}, u32[]{:S(2)}, u32[]{:S(2)}) collective-permute-start(bf16[3,128,512]{2,1,0:T(8,128)(2,1)} %get-tuple-element.31.refs_3_), channel_id=1, source_target_pairs={{0,1},{1,0},{2,3},{3,2},{4,5},{5,4},{6,7},{7,6},{8,9},{9,8},{10,11... | collective-permute-start | bytes 1179656 | tf_op jit(solution)/shard_map/ppermute | solution.py:256
  20.5 11.8 %copy-start = (bf16[384,512]{1,0:T(8,128)(2,1)S(1)}, bf16[384,512]{1,0:T(8,128)(2,1)}, u32[]{:S(2)}) copy-start(bf16[384,512]{1,0:T(8,128)(2,1)} %refs_0_.3) | copy-start | bytes 1179652
  20.5 11.8 %copy-start.1 = (bf16[3,128,512]{2,1,0:T(8,128)(2,1)S(1)}, bf16[3,128,512]{2,1,0:T(8,128)(2,1)}, u32[]{:S(2)}) copy-start(bf16[3,128,512]{2,1,0:T(8,128)(2,1)} %get-tuple-element.31.refs_3_) | copy-start | bytes 1179652
  20.5 11.8 %copy-start.2 = (f32[512]{0:T(512)S(1)}, f32[512]{0:T(512)}, u32[]{:S(2)}) copy-start(f32[512]{0:T(512)} %param.32) | copy-start | bytes 6148
  20.5 11.8 %copy-start.3 = (f32[512]{0:T(512)S(1)}, f32[512]{0:T(512)}, u32[]{:S(2)}) copy-start(f32[512]{0:T(512)} %param.33) | copy-start | bytes 6148
  20.5 11.8 %copy-start.4 = (f32[512]{0:T(512)S(1)}, f32[512]{0:T(512)}, u32[]{:S(2)}) copy-start(f32[512]{0:T(512)} %param.34) | copy-start | bytes 6148
  20.5 11.8 %copy-start.5 = (f32[512]{0:T(512)S(1)}, f32[512]{0:T(512)}, u32[]{:S(2)}) copy-start(f32[512]{0:T(512)} %param.35) | copy-start | bytes 6148
  29.4 1.8 %collective-permute-start.7 = (bf16[384,512]{1,0:T(8,128)(2,1)S(1)}, bf16[384,512]{1,0:T(8,128)(2,1)S(1)}, u32[]{:S(2)}, u32[]{:S(2)}) collective-permute-start(bf16[384,512]{1,0:T(8,128)(2,1)S(1)} %get-tuple-element.30.refs_1_), channel_id=1, source_target_pairs={{0,1},{1,0},{2,3},{3,2},{4,5},{5,4},{6,7},{7,6},{8,9},{9,8},{10,11... | collective-permute-start | bytes 1179656 | tf_op jit(solution)/shard_map/ppermute | solution.py:514
  30.6 1.7 %collective-permute-start.10 = (bf16[3,128,512]{2,1,0:T(8,128)(2,1)S(1)}, bf16[3,128,512]{2,1,0:T(8,128)(2,1)S(1)}, u32[]{:S(2)}, u32[]{:S(2)}) collective-permute-start(bf16[3,128,512]{2,1,0:T(8,128)(2,1)S(1)} %collective-permute-done.9.refs_5_), channel_id=1, source_target_pairs={{0,1},{1,0},{2,3},{3,2},{4,5},{5,4},{6,7},{7,6},{8,9},{9,8},{10,11... | collective-permute-start | bytes 1179656 | tf_op jit(solution)/shard_map/ppermute | solution.py:256

commit v23 on v21

--- a/solution.py
+++ b/solution.py
@@ -70,7 +70,7 @@
 
 def pick_kernel(part_count, near_cap, far_cap, far_ref, near_ref, latent_ref, out_ref, picked):
     me, sub, subs = my_part(), lax.axis_index("sub"), lax.axis_size("sub")
-    half = near_cap // subs
+    half, width = near_cap // subs, latent_ref.shape[1]
     columns = [as_columns(near_ref[0])]
     tile_place = lax.broadcasted_iota(jnp.int32, (tile_rows, lanes), 0)
     far = as_columns(far_ref[0, 0:1])
@@ -79,23 +79,27 @@
     for part in range(part_count):
         columns.append(jnp.where(tile_place == 0, far[part : part + 1], -1))
     hot = one_hot(jnp.concatenate(columns, axis=0), latent_ref.shape[0])
-    picked[...] = jnp.dot(hot, latent_ref[...], preferred_element_type=f32).astype(bf16)
+    rows = jnp.dot(hot, latent_ref[...], preferred_element_type=f32)
+    far_start = len(near_offsets) * near_cap
+    picked[...] = rows[:far_start].astype(bf16)
     for which, offset in enumerate(near_offsets):
         target = lax.rem(me + (offset + part_count), part_count)
         start = pl.multiple_of(which * near_cap + sub * half, half)
-        out_ref[target, :half] = picked[pl.ds(start, half)]
-    far_start = len(near_offsets) * near_cap
+        out_ref[target, :, :width] = picked[pl.ds(start, half)]
     for part in range(part_count):
         spot = far_start + part * tile_rows
-        out_ref[part, half:] = picked[spot : spot + tile_rows][:1]
+        far_row = rows[spot : spot + 1]
+        pieces = [far_row[:, at : at + lanes] for at in range(0, width, lanes)]
+        pieces.append(jnp.zeros((half - len(pieces), lanes), f32))
+        out_ref[part, :, width:] = jnp.concatenate(pieces, axis=0).astype(bf16)
 
 
 def exchange_halves(node_latent, near_rows, far_rows, part_count, earlier):
     near_cap, far_cap = near_rows.shape[2], far_rows.shape[2]
     subs = lax.axis_size("sub")
     width = node_latent.shape[1]
-    block = (part_count, near_cap // subs + 1, width)
-    picks = len(near_offsets) * near_cap + part_count * tile_rows
+    block = (part_count, near_cap // subs, width + lanes)
+    picks = len(near_offsets) * near_cap
     blocks = pl.pallas_call(
         functools.partial(pick_kernel, part_count, near_cap, far_cap),
         out_shape=pltpu.HBM(block, bf16),
@@ -187,7 +191,7 @@
 
 
 def place_halo(halo, part_count, near_cap, halved, got):
-    subs = lax.axis_size("sub")
+    subs, width = lax.axis_size("sub"), halo.shape[1]
     far_start = len(near_offsets) * near_cap
     used = far_start
     if halved:
@@ -197,12 +201,15 @@
             for turn in range(subs):
                 owner = wrap(lax.axis_index("sub") - turn, subs)
                 start = pl.multiple_of(which * near_cap + owner * half, half)
-                halo[pl.ds(start, half)] = got[turn][origin, :half]
-        far = [got[turn][part, half:] for part in range(part_count) for turn in range(subs)]
+                halo[pl.ds(start, half)] = got[turn][origin, :, :width]
+        far = []
+        for part in range(part_count):
+            for turn in range(subs):
+                tile = got[turn][part, :, width:].astype(f32)
+                pieces = [tile[at : at + 1] for at in range(width // lanes)]
+                far.append(jnp.concatenate(pieces, axis=1))
         used += len(far)
-        halo[far_start:used] = jnp.concatenate(
-            [row.astype(f32) for row in far], axis=0
-        ).astype(bf16)
+        halo[far_start:used] = jnp.concatenate(far, axis=0).astype(bf16)
     else:
         for rows in got:
             start = used - far_start if rows is not got[-1] else far_start

time: 35.3 us -> 35.7 us (1.011)
  waiting for transfers between devices: 6.4 us -> 3.84 us
  local copies, waits for them, and re-layouts: 0.03 us -> 1.57 us
  starting transfers between devices: 11.8 us -> 13.3 us
    unnamed x10 -> x14, local copies, waits for them, and re-layouts: 0.03 us -> 1.57 us
    ppermute x3, waiting for transfers between devices: 3.15 us -> 2.06 us  [from_feats(): lax.ppermute(weight, 'feat', [(at, (at + shift) % feats) for at in range(...]
    ppermute x7, waiting for transfers between devices: 1.45 us -> 0.58 us  [from_subs(): lax.ppermute(piece, 'sub', [(at, (at + turn) % subs) for at in range(subs)])]
    all_to_all x1, waiting for transfers between devices: 0.84 us -> 0.01 us  [exchange_halves(): lax.all_to_all(blocks, ('region', 'feat'), split_axis=0, concat_axis=0, t...]
    ppermute x7, starting transfers between devices: 0.75 us -> 1.42 us  [from_subs(): lax.ppermute(piece, 'sub', [(at, (at + turn) % subs) for at in range(subs)])]
    ppermute x3, starting transfers between devices: 6 us -> 6.56 us  [from_feats(): lax.ppermute(weight, 'feat', [(at, (at + shift) % feats) for at in range(...]
  transfers between devices with their start and end apart: 12 -> 12, of which waited for: 6 -> 3; matrix products, arithmetic and copies ran while one was open for 0% -> 0% of each run, Pallas kernels for 40% -> 40%
where the time goes in v23:
time: 35.7 us; the launch traced here: 35.4 us
  Pallas kernels  16 us (45%)
  starting transfers between devices  13.3 us (37%)
  waiting for transfers between devices  3.84 us (11%)
  local copies, waits for them, and re-layouts  1.57 us (4%)
  between operations  0.71 us (2%)
    pallas_call x1, Pallas kernels, shards(): pl.pallas_call(functools.partial(edge_kernel, pieces_count, len(got), par...  8.73 us
    ppermute x3, starting transfers between devices, from_feats(): lax.ppermute(weight, 'feat', [(at, (at + shift) % feats) for at in range(...  6.56 us
    all_to_all x1, starting transfers between devices, exchange_halves(): lax.all_to_all(blocks, ('region', 'feat'), split_axis=0, concat_axis=0, t...  4.88 us
    pallas_call x1, Pallas kernels, shards(): pl.pallas_call(functools.partial(gather_kernel, near_cap, far_cap, halved...  3.22 us
    pallas_call x1, Pallas kernels, exchange_halves(): pl.pallas_call(functools.partial(pick_kernel, part_count, near_cap, far_c...  2.07 us
    ppermute x3, waiting for transfers between devices, from_feats(): lax.ppermute(weight, 'feat', [(at, (at + shift) % feats) for at in range(...  2.06 us
    pallas_call x1, Pallas kernels, shards(): pl.pallas_call(functools.partial(node_kernel, pieces_count), out_shape=ja...  2.01 us
    unnamed x14, local copies, waits for them, and re-layouts  1.57 us
  transfers between devices with their start and end apart: 12, of which 3 were waited for; matrix products, arithmetic and copies ran while one was open for 0% of the time, Pallas kernels for 40%

profile of v23, /device:TPU:0, one launch (start us, length us, event | category | flops | bytes accessed | tf_op | source)
XLA Modules:
  0.0 35.4 jit_solution(12638637570045677163)
XLA Ops:
  0.6 0.5 %collective-permute-start.2 = (bf16[128,512]{1,0:T(8,128)(2,1)}, bf16[128,512]{1,0:T(8,128)(2,1)S(1)}, u32[]{:S(2)}, u32[]{:S(2)}) collective-permute-start(bf16[128,512]{1,0:T(8,128)(2,1)} %refs_10_.1), channel_id=1, source_target_pairs={{0,1},{1,0},{2,3},{3,2},{4,5},{5,4},{6,7},{7,6},{8,9},{9,8},{10,11... | collective-permute-start | bytes 393224 | tf_op jit(solution)/shard_map/ppermute | solution.py:249
  1.1 2.6 %collective-permute-start = (bf16[3,128,512]{2,1,0:T(8,128)(2,1)}, bf16[3,128,512]{2,1,0:T(8,128)(2,1)}, u32[]{:S(2)}, u32[]{:S(2)}) collective-permute-start(bf16[3,128,512]{2,1,0:T(8,128)(2,1)} %refs_6_.1), channel_id=1, source_target_pairs={{0,2},{2,0},{1,3},{3,1},{4,6},{6,4},{5,7},{7,5},{8,10},{10,8},{9,1... | collective-permute-start | bytes 1179656 | tf_op jit(solution)/shard_map/ppermute | solution.py:241
  3.7 2.1 %pick_halo.1 = bf16[8,16,640]{2,1,0:T(8,128)(2,1)} custom-call(s32[1,2,8]{2,1,0:T(2,128)} %bitcast.18, s32[1,4,32]{2,1,0:T(4,128)} %near_ref.1, bf16[384,512]{1,0:T(8,128)(2,1)} %refs_0_.3), custom_call_target="tpu_custom_call" | custom-call | tf_op jit(solution)/shard_map/pick_halo/pallas_call | solution.py:103
  5.8 0.0 collective-permute-done.2.refs_11_
  5.8 4.9 %all-to-all-start = ((bf16[8,16,640]{2,1,0:T(8,128)(2,1)}), bf16[8,16,640]{2,1,0:T(8,128)(2,1)S(1)}, u32[]{:S(2)}, u32[]{:S(2)}) async-start(bf16[8,16,640]{2,1,0:T(8,128)(2,1)} %pick_halo.1), calls=%async_computation | async-start | bytes 327680 | tf_op jit(solution)/shard_map/all_to_all | solution.py:114
  10.7 2.0 %collective-permute-start.1 = (bf16[128,512]{1,0:T(8,128)(2,1)}, bf16[128,512]{1,0:T(8,128)(2,1)S(1)}, u32[]{:S(2)}, u32[]{:S(2)}) collective-permute-start(bf16[128,512]{1,0:T(8,128)(2,1)} %refs_10_.1), channel_id=1, source_target_pairs={{0,2},{2,0},{1,3},{3,1},{4,6},{6,4},{5,7},{7,5},{8,10},{10,8},{9,1... | collective-permute-start | bytes 393224 | tf_op jit(solution)/shard_map/ppermute | solution.py:241
  12.7 3.2 %gather_latents.1 = (bf16[768,1792]{1,0:T(8,128)(2,1)S(1)}, bf16[768,1280]{1,0:T(8,128)(2,1)}, bf16[3,128,512]{2,1,0:T(8,128)(2,1)S(1)}) custom-call(s32[12,128]{1,0:T(8,128)} %bitcast.15, s32[12,128]{1,0:T(8,128)} %bitcast.16, bf16[384,512]{1,0:T(8,128)(2,1)} %refs_0_.3, bf16[2,128,512]{2,1,0:T(8,128)(2,1)} %node_in_ref.1, bf16[128,512]{1,0:T(8,128)(2,1)} %node_out_ref.1, ...), custom_call_target="tpu_custom_call" | custom-call | tf_op jit(solution)/shard_map/gather_latents/pallas_call | solution.py:437
  15.9 2.1 %collective-permute-done.1.refs_12_ = bf16[128,512]{1,0:T(8,128)(2,1)S(1)} collective-permute-done((bf16[128,512]{1,0:T(8,128)(2,1)}, bf16[128,512]{1,0:T(8,128)(2,1)S(1)}, u32[]{:S(2)}, u32[]{:S(2)}) %collective-permute-start.1) | collective-permute-done | bytes 131104 | tf_op jit(solution)/shard_map/ppermute | solution.py:241
  18.0 0.7 %copy-done.5 = bf16[128,512]{1,0:T(8,128)(2,1)} copy-done((bf16[128,512]{1,0:T(8,128)(2,1)}, bf16[128,512]{1,0:T(8,128)(2,1)S(1)}, u32[]{:S(2)}) %copy-start.5) | copy-done | bytes 131096
  18.6 0.0 collective-permute-done.refs_8_
  18.6 0.0 all-to-all-done.refs_4_
  18.6 0.5 %collective-permute-start.3 = (bf16[8,16,640]{2,1,0:T(8,128)(2,1)S(1)}, bf16[8,16,640]{2,1,0:T(8,128)(2,1)S(1)}, u32[]{:S(2)}, u32[]{:S(2)}) collective-permute-start(bf16[8,16,640]{2,1,0:T(8,128)(2,1)S(1)} %all-to-all-done.refs_4_), channel_id=1, source_target_pairs={{0,1},{1,0},{2,3},{3,2},{4,5},{5,4},{6,7},{7,6},{8,9},{9,8},{10,11... | collective-permute-start | bytes 491528 | tf_op jit(solution)/shard_map/ppermute | solution.py:249
  19.2 0.1 collective-permute-start.6
  19.2 2.0 %collective-permute-start.9 = (bf16[3,128,512]{2,1,0:T(8,128)(2,1)S(1)}, bf16[3,128,512]{2,1,0:T(8,128)(2,1)S(1)}, u32[]{:S(2)}, u32[]{:S(2)}) collective-permute-start(bf16[3,128,512]{2,1,0:T(8,128)(2,1)S(1)} %get-tuple-element.27.refs_3_), channel_id=1, source_target_pairs={{0,2},{2,0},{1,3},{3,1},{4,6},{6,4},{5,7},{7,5},{8,10},{10,8},{9,1... | collective-permute-start | bytes 1179656 | tf_op jit(solution)/shard_map/ppermute | solution.py:241
  21.2 0.0 collective-permute-done.4.refs_7_
  21.2 0.2 collective-permute-start.8
  21.4 0.9 %copy-done.6 = bf16[128,512]{1,0:T(8,128)(2,1)S(1)} copy-done((bf16[128,512]{1,0:T(8,128)(2,1)S(1)}, bf16[128,512]{1,0:T(8,128)(2,1)}, u32[]{:S(2)}) %copy-start.6) | copy-done | bytes 131096
  22.3 0.0 copy-start.4
  22.3 8.7 %edge_update.1 = (bf16[1536,512]{1,0:T(8,128)(2,1)}, bf16[384,512]{1,0:T(8,128)(2,1)S(1)}) custom-call(bf16[1536,512]{1,0:T(8,128)(2,1)} %refs_0_.2, bf16[768,1280]{1,0:T(8,128)(2,1)} %get-tuple-element.19.refs_1_, s32[12,128]{1,0:T(8,128)} %bitcast.17, bf16[768,1792]{1,0:T(8,128)(2,1)S(1)} %get-tuple-element.20.refs_3_, ...), custom_call_target="tpu_custom_call" | custom-call | flops 3825205248 | bytes 6291456 | tf_op jit(solution)/shard_map/edge_update/pallas_call | solution.py:485
  31.0 0.4 %collective-permute-start.7 = (bf16[384,512]{1,0:T(8,128)(2,1)S(1)}, bf16[384,512]{1,0:T(8,128)(2,1)S(1)}, u32[]{:S(2)}, u32[]{:S(2)}) collective-permute-start(bf16[384,512]{1,0:T(8,128)(2,1)S(1)} %get-tuple-element.26.refs_1_), channel_id=1, source_target_pairs={{0,1},{1,0},{2,3},{3,2},{4,5},{5,4},{6,7},{7,6},{8,9},{9,8},{10,11... | collective-permute-start | bytes 1179656 | tf_op jit(solution)/shard_map/ppermute | solution.py:519
  31.5 0.2 collective-permute-start.10
  31.6 1.2 %collective-permute-done.7.refs_2_ = bf16[384,512]{1,0:T(8,128)(2,1)S(1)} collective-permute-done((bf16[384,512]{1,0:T(8,128)(2,1)S(1)}, bf16[384,512]{1,0:T(8,128)(2,1)S(1)}, u32[]{:S(2)}, u32[]{:S(2)}) %collective-permute-start.7) | collective-permute-done | bytes 393248 | tf_op jit(solution)/shard_map/ppermute | solution.py:519
  32.8 0.6 %collective-permute-done.10.refs_6_ = bf16[3,128,512]{2,1,0:T(8,128)(2,1)S(1)} collective-permute-done((bf16[3,128,512]{2,1,0:T(8,128)(2,1)S(1)}, bf16[3,128,512]{2,1,0:T(8,128)(2,1)S(1)}, u32[]{:S(2)}, u32[]{:S(2)}) %collective-permute-start.10) | collective-permute-done | bytes 393248 | tf_op jit(solution)/shard_map/ppermute | solution.py:249
  33.4 2.0 %node_update.1 = bf16[384,512]{1,0:T(8,128)(2,1)} custom-call(bf16[384,512]{1,0:T(8,128)(2,1)S(1)} %copy-done, bf16[384,512]{1,0:T(8,128)(2,1)S(1)} %get-tuple-element.26.refs_1_, bf16[384,512]{1,0:T(8,128)(2,1)S(1)} %collective-permute-done.7.refs_2_, bf16[3,128,512]{2,1,0:T(8,128)(2,1)S(1)} %get-tuple-element.27.refs_3_, ...), custom_call_target="tpu_custom_call" | custom-call | flops 603979776 | bytes 1966080 | tf_op jit(solution)/shard_map/node_update/pallas_call | solution.py:522
  (18 shorter events, 0.0 us)
Async XLA Ops:
  0.6 5.2 %collective-permute-start.2 = (bf16[128,512]{1,0:T(8,128)(2,1)}, bf16[128,512]{1,0:T(8,128)(2,1)S(1)}, u32[]{:S(2)}, u32[]{:S(2)}) collective-permute-start(bf16[128,512]{1,0:T(8,128)(2,1)} %refs_10_.1), channel_id=1, source_target_pairs={{0,1},{1,0},{2,3},{3,2},{4,5},{5,4},{6,7},{7,6},{8,9},{9,8},{10,11... | collective-permute-start | bytes 393224 | tf_op jit(solution)/shard_map/ppermute | solution.py:249
  1.1 17.5 %collective-permute-start = (bf16[3,128,512]{2,1,0:T(8,128)(2,1)}, bf16[3,128,512]{2,1,0:T(8,128)(2,1)}, u32[]{:S(2)}, u32[]{:S(2)}) collective-permute-start(bf16[3,128,512]{2,1,0:T(8,128)(2,1)} %refs_6_.1), channel_id=1, source_target_pairs={{0,2},{2,0},{1,3},{3,1},{4,6},{6,4},{5,7},{7,5},{8,10},{10,8},{9,1... | collective-permute-start | bytes 1179656 | tf_op jit(solution)/shard_map/ppermute | solution.py:241
  5.8 12.8 %all-to-all-start = ((bf16[8,16,640]{2,1,0:T(8,128)(2,1)}), bf16[8,16,640]{2,1,0:T(8,128)(2,1)S(1)}, u32[]{:S(2)}, u32[]{:S(2)}) async-start(bf16[8,16,640]{2,1,0:T(8,128)(2,1)} %pick_halo.1), calls=%async_computation | async-start | bytes 327680 | tf_op jit(solution)/shard_map/all_to_all | solution.py:114
  10.7 7.3 %collective-permute-start.1 = (bf16[128,512]{1,0:T(8,128)(2,1)}, bf16[128,512]{1,0:T(8,128)(2,1)S(1)}, u32[]{:S(2)}, u32[]{:S(2)}) collective-permute-start(bf16[128,512]{1,0:T(8,128)(2,1)} %refs_10_.1), channel_id=1, source_target_pairs={{0,2},{2,0},{1,3},{3,1},{4,6},{6,4},{5,7},{7,5},{8,10},{10,8},{9,1... | collective-permute-start | bytes 393224 | tf_op jit(solution)/shard_map/ppermute | solution.py:241
  12.7 8.5 %collective-permute-start.4 = (bf16[3,128,512]{2,1,0:T(8,128)(2,1)}, bf16[3,128,512]{2,1,0:T(8,128)(2,1)}, u32[]{:S(2)}, u32[]{:S(2)}) collective-permute-start(bf16[3,128,512]{2,1,0:T(8,128)(2,1)} %refs_6_.1), channel_id=1, source_target_pairs={{0,1},{1,0},{2,3},{3,2},{4,5},{5,4},{6,7},{7,6},{8,9},{9,8},{10,11... | collective-permute-start | bytes 1179656 | tf_op jit(solution)/shard_map/ppermute | solution.py:249
  18.0 0.7 %copy-start.5 = (bf16[128,512]{1,0:T(8,128)(2,1)}, bf16[128,512]{1,0:T(8,128)(2,1)S(1)}, u32[]{:S(2)}) copy-start(bf16[128,512]{1,0:T(8,128)(2,1)S(1)} %collective-permute-done.1.refs_12_) | copy-start | bytes 393220
  18.6 2.7 %collective-permute-start.5 = (bf16[3,128,512]{2,1,0:T(8,128)(2,1)}, bf16[3,128,512]{2,1,0:T(8,128)(2,1)S(1)}, u32[]{:S(2)}, u32[]{:S(2)}) collective-permute-start(bf16[3,128,512]{2,1,0:T(8,128)(2,1)} %collective-permute-done.refs_8_), channel_id=1, source_target_pairs={{0,1},{1,0},{2,3},{3,2},{4,5},{5,4},{6,7},{7,6},{8,9},{9,8},{10,11... | collective-permute-start | bytes 1179656 | tf_op jit(solution)/shard_map/ppermute | solution.py:249
  18.6 2.7 %collective-permute-start.3 = (bf16[8,16,640]{2,1,0:T(8,128)(2,1)S(1)}, bf16[8,16,640]{2,1,0:T(8,128)(2,1)S(1)}, u32[]{:S(2)}, u32[]{:S(2)}) collective-permute-start(bf16[8,16,640]{2,1,0:T(8,128)(2,1)S(1)} %all-to-all-done.refs_4_), channel_id=1, source_target_pairs={{0,1},{1,0},{2,3},{3,2},{4,5},{5,4},{6,7},{7,6},{8,9},{9,8},{10,11... | collective-permute-start | bytes 491528 | tf_op jit(solution)/shard_map/ppermute | solution.py:249
  19.2 2.2 %collective-permute-start.6 = (bf16[128,512]{1,0:T(8,128)(2,1)}, bf16[128,512]{1,0:T(8,128)(2,1)S(1)}, u32[]{:S(2)}, u32[]{:S(2)}) collective-permute-start(bf16[128,512]{1,0:T(8,128)(2,1)} %copy-done.5), channel_id=1, source_target_pairs={{0,1},{1,0},{2,3},{3,2},{4,5},{5,4},{6,7},{7,6},{8,9},{9,8},{10,11... | collective-permute-start | bytes 393224 | tf_op jit(solution)/shard_map/ppermute | solution.py:249
  19.2 12.2 %collective-permute-start.9 = (bf16[3,128,512]{2,1,0:T(8,128)(2,1)S(1)}, bf16[3,128,512]{2,1,0:T(8,128)(2,1)S(1)}, u32[]{:S(2)}, u32[]{:S(2)}) collective-permute-start(bf16[3,128,512]{2,1,0:T(8,128)(2,1)S(1)} %get-tuple-element.27.refs_3_), channel_id=1, source_target_pairs={{0,2},{2,0},{1,3},{3,1},{4,6},{6,4},{5,7},{7,5},{8,10},{10,8},{9,1... | collective-permute-start | bytes 1179656 | tf_op jit(solution)/shard_map/ppermute | solution.py:241
  21.2 10.4 %collective-permute-start.8 = (bf16[3,128,512]{2,1,0:T(8,128)(2,1)S(1)}, bf16[3,128,512]{2,1,0:T(8,128)(2,1)S(1)}, u32[]{:S(2)}, u32[]{:S(2)}) collective-permute-start(bf16[3,128,512]{2,1,0:T(8,128)(2,1)S(1)} %get-tuple-element.27.refs_3_), channel_id=1, source_target_pairs={{0,1},{1,0},{2,3},{3,2},{4,5},{5,4},{6,7},{7,6},{8,9},{9,8},{10,11... | collective-permute-start | bytes 1179656 | tf_op jit(solution)/shard_map/ppermute | solution.py:249
  21.4 0.9 %copy-start.6 = (bf16[128,512]{1,0:T(8,128)(2,1)S(1)}, bf16[128,512]{1,0:T(8,128)(2,1)}, u32[]{:S(2)}) copy-start(bf16[128,512]{1,0:T(8,128)(2,1)} %copy-done.5) | copy-start | bytes 393220
  22.3 11.1 %copy-start = (bf16[384,512]{1,0:T(8,128)(2,1)S(1)}, bf16[384,512]{1,0:T(8,128)(2,1)}, u32[]{:S(2)}) copy-start(bf16[384,512]{1,0:T(8,128)(2,1)} %refs_0_.3) | copy-start | bytes 1179652
  22.3 11.1 %copy-start.1 = (f32[512]{0:T(512)S(1)}, f32[512]{0:T(512)}, u32[]{:S(2)}) copy-start(f32[512]{0:T(512)} %param.32) | copy-start | bytes 6148
  22.3 11.1 %copy-start.2 = (f32[512]{0:T(512)S(1)}, f32[512]{0:T(512)}, u32[]{:S(2)}) copy-start(f32[512]{0:T(512)} %param.33) | copy-start | bytes 6148
  22.3 11.1 %copy-start.3 = (f32[512]{0:T(512)S(1)}, f32[512]{0:T(512)}, u32[]{:S(2)}) copy-start(f32[512]{0:T(512)} %param.34) | copy-start | bytes 6148
  22.3 11.1 %copy-start.4 = (f32[512]{0:T(512)S(1)}, f32[512]{0:T(512)}, u32[]{:S(2)}) copy-start(f32[512]{0:T(512)} %param.35) | copy-start | bytes 6148
  31.0 1.8 %collective-permute-start.7 = (bf16[384,512]{1,0:T(8,128)(2,1)S(1)}, bf16[384,512]{1,0:T(8,128)(2,1)S(1)}, u32[]{:S(2)}, u32[]{:S(2)}) collective-permute-start(bf16[384,512]{1,0:T(8,128)(2,1)S(1)} %get-tuple-element.26.refs_1_), channel_id=1, source_target_pairs={{0,1},{1,0},{2,3},{3,2},{4,5},{5,4},{6,7},{7,6},{8,9},{9,8},{10,11... | collective-permute-start | bytes 1179656 | tf_op jit(solution)/shard_map/ppermute | solution.py:519
  31.5 1.9 %collective-permute-start.10 = (bf16[3,128,512]{2,1,0:T(8,128)(2,1)S(1)}, bf16[3,128,512]{2,1,0:T(8,128)(2,1)S(1)}, u32[]{:S(2)}, u32[]{:S(2)}) collective-permute-start(bf16[3,128,512]{2,1,0:T(8,128)(2,1)S(1)} %collective-permute-done.9.refs_5_), channel_id=1, source_target_pairs={{0,1},{1,0},{2,3},{3,2},{4,5},{5,4},{6,7},{7,6},{8,9},{9,8},{10,11... | collective-permute-start | bytes 1179656 | tf_op jit(solution)/shard_map/ppermute | solution.py:249

commit v24 on v22

--- a/solution.py
+++ b/solution.py
@@ -369,7 +369,7 @@
 def node_kernel(pieces_count, *refs):
     latent_ref, own_ref, other_ref = refs[:3]
     pieces = refs[3 : 3 + pieces_count]
-    in_bias, out_bias, gain, offset, new_ref, weights = refs[3 + pieces_count :]
+    in_bias, out_bias, gain, offset, new_hbm, weights, made, sems = refs[3 + pieces_count :]
     width = latent_ref.shape[1]
     for piece, owner in zip(pieces, owners()):
         for which in range(piece.shape[0]):
@@ -383,9 +383,17 @@
     )
     hidden = silu(preact + in_bias[...]).astype(bf16)
     output = jnp.dot(hidden, weights[2 * width :], preferred_element_type=f32) + out_bias[...]
-    new_ref[...] = (
-        latent.astype(f32) + layer_norm(output, gain[...], offset[...])
-    ).astype(bf16)
+    third = latent.shape[0] // 3
+    copies = []
+    for part in range(3):
+        here = slice(part * third, (part + 1) * third)
+        normed = layer_norm(output[here], gain[...], offset[...])
+        made[here] = (latent[here].astype(f32) + normed).astype(bf16)
+        spot = pl.ds(part * third, third)
+        copies.append(pltpu.make_async_copy(made.at[spot], new_hbm.at[spot], sems.at[part]))
+        copies[-1].start()
+    for copy in copies:
+        copy.wait()
 
 
 def shards(
@@ -516,11 +524,13 @@
     rows = [value.reshape(1, -1) for value in (node_in_bias, node_out_bias, node_gain, node_offset)]
     node_new = pl.pallas_call(
         functools.partial(node_kernel, pieces_count),
-        out_shape=jax.ShapeDtypeStruct((node_count, width), bf16),
+        out_shape=pltpu.HBM((node_count, width), bf16),
         in_specs=[vmem] * (3 + pieces_count + 4),
-        out_specs=vmem,
+        out_specs=hbm,
         scratch_shapes=[
             pltpu.VMEM((3 * width, width), bf16),
+            pltpu.VMEM((node_count, width), bf16),
+            pltpu.SemaphoreType.DMA((3,)),
         ],
         compiler_params=pltpu.CompilerParams(vmem_limit_bytes=grant),
         cost_estimate=pl.CostEstimate(

time: 34.6 us -> 34.6 us (level)
  no operation moved by 1% of the time
where the time goes in v24:
time: 34.6 us; the launch traced here: 34.3 us
  Pallas kernels  17.6 us (51%)
  starting transfers between devices  12.4 us (36%)
  waiting for transfers between devices  3.41 us (10%)
  between operations  0.74 us (2%)
    pallas_call x1, Pallas kernels, shards(): pl.pallas_call(functools.partial(edge_kernel, pieces_count, len(got), par...  8.86 us
    ppermute x3, starting transfers between devices, from_feats(): lax.ppermute(weight, 'feat', [(at, (at + shift) % feats) for at in range(...  6.3 us
    all_to_all x1, starting transfers between devices, exchange_halves(): lax.all_to_all(blocks, ('region', 'feat'), split_axis=0, concat_axis=0, t...  4.88 us
    pallas_call x1, Pallas kernels, shards(): pl.pallas_call(functools.partial(gather_kernel, near_cap, far_cap, halved...  4.77 us
    pallas_call x1, Pallas kernels, exchange_halves(): pl.pallas_call(functools.partial(pick_kernel, part_count, near_cap, far_c...  2.07 us
    pallas_call x1, Pallas kernels, shards(): pl.pallas_call(functools.partial(node_kernel, pieces_count), out_shape=pl...  1.94 us
    ppermute x3, waiting for transfers between devices, from_feats(): lax.ppermute(weight, 'feat', [(at, (at + shift) % feats) for at in range(...  1.56 us
    ppermute x7, waiting for transfers between devices, from_subs(): lax.ppermute(piece, 'sub', [(at, (at + turn) % subs) for at in range(subs)])  1.23 us
  transfers between devices with their start and end apart: 12, of which 5 were waited for; matrix products, arithmetic and copies ran while one was open for 0% of the time, Pallas kernels for 46%

profile of v24, /device:TPU:0, one launch (start us, length us, event | category | flops | bytes accessed | tf_op | source)
XLA Modules:
  0.0 34.3 jit_solution(9144340239705458442)
XLA Ops:
  0.6 3.0 %collective-permute-start = (bf16[3,128,512]{2,1,0:T(8,128)(2,1)}, bf16[3,128,512]{2,1,0:T(8,128)(2,1)}, u32[]{:S(2)}, u32[]{:S(2)}) collective-permute-start(bf16[3,128,512]{2,1,0:T(8,128)(2,1)} %refs_6_.1), channel_id=1, source_target_pairs={{0,2},{2,0},{1,3},{3,1},{4,6},{6,4},{5,7},{7,5},{8,10},{10,8},{9,1... | collective-permute-start | bytes 1179656 | tf_op jit(solution)/shard_map/ppermute | solution.py:248
  3.6 2.1 %pick_halo.1 = bf16[8,16,640]{2,1,0:T(8,128)(2,1)} custom-call(s32[1,2,8]{2,1,0:T(2,128)} %bitcast.17, s32[1,4,32]{2,1,0:T(4,128)} %near_ref.1, bf16[384,512]{1,0:T(8,128)(2,1)} %refs_0_.3), custom_call_target="tpu_custom_call" | custom-call | tf_op jit(solution)/shard_map/pick_halo/pallas_call | solution.py:105
  5.7 4.9 %all-to-all-start = ((bf16[8,16,640]{2,1,0:T(8,128)(2,1)}), bf16[8,16,640]{2,1,0:T(8,128)(2,1)S(1)}, u32[]{:S(2)}, u32[]{:S(2)}) async-start(bf16[8,16,640]{2,1,0:T(8,128)(2,1)} %pick_halo.1), calls=%async_computation | async-start | bytes 327680 | tf_op jit(solution)/shard_map/all_to_all | solution.py:115
  10.6 0.0 collective-permute-start.2
  10.6 2.0 %collective-permute-start.1 = (bf16[128,512]{1,0:T(8,128)(2,1)}, bf16[128,512]{1,0:T(8,128)(2,1)S(1)}, u32[]{:S(2)}, u32[]{:S(2)}) collective-permute-start(bf16[128,512]{1,0:T(8,128)(2,1)} %refs_10_.1), channel_id=1, source_target_pairs={{0,2},{2,0},{1,3},{3,1},{4,6},{6,4},{5,7},{7,5},{8,10},{10,8},{9,1... | collective-permute-start | bytes 393224 | tf_op jit(solution)/shard_map/ppermute | solution.py:248
  12.6 0.2 collective-permute-start.4
  12.8 4.8 %gather_latents.1 = (bf16[512,1792]{1,0:T(8,128)(2,1)S(1)}, bf16[1024,1280]{1,0:T(8,128)(2,1)}, bf16[384,1536]{1,0:T(8,128)(2,1)S(1)}, bf16[3,128,512]{2,1,0:T(8,128)(2,1)}) custom-call(s32[12,128]{1,0:T(8,128)} %bitcast.15, s32[12,128]{1,0:T(8,128)} %bitcast.16, bf16[384,512]{1,0:T(8,128)(2,1)} %refs_0_.3, bf16[2,128,512]{2,1,0:T(8,128)(2,1)} %node_in_ref.1, ...), custom_call_target="tpu_custom_call" | custom-call | tf_op jit(solution)/shard_map/gather_latents/pallas_call | solution.py:442
  17.6 0.7 %collective-permute-done.1.refs_12_ = bf16[128,512]{1,0:T(8,128)(2,1)S(1)} collective-permute-done((bf16[128,512]{1,0:T(8,128)(2,1)}, bf16[128,512]{1,0:T(8,128)(2,1)S(1)}, u32[]{:S(2)}, u32[]{:S(2)}) %collective-permute-start.1) | collective-permute-done | bytes 131104 | tf_op jit(solution)/shard_map/ppermute | solution.py:248
  18.3 0.5 %collective-permute-start.3 = (bf16[8,16,640]{2,1,0:T(8,128)(2,1)S(1)}, bf16[8,16,640]{2,1,0:T(8,128)(2,1)S(1)}, u32[]{:S(2)}, u32[]{:S(2)}) collective-permute-start(bf16[8,16,640]{2,1,0:T(8,128)(2,1)S(1)} %all-to-all-done.refs_4_), channel_id=1, source_target_pairs={{0,1},{1,0},{2,3},{3,2},{4,5},{5,4},{6,7},{7,6},{8,9},{9,8},{10,11... | collective-permute-start | bytes 491528 | tf_op jit(solution)/shard_map/ppermute | solution.py:256
  18.8 0.1 collective-permute-start.6
  18.9 1.3 %collective-permute-start.9 = (bf16[3,128,512]{2,1,0:T(8,128)(2,1)}, bf16[3,128,512]{2,1,0:T(8,128)(2,1)S(1)}, u32[]{:S(2)}, u32[]{:S(2)}) collective-permute-start(bf16[3,128,512]{2,1,0:T(8,128)(2,1)} %get-tuple-element.31.refs_3_), channel_id=1, source_target_pairs={{0,2},{2,0},{1,3},{3,1},{4,6},{6,4},{5,7},{7,5},{8,10},{10,8},{9,1... | collective-permute-start | bytes 1179656 | tf_op jit(solution)/shard_map/ppermute | solution.py:248
  20.2 0.2 collective-permute-start.8
  20.3 0.1 collective-permute-done.6.refs_13_
  20.5 0.0 copy-start.1
  20.5 0.0 copy-start.2
  20.5 0.0 copy-start.3
  20.5 0.0 copy-start.4
  20.5 0.0 copy-start.5
  20.5 8.9 %edge_update.1 = (bf16[1536,512]{1,0:T(8,128)(2,1)}, bf16[384,512]{1,0:T(8,128)(2,1)S(1)}) custom-call(bf16[1536,512]{1,0:T(8,128)(2,1)} %refs_0_.2, bf16[1024,1280]{1,0:T(8,128)(2,1)} %get-tuple-element.22.refs_1_, bf16[384,1536]{1,0:T(8,128)(2,1)S(1)} %get-tuple-element.23.refs_2_, bf16[512,1792]{1,0:T(8,128)(2,1)S(1)} %get-tuple-element.24.refs_3_, ...), custom_call_target="tpu_custom_call" | custom-call | flops 3825205248 | bytes 6291456 | tf_op jit(solution)/shard_map/edge_update/pallas_call | solution.py:491
  29.4 0.3 collective-permute-start.7
  29.7 0.9 %collective-permute-done.9.refs_5_ = bf16[3,128,512]{2,1,0:T(8,128)(2,1)S(1)} collective-permute-done((bf16[3,128,512]{2,1,0:T(8,128)(2,1)}, bf16[3,128,512]{2,1,0:T(8,128)(2,1)S(1)}, u32[]{:S(2)}, u32[]{:S(2)}) %collective-permute-start.9) | collective-permute-done | bytes 393248 | tf_op jit(solution)/shard_map/ppermute | solution.py:248
  30.6 0.6 %collective-permute-done.7.refs_2_ = bf16[384,512]{1,0:T(8,128)(2,1)S(1)} collective-permute-done((bf16[384,512]{1,0:T(8,128)(2,1)S(1)}, bf16[384,512]{1,0:T(8,128)(2,1)S(1)}, u32[]{:S(2)}, u32[]{:S(2)}) %collective-permute-start.7) | collective-permute-done | bytes 393248 | tf_op jit(solution)/shard_map/ppermute | solution.py:522
  31.2 1.1 %collective-permute-done.10.refs_6_ = bf16[3,128,512]{2,1,0:T(8,128)(2,1)S(1)} collective-permute-done((bf16[3,128,512]{2,1,0:T(8,128)(2,1)S(1)}, bf16[3,128,512]{2,1,0:T(8,128)(2,1)S(1)}, u32[]{:S(2)}, u32[]{:S(2)}) %collective-permute-start.10) | collective-permute-done | bytes 393248 | tf_op jit(solution)/shard_map/ppermute | solution.py:256
  32.3 1.9 %node_update.1 = bf16[384,512]{1,0:T(8,128)(2,1)} custom-call(bf16[384,512]{1,0:T(8,128)(2,1)S(1)} %copy-done, bf16[384,512]{1,0:T(8,128)(2,1)S(1)} %get-tuple-element.30.refs_1_, bf16[384,512]{1,0:T(8,128)(2,1)S(1)} %collective-permute-done.7.refs_2_, bf16[3,128,512]{2,1,0:T(8,128)(2,1)S(1)} %copy-done.1, ...), custom_call_target="tpu_custom_call" | custom-call | flops 603979776 | bytes 1966080 | tf_op jit(solution)/shard_map/node_update/pallas_call | solution.py:525
  (16 shorter events, 0.0 us)
Async XLA Ops:
  0.6 17.7 %collective-permute-start = (bf16[3,128,512]{2,1,0:T(8,128)(2,1)}, bf16[3,128,512]{2,1,0:T(8,128)(2,1)}, u32[]{:S(2)}, u32[]{:S(2)}) collective-permute-start(bf16[3,128,512]{2,1,0:T(8,128)(2,1)} %refs_6_.1), channel_id=1, source_target_pairs={{0,2},{2,0},{1,3},{3,1},{4,6},{6,4},{5,7},{7,5},{8,10},{10,8},{9,1... | collective-permute-start | bytes 1179656 | tf_op jit(solution)/shard_map/ppermute | solution.py:248
  5.7 12.6 %all-to-all-start = ((bf16[8,16,640]{2,1,0:T(8,128)(2,1)}), bf16[8,16,640]{2,1,0:T(8,128)(2,1)S(1)}, u32[]{:S(2)}, u32[]{:S(2)}) async-start(bf16[8,16,640]{2,1,0:T(8,128)(2,1)} %pick_halo.1), calls=%async_computation | async-start | bytes 327680 | tf_op jit(solution)/shard_map/all_to_all | solution.py:115
  10.6 2.3 %collective-permute-start.2 = (bf16[128,512]{1,0:T(8,128)(2,1)}, bf16[128,512]{1,0:T(8,128)(2,1)S(1)}, u32[]{:S(2)}, u32[]{:S(2)}) collective-permute-start(bf16[128,512]{1,0:T(8,128)(2,1)} %refs_10_.1), channel_id=1, source_target_pairs={{0,1},{1,0},{2,3},{3,2},{4,5},{5,4},{6,7},{7,6},{8,9},{9,8},{10,11... | collective-permute-start | bytes 393224 | tf_op jit(solution)/shard_map/ppermute | solution.py:256
  10.6 7.7 %collective-permute-start.1 = (bf16[128,512]{1,0:T(8,128)(2,1)}, bf16[128,512]{1,0:T(8,128)(2,1)S(1)}, u32[]{:S(2)}, u32[]{:S(2)}) collective-permute-start(bf16[128,512]{1,0:T(8,128)(2,1)} %refs_10_.1), channel_id=1, source_target_pairs={{0,2},{2,0},{1,3},{3,1},{4,6},{6,4},{5,7},{7,5},{8,10},{10,8},{9,1... | collective-permute-start | bytes 393224 | tf_op jit(solution)/shard_map/ppermute | solution.py:248
  12.6 7.6 %collective-permute-start.4 = (bf16[3,128,512]{2,1,0:T(8,128)(2,1)}, bf16[3,128,512]{2,1,0:T(8,128)(2,1)}, u32[]{:S(2)}, u32[]{:S(2)}) collective-permute-start(bf16[3,128,512]{2,1,0:T(8,128)(2,1)} %refs_6_.1), channel_id=1, source_target_pairs={{0,1},{1,0},{2,3},{3,2},{4,5},{5,4},{6,7},{7,6},{8,9},{9,8},{10,11... | collective-permute-start | bytes 1179656 | tf_op jit(solution)/shard_map/ppermute | solution.py:256
  18.3 2.2 %collective-permute-start.5 = (bf16[3,128,512]{2,1,0:T(8,128)(2,1)}, bf16[3,128,512]{2,1,0:T(8,128)(2,1)S(1)}, u32[]{:S(2)}, u32[]{:S(2)}) collective-permute-start(bf16[3,128,512]{2,1,0:T(8,128)(2,1)} %collective-permute-done.refs_8_), channel_id=1, source_target_pairs={{0,1},{1,0},{2,3},{3,2},{4,5},{5,4},{6,7},{7,6},{8,9},{9,8},{10,11... | collective-permute-start | bytes 1179656 | tf_op jit(solution)/shard_map/ppermute | solution.py:256
  18.3 2.1 %collective-permute-start.3 = (bf16[8,16,640]{2,1,0:T(8,128)(2,1)S(1)}, bf16[8,16,640]{2,1,0:T(8,128)(2,1)S(1)}, u32[]{:S(2)}, u32[]{:S(2)}) collective-permute-start(bf16[8,16,640]{2,1,0:T(8,128)(2,1)S(1)} %all-to-all-done.refs_4_), channel_id=1, source_target_pairs={{0,1},{1,0},{2,3},{3,2},{4,5},{5,4},{6,7},{7,6},{8,9},{9,8},{10,11... | collective-permute-start | bytes 491528 | tf_op jit(solution)/shard_map/ppermute | solution.py:256
  18.8 1.6 %collective-permute-start.6 = (bf16[128,512]{1,0:T(8,128)(2,1)S(1)}, bf16[128,512]{1,0:T(8,128)(2,1)S(1)}, u32[]{:S(2)}, u32[]{:S(2)}) collective-permute-start(bf16[128,512]{1,0:T(8,128)(2,1)S(1)} %collective-permute-done.1.refs_12_), channel_id=1, source_target_pairs={{0,1},{1,0},{2,3},{3,2},{4,5},{5,4},{6,7},{7,6},{8,9},{9,8},{10,11... | collective-permute-start | bytes 393224 | tf_op jit(solution)/shard_map/ppermute | solution.py:256
  18.9 11.7 %collective-permute-start.9 = (bf16[3,128,512]{2,1,0:T(8,128)(2,1)}, bf16[3,128,512]{2,1,0:T(8,128)(2,1)S(1)}, u32[]{:S(2)}, u32[]{:S(2)}) collective-permute-start(bf16[3,128,512]{2,1,0:T(8,128)(2,1)} %get-tuple-element.31.refs_3_), channel_id=1, source_target_pairs={{0,2},{2,0},{1,3},{3,1},{4,6},{6,4},{5,7},{7,5},{8,10},{10,8},{9,1... | collective-permute-start | bytes 1179656 | tf_op jit(solution)/shard_map/ppermute | solution.py:248
  20.2 10.4 %collective-permute-start.8 = (bf16[3,128,512]{2,1,0:T(8,128)(2,1)}, bf16[3,128,512]{2,1,0:T(8,128)(2,1)S(1)}, u32[]{:S(2)}, u32[]{:S(2)}) collective-permute-start(bf16[3,128,512]{2,1,0:T(8,128)(2,1)} %get-tuple-element.31.refs_3_), channel_id=1, source_target_pairs={{0,1},{1,0},{2,3},{3,2},{4,5},{5,4},{6,7},{7,6},{8,9},{9,8},{10,11... | collective-permute-start | bytes 1179656 | tf_op jit(solution)/shard_map/ppermute | solution.py:256
  20.5 11.8 %copy-start = (bf16[384,512]{1,0:T(8,128)(2,1)S(1)}, bf16[384,512]{1,0:T(8,128)(2,1)}, u32[]{:S(2)}) copy-start(bf16[384,512]{1,0:T(8,128)(2,1)} %refs_0_.3) | copy-start | bytes 1179652
  20.5 11.8 %copy-start.1 = (bf16[3,128,512]{2,1,0:T(8,128)(2,1)S(1)}, bf16[3,128,512]{2,1,0:T(8,128)(2,1)}, u32[]{:S(2)}) copy-start(bf16[3,128,512]{2,1,0:T(8,128)(2,1)} %get-tuple-element.31.refs_3_) | copy-start | bytes 1179652
  20.5 11.8 %copy-start.2 = (f32[512]{0:T(512)S(1)}, f32[512]{0:T(512)}, u32[]{:S(2)}) copy-start(f32[512]{0:T(512)} %param.32) | copy-start | bytes 6148
  20.5 11.8 %copy-start.3 = (f32[512]{0:T(512)S(1)}, f32[512]{0:T(512)}, u32[]{:S(2)}) copy-start(f32[512]{0:T(512)} %param.33) | copy-start | bytes 6148
  20.5 11.8 %copy-start.4 = (f32[512]{0:T(512)S(1)}, f32[512]{0:T(512)}, u32[]{:S(2)}) copy-start(f32[512]{0:T(512)} %param.34) | copy-start | bytes 6148
  20.5 11.8 %copy-start.5 = (f32[512]{0:T(512)S(1)}, f32[512]{0:T(512)}, u32[]{:S(2)}) copy-start(f32[512]{0:T(512)} %param.35) | copy-start | bytes 6148
  29.4 1.8 %collective-permute-start.7 = (bf16[384,512]{1,0:T(8,128)(2,1)S(1)}, bf16[384,512]{1,0:T(8,128)(2,1)S(1)}, u32[]{:S(2)}, u32[]{:S(2)}) collective-permute-start(bf16[384,512]{1,0:T(8,128)(2,1)S(1)} %get-tuple-element.30.refs_1_), channel_id=1, source_target_pairs={{0,1},{1,0},{2,3},{3,2},{4,5},{5,4},{6,7},{7,6},{8,9},{9,8},{10,11... | collective-permute-start | bytes 1179656 | tf_op jit(solution)/shard_map/ppermute | solution.py:522
  30.6 1.7 %collective-permute-start.10 = (bf16[3,128,512]{2,1,0:T(8,128)(2,1)S(1)}, bf16[3,128,512]{2,1,0:T(8,128)(2,1)S(1)}, u32[]{:S(2)}, u32[]{:S(2)}) collective-permute-start(bf16[3,128,512]{2,1,0:T(8,128)(2,1)S(1)} %collective-permute-done.9.refs_5_), channel_id=1, source_target_pairs={{0,1},{1,0},{2,3},{3,2},{4,5},{5,4},{6,7},{7,6},{8,9},{9,8},{10,11... | collective-permute-start | bytes 1179656 | tf_op jit(solution)/shard_map/ppermute | solution.py:256
